TPU v7x, 32 devices: a whole 2x2x4 slice. The times are simulated.
32 devices in a mesh: blocks: 2 (over x), slab: 16 (over z, y, core).
Axes of the slice: x: 2, y: 2, z: 4, core: 2. Of those that a mesh axis runs over, the one named last changes fastest.
Arguments:
- estimate: float32 [64, 256, 128], P('blocks', 'slab'), parts along dimension 0, may hold values from 0.25 to 8, as said below
- raw_views: float32 [6, 64, 256, 128], P(None, 'blocks', 'slab'), parts along dimension 1, may hold values from 0.1 to 30, as said below
- psf_taps: float32 [6, 3, 31], replicated, may hold values from 0 to 1, as said below
Outputs:
- restored: float32 [64, 256, 128], P('blocks', 'slab'), parts along dimension 0
There are 2 independent parts, one for each index of `blocks`. A program takes and returns all parts, laid end to end along the dimension named above; an argument that names none is the same for every part. Nothing has to cross between parts.
Inputs may be any that keep to these rules, and one draw needn't show every extreme that they name: `estimate`: positive. `raw_views`: positive. `psf_taps`: every tap is positive, and each view's taps along each dimension sum to 1.
All inputs are finite; a program needn't handle non-finite values.
Results may differ from a plain program's by a relative error of at most 0.0001.
Values sent between devices are 32-bit elements; how exact they have to be, the bound alone decides.
No kernel may reach another device: no remote copies, remote signals or barrier semaphores. Data moves between devices by JAX's collectives and lax.ppermute only.
A program may use at most 64 MiB of HBM per device.

v0:
```python
import functools

import jax
import jax.numpy as jnp
import numpy as np
from jax import lax
from jax.experimental import pallas as pl
from jax.experimental.pallas import tpu as pltpu
from jax.sharding import PartitionSpec as P

F32 = jnp.float32
BF16 = jnp.bfloat16
VMEM = pltpu.MemorySpace.VMEM
SMEM = pltpu.MemorySpace.SMEM
FULL = pl.BlockSpec(memory_space=VMEM)
LIMIT = 56 * 1024 * 1024


def split(value):
    high = value.astype(BF16)
    low = (value - high.astype(F32)).astype(BF16)
    return high, low


def dot(a, b):
    return jnp.dot(a, b, preferred_element_type=F32)


def placed_row(taps, lane_of_tap, width):
    count = taps.shape[1]
    tap = lax.broadcasted_iota(jnp.int32, (count, width), 0)
    lane = lax.broadcasted_iota(jnp.int32, (count, width), 1)
    onehot = jnp.where(lane == lane_of_tap(tap), 1.0, 0.0).astype(F32)
    return jnp.dot(taps, onehot, precision=lax.Precision.HIGHEST, preferred_element_type=F32)


def slanted(row, height):
    full = jnp.broadcast_to(row, (height, row.shape[1]))
    return pltpu.roll(full, 0, 1, stride=1, stride_axis=0)


def weights_kernel(rows, taps_ref, *outs):
    views, _, count = taps_ref.shape
    margin = count // 2
    for flip in (False, True):
        wy, wx, wz = outs[3 * flip : 3 * flip + 3]
        order = (lambda k: count - 1 - k) if flip else (lambda k: k)
        out_rows = rows if flip else 3 * rows
        in_rows = out_rows + 2 * rows
        planes = wz.shape[1] // 8
        cols = wx.shape[1] // 2
        row_y = placed_row(taps_ref[:, 1, :], lambda k: order(k) + rows - margin, 256)
        high = row_y.astype(BF16).astype(F32)
        low = row_y - high
        row_y = high + pltpu.roll(high, in_rows, 1) + pltpu.roll(low, 2 * in_rows, 1)
        row_x = placed_row(taps_ref[:, 2, :], lambda k: lax.rem(margin - order(k) + 2 * cols, 2 * cols), 2 * cols)
        width_z = 16 * planes
        row_z = placed_row(
            taps_ref[:, 0, :], lambda k: lax.rem(8 * (order(k) - margin) + width_z, width_z), width_z
        )
        for v in range(views):
            band = slanted(row_y[v : v + 1], out_rows)
            wy[v * out_rows : (v + 1) * out_rows, :] = band[:, : 3 * in_rows].astype(BF16)
            high, low = split(slanted(row_x[v : v + 1], cols)[:, :cols])
            wx[v, :cols, :cols] = high
            wx[v, cols:, :cols] = high
            wx[v, :cols, cols:] = low
            wx[v, cols:, cols:] = low
            size = 8 * planes
            high, low = split(slanted(row_z[v : v + 1], size)[:, :size])
            wz[v, :, :size] = high
            wz[v, :, size : 2 * size] = high
            wz[v, :, 2 * size :] = low


def make_weights(taps, planes, rows, cols):
    views = taps.shape[0]
    shapes = []
    for out_rows in (3 * rows, rows):
        shapes += [
            jax.ShapeDtypeStruct((views * out_rows, 3 * (out_rows + 2 * rows)), BF16),
            jax.ShapeDtypeStruct((views, 2 * cols, 2 * cols), BF16),
            jax.ShapeDtypeStruct((views, 8 * planes, 24 * planes), BF16),
        ]
    outs = pl.pallas_call(
        functools.partial(weights_kernel, rows),
        out_shape=shapes,
        in_specs=[FULL],
        out_specs=[FULL] * 6,
        compiler_params=pltpu.CompilerParams(vmem_limit_bytes=LIMIT),
        cost_estimate=pl.CostEstimate(flops=10**7, bytes_accessed=10**7, transcendentals=0),
        name="weights",
    )(taps)
    return outs[:3], outs[3:]


def stacked(pieces):
    columns = []
    for piece in pieces:
        high, low = split(piece)
        columns.append(jnp.concatenate([high, low, high], axis=0))
    return jnp.concatenate(columns, axis=1)


def two_groups(rows_ref, wx, wz, planes, cols):
    both = dot(rows_ref.reshape(planes * 16, 2 * cols), wx)
    value = (both[:, :cols] + both[:, cols:]).reshape(planes, 16, cols)
    return dot(wz, stacked([value[:, 8 * g : 8 * g + 8, :].reshape(planes * 8, cols) for g in range(2)]))


def forward_rows(parity, far_before, near, own, far_after, wy, ys):
    planes, rows, cols = own.shape
    views = ys.shape[0]
    height = 3 * rows
    side = parity[0]

    def plane(z):
        return jnp.concatenate(
            [far_before[z], near[1 - side, z], own[z], near[side, z], far_after[z]], axis=0
        )

    for z in range(0, planes, 2):
        result = dot(wy[...], stacked([plane(z), plane(z + 1)]))
        high, low = split(result)
        for j in range(2):
            for v in range(views):
                there = (slice(v * height, (v + 1) * height), slice(j * cols, (j + 1) * cols))
                ys[v, z + j, :, :cols] = high[there]
                ys[v, z + j, :, cols:] = low[there]


def forward_view(view, ys, wx, wz, out):
    planes, height, cols = out.shape
    for pair in range(height // 16):
        result = two_groups(ys[view, :, 16 * pair : 16 * pair + 16, :], wx, wz, planes, cols)
        for j in range(2):
            at = 16 * pair + 8 * j
            out[:, at : at + 8, :] = result[:, j * cols : (j + 1) * cols].reshape(planes, 8, cols)


def adjoint_view(blurred, before, raw, after, wy, wx, wz, ya, acc):
    planes, rows, cols = raw.shape

    def quotient(z):
        counts = jnp.concatenate([before[z], raw[z], after[z]], axis=0)
        inside = counts > 0.0
        return jnp.where(inside, counts / jnp.where(inside, blurred[z], 1.0), 0.0)

    for z in range(0, planes, 2):
        high, low = split(dot(wy, stacked([quotient(z), quotient(z + 1)])))
        for j in range(2):
            ya[z + j, :, :cols] = high[:, j * cols : (j + 1) * cols]
            ya[z + j, :, cols:] = low[:, j * cols : (j + 1) * cols]
    for pair in range(rows // 16):
        result = two_groups(ya[:, 16 * pair : 16 * pair + 16, :], wx, wz, planes, cols)
        for j in range(2):
            at = 16 * pair + 8 * j
            acc[:, at : at + 8, :] += jnp.log(result[:, j * cols : (j + 1) * cols]).reshape(planes, 8, cols)


def forward_kernel(parity, far_before, near, own, far_after, wy, wx, wz, out, ys):
    @pl.when(pl.program_id(0) == 0)
    def _():
        forward_rows(parity, far_before, near, own, far_after, wy, ys)

    forward_view(pl.program_id(0), ys, wx[0], wz[0], out.at[0])


def weighted_sums(values, wzs, wyx, sums, at):
    planes, rows, cols = values.shape
    for v in range(wyx.shape[0]):
        total = jnp.zeros((rows, cols), F32)
        for z in range(planes):
            total = total + wzs[v, z] * values[z]
        sums[at + v : at + v + 1, :] = jnp.sum(total * wyx[v], axis=0, keepdims=True)


def first_adjoint_kernel(current, blurred, before, raw, after, wy, wx, wz, wzs, wyx, out, sums, ya, acc):
    view, views = pl.program_id(0), wyx.shape[0]

    @pl.when(view == 0)
    def _():
        acc[...] = jnp.zeros_like(acc)

    sums[pl.ds(view, 1), :] = jnp.sum(jnp.sum(raw[0], axis=0), axis=0, keepdims=True)
    adjoint_view(blurred.at[0], before.at[0], raw.at[0], after.at[0], wy[0], wx[0], wz[0], ya, acc)

    @pl.when(view == views - 1)
    def _():
        out[...] = current[...] * jnp.exp(acc[...] * (1.0 / views))
        weighted_sums(current, wzs, wyx, sums, views)
        weighted_sums(out, wzs, wyx, sums, 2 * views)


def iteration_kernel(
    parity, far_before, near, own, far_after, before, raw, after, wy, wx, wz, wya, wxa, wza, out, ys, blurred, ya, acc
):
    view = pl.program_id(0)

    @pl.when(view == 0)
    def _():
        acc[...] = jnp.zeros_like(acc)
        forward_rows(parity, far_before, near, own, far_after, wy, ys)

    forward_view(view, ys, wx[0], wz[0], blurred)
    adjoint_view(blurred, before.at[0], raw.at[0], after.at[0], wya[0], wxa[0], wza[0], ya, acc)

    @pl.when(view == pl.num_programs(0) - 1)
    def _():
        out[...] = own[...] * jnp.exp(acc[...] * (1.0 / ys.shape[0]))


def whole(array):
    return pl.BlockSpec(array.shape, lambda v: (0,) * array.ndim)


def one_view(array):
    return pl.BlockSpec((1,) + array.shape[1:], lambda v: (v,) + (0,) * (array.ndim - 1))


def params(flops, moved):
    return dict(
        compiler_params=pltpu.CompilerParams(vmem_limit_bytes=LIMIT),
        cost_estimate=pl.CostEstimate(flops=flops, bytes_accessed=moved, transcendentals=10**5),
    )


def row_scratch(views, planes, rows, cols):
    return pltpu.VMEM((views, planes, 3 * rows, 2 * cols), BF16)


def adjoint_scratch(planes, rows, cols):
    return [pltpu.VMEM((planes, rows, 2 * cols), BF16), pltpu.VMEM((planes, rows, cols), F32)]


def forward(parity, slabs, weights):
    planes, rows, cols = slabs[0].shape
    wy, wx, wz = weights
    views = wx.shape[0]
    out = jax.ShapeDtypeStruct((views, planes, 3 * rows, cols), F32)
    return pl.pallas_call(
        forward_kernel,
        grid=(views,),
        out_shape=out,
        in_specs=[pl.BlockSpec(memory_space=SMEM)]
        + [whole(s) for s in slabs]
        + [whole(wy), one_view(wx), one_view(wz)],
        out_specs=one_view(out),
        scratch_shapes=[row_scratch(views, planes, rows, cols)],
        name="forward",
        **params(10**10, 10**7),
    )(parity, *slabs, *weights)


def first_adjoint(current, blurred, before, raw, after, weights, wzs, wyx):
    wy, wx, wz = weights
    views = raw.shape[0]
    shapes = [jax.ShapeDtypeStruct(current.shape, F32), jax.ShapeDtypeStruct((3 * views, current.shape[2]), F32)]
    return pl.pallas_call(
        first_adjoint_kernel,
        grid=(views,),
        out_shape=shapes,
        in_specs=[whole(current)]
        + [one_view(a) for a in (blurred, before, raw, after, wy, wx, wz)]
        + [pl.BlockSpec(memory_space=SMEM), whole(wyx)],
        out_specs=[whole(s) for s in shapes],
        scratch_shapes=adjoint_scratch(*current.shape),
        name="adjoint",
        **params(10**10, 10**7),
    )(current, blurred, before, raw, after, wy, wx, wz, wzs, wyx)


def full_iteration(parity, slabs, before, raw, after, weights, adjoint_weights):
    current = slabs[2]
    planes, rows, cols = current.shape
    views = raw.shape[0]
    wy, wx, wz = weights
    return pl.pallas_call(
        iteration_kernel,
        grid=(views,),
        out_shape=jax.ShapeDtypeStruct(current.shape, F32),
        in_specs=[pl.BlockSpec(memory_space=SMEM)]
        + [whole(s) for s in slabs]
        + [one_view(a) for a in (before, raw, after)]
        + [whole(wy), one_view(wx), one_view(wz)]
        + [one_view(a) for a in adjoint_weights],
        out_specs=whole(current),
        scratch_shapes=[
            row_scratch(views, planes, rows, cols),
            pltpu.VMEM((planes, 3 * rows, cols), F32),
        ]
        + adjoint_scratch(planes, rows, cols),
        name="iteration",
        **params(2 * 10**10, 2 * 10**7),
    )(parity, *slabs, before, raw, after, *weights, *adjoint_weights)


def two_slabs_away(value, count):
    up = [(i, i + 2) for i in range(count - 2)]
    down = [(j, i) for i, j in up]
    return lax.ppermute(value, "slab", up), lax.ppermute(value, "slab", down)


def with_near(value, far_before, far_after, parity, count):
    swap = [(i, i + 1 - 2 * (i % 2)) for i in range(count)]
    passed = jnp.stack([value, jnp.where(parity[0] == 0, far_after, far_before)])
    near = lax.ppermute(passed, "slab", swap)
    return far_before, near, value, far_after


def tap_sums(taps, offset, extent, total):
    count = taps.shape[1]
    target = offset + jnp.arange(extent)[None, :] - jnp.arange(count)[:, None] + count // 2
    reach = jnp.where((target >= 0) & (target < total), 1.0, 0.0).astype(F32)
    return jnp.sum(taps[:, :, None] * reach[None], axis=1)


def per_device(estimate, raw, taps):
    views = raw.shape[0]
    planes, rows, cols = estimate.shape
    count = lax.axis_size("slab")
    assert rows >= taps.shape[2] // 2 and count % 2 == 0
    up = [(i, i + 1) for i in range(count - 1)]
    down = [(j, i) for i, j in up]
    place = lax.axis_index("slab")
    parity = (place % 2).reshape(1)

    far = two_slabs_away(estimate, count)
    before = lax.ppermute(raw, "slab", up)
    after = lax.ppermute(raw, "slab", down)

    wzs = tap_sums(taps[:, 0], 0, planes, planes)
    wy_sums = tap_sums(taps[:, 1], place * rows, rows, count * rows)
    wx_sums = tap_sums(taps[:, 2], 0, cols, cols)
    wyx = wy_sums[:, :, None] * wx_sums[:, None, :]

    forward_weights, (wy, wx, wz) = make_weights(taps, planes, rows, cols)
    adjoint_weights = (wy.reshape(views, rows, -1), wx, wz)

    slabs = with_near(estimate, *far, parity, count)
    blurred = forward(parity, slabs, forward_weights)
    current, sums = first_adjoint(estimate, blurred, before, raw, after, adjoint_weights, wzs, wyx)
    gathered = lax.all_gather(sums, "slab", tiled=True)

    slabs = with_near(current, *two_slabs_away(current, count), parity, count)
    current = full_iteration(parity, slabs, before, raw, after, forward_weights, adjoint_weights)

    current, gathered = lax.optimization_barrier((current, gathered))
    total, first, second = jnp.sum(gathered.reshape(count, 3, views, cols), axis=(0, 3))
    scale = jnp.log(first / total) + jnp.log(second / total)
    return current * jnp.exp(jnp.mean(scale))


def solution(mesh):
    placed = (P("blocks", "slab", None), P(None, "blocks", "slab", None), P())
    return jax.shard_map(
        per_device, mesh=mesh, in_specs=placed, out_specs=P("blocks", "slab", None), check_vma=False
    )
```

profile of v0, /device:TPU:0, one launch (start us, length us, event | category | flops | bytes accessed | tf_op | source)
XLA Modules:
  0.0 118.3 jit_solution(392092262155210200)
XLA Ops:
  0.0 4.9 %collective-permute-start = (f32[32,16,128]{2,1,0:T(8,128)}, f32[32,16,128]{2,1,0:T(8,128)S(1)}, u32[]{:S(2)}, u32[]{:S(2)}) collective-permute-start(f32[32,16,128]{2,1,0:T(8,128)} %current.1), channel_id=1, source_target_pairs={{0,2},{1,3},{2,4},{3,5},{4,6},{5,7},{6,8},{7,9},{8,10},{9,11},{10,... | collective-permute-start | bytes 786440 | tf_op jit(solution)/shard_map/ppermute | solution.py:301
  4.9 1.3 %collective-permute-start.1 = (f32[32,16,128]{2,1,0:T(8,128)}, f32[32,16,128]{2,1,0:T(8,128)S(1)}, u32[]{:S(2)}, u32[]{:S(2)}) collective-permute-start(f32[32,16,128]{2,1,0:T(8,128)} %current.1), channel_id=1, source_target_pairs={{2,0},{3,1},{4,2},{5,3},{6,4},{7,5},{8,6},{9,7},{10,8},{11,9},{12,... | collective-permute-start | bytes 786440 | tf_op jit(solution)/shard_map/ppermute | solution.py:301
  6.2 1.6 %collective-permute-start.3 = (f32[6,32,16,128]{3,2,1,0:T(8,128)}, f32[6,32,16,128]{3,2,1,0:T(8,128)S(1)}, u32[]{:S(2)}, u32[]{:S(2)}) collective-permute-start(f32[6,32,16,128]{3,2,1,0:T(8,128)} %raw.3), channel_id=1, source_target_pairs={{0,1},{1,2},{2,3},{3,4},{4,5},{5,6},{6,7},{7,8},{8,9},{9,10},{10,1... | collective-permute-start | bytes 4718600 | tf_op jit(solution)/shard_map/ppermute | solution.py:329
  7.8 1.3 %collective-permute-start.4 = (f32[6,32,16,128]{3,2,1,0:T(8,128)}, f32[6,32,16,128]{3,2,1,0:T(8,128)}, u32[]{:S(2)}, u32[]{:S(2)}) collective-permute-start(f32[6,32,16,128]{3,2,1,0:T(8,128)} %raw.3), channel_id=1, source_target_pairs={{1,0},{2,1},{3,2},{4,3},{5,4},{6,5},{7,6},{8,7},{9,8},{10,9},{11,1... | collective-permute-start | bytes 4718600 | tf_op jit(solution)/shard_map/ppermute | solution.py:330
  9.1 0.8 fusion.12
  9.9 0.1 fusion.11
  10.0 4.7 %weights.1 = (bf16[288,240]{1,0:T(8,128)(2,1)}, bf16[6,256,256]{2,1,0:T(8,128)(2,1)}, bf16[6,256,768]{2,1,0:T(8,128)(2,1)}, bf16[96,144]{1,0:T(8,128)(2,1)}, bf1...) custom-call(f32[6,3,31]{2,1,0:T(4,128)} %taps_ref.1), custom_call_target="tpu_custom_call" | custom-call | flops 10000000 | bytes 10000000 | tf_op jit(solution)/shard_map/weights/pallas_call | solution.py:85
  14.7 0.1 multiply_reduce_fusion.2
  14.8 2.6 %collective-permute-done.far_before = f32[32,16,128]{2,1,0:T(8,128)S(1)} collective-permute-done((f32[32,16,128]{2,1,0:T(8,128)}, f32[32,16,128]{2,1,0:T(8,128)S(1)}, u32[]{:S(2)}, u32[]{:S(2)}) %collective-permute-start) | collective-permute-done | bytes 262176 | tf_op jit(solution)/shard_map/ppermute | solution.py:301
  17.4 1.1 pad_maximum_fusion
  18.6 1.2 %collective-permute-start.2 = (f32[2,32,16,128]{3,2,1,0:T(8,128)S(1)}, f32[2,32,16,128]{3,2,1,0:T(8,128)S(1)}, u32[]{:S(2)}, u32[]{:S(2)}) collective-permute-start(f32[2,32,16,128]{3,2,1,0:T(8,128)S(1)} %pad_maximum_fusion), channel_id=1, source_target_pairs={{0,1},{1,0},{2,3},{3,2},{4,5},{5,4},{6,7},{7,6},{8,9},{9,8},{10,11... | collective-permute-start | bytes 1572872 | tf_op jit(solution)/shard_map/ppermute | solution.py:307
  19.8 0.1 multiply_reduce_fusion
  19.9 0.7 multiply_reduce_fusion.1.wzs
  20.6 0.7 broadcast_multiply_fusion.1.wyx
  21.3 0.0 collective-permute-done.2.near
  21.3 0.8 copy-done.6
  22.1 9.5 %forward.1.blurred = f32[6,32,48,128]{3,2,1,0:T(8,128)} custom-call(s32[1]{0:T(128)} %bitcast.parity, f32[32,16,128]{2,1,0:T(8,128)} %copy-done, f32[2,32,16,128]{3,2,1,0:T(8,128)} %copy-done.6, f32[32,16,128]{2,1,0:T(8,128)} %current.1, f32[32,16,128]{2,1,0:T(8,128)} %copy-done.1, bf16[288,240]{1,0:T(8,128)(2,1)} %get-tuple-element.15.wy, ...), custom_call_target="tpu_custom_call" | custom-call | flops 10000000000 | bytes 10000000 | tf_op jit(solution)/shard_map/forward/pallas_call | solution.py:241
  31.7 1.1 copy-done.4
  32.8 9.6 %adjoint.1 = (f32[32,16,128]{2,1,0:T(8,128)}, f32[18,128]{1,0:T(8,128)}) custom-call(f32[32,16,128]{2,1,0:T(8,128)} %current.1, f32[6,32,48,128]{3,2,1,0:T(8,128)} %forward.1.blurred, f32[6,32,16,128]{3,2,1,0:T(8,128)} %copy-done.4, f32[6,32,16,128]{3,2,1,0:T(8,128)} %raw.3, f32[6,32,16,128]{3,2,1,0:T(8,128)} %collective-permute-done.4.after, ...), custom_call_target="tpu_custom_call" | custom-call | flops 10000000000 | bytes 10000000 | tf_op jit(solution)/shard_map/adjoint/pallas_call | solution.py:259
  42.5 22.7 %collective-permute-start.5 = (f32[32,16,128]{2,1,0:T(8,128)}, f32[32,16,128]{2,1,0:T(8,128)S(1)}, u32[]{:S(2)}, u32[]{:S(2)}) collective-permute-start(f32[32,16,128]{2,1,0:T(8,128)} %get-tuple-element.21.own), channel_id=1, source_target_pairs={{0,2},{1,3},{2,4},{3,5},{4,6},{5,7},{6,8},{7,9},{8,10},{9,11},{10,... | collective-permute-start | bytes 786440 | tf_op jit(solution)/shard_map/ppermute | solution.py:301
  65.1 1.3 %collective-permute-start.6 = (f32[32,16,128]{2,1,0:T(8,128)}, f32[32,16,128]{2,1,0:T(8,128)S(1)}, u32[]{:S(2)}, u32[]{:S(2)}) collective-permute-start(f32[32,16,128]{2,1,0:T(8,128)} %get-tuple-element.21.own), channel_id=1, source_target_pairs={{2,0},{3,1},{4,2},{5,3},{6,4},{7,5},{8,6},{9,7},{10,8},{11,9},{12,... | collective-permute-start | bytes 786440 | tf_op jit(solution)/shard_map/ppermute | solution.py:301
  66.4 3.1 %collective-permute-done.5.far_before = f32[32,16,128]{2,1,0:T(8,128)S(1)} collective-permute-done((f32[32,16,128]{2,1,0:T(8,128)}, f32[32,16,128]{2,1,0:T(8,128)S(1)}, u32[]{:S(2)}, u32[]{:S(2)}) %collective-permute-start.5) | collective-permute-done | bytes 262176 | tf_op jit(solution)/shard_map/ppermute | solution.py:301
  69.5 5.1 %collective-permute-done.6.far_after = f32[32,16,128]{2,1,0:T(8,128)S(1)} collective-permute-done((f32[32,16,128]{2,1,0:T(8,128)}, f32[32,16,128]{2,1,0:T(8,128)S(1)}, u32[]{:S(2)}, u32[]{:S(2)}) %collective-permute-start.6) | collective-permute-done | bytes 262176 | tf_op jit(solution)/shard_map/ppermute | solution.py:301
  74.7 1.1 pad_maximum_fusion.1
  75.7 0.1 collective-permute-start.7
  75.8 23.9 %all-gather = f32[16,18,128]{2,1,0:T(8,128)S(1)} all-gather(f32[1,18,128]{2,1,0:T(8,128)} %bitcast.19), channel_id=1, replica_groups=mesh['blocks'=2,'slab'=16] {'slab'}, dimensions={0}, use_global_device_ids=true | all-gather | bytes 156672 | tf_op jit(solution)/shard_map/all_gather | solution.py:343
  99.8 0.8 copy-done.5
  100.6 14.5 %iteration.1 = f32[32,16,128]{2,1,0:T(8,128)} custom-call(s32[1]{0:T(128)} %bitcast.parity, f32[32,16,128]{2,1,0:T(8,128)} %copy-done.2, f32[2,32,16,128]{3,2,1,0:T(8,128)} %copy-done.5, f32[32,16,128]{2,1,0:T(8,128)} %get-tuple-element.21.own, f32[32,16,128]{2,1,0:T(8,128)} %copy-done.3, f32[6,32,16,128]{3,2,1,0:T(8,128)} %copy-done.4, ...), custom_call_target="tpu_custom_call" | custom-call | flops 20000000000 | bytes 20000000 | tf_op jit(solution)/shard_map/iteration/pallas_call | solution.py:278
  115.0 0.1 reduce_sum.55
  115.2 0.1 reduce_sum.56
  115.4 0.6 add_reduce_fusion
  116.7 1.7 %broadcast_multiply_fusion = f32[32,16,128]{2,1,0:T(8,128)} fusion(f32[32,16,128]{2,1,0:T(8,128)} %iteration.1, f32[]{:T(128)S(6)} %exp.3), kind=kLoop, calls=%fused_computation.4 | loop fusion | flops 65536 | bytes 524292 | tf_op jit(solution)/shard_map/mul | solution.py:351
  (24 shorter events, 0.2 us)
Async XLA Ops:
  0.0 17.4 %collective-permute-start = (f32[32,16,128]{2,1,0:T(8,128)}, f32[32,16,128]{2,1,0:T(8,128)S(1)}, u32[]{:S(2)}, u32[]{:S(2)}) collective-permute-start(f32[32,16,128]{2,1,0:T(8,128)} %current.1), channel_id=1, source_target_pairs={{0,2},{1,3},{2,4},{3,5},{4,6},{5,7},{6,8},{7,9},{8,10},{9,11},{10,... | collective-permute-start | bytes 786440 | tf_op jit(solution)/shard_map/ppermute | solution.py:301
  4.9 12.5 %collective-permute-start.1 = (f32[32,16,128]{2,1,0:T(8,128)}, f32[32,16,128]{2,1,0:T(8,128)S(1)}, u32[]{:S(2)}, u32[]{:S(2)}) collective-permute-start(f32[32,16,128]{2,1,0:T(8,128)} %current.1), channel_id=1, source_target_pairs={{2,0},{3,1},{4,2},{5,3},{6,4},{7,5},{8,6},{9,7},{10,8},{11,9},{12,... | collective-permute-start | bytes 786440 | tf_op jit(solution)/shard_map/ppermute | solution.py:301
  6.2 25.5 %collective-permute-start.3 = (f32[6,32,16,128]{3,2,1,0:T(8,128)}, f32[6,32,16,128]{3,2,1,0:T(8,128)S(1)}, u32[]{:S(2)}, u32[]{:S(2)}) collective-permute-start(f32[6,32,16,128]{3,2,1,0:T(8,128)} %raw.3), channel_id=1, source_target_pairs={{0,1},{1,2},{2,3},{3,4},{4,5},{5,6},{6,7},{7,8},{8,9},{9,10},{10,1... | collective-permute-start | bytes 4718600 | tf_op jit(solution)/shard_map/ppermute | solution.py:329
  7.8 23.9 %collective-permute-start.4 = (f32[6,32,16,128]{3,2,1,0:T(8,128)}, f32[6,32,16,128]{3,2,1,0:T(8,128)}, u32[]{:S(2)}, u32[]{:S(2)}) collective-permute-start(f32[6,32,16,128]{3,2,1,0:T(8,128)} %raw.3), channel_id=1, source_target_pairs={{1,0},{2,1},{3,2},{4,3},{5,4},{6,5},{7,6},{8,7},{9,8},{10,9},{11,1... | collective-permute-start | bytes 4718600 | tf_op jit(solution)/shard_map/ppermute | solution.py:330
  17.4 4.0 %copy-start = (f32[32,16,128]{2,1,0:T(8,128)}, f32[32,16,128]{2,1,0:T(8,128)S(1)}, u32[]{:S(2)}) copy-start(f32[32,16,128]{2,1,0:T(8,128)S(1)} %collective-permute-done.far_before) | copy-start | bytes 786436
  17.4 4.0 %copy-start.1 = (f32[32,16,128]{2,1,0:T(8,128)}, f32[32,16,128]{2,1,0:T(8,128)S(1)}, u32[]{:S(2)}) copy-start(f32[32,16,128]{2,1,0:T(8,128)S(1)} %collective-permute-done.1.far_after) | copy-start | bytes 786436
  18.6 2.8 %collective-permute-start.2 = (f32[2,32,16,128]{3,2,1,0:T(8,128)S(1)}, f32[2,32,16,128]{3,2,1,0:T(8,128)S(1)}, u32[]{:S(2)}, u32[]{:S(2)}) collective-permute-start(f32[2,32,16,128]{3,2,1,0:T(8,128)S(1)} %pad_maximum_fusion), channel_id=1, source_target_pairs={{0,1},{1,0},{2,3},{3,2},{4,5},{5,4},{6,7},{7,6},{8,9},{9,8},{10,11... | collective-permute-start | bytes 1572872 | tf_op jit(solution)/shard_map/ppermute | solution.py:307
  21.3 0.8 copy-start.6
  31.7 1.1 copy-start.4
  42.5 27.0 %collective-permute-start.5 = (f32[32,16,128]{2,1,0:T(8,128)}, f32[32,16,128]{2,1,0:T(8,128)S(1)}, u32[]{:S(2)}, u32[]{:S(2)}) collective-permute-start(f32[32,16,128]{2,1,0:T(8,128)} %get-tuple-element.21.own), channel_id=1, source_target_pairs={{0,2},{1,3},{2,4},{3,5},{4,6},{5,7},{6,8},{7,9},{8,10},{9,11},{10,... | collective-permute-start | bytes 786440 | tf_op jit(solution)/shard_map/ppermute | solution.py:301
  65.1 9.5 %collective-permute-start.6 = (f32[32,16,128]{2,1,0:T(8,128)}, f32[32,16,128]{2,1,0:T(8,128)S(1)}, u32[]{:S(2)}, u32[]{:S(2)}) collective-permute-start(f32[32,16,128]{2,1,0:T(8,128)} %get-tuple-element.21.own), channel_id=1, source_target_pairs={{2,0},{3,1},{4,2},{5,3},{6,4},{7,5},{8,6},{9,7},{10,8},{11,9},{12,... | collective-permute-start | bytes 786440 | tf_op jit(solution)/shard_map/ppermute | solution.py:301
  69.5 30.3 %copy-start.2 = (f32[32,16,128]{2,1,0:T(8,128)}, f32[32,16,128]{2,1,0:T(8,128)S(1)}, u32[]{:S(2)}) copy-start(f32[32,16,128]{2,1,0:T(8,128)S(1)} %collective-permute-done.5.far_before) | copy-start | bytes 786436
  74.6 25.1 %copy-start.3 = (f32[32,16,128]{2,1,0:T(8,128)}, f32[32,16,128]{2,1,0:T(8,128)S(1)}, u32[]{:S(2)}) copy-start(f32[32,16,128]{2,1,0:T(8,128)S(1)} %collective-permute-done.6.far_after) | copy-start | bytes 786436
  75.7 24.0 %collective-permute-start.7 = (f32[2,32,16,128]{3,2,1,0:T(8,128)S(1)}, f32[2,32,16,128]{3,2,1,0:T(8,128)S(1)}, u32[]{:S(2)}, u32[]{:S(2)}) collective-permute-start(f32[2,32,16,128]{3,2,1,0:T(8,128)S(1)} %pad_maximum_fusion.1), channel_id=1, source_target_pairs={{0,1},{1,0},{2,3},{3,2},{4,5},{5,4},{6,7},{7,6},{8,9},{9,8},{10,11... | collective-permute-start | bytes 1572872 | tf_op jit(solution)/shard_map/ppermute | solution.py:307
  99.8 0.8 copy-start.5
where the time goes:
time: 119 us; the launch traced here: 118 us
  Pallas kernels  38.3 us (32%)
  starting transfers between devices  34.3 us (29%)
  blocking collectives  23.9 us (20%)
  waiting for transfers between devices  10.8 us (9%)
  other arithmetic  6.41 us (5%)
  local copies, waits for them, and re-layouts  3.69 us (3%)
    ppermute x4, starting transfers between devices, two_slabs_away(): return (lax.ppermute(value, 'slab', up), lax.ppermute(value, 'slab', down))  30.1 us
    all_gather x1, blocking collectives, per_device(): gathered = lax.all_gather(sums, 'slab', tiled=True)  23.9 us
    pallas_call x1, Pallas kernels, full_iteration(): pl.pallas_call(iteration_kernel, grid=(views,), out_shape=jax.ShapeDtypeS...  14.5 us
    ppermute x4, waiting for transfers between devices, two_slabs_away(): return (lax.ppermute(value, 'slab', up), lax.ppermute(value, 'slab', down))  10.8 us
    pallas_call x1, Pallas kernels, first_adjoint(): pl.pallas_call(first_adjoint_kernel, grid=(views,), out_shape=shapes, in_...  9.65 us
    pallas_call x1, Pallas kernels, forward(): pl.pallas_call(forward_kernel, grid=(views,), out_shape=out, in_specs=[pl...  9.54 us
    pallas_call x1, Pallas kernels, make_weights(): pl.pallas_call(functools.partial(weights_kernel, rows), out_shape=shapes,...  4.68 us
    unnamed x15, local copies, waits for them, and re-layouts  2.71 us
  transfers between devices with their start and end apart: 8, of which 3 were waited for; matrix products, arithmetic and copies ran while one was open for 3% of the time, Pallas kernels for 12%

commit v1 on v0

--- a/solution.py
+++ b/solution.py
@@ -13,7 +13,8 @@
 VMEM = pltpu.MemorySpace.VMEM
 SMEM = pltpu.MemorySpace.SMEM
 FULL = pl.BlockSpec(memory_space=VMEM)
-LIMIT = 56 * 1024 * 1024
+LIMIT = 24 * 1024 * 1024
+TINY = float(np.finfo(np.float32).tiny)
 
 
 def split(value):
@@ -143,8 +144,9 @@
 
     def quotient(z):
         counts = jnp.concatenate([before[z], raw[z], after[z]], axis=0)
-        inside = counts > 0.0
-        return jnp.where(inside, counts / jnp.where(inside, blurred[z], 1.0), 0.0)
+        below = jnp.maximum(blurred[z], TINY)
+        inverse = pl.reciprocal(below, approx=True)
+        return counts * (inverse * (2.0 - below * inverse))
 
     for z in range(0, planes, 2):
         high, low = split(dot(wy, stacked([quotient(z), quotient(z + 1)])))
@@ -319,7 +321,7 @@
     views = raw.shape[0]
     planes, rows, cols = estimate.shape
     count = lax.axis_size("slab")
-    assert rows >= taps.shape[2] // 2 and count % 2 == 0
+    assert rows >= taps.shape[2] // 2 and count & (count - 1) == 0
     up = [(i, i + 1) for i in range(count - 1)]
     down = [(j, i) for i, j in up]
     place = lax.axis_index("slab")
@@ -340,13 +342,20 @@
     slabs = with_near(estimate, *far, parity, count)
     blurred = forward(parity, slabs, forward_weights)
     current, sums = first_adjoint(estimate, blurred, before, raw, after, adjoint_weights, wzs, wyx)
-    gathered = lax.all_gather(sums, "slab", tiled=True)
-
-    slabs = with_near(current, *two_slabs_away(current, count), parity, count)
+
+    far = two_slabs_away(current, count)
+    sums, others, distance = sums, None, 1
+    while distance < count:
+        sums = sums if others is None else sums + others
+        others = lax.ppermute(sums, "slab", [(i, i ^ distance) for i in range(count)])
+        distance *= 2
+        if distance == 8:
+            *far, sums, others = lax.optimization_barrier((*far, sums, others))
+    slabs = with_near(current, *far, parity, count)
     current = full_iteration(parity, slabs, before, raw, after, forward_weights, adjoint_weights)
 
-    current, gathered = lax.optimization_barrier((current, gathered))
-    total, first, second = jnp.sum(gathered.reshape(count, 3, views, cols), axis=(0, 3))
+    current, sums, others = lax.optimization_barrier((current, sums, others))
+    total, first, second = jnp.sum((sums + others).reshape(3, views, cols), axis=2)
     scale = jnp.log(first / total) + jnp.log(second / total)
     return current * jnp.exp(jnp.mean(scale))
 

time: 119 us -> 95.8 us (0.81)
  blocking collectives: 23.9 us -> 0 us
  starting transfers between devices: 34.3 us -> 47 us
  Pallas kernels: 38.3 us -> 26.9 us
  waiting for transfers between devices: 10.8 us -> 14.9 us
  other arithmetic: 6.41 us -> 3.08 us
  local copies, waits for them, and re-layouts: 3.69 us -> 2.5 us
    all_gather x1 -> x0, blocking collectives: 23.9 us -> none  [per_device(): gathered = lax.all_gather(sums, 'slab', tiled=True)]
    ppermute x0 -> x4, starting transfers between devices: none -> 9.62 us  [per_device(): lax.ppermute(sums, 'slab', [(i, i ^ distance) for i in range(count)])]
    ppermute x0 -> x4, waiting for transfers between devices: none -> 8.31 us  [per_device(): lax.ppermute(sums, 'slab', [(i, i ^ distance) for i in range(count)])]
    ppermute x4, waiting for transfers between devices: 10.8 us -> 4.95 us  [two_slabs_away(): return (lax.ppermute(value, 'slab', up), lax.ppermute(value, 'slab', down))]
    ppermute x4, starting transfers between devices: 30.1 us -> 34.4 us  [two_slabs_away(): return (lax.ppermute(value, 'slab', up), lax.ppermute(value, 'slab', down))]
    pallas_call x1, Pallas kernels: 9.54 us -> 6.03 us  [forward(): pl.pallas_call(forward_kernel, grid=(views,), out_shape=out, in_specs=[pl...]
    pallas_call x1, Pallas kernels: 4.68 us -> 1.61 us  [make_weights(): pl.pallas_call(functools.partial(weights_kernel, rows), out_shape=shapes,...]
    pallas_call x1, Pallas kernels: 9.65 us -> 6.81 us  [first_adjoint(): pl.pallas_call(first_adjoint_kernel, grid=(views,), out_shape=shapes, in_...]
  transfers between devices with their start and end apart: 8 -> 12, of which waited for: 3 -> 5; matrix products, arithmetic and copies ran while one was open for 3% -> 2% of each run, Pallas kernels for 12% -> 21%
where the time goes in v1:
time: 95.8 us; the launch traced here: 95.3 us
  starting transfers between devices  47 us (49%)
  Pallas kernels  26.9 us (28%)
  waiting for transfers between devices  14.9 us (16%)
  other arithmetic  3.08 us (3%)
  local copies, waits for them, and re-layouts  2.5 us (3%)
    ppermute x4, starting transfers between devices, two_slabs_away(): return (lax.ppermute(value, 'slab', up), lax.ppermute(value, 'slab', down))  34.4 us
    pallas_call x1, Pallas kernels, full_iteration(): pl.pallas_call(iteration_kernel, grid=(views,), out_shape=jax.ShapeDtypeS...  12.5 us
    ppermute x4, starting transfers between devices, per_device(): lax.ppermute(sums, 'slab', [(i, i ^ distance) for i in range(count)])  9.62 us
    ppermute x4, waiting for transfers between devices, per_device(): lax.ppermute(sums, 'slab', [(i, i ^ distance) for i in range(count)])  8.31 us
    pallas_call x1, Pallas kernels, first_adjoint(): pl.pallas_call(first_adjoint_kernel, grid=(views,), out_shape=shapes, in_...  6.81 us
    pallas_call x1, Pallas kernels, forward(): pl.pallas_call(forward_kernel, grid=(views,), out_shape=out, in_specs=[pl...  6.03 us
    ppermute x4, waiting for transfers between devices, two_slabs_away(): return (lax.ppermute(value, 'slab', up), lax.ppermute(value, 'slab', down))  4.95 us
  transfers between devices with their start and end apart: 12, of which 5 were waited for; matrix products, arithmetic and copies ran while one was open for 2% of the time, Pallas kernels for 21%

profile of v1, /device:TPU:0, one launch (start us, length us, event | category | flops | bytes accessed | tf_op | source)
XLA Modules:
  0.0 95.3 jit_solution(17877930389692820204)
XLA Ops:
  0.0 4.9 %collective-permute-start = (f32[32,16,128]{2,1,0:T(8,128)}, f32[32,16,128]{2,1,0:T(8,128)S(1)}, u32[]{:S(2)}, u32[]{:S(2)}) collective-permute-start(f32[32,16,128]{2,1,0:T(8,128)} %current.1), channel_id=1, source_target_pairs={{0,2},{1,3},{2,4},{3,5},{4,6},{5,7},{6,8},{7,9},{8,10},{9,11},{10,... | collective-permute-start | bytes 786440 | tf_op jit(solution)/shard_map/ppermute | solution.py:303
  4.9 1.3 %collective-permute-start.1 = (f32[32,16,128]{2,1,0:T(8,128)}, f32[32,16,128]{2,1,0:T(8,128)S(1)}, u32[]{:S(2)}, u32[]{:S(2)}) collective-permute-start(f32[32,16,128]{2,1,0:T(8,128)} %current.1), channel_id=1, source_target_pairs={{2,0},{3,1},{4,2},{5,3},{6,4},{7,5},{8,6},{9,7},{10,8},{11,9},{12,... | collective-permute-start | bytes 786440 | tf_op jit(solution)/shard_map/ppermute | solution.py:303
  6.2 1.6 %collective-permute-start.3 = (f32[6,32,16,128]{3,2,1,0:T(8,128)}, f32[6,32,16,128]{3,2,1,0:T(8,128)S(1)}, u32[]{:S(2)}, u32[]{:S(2)}) collective-permute-start(f32[6,32,16,128]{3,2,1,0:T(8,128)} %raw.3), channel_id=1, source_target_pairs={{0,1},{1,2},{2,3},{3,4},{4,5},{5,6},{6,7},{7,8},{8,9},{9,10},{10,1... | collective-permute-start | bytes 4718600 | tf_op jit(solution)/shard_map/ppermute | solution.py:331
  7.8 1.3 %collective-permute-start.4 = (f32[6,32,16,128]{3,2,1,0:T(8,128)}, f32[6,32,16,128]{3,2,1,0:T(8,128)}, u32[]{:S(2)}, u32[]{:S(2)}) collective-permute-start(f32[6,32,16,128]{3,2,1,0:T(8,128)} %raw.3), channel_id=1, source_target_pairs={{1,0},{2,1},{3,2},{4,3},{5,4},{6,5},{7,6},{8,7},{9,8},{10,9},{11,1... | collective-permute-start | bytes 4718600 | tf_op jit(solution)/shard_map/ppermute | solution.py:332
  9.1 0.8 fusion.12
  9.9 0.1 fusion.11
  10.0 0.7 copy-done.2
  10.7 1.6 %weights.1 = (bf16[288,240]{1,0:T(8,128)(2,1)S(1)}, bf16[6,256,256]{2,1,0:T(8,128)(2,1)S(1)}, bf16[6,256,768]{2,1,0:T(8,128)(2,1)S(1)}, bf16[96,144]{1,0:T(8,128...) custom-call(f32[6,3,31]{2,1,0:T(4,128)S(1)} %copy-done.2), custom_call_target="tpu_custom_call" | custom-call | flops 10000000 | bytes 10000000 | tf_op jit(solution)/shard_map/weights/pallas_call | solution.py:86
  12.3 0.1 multiply_reduce_fusion.2
  12.4 4.9 %collective-permute-done.far_before = f32[32,16,128]{2,1,0:T(8,128)S(1)} collective-permute-done((f32[32,16,128]{2,1,0:T(8,128)}, f32[32,16,128]{2,1,0:T(8,128)S(1)}, u32[]{:S(2)}, u32[]{:S(2)}) %collective-permute-start) | collective-permute-done | bytes 262176 | tf_op jit(solution)/shard_map/ppermute | solution.py:303
  17.4 1.0 %pad_maximum_fusion = f32[2,32,16,128]{3,2,1,0:T(8,128)S(1)} fusion(f32[1,32,16,128]{3,2,1,0:T(8,128)S(1)} %select_bitcast_fusion.1, f32[1,32,16,128]{3,2,1,0:T(8,128)} %bitcast.15), kind=kLoop, calls=%fused_computation | loop fusion | flops 131072 | bytes 1048576 | tf_op jit(solution)/shard_map/stack | solution.py:308
  18.4 0.1 collective-permute-start.2
  18.5 0.1 multiply_reduce_fusion
  18.6 0.1 multiply_reduce_fusion.1.wzs
  18.7 0.1 broadcast_multiply_fusion.1.wyx
  18.8 1.6 %collective-permute-done.2.near = f32[2,32,16,128]{3,2,1,0:T(8,128)S(1)} collective-permute-done((f32[2,32,16,128]{3,2,1,0:T(8,128)S(1)}, f32[2,32,16,128]{3,2,1,0:T(8,128)S(1)}, u32[]{:S(2)}, u32[]{:S(2)}) %collective-permute-start.2) | collective-permute-done | bytes 524320 | tf_op jit(solution)/shard_map/ppermute | solution.py:309
  20.4 0.9 copy-done
  21.3 6.0 %forward.1.blurred = f32[6,32,48,128]{3,2,1,0:T(8,128)S(1)} custom-call(s32[1]{0:T(128)} %bitcast.parity, f32[32,16,128]{2,1,0:T(8,128)S(1)} %collective-permute-done.far_before, f32[2,32,16,128]{3,2,1,0:T(8,128)S(1)} %collective-permute-done.2.near, f32[32,16,128]{2,1,0:T(8,128)S(1)} %copy-done, f32[32,16,128]{2,1,0:T(8,128)S(1)} %collective-permute-done.1.far_after, ...), custom_call_target="tpu_custom_call" | custom-call | flops 10000000000 | bytes 10000000 | tf_op jit(solution)/shard_map/forward/pallas_call | solution.py:243
  27.4 6.8 %adjoint.1 = (f32[32,16,128]{2,1,0:T(8,128)S(1)}, f32[18,128]{1,0:T(8,128)S(1)}) custom-call(f32[32,16,128]{2,1,0:T(8,128)S(1)} %copy-done.1, f32[6,32,48,128]{3,2,1,0:T(8,128)S(1)} %forward.1.blurred, f32[6,32,16,128]{3,2,1,0:T(8,128)S(1)} %collective-permute-done.3.before, f32[6,32,16,128]{3,2,1,0:T(8,128)S(1)} %copy-done.3, ...), custom_call_target="tpu_custom_call" | custom-call | flops 10000000000 | bytes 10000000 | tf_op jit(solution)/shard_map/adjoint/pallas_call | solution.py:261
  34.2 27.0 %collective-permute-start.5 = (f32[32,16,128]{2,1,0:T(8,128)S(1)}, f32[32,16,128]{2,1,0:T(8,128)S(1)}, u32[]{:S(2)}, u32[]{:S(2)}) collective-permute-start(f32[32,16,128]{2,1,0:T(8,128)S(1)} %get-tuple-element.26.own), channel_id=1, source_target_pairs={{0,2},{1,3},{2,4},{3,5},{4,6},{5,7},{6,8},{7,9},{8,10},{9,11},{10,... | collective-permute-start | bytes 786440 | tf_op jit(solution)/shard_map/ppermute | solution.py:303
  61.2 1.3 %collective-permute-start.6 = (f32[32,16,128]{2,1,0:T(8,128)S(1)}, f32[32,16,128]{2,1,0:T(8,128)S(1)}, u32[]{:S(2)}, u32[]{:S(2)}) collective-permute-start(f32[32,16,128]{2,1,0:T(8,128)S(1)} %get-tuple-element.26.own), channel_id=1, source_target_pairs={{2,0},{3,1},{4,2},{5,3},{6,4},{7,5},{8,6},{9,7},{10,8},{11,9},{12,... | collective-permute-start | bytes 786440 | tf_op jit(solution)/shard_map/ppermute | solution.py:303
  62.5 0.1 collective-permute-start.7
  62.6 1.2 %collective-permute-done.7 = f32[18,128]{1,0:T(8,128)S(1)} collective-permute-done((f32[18,128]{1,0:T(8,128)S(1)}, f32[18,128]{1,0:T(8,128)S(1)}, u32[]{:S(2)}, u32[]{:S(2)}) %collective-permute-start.7) | collective-permute-done | bytes 9248 | tf_op jit(solution)/shard_map/ppermute | solution.py:350
  63.7 2.6 %collective-permute-start.8 = (f32[18,128]{1,0:T(8,128)S(1)}, f32[18,128]{1,0:T(8,128)S(1)}, u32[]{:S(2)}, u32[]{:S(2)}) collective-permute-start(f32[18,128]{1,0:T(8,128)S(1)} %add.69), channel_id=1, source_target_pairs={{0,2},{1,3},{2,0},{3,1},{4,6},{5,7},{6,4},{7,5},{8,10},{9,11},{10,... | collective-permute-start | bytes 27656 | tf_op jit(solution)/shard_map/ppermute | solution.py:350
  66.4 5.5 %collective-permute-done.8 = f32[18,128]{1,0:T(8,128)S(1)} collective-permute-done((f32[18,128]{1,0:T(8,128)S(1)}, f32[18,128]{1,0:T(8,128)S(1)}, u32[]{:S(2)}, u32[]{:S(2)}) %collective-permute-start.8) | collective-permute-done | bytes 9248 | tf_op jit(solution)/shard_map/ppermute | solution.py:350
  71.9 3.8 %collective-permute-start.9 = (f32[18,128]{1,0:T(8,128)S(1)}, f32[18,128]{1,0:T(8,128)S(1)}, u32[]{:S(2)}, u32[]{:S(2)}) collective-permute-start(f32[18,128]{1,0:T(8,128)S(1)} %add.70), channel_id=1, source_target_pairs={{0,4},{1,5},{2,6},{3,7},{4,0},{5,1},{6,2},{7,3},{8,12},{9,13},{10,... | collective-permute-start | bytes 27656 | tf_op jit(solution)/shard_map/ppermute | solution.py:350
  75.7 1.7 %collective-permute-done.9 = f32[18,128]{1,0:T(8,128)S(1)} collective-permute-done((f32[18,128]{1,0:T(8,128)S(1)}, f32[18,128]{1,0:T(8,128)S(1)}, u32[]{:S(2)}, u32[]{:S(2)}) %collective-permute-start.9) | collective-permute-done | bytes 9248 | tf_op jit(solution)/shard_map/ppermute | solution.py:350
  77.5 3.1 %collective-permute-start.11 = (f32[18,128]{1,0:T(8,128)S(1)}, f32[18,128]{1,0:T(8,128)S(1)}, u32[]{:S(2)}, u32[]{:S(2)}) collective-permute-start(f32[18,128]{1,0:T(8,128)S(1)} %add.71), channel_id=1, source_target_pairs={{0,8},{1,9},{2,10},{3,11},{4,12},{5,13},{6,14},{7,15},{8,0},{9,1},... | collective-permute-start | bytes 27656 | tf_op jit(solution)/shard_map/ppermute | solution.py:350
  80.6 12.5 %iteration.1 = f32[32,16,128]{2,1,0:T(8,128)S(1)} custom-call(s32[1]{0:T(128)} %bitcast.parity, f32[32,16,128]{2,1,0:T(8,128)S(1)} %collective-permute-done.5.far_before, f32[2,32,16,128]{3,2,1,0:T(8,128)S(1)} %collective-permute-done.10.near, f32[32,16,128]{2,1,0:T(8,128)S(1)} %get-tuple-element.26.own, ...), custom_call_target="tpu_custom_call" | custom-call | flops 20000000000 | bytes 20000000 | tf_op jit(solution)/shard_map/iteration/pallas_call | solution.py:280
  93.1 0.1 add_reduce_fusion
  93.2 0.7 add_reduce_fusion.1
  94.6 0.7 broadcast_multiply_fusion
  (25 shorter events, 0.2 us)
Async XLA Ops:
  0.0 17.4 %collective-permute-start = (f32[32,16,128]{2,1,0:T(8,128)}, f32[32,16,128]{2,1,0:T(8,128)S(1)}, u32[]{:S(2)}, u32[]{:S(2)}) collective-permute-start(f32[32,16,128]{2,1,0:T(8,128)} %current.1), channel_id=1, source_target_pairs={{0,2},{1,3},{2,4},{3,5},{4,6},{5,7},{6,8},{7,9},{8,10},{9,11},{10,... | collective-permute-start | bytes 786440 | tf_op jit(solution)/shard_map/ppermute | solution.py:303
  4.9 12.5 %collective-permute-start.1 = (f32[32,16,128]{2,1,0:T(8,128)}, f32[32,16,128]{2,1,0:T(8,128)S(1)}, u32[]{:S(2)}, u32[]{:S(2)}) collective-permute-start(f32[32,16,128]{2,1,0:T(8,128)} %current.1), channel_id=1, source_target_pairs={{2,0},{3,1},{4,2},{5,3},{6,4},{7,5},{8,6},{9,7},{10,8},{11,9},{12,... | collective-permute-start | bytes 786440 | tf_op jit(solution)/shard_map/ppermute | solution.py:303
  6.2 21.2 %collective-permute-start.3 = (f32[6,32,16,128]{3,2,1,0:T(8,128)}, f32[6,32,16,128]{3,2,1,0:T(8,128)S(1)}, u32[]{:S(2)}, u32[]{:S(2)}) collective-permute-start(f32[6,32,16,128]{3,2,1,0:T(8,128)} %raw.3), channel_id=1, source_target_pairs={{0,1},{1,2},{2,3},{3,4},{4,5},{5,6},{6,7},{7,8},{8,9},{9,10},{10,1... | collective-permute-start | bytes 4718600 | tf_op jit(solution)/shard_map/ppermute | solution.py:331
  7.8 19.6 %collective-permute-start.4 = (f32[6,32,16,128]{3,2,1,0:T(8,128)}, f32[6,32,16,128]{3,2,1,0:T(8,128)}, u32[]{:S(2)}, u32[]{:S(2)}) collective-permute-start(f32[6,32,16,128]{3,2,1,0:T(8,128)} %raw.3), channel_id=1, source_target_pairs={{1,0},{2,1},{3,2},{4,3},{5,4},{6,5},{7,6},{8,7},{9,8},{10,9},{11,1... | collective-permute-start | bytes 4718600 | tf_op jit(solution)/shard_map/ppermute | solution.py:332
  10.0 0.7 copy-start.2
  18.4 2.0 %collective-permute-start.2 = (f32[2,32,16,128]{3,2,1,0:T(8,128)S(1)}, f32[2,32,16,128]{3,2,1,0:T(8,128)S(1)}, u32[]{:S(2)}, u32[]{:S(2)}) collective-permute-start(f32[2,32,16,128]{3,2,1,0:T(8,128)S(1)} %pad_maximum_fusion), channel_id=1, source_target_pairs={{0,1},{1,0},{2,3},{3,2},{4,5},{5,4},{6,7},{7,6},{8,9},{9,8},{10,11... | collective-permute-start | bytes 1572872 | tf_op jit(solution)/shard_map/ppermute | solution.py:309
  20.4 1.0 copy-start
  21.3 6.1 %copy-start.1 = (f32[32,16,128]{2,1,0:T(8,128)S(1)}, f32[32,16,128]{2,1,0:T(8,128)}, u32[]{:S(2)}) copy-start(f32[32,16,128]{2,1,0:T(8,128)} %current.1) | copy-start | bytes 786436
  21.3 6.1 %copy-start.3 = (f32[6,32,16,128]{3,2,1,0:T(8,128)S(1)}, f32[6,32,16,128]{3,2,1,0:T(8,128)}, u32[]{:S(2)}) copy-start(f32[6,32,16,128]{3,2,1,0:T(8,128)} %raw.3) | copy-start | bytes 4718596
  34.2 43.1 %collective-permute-start.5 = (f32[32,16,128]{2,1,0:T(8,128)S(1)}, f32[32,16,128]{2,1,0:T(8,128)S(1)}, u32[]{:S(2)}, u32[]{:S(2)}) collective-permute-start(f32[32,16,128]{2,1,0:T(8,128)S(1)} %get-tuple-element.26.own), channel_id=1, source_target_pairs={{0,2},{1,3},{2,4},{3,5},{4,6},{5,7},{6,8},{7,9},{8,10},{9,11},{10,... | collective-permute-start | bytes 786440 | tf_op jit(solution)/shard_map/ppermute | solution.py:303
  61.2 16.2 %collective-permute-start.6 = (f32[32,16,128]{2,1,0:T(8,128)S(1)}, f32[32,16,128]{2,1,0:T(8,128)S(1)}, u32[]{:S(2)}, u32[]{:S(2)}) collective-permute-start(f32[32,16,128]{2,1,0:T(8,128)S(1)} %get-tuple-element.26.own), channel_id=1, source_target_pairs={{2,0},{3,1},{4,2},{5,3},{6,4},{7,5},{8,6},{9,7},{10,8},{11,9},{12,... | collective-permute-start | bytes 786440 | tf_op jit(solution)/shard_map/ppermute | solution.py:303
  62.5 1.2 %collective-permute-start.7 = (f32[18,128]{1,0:T(8,128)S(1)}, f32[18,128]{1,0:T(8,128)S(1)}, u32[]{:S(2)}, u32[]{:S(2)}) collective-permute-start(f32[18,128]{1,0:T(8,128)S(1)} %get-tuple-element.27), channel_id=1, source_target_pairs={{0,1},{1,0},{2,3},{3,2},{4,5},{5,4},{6,7},{7,6},{8,9},{9,8},{10,11... | collective-permute-start | bytes 27656 | tf_op jit(solution)/shard_map/ppermute | solution.py:350
  63.7 8.1 %collective-permute-start.8 = (f32[18,128]{1,0:T(8,128)S(1)}, f32[18,128]{1,0:T(8,128)S(1)}, u32[]{:S(2)}, u32[]{:S(2)}) collective-permute-start(f32[18,128]{1,0:T(8,128)S(1)} %add.69), channel_id=1, source_target_pairs={{0,2},{1,3},{2,0},{3,1},{4,6},{5,7},{6,4},{7,5},{8,10},{9,11},{10,... | collective-permute-start | bytes 27656 | tf_op jit(solution)/shard_map/ppermute | solution.py:350
  71.9 5.5 %collective-permute-start.9 = (f32[18,128]{1,0:T(8,128)S(1)}, f32[18,128]{1,0:T(8,128)S(1)}, u32[]{:S(2)}, u32[]{:S(2)}) collective-permute-start(f32[18,128]{1,0:T(8,128)S(1)} %add.70), channel_id=1, source_target_pairs={{0,4},{1,5},{2,6},{3,7},{4,0},{5,1},{6,2},{7,3},{8,12},{9,13},{10,... | collective-permute-start | bytes 27656 | tf_op jit(solution)/shard_map/ppermute | solution.py:350
  77.4 3.2 %collective-permute-start.10 = (f32[2,32,16,128]{3,2,1,0:T(8,128)S(1)}, f32[2,32,16,128]{3,2,1,0:T(8,128)S(1)}, u32[]{:S(2)}, u32[]{:S(2)}) collective-permute-start(f32[2,32,16,128]{3,2,1,0:T(8,128)S(1)} %pad_maximum_fusion.1), channel_id=1, source_target_pairs={{0,1},{1,0},{2,3},{3,2},{4,5},{5,4},{6,7},{7,6},{8,9},{9,8},{10,11... | collective-permute-start | bytes 1572872 | tf_op jit(solution)/shard_map/ppermute | solution.py:309
  77.5 15.6 %collective-permute-start.11 = (f32[18,128]{1,0:T(8,128)S(1)}, f32[18,128]{1,0:T(8,128)S(1)}, u32[]{:S(2)}, u32[]{:S(2)}) collective-permute-start(f32[18,128]{1,0:T(8,128)S(1)} %add.71), channel_id=1, source_target_pairs={{0,8},{1,9},{2,10},{3,11},{4,12},{5,13},{6,14},{7,15},{8,0},{9,1},... | collective-permute-start | bytes 27656 | tf_op jit(solution)/shard_map/ppermute | solution.py:350

commit v2 on v1

--- a/solution.py
+++ b/solution.py
@@ -13,7 +13,8 @@
 VMEM = pltpu.MemorySpace.VMEM
 SMEM = pltpu.MemorySpace.SMEM
 FULL = pl.BlockSpec(memory_space=VMEM)
-LIMIT = 24 * 1024 * 1024
+LIMIT = 30 * 1024 * 1024
+STEP = 2
 TINY = float(np.finfo(np.float32).tiny)
 
 
@@ -53,15 +54,22 @@
         row_y = placed_row(taps_ref[:, 1, :], lambda k: order(k) + rows - margin, 256)
         high = row_y.astype(BF16).astype(F32)
         low = row_y - high
-        row_y = high + pltpu.roll(high, in_rows, 1) + pltpu.roll(low, 2 * in_rows, 1)
+        if flip:
+            row_y = [part + pltpu.roll(part, in_rows, 1) for part in (high, low)]
+        else:
+            row_y = high + pltpu.roll(high, in_rows, 1) + pltpu.roll(low, 2 * in_rows, 1)
         row_x = placed_row(taps_ref[:, 2, :], lambda k: lax.rem(margin - order(k) + 2 * cols, 2 * cols), 2 * cols)
         width_z = 16 * planes
         row_z = placed_row(
             taps_ref[:, 0, :], lambda k: lax.rem(8 * (order(k) - margin) + width_z, width_z), width_z
         )
         for v in range(views):
-            band = slanted(row_y[v : v + 1], out_rows)
-            wy[v * out_rows : (v + 1) * out_rows, :] = band[:, : 3 * in_rows].astype(BF16)
+            if flip:
+                for j, row in enumerate(row_y):
+                    wy[v, j * rows : (j + 1) * rows, :] = slanted(row[v : v + 1], rows)[:, : 2 * in_rows].astype(BF16)
+            else:
+                band = slanted(row_y[v : v + 1], out_rows)
+                wy[v * out_rows : (v + 1) * out_rows, :] = band[:, : 3 * in_rows].astype(BF16)
             high, low = split(slanted(row_x[v : v + 1], cols)[:, :cols])
             wx[v, :cols, :cols] = high
             wx[v, cols:, :cols] = high
@@ -77,9 +85,9 @@
 def make_weights(taps, planes, rows, cols):
     views = taps.shape[0]
     shapes = []
-    for out_rows in (3 * rows, rows):
+    for row_weights in ((views * 3 * rows, 15 * rows), (views, 2 * rows, 6 * rows)):
         shapes += [
-            jax.ShapeDtypeStruct((views * out_rows, 3 * (out_rows + 2 * rows)), BF16),
+            jax.ShapeDtypeStruct(row_weights, BF16),
             jax.ShapeDtypeStruct((views, 2 * cols, 2 * cols), BF16),
             jax.ShapeDtypeStruct((views, 8 * planes, 24 * planes), BF16),
         ]
@@ -139,25 +147,31 @@
             out[:, at : at + 8, :] = result[:, j * cols : (j + 1) * cols].reshape(planes, 8, cols)
 
 
-def adjoint_view(blurred, before, raw, after, wy, wx, wz, ya, acc):
-    planes, rows, cols = raw.shape
-
-    def quotient(z):
-        counts = jnp.concatenate([before[z], raw[z], after[z]], axis=0)
-        below = jnp.maximum(blurred[z], TINY)
+def adjoint_views(blurred, before, raw, after, wy, wx, wz, ya, acc):
+    _, planes, rows, cols = raw.shape
+
+    def quotient(v, z):
+        counts = jnp.concatenate([before[v, z], raw[v, z], after[v, z]], axis=0)
+        below = jnp.maximum(blurred[v, z], TINY)
         inverse = pl.reciprocal(below, approx=True)
         return counts * (inverse * (2.0 - below * inverse))
 
-    for z in range(0, planes, 2):
-        high, low = split(dot(wy, stacked([quotient(z), quotient(z + 1)])))
-        for j in range(2):
-            ya[z + j, :, :cols] = high[:, j * cols : (j + 1) * cols]
-            ya[z + j, :, cols:] = low[:, j * cols : (j + 1) * cols]
+    for v in range(STEP):
+        for z in range(0, planes, 2):
+            high, low = split(jnp.concatenate([quotient(v, z), quotient(v, z + 1)], axis=1))
+            both = dot(wy[v], jnp.concatenate([high, low], axis=0))
+            high, low = split(both[:rows] + both[rows:])
+            for j in range(2):
+                ya[v, z + j, :, :cols] = high[:, j * cols : (j + 1) * cols]
+                ya[v, z + j, :, cols:] = low[:, j * cols : (j + 1) * cols]
     for pair in range(rows // 16):
-        result = two_groups(ya[:, 16 * pair : 16 * pair + 16, :], wx, wz, planes, cols)
+        chosen = slice(16 * pair, 16 * pair + 16)
+        logs = 0.0
+        for v in range(STEP):
+            logs = logs + jnp.log(two_groups(ya[v, :, chosen, :], wx[v], wz[v], planes, cols))
         for j in range(2):
             at = 16 * pair + 8 * j
-            acc[:, at : at + 8, :] += jnp.log(result[:, j * cols : (j + 1) * cols]).reshape(planes, 8, cols)
+            acc[:, at : at + 8, :] += logs[:, j * cols : (j + 1) * cols].reshape(planes, 8, cols)
 
 
 def forward_kernel(parity, far_before, near, own, far_after, wy, wx, wz, out, ys):
@@ -165,7 +179,8 @@
     def _():
         forward_rows(parity, far_before, near, own, far_after, wy, ys)
 
-    forward_view(pl.program_id(0), ys, wx[0], wz[0], out.at[0])
+    for v in range(STEP):
+        forward_view(STEP * pl.program_id(0) + v, ys, wx[v], wz[v], out.at[v])
 
 
 def weighted_sums(values, wzs, wyx, sums, at):
@@ -178,46 +193,55 @@
 
 
 def first_adjoint_kernel(current, blurred, before, raw, after, wy, wx, wz, wzs, wyx, out, sums, ya, acc):
-    view, views = pl.program_id(0), wyx.shape[0]
-
-    @pl.when(view == 0)
+    step, views = pl.program_id(0), wyx.shape[0]
+
+    @pl.when(step == 0)
     def _():
         acc[...] = jnp.zeros_like(acc)
-
-    sums[pl.ds(view, 1), :] = jnp.sum(jnp.sum(raw[0], axis=0), axis=0, keepdims=True)
-    adjoint_view(blurred.at[0], before.at[0], raw.at[0], after.at[0], wy[0], wx[0], wz[0], ya, acc)
-
-    @pl.when(view == views - 1)
+        sums[...] = jnp.zeros_like(sums)
+
+    for v in range(STEP):
+        total = jnp.sum(jnp.sum(raw[v], axis=0), axis=0, keepdims=True)
+        sums[pl.ds(STEP * step + v, 1), :] = total
+    adjoint_views(blurred, before, raw, after, wy, wx, wz, ya, acc)
+
+    @pl.when(step == pl.num_programs(0) - 1)
     def _():
         out[...] = current[...] * jnp.exp(acc[...] * (1.0 / views))
-        weighted_sums(current, wzs, wyx, sums, views)
-        weighted_sums(out, wzs, wyx, sums, 2 * views)
+        weighted_sums(current, wzs, wyx, sums, sums.shape[0] // 3)
+        weighted_sums(out, wzs, wyx, sums, 2 * sums.shape[0] // 3)
 
 
 def iteration_kernel(
-    parity, far_before, near, own, far_after, before, raw, after, wy, wx, wz, wya, wxa, wza, out, ys, blurred, ya, acc
+    parity, far_before, near, own, far_after, before, raw, after, wy, wx, wz, wya, wxa, wza, part, rest,
+    out, ys, blurred, ya, acc,
 ):
-    view = pl.program_id(0)
-
-    @pl.when(view == 0)
+    step, views = pl.program_id(0), ys.shape[0]
+
+    @pl.when(step == 0)
     def _():
         acc[...] = jnp.zeros_like(acc)
         forward_rows(parity, far_before, near, own, far_after, wy, ys)
 
-    forward_view(view, ys, wx[0], wz[0], blurred)
-    adjoint_view(blurred, before.at[0], raw.at[0], after.at[0], wya[0], wxa[0], wza[0], ya, acc)
-
-    @pl.when(view == pl.num_programs(0) - 1)
-    def _():
-        out[...] = own[...] * jnp.exp(acc[...] * (1.0 / ys.shape[0]))
+    for v in range(STEP):
+        forward_view(STEP * step + v, ys, wx[v], wz[v], blurred.at[v])
+    adjoint_views(blurred, before, raw, after, wya, wxa, wza, ya, acc)
+
+    @pl.when(step == pl.num_programs(0) - 1)
+    def _():
+        sums = jnp.sum(part[...] + rest[...], axis=1, keepdims=True)
+        space = sums.shape[0] // 3
+        total, first, second = (sums[i * space : i * space + views] for i in range(3))
+        scale = jnp.sum(jnp.log(first / total) + jnp.log(second / total), axis=0, keepdims=True)
+        out[...] = own[...] * jnp.exp((acc[...] + scale[None]) * (1.0 / views))
 
 
 def whole(array):
     return pl.BlockSpec(array.shape, lambda v: (0,) * array.ndim)
 
 
-def one_view(array):
-    return pl.BlockSpec((1,) + array.shape[1:], lambda v: (v,) + (0,) * (array.ndim - 1))
+def step_views(array):
+    return pl.BlockSpec((STEP,) + array.shape[1:], lambda v: (v,) + (0,) * (array.ndim - 1))
 
 
 def params(flops, moved):
@@ -232,7 +256,7 @@
 
 
 def adjoint_scratch(planes, rows, cols):
-    return [pltpu.VMEM((planes, rows, 2 * cols), BF16), pltpu.VMEM((planes, rows, cols), F32)]
+    return [pltpu.VMEM((STEP, planes, rows, 2 * cols), BF16), pltpu.VMEM((planes, rows, cols), F32)]
 
 
 def forward(parity, slabs, weights):
@@ -242,12 +266,12 @@
     out = jax.ShapeDtypeStruct((views, planes, 3 * rows, cols), F32)
     return pl.pallas_call(
         forward_kernel,
-        grid=(views,),
+        grid=(views // STEP,),
         out_shape=out,
         in_specs=[pl.BlockSpec(memory_space=SMEM)]
         + [whole(s) for s in slabs]
-        + [whole(wy), one_view(wx), one_view(wz)],
-        out_specs=one_view(out),
+        + [whole(wy), step_views(wx), step_views(wz)],
+        out_specs=step_views(out),
         scratch_shapes=[row_scratch(views, planes, rows, cols)],
         name="forward",
         **params(10**10, 10**7),
@@ -257,13 +281,13 @@
 def first_adjoint(current, blurred, before, raw, after, weights, wzs, wyx):
     wy, wx, wz = weights
     views = raw.shape[0]
-    shapes = [jax.ShapeDtypeStruct(current.shape, F32), jax.ShapeDtypeStruct((3 * views, current.shape[2]), F32)]
+    shapes = [jax.ShapeDtypeStruct(current.shape, F32), jax.ShapeDtypeStruct((24 * -(-views // 8), current.shape[2]), F32)]
     return pl.pallas_call(
         first_adjoint_kernel,
-        grid=(views,),
+        grid=(views // STEP,),
         out_shape=shapes,
         in_specs=[whole(current)]
-        + [one_view(a) for a in (blurred, before, raw, after, wy, wx, wz)]
+        + [step_views(a) for a in (blurred, before, raw, after, wy, wx, wz)]
         + [pl.BlockSpec(memory_space=SMEM), whole(wyx)],
         out_specs=[whole(s) for s in shapes],
         scratch_shapes=adjoint_scratch(*current.shape),
@@ -272,29 +296,30 @@
     )(current, blurred, before, raw, after, wy, wx, wz, wzs, wyx)
 
 
-def full_iteration(parity, slabs, before, raw, after, weights, adjoint_weights):
+def full_iteration(parity, slabs, before, raw, after, weights, adjoint_weights, part, rest):
     current = slabs[2]
     planes, rows, cols = current.shape
     views = raw.shape[0]
     wy, wx, wz = weights
     return pl.pallas_call(
         iteration_kernel,
-        grid=(views,),
+        grid=(views // STEP,),
         out_shape=jax.ShapeDtypeStruct(current.shape, F32),
         in_specs=[pl.BlockSpec(memory_space=SMEM)]
         + [whole(s) for s in slabs]
-        + [one_view(a) for a in (before, raw, after)]
-        + [whole(wy), one_view(wx), one_view(wz)]
-        + [one_view(a) for a in adjoint_weights],
+        + [step_views(a) for a in (before, raw, after)]
+        + [whole(wy), step_views(wx), step_views(wz)]
+        + [step_views(a) for a in adjoint_weights]
+        + [whole(part), whole(rest)],
         out_specs=whole(current),
         scratch_shapes=[
             row_scratch(views, planes, rows, cols),
-            pltpu.VMEM((planes, 3 * rows, cols), F32),
+            pltpu.VMEM((STEP, planes, 3 * rows, cols), F32),
         ]
         + adjoint_scratch(planes, rows, cols),
         name="iteration",
         **params(2 * 10**10, 2 * 10**7),
-    )(parity, *slabs, before, raw, after, *weights, *adjoint_weights)
+    )(parity, *slabs, before, raw, after, *weights, *adjoint_weights, part, rest)
 
 
 def two_slabs_away(value, count):
@@ -336,28 +361,25 @@
     wx_sums = tap_sums(taps[:, 2], 0, cols, cols)
     wyx = wy_sums[:, :, None] * wx_sums[:, None, :]
 
-    forward_weights, (wy, wx, wz) = make_weights(taps, planes, rows, cols)
-    adjoint_weights = (wy.reshape(views, rows, -1), wx, wz)
+    forward_weights, adjoint_weights = make_weights(taps, planes, rows, cols)
 
     slabs = with_near(estimate, *far, parity, count)
     blurred = forward(parity, slabs, forward_weights)
     current, sums = first_adjoint(estimate, blurred, before, raw, after, adjoint_weights, wzs, wyx)
 
     far = two_slabs_away(current, count)
-    sums, others, distance = sums, None, 1
-    while distance < count:
+    rounds = [1 << b for b in range(count.bit_length() - 1)]
+    rounds = rounds[:1] + rounds[2:] + rounds[1:2]
+    others = None
+    for r, distance in enumerate(rounds):
         sums = sums if others is None else sums + others
         others = lax.ppermute(sums, "slab", [(i, i ^ distance) for i in range(count)])
-        distance *= 2
-        if distance == 8:
+        if r == 1:
             *far, sums, others = lax.optimization_barrier((*far, sums, others))
     slabs = with_near(current, *far, parity, count)
-    current = full_iteration(parity, slabs, before, raw, after, forward_weights, adjoint_weights)
-
-    current, sums, others = lax.optimization_barrier((current, sums, others))
-    total, first, second = jnp.sum((sums + others).reshape(3, views, cols), axis=2)
-    scale = jnp.log(first / total) + jnp.log(second / total)
-    return current * jnp.exp(jnp.mean(scale))
+    return full_iteration(
+        parity, slabs, before, raw, after, forward_weights, adjoint_weights, sums, others
+    )
 
 
 def solution(mesh):

time: 95.8 us -> 92.4 us (0.965)
  waiting for transfers between devices: 14.9 us -> 16.7 us
  Pallas kernels: 26.9 us -> 25.2 us
  other arithmetic: 3.08 us -> 1.56 us
  starting transfers between devices: 47 us -> 45.9 us
    pallas_call x3, Pallas kernels: 25.3 us -> 23.5 us  [the longest x1 11.1 us: full_iteration(): pl.pallas_call(iteration_kernel, grid=(views // STEP,), out_shape=jax.Sha...]
    ppermute x4, waiting for transfers between devices: 8.31 us -> 9.71 us  [per_device(): lax.ppermute(sums, 'slab', [(i, i ^ distance) for i in range(count)])]
  transfers between devices with their start and end apart: 12 -> 12, of which waited for: 5 -> 7; matrix products, arithmetic and copies ran while one was open for 2% -> 3% of each run, Pallas kernels for 21% -> 9%
where the time goes in v2:
time: 92.4 us; the launch traced here: 92 us
  starting transfers between devices  45.9 us (50%)
  Pallas kernels  25.2 us (27%)
  waiting for transfers between devices  16.7 us (18%)
  local copies, waits for them, and re-layouts  2.5 us (3%)
  other arithmetic  1.56 us (2%)
    ppermute x4, starting transfers between devices, two_slabs_away(): return (lax.ppermute(value, 'slab', up), lax.ppermute(value, 'slab', down))  33.7 us
    pallas_call x1, Pallas kernels, full_iteration(): pl.pallas_call(iteration_kernel, grid=(views // STEP,), out_shape=jax.Sha...  11.1 us
    ppermute x4, waiting for transfers between devices, per_device(): lax.ppermute(sums, 'slab', [(i, i ^ distance) for i in range(count)])  9.71 us
    ppermute x4, starting transfers between devices, per_device(): lax.ppermute(sums, 'slab', [(i, i ^ distance) for i in range(count)])  8.9 us
    pallas_call x1, Pallas kernels, forward(): pl.pallas_call(forward_kernel, grid=(views // STEP,), out_shape=out, in_s...  6.76 us
    pallas_call x1, Pallas kernels, first_adjoint(): pl.pallas_call(first_adjoint_kernel, grid=(views // STEP,), out_shape=sha...  5.67 us
    ppermute x4, waiting for transfers between devices, two_slabs_away(): return (lax.ppermute(value, 'slab', up), lax.ppermute(value, 'slab', down))  5.38 us
  transfers between devices with their start and end apart: 12, of which 7 were waited for; matrix products, arithmetic and copies ran while one was open for 3% of the time, Pallas kernels for 9%

profile of v2, /device:TPU:0, one launch (start us, length us, event | category | flops | bytes accessed | tf_op | source)
XLA Modules:
  0.0 92.0 jit_solution(16014326350224146047)
XLA Ops:
  0.0 4.9 %collective-permute-start = (f32[32,16,128]{2,1,0:T(8,128)}, f32[32,16,128]{2,1,0:T(8,128)S(1)}, u32[]{:S(2)}, u32[]{:S(2)}) collective-permute-start(f32[32,16,128]{2,1,0:T(8,128)} %current.1), channel_id=1, source_target_pairs={{0,2},{1,3},{2,4},{3,5},{4,6},{5,7},{6,8},{7,9},{8,10},{9,11},{10,... | collective-permute-start | bytes 786440 | tf_op jit(solution)/shard_map/ppermute | solution.py:328
  4.9 1.3 %collective-permute-start.1 = (f32[32,16,128]{2,1,0:T(8,128)}, f32[32,16,128]{2,1,0:T(8,128)S(1)}, u32[]{:S(2)}, u32[]{:S(2)}) collective-permute-start(f32[32,16,128]{2,1,0:T(8,128)} %current.1), channel_id=1, source_target_pairs={{2,0},{3,1},{4,2},{5,3},{6,4},{7,5},{8,6},{9,7},{10,8},{11,9},{12,... | collective-permute-start | bytes 786440 | tf_op jit(solution)/shard_map/ppermute | solution.py:328
  6.2 1.6 %collective-permute-start.3 = (f32[6,32,16,128]{3,2,1,0:T(8,128)}, f32[6,32,16,128]{3,2,1,0:T(8,128)S(1)}, u32[]{:S(2)}, u32[]{:S(2)}) collective-permute-start(f32[6,32,16,128]{3,2,1,0:T(8,128)} %raw.3), channel_id=1, source_target_pairs={{0,1},{1,2},{2,3},{3,4},{4,5},{5,6},{6,7},{7,8},{8,9},{9,10},{10,1... | collective-permute-start | bytes 4718600 | tf_op jit(solution)/shard_map/ppermute | solution.py:356
  7.8 1.3 %collective-permute-start.4 = (f32[6,32,16,128]{3,2,1,0:T(8,128)}, f32[6,32,16,128]{3,2,1,0:T(8,128)}, u32[]{:S(2)}, u32[]{:S(2)}) collective-permute-start(f32[6,32,16,128]{3,2,1,0:T(8,128)} %raw.3), channel_id=1, source_target_pairs={{1,0},{2,1},{3,2},{4,3},{5,4},{6,5},{7,6},{8,7},{9,8},{10,9},{11,1... | collective-permute-start | bytes 4718600 | tf_op jit(solution)/shard_map/ppermute | solution.py:357
  9.1 0.8 fusion.12
  9.9 0.1 fusion.11
  10.0 0.7 copy-done.2
  10.7 1.6 %weights.1 = (bf16[288,240]{1,0:T(8,128)(2,1)S(1)}, bf16[6,256,256]{2,1,0:T(8,128)(2,1)S(1)}, bf16[6,256,768]{2,1,0:T(8,128)(2,1)S(1)}, bf16[6,32,96]{2,1,0:T(8,...) custom-call(f32[6,3,31]{2,1,0:T(4,128)S(1)} %copy-done.2), custom_call_target="tpu_custom_call" | custom-call | flops 10000000 | bytes 10000000 | tf_op jit(solution)/shard_map/weights/pallas_call | solution.py:94
  12.4 0.1 multiply_reduce_fusion.2
  12.4 4.9 %collective-permute-done.far_before = f32[32,16,128]{2,1,0:T(8,128)S(1)} collective-permute-done((f32[32,16,128]{2,1,0:T(8,128)}, f32[32,16,128]{2,1,0:T(8,128)S(1)}, u32[]{:S(2)}, u32[]{:S(2)}) %collective-permute-start) | collective-permute-done | bytes 262176 | tf_op jit(solution)/shard_map/ppermute | solution.py:328
  17.4 1.0 %pad_maximum_fusion = f32[2,32,16,128]{3,2,1,0:T(8,128)S(1)} fusion(f32[1,32,16,128]{3,2,1,0:T(8,128)S(1)} %select_bitcast_fusion.1, f32[1,32,16,128]{3,2,1,0:T(8,128)} %bitcast.14), kind=kLoop, calls=%fused_computation | loop fusion | flops 131072 | bytes 1048576 | tf_op jit(solution)/shard_map/stack | solution.py:333
  18.4 0.1 collective-permute-start.2
  18.5 0.1 multiply_reduce_fusion
  18.6 0.1 multiply_reduce_fusion.1.wzs
  18.7 0.1 broadcast_multiply_fusion.wyx
  18.8 1.6 %collective-permute-done.2.near = f32[2,32,16,128]{3,2,1,0:T(8,128)S(1)} collective-permute-done((f32[2,32,16,128]{3,2,1,0:T(8,128)S(1)}, f32[2,32,16,128]{3,2,1,0:T(8,128)S(1)}, u32[]{:S(2)}, u32[]{:S(2)}) %collective-permute-start.2) | collective-permute-done | bytes 524320 | tf_op jit(solution)/shard_map/ppermute | solution.py:334
  20.4 0.9 %copy-done = f32[32,16,128]{2,1,0:T(8,128)S(1)} copy-done((f32[32,16,128]{2,1,0:T(8,128)S(1)}, f32[32,16,128]{2,1,0:T(8,128)}, u32[]{:S(2)}) %copy-start) | copy-done | bytes 262168
  21.3 6.8 %forward.1.blurred = f32[6,32,48,128]{3,2,1,0:T(8,128)S(1)} custom-call(s32[1]{0:T(128)} %bitcast.parity, f32[32,16,128]{2,1,0:T(8,128)S(1)} %collective-permute-done.far_before, f32[2,32,16,128]{3,2,1,0:T(8,128)S(1)} %collective-permute-done.2.near, f32[32,16,128]{2,1,0:T(8,128)S(1)} %copy-done, f32[32,16,128]{2,1,0:T(8,128)S(1)} %collective-permute-done.1.far_after, ...), custom_call_target="tpu_custom_call" | custom-call | flops 10000000000 | bytes 10000000 | tf_op jit(solution)/shard_map/forward/pallas_call | solution.py:267
  28.1 5.7 %adjoint.1 = (f32[32,16,128]{2,1,0:T(8,128)S(1)}, f32[24,128]{1,0:T(8,128)S(1)}) custom-call(f32[32,16,128]{2,1,0:T(8,128)S(1)} %copy-done.1, f32[6,32,48,128]{3,2,1,0:T(8,128)S(1)} %forward.1.blurred, f32[6,32,16,128]{3,2,1,0:T(8,128)S(1)} %collective-permute-done.3.before, f32[6,32,16,128]{3,2,1,0:T(8,128)S(1)} %copy-done.3, ...), custom_call_target="tpu_custom_call" | custom-call | flops 10000000000 | bytes 10000000 | tf_op jit(solution)/shard_map/adjoint/pallas_call | solution.py:285
  33.8 26.2 %collective-permute-start.5 = (f32[32,16,128]{2,1,0:T(8,128)S(1)}, f32[32,16,128]{2,1,0:T(8,128)S(1)}, u32[]{:S(2)}, u32[]{:S(2)}) collective-permute-start(f32[32,16,128]{2,1,0:T(8,128)S(1)} %get-tuple-element.23.own), channel_id=1, source_target_pairs={{0,2},{1,3},{2,4},{3,5},{4,6},{5,7},{6,8},{7,9},{8,10},{9,11},{10,... | collective-permute-start | bytes 786440 | tf_op jit(solution)/shard_map/ppermute | solution.py:328
  60.1 1.3 %collective-permute-start.6 = (f32[32,16,128]{2,1,0:T(8,128)S(1)}, f32[32,16,128]{2,1,0:T(8,128)S(1)}, u32[]{:S(2)}, u32[]{:S(2)}) collective-permute-start(f32[32,16,128]{2,1,0:T(8,128)S(1)} %get-tuple-element.23.own), channel_id=1, source_target_pairs={{2,0},{3,1},{4,2},{5,3},{6,4},{7,5},{8,6},{9,7},{10,8},{11,9},{12,... | collective-permute-start | bytes 786440 | tf_op jit(solution)/shard_map/ppermute | solution.py:328
  61.4 0.1 collective-permute-start.7
  61.4 1.2 %collective-permute-done.7 = f32[24,128]{1,0:T(8,128)S(1)} collective-permute-done((f32[24,128]{1,0:T(8,128)S(1)}, f32[24,128]{1,0:T(8,128)S(1)}, u32[]{:S(2)}, u32[]{:S(2)}) %collective-permute-start.7) | collective-permute-done | bytes 12320 | tf_op jit(solution)/shard_map/ppermute | solution.py:376
  62.6 3.5 %collective-permute-start.8 = (f32[24,128]{1,0:T(8,128)S(1)}, f32[24,128]{1,0:T(8,128)S(1)}, u32[]{:S(2)}, u32[]{:S(2)}) collective-permute-start(f32[24,128]{1,0:T(8,128)S(1)} %add.63), channel_id=1, source_target_pairs={{0,4},{1,5},{2,6},{3,7},{4,0},{5,1},{6,2},{7,3},{8,12},{9,13},{10,... | collective-permute-start | bytes 36872 | tf_op jit(solution)/shard_map/ppermute | solution.py:376
  66.1 3.9 %collective-permute-done.8 = f32[24,128]{1,0:T(8,128)S(1)} collective-permute-done((f32[24,128]{1,0:T(8,128)S(1)}, f32[24,128]{1,0:T(8,128)S(1)}, u32[]{:S(2)}, u32[]{:S(2)}) %collective-permute-start.8) | collective-permute-done | bytes 12320 | tf_op jit(solution)/shard_map/ppermute | solution.py:376
  70.0 0.5 collective-permute-done.6.far_after
  70.5 0.4 collective-permute-start.9
  70.9 4.6 %collective-permute-start.10 = (f32[24,128]{1,0:T(8,128)S(1)}, f32[24,128]{1,0:T(8,128)S(1)}, u32[]{:S(2)}, u32[]{:S(2)}) collective-permute-start(f32[24,128]{1,0:T(8,128)S(1)} %add.64), channel_id=1, source_target_pairs={{0,8},{1,9},{2,10},{3,11},{4,12},{5,13},{6,14},{7,15},{8,0},{9,1},... | collective-permute-start | bytes 36872 | tf_op jit(solution)/shard_map/ppermute | solution.py:376
  75.5 1.7 %collective-permute-done.10 = f32[24,128]{1,0:T(8,128)S(1)} collective-permute-done((f32[24,128]{1,0:T(8,128)S(1)}, f32[24,128]{1,0:T(8,128)S(1)}, u32[]{:S(2)}, u32[]{:S(2)}) %collective-permute-start.10) | collective-permute-done | bytes 12320 | tf_op jit(solution)/shard_map/ppermute | solution.py:376
  77.2 0.7 collective-permute-start.11
  77.9 3.0 %collective-permute-done.11.rest = f32[24,128]{1,0:T(8,128)S(1)} collective-permute-done((f32[24,128]{1,0:T(8,128)S(1)}, f32[24,128]{1,0:T(8,128)S(1)}, u32[]{:S(2)}, u32[]{:S(2)}) %collective-permute-start.11) | collective-permute-done | bytes 12320 | tf_op jit(solution)/shard_map/ppermute | solution.py:376
  80.9 11.1 %iteration.1 = f32[32,16,128]{2,1,0:T(8,128)} custom-call(s32[1]{0:T(128)} %bitcast.parity, f32[32,16,128]{2,1,0:T(8,128)S(1)} %collective-permute-done.5.far_before, f32[2,32,16,128]{3,2,1,0:T(8,128)S(1)} %collective-permute-done.9.near, f32[32,16,128]{2,1,0:T(8,128)S(1)} %get-tuple-element.23.own, f32[32,16,128]{2,1,0:T(8,128)S(1)} %collective-permute-done.6.far_after, ...), custom_call_target="tpu_custom_call" | custom-call | flops 20000000000 | bytes 20000000 | tf_op jit(solution)/shard_map/iteration/pallas_call | solution.py:304
  (22 shorter events, 0.2 us)
Async XLA Ops:
  0.0 17.4 %collective-permute-start = (f32[32,16,128]{2,1,0:T(8,128)}, f32[32,16,128]{2,1,0:T(8,128)S(1)}, u32[]{:S(2)}, u32[]{:S(2)}) collective-permute-start(f32[32,16,128]{2,1,0:T(8,128)} %current.1), channel_id=1, source_target_pairs={{0,2},{1,3},{2,4},{3,5},{4,6},{5,7},{6,8},{7,9},{8,10},{9,11},{10,... | collective-permute-start | bytes 786440 | tf_op jit(solution)/shard_map/ppermute | solution.py:328
  4.9 12.5 %collective-permute-start.1 = (f32[32,16,128]{2,1,0:T(8,128)}, f32[32,16,128]{2,1,0:T(8,128)S(1)}, u32[]{:S(2)}, u32[]{:S(2)}) collective-permute-start(f32[32,16,128]{2,1,0:T(8,128)} %current.1), channel_id=1, source_target_pairs={{2,0},{3,1},{4,2},{5,3},{6,4},{7,5},{8,6},{9,7},{10,8},{11,9},{12,... | collective-permute-start | bytes 786440 | tf_op jit(solution)/shard_map/ppermute | solution.py:328
  6.2 21.9 %collective-permute-start.3 = (f32[6,32,16,128]{3,2,1,0:T(8,128)}, f32[6,32,16,128]{3,2,1,0:T(8,128)S(1)}, u32[]{:S(2)}, u32[]{:S(2)}) collective-permute-start(f32[6,32,16,128]{3,2,1,0:T(8,128)} %raw.3), channel_id=1, source_target_pairs={{0,1},{1,2},{2,3},{3,4},{4,5},{5,6},{6,7},{7,8},{8,9},{9,10},{10,1... | collective-permute-start | bytes 4718600 | tf_op jit(solution)/shard_map/ppermute | solution.py:356
  7.8 20.4 %collective-permute-start.4 = (f32[6,32,16,128]{3,2,1,0:T(8,128)}, f32[6,32,16,128]{3,2,1,0:T(8,128)}, u32[]{:S(2)}, u32[]{:S(2)}) collective-permute-start(f32[6,32,16,128]{3,2,1,0:T(8,128)} %raw.3), channel_id=1, source_target_pairs={{1,0},{2,1},{3,2},{4,3},{5,4},{6,5},{7,6},{8,7},{9,8},{10,9},{11,1... | collective-permute-start | bytes 4718600 | tf_op jit(solution)/shard_map/ppermute | solution.py:357
  10.0 0.7 copy-start.2
  18.4 2.0 %collective-permute-start.2 = (f32[2,32,16,128]{3,2,1,0:T(8,128)S(1)}, f32[2,32,16,128]{3,2,1,0:T(8,128)S(1)}, u32[]{:S(2)}, u32[]{:S(2)}) collective-permute-start(f32[2,32,16,128]{3,2,1,0:T(8,128)S(1)} %pad_maximum_fusion), channel_id=1, source_target_pairs={{0,1},{1,0},{2,3},{3,2},{4,5},{5,4},{6,7},{7,6},{8,9},{9,8},{10,11... | collective-permute-start | bytes 1572872 | tf_op jit(solution)/shard_map/ppermute | solution.py:334
  20.4 1.0 %copy-start = (f32[32,16,128]{2,1,0:T(8,128)S(1)}, f32[32,16,128]{2,1,0:T(8,128)}, u32[]{:S(2)}) copy-start(f32[32,16,128]{2,1,0:T(8,128)} %current.1) | copy-start | bytes 786436
  21.3 6.8 %copy-start.1 = (f32[32,16,128]{2,1,0:T(8,128)S(1)}, f32[32,16,128]{2,1,0:T(8,128)}, u32[]{:S(2)}) copy-start(f32[32,16,128]{2,1,0:T(8,128)} %current.1) | copy-start | bytes 786436
  21.3 6.8 %copy-start.3 = (f32[6,32,16,128]{3,2,1,0:T(8,128)S(1)}, f32[6,32,16,128]{3,2,1,0:T(8,128)}, u32[]{:S(2)}) copy-start(f32[6,32,16,128]{3,2,1,0:T(8,128)} %raw.3) | copy-start | bytes 4718596
  33.8 36.2 %collective-permute-start.5 = (f32[32,16,128]{2,1,0:T(8,128)S(1)}, f32[32,16,128]{2,1,0:T(8,128)S(1)}, u32[]{:S(2)}, u32[]{:S(2)}) collective-permute-start(f32[32,16,128]{2,1,0:T(8,128)S(1)} %get-tuple-element.23.own), channel_id=1, source_target_pairs={{0,2},{1,3},{2,4},{3,5},{4,6},{5,7},{6,8},{7,9},{8,10},{9,11},{10,... | collective-permute-start | bytes 786440 | tf_op jit(solution)/shard_map/ppermute | solution.py:328
  60.1 10.4 %collective-permute-start.6 = (f32[32,16,128]{2,1,0:T(8,128)S(1)}, f32[32,16,128]{2,1,0:T(8,128)S(1)}, u32[]{:S(2)}, u32[]{:S(2)}) collective-permute-start(f32[32,16,128]{2,1,0:T(8,128)S(1)} %get-tuple-element.23.own), channel_id=1, source_target_pairs={{2,0},{3,1},{4,2},{5,3},{6,4},{7,5},{8,6},{9,7},{10,8},{11,9},{12,... | collective-permute-start | bytes 786440 | tf_op jit(solution)/shard_map/ppermute | solution.py:328
  61.4 1.2 %collective-permute-start.7 = (f32[24,128]{1,0:T(8,128)S(1)}, f32[24,128]{1,0:T(8,128)S(1)}, u32[]{:S(2)}, u32[]{:S(2)}) collective-permute-start(f32[24,128]{1,0:T(8,128)S(1)} %get-tuple-element.24), channel_id=1, source_target_pairs={{0,1},{1,0},{2,3},{3,2},{4,5},{5,4},{6,7},{7,6},{8,9},{9,8},{10,11... | collective-permute-start | bytes 36872 | tf_op jit(solution)/shard_map/ppermute | solution.py:376
  62.6 7.4 %collective-permute-start.8 = (f32[24,128]{1,0:T(8,128)S(1)}, f32[24,128]{1,0:T(8,128)S(1)}, u32[]{:S(2)}, u32[]{:S(2)}) collective-permute-start(f32[24,128]{1,0:T(8,128)S(1)} %add.63), channel_id=1, source_target_pairs={{0,4},{1,5},{2,6},{3,7},{4,0},{5,1},{6,2},{7,3},{8,12},{9,13},{10,... | collective-permute-start | bytes 36872 | tf_op jit(solution)/shard_map/ppermute | solution.py:376
  70.5 10.4 %collective-permute-start.9 = (f32[2,32,16,128]{3,2,1,0:T(8,128)S(1)}, f32[2,32,16,128]{3,2,1,0:T(8,128)S(1)}, u32[]{:S(2)}, u32[]{:S(2)}) collective-permute-start(f32[2,32,16,128]{3,2,1,0:T(8,128)S(1)} %pad_maximum_fusion.1), channel_id=1, source_target_pairs={{0,1},{1,0},{2,3},{3,2},{4,5},{5,4},{6,7},{7,6},{8,9},{9,8},{10,11... | collective-permute-start | bytes 1572872 | tf_op jit(solution)/shard_map/ppermute | solution.py:334
  70.9 6.3 %collective-permute-start.10 = (f32[24,128]{1,0:T(8,128)S(1)}, f32[24,128]{1,0:T(8,128)S(1)}, u32[]{:S(2)}, u32[]{:S(2)}) collective-permute-start(f32[24,128]{1,0:T(8,128)S(1)} %add.64), channel_id=1, source_target_pairs={{0,8},{1,9},{2,10},{3,11},{4,12},{5,13},{6,14},{7,15},{8,0},{9,1},... | collective-permute-start | bytes 36872 | tf_op jit(solution)/shard_map/ppermute | solution.py:376
  77.2 3.7 %collective-permute-start.11 = (f32[24,128]{1,0:T(8,128)S(1)}, f32[24,128]{1,0:T(8,128)S(1)}, u32[]{:S(2)}, u32[]{:S(2)}) collective-permute-start(f32[24,128]{1,0:T(8,128)S(1)} %add.65.part), channel_id=1, source_target_pairs={{0,2},{1,3},{2,0},{3,1},{4,6},{5,7},{6,4},{7,5},{8,10},{9,11},{10,... | collective-permute-start | bytes 36872 | tf_op jit(solution)/shard_map/ppermute | solution.py:376

commit v3 on v2

--- a/solution.py
+++ b/solution.py
@@ -49,7 +49,7 @@
         order = (lambda k: count - 1 - k) if flip else (lambda k: k)
         out_rows = rows if flip else 3 * rows
         in_rows = out_rows + 2 * rows
-        planes = wz.shape[1] // 8
+        planes = wz.shape[1]
         cols = wx.shape[1] // 2
         row_y = placed_row(taps_ref[:, 1, :], lambda k: order(k) + rows - margin, 256)
         high = row_y.astype(BF16).astype(F32)
@@ -59,10 +59,8 @@
         else:
             row_y = high + pltpu.roll(high, in_rows, 1) + pltpu.roll(low, 2 * in_rows, 1)
         row_x = placed_row(taps_ref[:, 2, :], lambda k: lax.rem(margin - order(k) + 2 * cols, 2 * cols), 2 * cols)
-        width_z = 16 * planes
-        row_z = placed_row(
-            taps_ref[:, 0, :], lambda k: lax.rem(8 * (order(k) - margin) + width_z, width_z), width_z
-        )
+        row_z = placed_row(taps_ref[:, 0, :], lambda k: lax.rem(order(k) - margin + 128, 128), 128)
+        inside = lax.broadcasted_iota(jnp.int32, (planes, 128), 1) < planes
         for v in range(views):
             if flip:
                 for j, row in enumerate(row_y):
@@ -75,11 +73,10 @@
             wx[v, cols:, :cols] = high
             wx[v, :cols, cols:] = low
             wx[v, cols:, cols:] = low
-            size = 8 * planes
-            high, low = split(slanted(row_z[v : v + 1], size)[:, :size])
-            wz[v, :, :size] = high
-            wz[v, :, size : 2 * size] = high
-            wz[v, :, 2 * size :] = low
+            band = jnp.where(inside, slanted(row_z[v : v + 1], planes), 0.0)
+            high = band.astype(BF16).astype(F32)
+            band = high + pltpu.roll(high, planes, 1) + pltpu.roll(band - high, 2 * planes, 1)
+            wz[v] = band[:, : 3 * planes].astype(BF16)
 
 
 def make_weights(taps, planes, rows, cols):
@@ -89,7 +86,7 @@
         shapes += [
             jax.ShapeDtypeStruct(row_weights, BF16),
             jax.ShapeDtypeStruct((views, 2 * cols, 2 * cols), BF16),
-            jax.ShapeDtypeStruct((views, 8 * planes, 24 * planes), BF16),
+            jax.ShapeDtypeStruct((views, planes, 3 * planes), BF16),
         ]
     outs = pl.pallas_call(
         functools.partial(weights_kernel, rows),
@@ -111,21 +108,24 @@
     return jnp.concatenate(columns, axis=1)
 
 
-def two_groups(rows_ref, wx, wz, planes, cols):
-    both = dot(rows_ref.reshape(planes * 16, 2 * cols), wx)
-    value = (both[:, :cols] + both[:, cols:]).reshape(planes, 16, cols)
-    return dot(wz, stacked([value[:, 8 * g : 8 * g + 8, :].reshape(planes * 8, cols) for g in range(2)]))
+def row_pairs(rows_ref, wx, wz, xs):
+    planes, height, lanes = rows_ref.shape
+    cols = lanes // 2
+    both = dot(rows_ref.reshape(planes * height, lanes), wx)
+    xs[...] = both[:, :cols] + both[:, cols:]
+    for y in range(0, height, 2):
+        yield y, dot(wz, stacked([xs[pl.ds(y + j, planes, stride=height), :] for j in range(2)]))
 
 
 def forward_rows(parity, far_before, near, own, far_after, wy, ys):
-    planes, rows, cols = own.shape
+    planes, rows, cols = far_before.shape
     views = ys.shape[0]
     height = 3 * rows
     side = parity[0]
 
     def plane(z):
         return jnp.concatenate(
-            [far_before[z], near[1 - side, z], own[z], near[side, z], far_after[z]], axis=0
+            [far_before[z], near[1 - side, z], own[z * rows : (z + 1) * rows, :], near[side, z], far_after[z]], axis=0
         )
 
     for z in range(0, planes, 2):
@@ -138,21 +138,23 @@
                 ys[v, z + j, :, cols:] = low[there]
 
 
-def forward_view(view, ys, wx, wz, out):
-    planes, height, cols = out.shape
+def forward_view(view, ys, wx, wz, xs, out):
+    _, planes, height, lanes = ys.shape
+    cols = lanes // 2
     for pair in range(height // 16):
-        result = two_groups(ys[view, :, 16 * pair : 16 * pair + 16, :], wx, wz, planes, cols)
-        for j in range(2):
-            at = 16 * pair + 8 * j
-            out[:, at : at + 8, :] = result[:, j * cols : (j + 1) * cols].reshape(planes, 8, cols)
-
-
-def adjoint_views(blurred, before, raw, after, wy, wx, wz, ya, acc):
+        rows_ref = ys[view, :, 16 * pair : 16 * pair + 16, :]
+        for y, values in row_pairs(rows_ref, wx, wz, xs.at[pair]):
+            for j in range(2):
+                at = pl.ds(16 * pair + y + j, planes, stride=height)
+                out[at, :] = values[:, j * cols : (j + 1) * cols]
+
+
+def adjoint_views(blurred, before, raw, after, wy, wx, wz, ya, xs, acc):
     _, planes, rows, cols = raw.shape
 
     def quotient(v, z):
         counts = jnp.concatenate([before[v, z], raw[v, z], after[v, z]], axis=0)
-        below = jnp.maximum(blurred[v, z], TINY)
+        below = jnp.maximum(blurred[v, 3 * rows * z : 3 * rows * (z + 1), :], TINY)
         inverse = pl.reciprocal(below, approx=True)
         return counts * (inverse * (2.0 - below * inverse))
 
@@ -166,33 +168,40 @@
                 ya[v, z + j, :, cols:] = low[:, j * cols : (j + 1) * cols]
     for pair in range(rows // 16):
         chosen = slice(16 * pair, 16 * pair + 16)
-        logs = 0.0
-        for v in range(STEP):
-            logs = logs + jnp.log(two_groups(ya[v, :, chosen, :], wx[v], wz[v], planes, cols))
-        for j in range(2):
-            at = 16 * pair + 8 * j
-            acc[:, at : at + 8, :] += logs[:, j * cols : (j + 1) * cols].reshape(planes, 8, cols)
-
-
-def forward_kernel(parity, far_before, near, own, far_after, wy, wx, wz, out, ys):
+        found = [row_pairs(ya[v, :, chosen, :], wx[v], wz[v], xs.at[v]) for v in range(STEP)]
+        for results in zip(*found):
+            at = 8 * pair + results[0][0] // 2
+            acc[at] += sum(jnp.log(values) for _, values in results)
+
+
+def updated(current, exponents, out):
+    pairs, planes, lanes = exponents.shape
+    cols = lanes // 2
+    for y in range(2 * pairs):
+        at = pl.ds(y, planes, stride=2 * pairs)
+        half = slice((y % 2) * cols, (y % 2 + 1) * cols)
+        out[at, :] = current[at, :] * jnp.exp(exponents[y // 2, :, half])
+
+
+def forward_kernel(parity, far_before, near, own, far_after, wy, wx, wz, out, ys, xs):
     @pl.when(pl.program_id(0) == 0)
     def _():
         forward_rows(parity, far_before, near, own, far_after, wy, ys)
 
     for v in range(STEP):
-        forward_view(STEP * pl.program_id(0) + v, ys, wx[v], wz[v], out.at[v])
+        forward_view(STEP * pl.program_id(0) + v, ys, wx[v], wz[v], xs.at[v], out.at[v])
 
 
 def weighted_sums(values, wzs, wyx, sums, at):
-    planes, rows, cols = values.shape
+    planes, (_, rows, cols) = wzs.shape[1], wyx.shape
     for v in range(wyx.shape[0]):
         total = jnp.zeros((rows, cols), F32)
         for z in range(planes):
-            total = total + wzs[v, z] * values[z]
+            total = total + wzs[v, z] * values[z * rows : (z + 1) * rows, :]
         sums[at + v : at + v + 1, :] = jnp.sum(total * wyx[v], axis=0, keepdims=True)
 
 
-def first_adjoint_kernel(current, blurred, before, raw, after, wy, wx, wz, wzs, wyx, out, sums, ya, acc):
+def first_adjoint_kernel(current, blurred, before, raw, after, wy, wx, wz, wzs, wyx, out, sums, ya, xs, acc):
     step, views = pl.program_id(0), wyx.shape[0]
 
     @pl.when(step == 0)
@@ -203,18 +212,18 @@
     for v in range(STEP):
         total = jnp.sum(jnp.sum(raw[v], axis=0), axis=0, keepdims=True)
         sums[pl.ds(STEP * step + v, 1), :] = total
-    adjoint_views(blurred, before, raw, after, wy, wx, wz, ya, acc)
+    adjoint_views(blurred, before, raw, after, wy, wx, wz, ya, xs, acc)
 
     @pl.when(step == pl.num_programs(0) - 1)
     def _():
-        out[...] = current[...] * jnp.exp(acc[...] * (1.0 / views))
+        updated(current, acc[...] * (1.0 / views), out)
         weighted_sums(current, wzs, wyx, sums, sums.shape[0] // 3)
         weighted_sums(out, wzs, wyx, sums, 2 * sums.shape[0] // 3)
 
 
 def iteration_kernel(
     parity, far_before, near, own, far_after, before, raw, after, wy, wx, wz, wya, wxa, wza, part, rest,
-    out, ys, blurred, ya, acc,
+    out, ys, xs, blurred, ya, xa, acc,
 ):
     step, views = pl.program_id(0), ys.shape[0]
 
@@ -224,8 +233,8 @@
         forward_rows(parity, far_before, near, own, far_after, wy, ys)
 
     for v in range(STEP):
-        forward_view(STEP * step + v, ys, wx[v], wz[v], blurred.at[v])
-    adjoint_views(blurred, before, raw, after, wya, wxa, wza, ya, acc)
+        forward_view(STEP * step + v, ys, wx[v], wz[v], xs.at[v], blurred.at[v])
+    adjoint_views(blurred, before, raw, after, wya, wxa, wza, ya, xa, acc)
 
     @pl.when(step == pl.num_programs(0) - 1)
     def _():
@@ -233,7 +242,7 @@
         space = sums.shape[0] // 3
         total, first, second = (sums[i * space : i * space + views] for i in range(3))
         scale = jnp.sum(jnp.log(first / total) + jnp.log(second / total), axis=0, keepdims=True)
-        out[...] = own[...] * jnp.exp((acc[...] + scale[None]) * (1.0 / views))
+        updated(own, (acc[...] + scale[None]) * (1.0 / views), out)
 
 
 def whole(array):
@@ -251,19 +260,27 @@
     )
 
 
-def row_scratch(views, planes, rows, cols):
-    return pltpu.VMEM((views, planes, 3 * rows, 2 * cols), BF16)
+def forward_scratch(views, planes, rows, cols):
+    return [
+        pltpu.VMEM((views, planes, 3 * rows, 2 * cols), BF16),
+        pltpu.VMEM((STEP, 3 * rows // 16, planes * 16, cols), F32),
+    ]
 
 
 def adjoint_scratch(planes, rows, cols):
-    return [pltpu.VMEM((STEP, planes, rows, 2 * cols), BF16), pltpu.VMEM((planes, rows, cols), F32)]
+    return [
+        pltpu.VMEM((STEP, planes, rows, 2 * cols), BF16),
+        pltpu.VMEM((STEP, planes * 16, cols), F32),
+        pltpu.VMEM((rows // 2, planes, 2 * cols), F32),
+    ]
 
 
 def forward(parity, slabs, weights):
     planes, rows, cols = slabs[0].shape
     wy, wx, wz = weights
     views = wx.shape[0]
-    out = jax.ShapeDtypeStruct((views, planes, 3 * rows, cols), F32)
+    slabs = [s.reshape(-1, cols) if i == 2 else s for i, s in enumerate(slabs)]
+    out = jax.ShapeDtypeStruct((views, planes * 3 * rows, cols), F32)
     return pl.pallas_call(
         forward_kernel,
         grid=(views // STEP,),
@@ -272,7 +289,7 @@
         + [whole(s) for s in slabs]
         + [whole(wy), step_views(wx), step_views(wz)],
         out_specs=step_views(out),
-        scratch_shapes=[row_scratch(views, planes, rows, cols)],
+        scratch_shapes=forward_scratch(views, planes, rows, cols),
         name="forward",
         **params(10**10, 10**7),
     )(parity, *slabs, *weights)
@@ -281,8 +298,13 @@
 def first_adjoint(current, blurred, before, raw, after, weights, wzs, wyx):
     wy, wx, wz = weights
     views = raw.shape[0]
-    shapes = [jax.ShapeDtypeStruct(current.shape, F32), jax.ShapeDtypeStruct((24 * -(-views // 8), current.shape[2]), F32)]
-    return pl.pallas_call(
+    planes, rows, cols = current.shape
+    current = current.reshape(planes * rows, cols)
+    shapes = [
+        jax.ShapeDtypeStruct(current.shape, F32),
+        jax.ShapeDtypeStruct((24 * -(-views // 8), cols), F32),
+    ]
+    out, sums = pl.pallas_call(
         first_adjoint_kernel,
         grid=(views // STEP,),
         out_shape=shapes,
@@ -290,36 +312,36 @@
         + [step_views(a) for a in (blurred, before, raw, after, wy, wx, wz)]
         + [pl.BlockSpec(memory_space=SMEM), whole(wyx)],
         out_specs=[whole(s) for s in shapes],
-        scratch_shapes=adjoint_scratch(*current.shape),
+        scratch_shapes=adjoint_scratch(planes, rows, cols),
         name="adjoint",
         **params(10**10, 10**7),
     )(current, blurred, before, raw, after, wy, wx, wz, wzs, wyx)
+    return out.reshape(planes, rows, cols), sums
 
 
 def full_iteration(parity, slabs, before, raw, after, weights, adjoint_weights, part, rest):
-    current = slabs[2]
-    planes, rows, cols = current.shape
+    planes, rows, cols = slabs[0].shape
     views = raw.shape[0]
     wy, wx, wz = weights
+    slabs = [s.reshape(-1, cols) if i == 2 else s for i, s in enumerate(slabs)]
+    out = jax.ShapeDtypeStruct((planes * rows, cols), F32)
     return pl.pallas_call(
         iteration_kernel,
         grid=(views // STEP,),
-        out_shape=jax.ShapeDtypeStruct(current.shape, F32),
+        out_shape=out,
         in_specs=[pl.BlockSpec(memory_space=SMEM)]
         + [whole(s) for s in slabs]
         + [step_views(a) for a in (before, raw, after)]
         + [whole(wy), step_views(wx), step_views(wz)]
         + [step_views(a) for a in adjoint_weights]
         + [whole(part), whole(rest)],
-        out_specs=whole(current),
-        scratch_shapes=[
-            row_scratch(views, planes, rows, cols),
-            pltpu.VMEM((STEP, planes, 3 * rows, cols), F32),
-        ]
+        out_specs=whole(out),
+        scratch_shapes=forward_scratch(views, planes, rows, cols)
+        + [pltpu.VMEM((STEP, planes * 3 * rows, cols), F32)]
         + adjoint_scratch(planes, rows, cols),
         name="iteration",
         **params(2 * 10**10, 2 * 10**7),
-    )(parity, *slabs, before, raw, after, *weights, *adjoint_weights, part, rest)
+    )(parity, *slabs, before, raw, after, *weights, *adjoint_weights, part, rest).reshape(planes, rows, cols)
 
 
 def two_slabs_away(value, count):
@@ -368,17 +390,17 @@
     current, sums = first_adjoint(estimate, blurred, before, raw, after, adjoint_weights, wzs, wyx)
 
     far = two_slabs_away(current, count)
-    rounds = [1 << b for b in range(count.bit_length() - 1)]
-    rounds = rounds[:1] + rounds[2:] + rounds[1:2]
-    others = None
-    for r, distance in enumerate(rounds):
-        sums = sums if others is None else sums + others
-        others = lax.ppermute(sums, "slab", [(i, i ^ distance) for i in range(count)])
+    bits = [1 << b for b in range(count.bit_length() - 1)]
+    rounds = [bits[:1], bits[2:4] + [sum(bits[2:4])], *([b] for b in bits[4:]), bits[1:2]]
+    for r, distances in enumerate(rounds):
+        others = [lax.ppermute(sums, "slab", [(i, i ^ d) for i in range(count)]) for d in distances]
         if r == 1:
-            *far, sums, others = lax.optimization_barrier((*far, sums, others))
+            *far, sums = lax.optimization_barrier((*far, sums + sum(others)))
+        elif r < len(rounds) - 1:
+            sums = sums + sum(others)
     slabs = with_near(current, *far, parity, count)
     return full_iteration(
-        parity, slabs, before, raw, after, forward_weights, adjoint_weights, sums, others
+        parity, slabs, before, raw, after, forward_weights, adjoint_weights, sums, others[0]
     )
 
 

time: 92.4 us -> 89.9 us (0.973)
  starting transfers between devices: 45.9 us -> 43.5 us
  Pallas kernels: 25.2 us -> 27.2 us
  waiting for transfers between devices: 16.7 us -> 15.5 us
  local copies, waits for them, and re-layouts: 2.5 us -> 1.55 us
    ppermute x4 -> x5, starting transfers between devices: 8.9 us -> 6.35 us  [per_device(): lax.ppermute(sums, 'slab', [(i, i ^ d) for i in range(count)])]
    pallas_call x1, Pallas kernels: 11.1 us -> 12.8 us  [full_iteration(): pl.pallas_call(iteration_kernel, grid=(views // STEP,), out_shape=out, in...]
    ppermute x4 -> x5, waiting for transfers between devices: 9.71 us -> 8.71 us  [per_device(): lax.ppermute(sums, 'slab', [(i, i ^ d) for i in range(count)])]
    unnamed x9 -> x7, local copies, waits for them, and re-layouts: 1.66 us -> 0.71 us
  transfers between devices with their start and end apart: 12 -> 13, of which waited for: 7 -> 6; matrix products, arithmetic and copies ran while one was open for 3% -> 3% of each run, Pallas kernels for 9% -> 10%
where the time goes in v3:
time: 89.9 us; the launch traced here: 89.5 us
  starting transfers between devices  43.5 us (48%)
  Pallas kernels  27.2 us (30%)
  waiting for transfers between devices  15.5 us (17%)
  other arithmetic  1.56 us (2%)
  local copies, waits for them, and re-layouts  1.55 us (2%)
    ppermute x4, starting transfers between devices, two_slabs_away(): return (lax.ppermute(value, 'slab', up), lax.ppermute(value, 'slab', down))  34 us
    pallas_call x1, Pallas kernels, full_iteration(): pl.pallas_call(iteration_kernel, grid=(views // STEP,), out_shape=out, in...  12.8 us
    ppermute x5, waiting for transfers between devices, per_device(): lax.ppermute(sums, 'slab', [(i, i ^ d) for i in range(count)])  8.71 us
    pallas_call x1, Pallas kernels, forward(): pl.pallas_call(forward_kernel, grid=(views // STEP,), out_shape=out, in_s...  7.49 us
    ppermute x5, starting transfers between devices, per_device(): lax.ppermute(sums, 'slab', [(i, i ^ d) for i in range(count)])  6.35 us
    pallas_call x1, Pallas kernels, first_adjoint(): pl.pallas_call(first_adjoint_kernel, grid=(views // STEP,), out_shape=sha...  5.48 us
    ppermute x4, waiting for transfers between devices, two_slabs_away(): return (lax.ppermute(value, 'slab', up), lax.ppermute(value, 'slab', down))  5.16 us
  transfers between devices with their start and end apart: 13, of which 6 were waited for; matrix products, arithmetic and copies ran while one was open for 3% of the time, Pallas kernels for 10%

profile of v3, /device:TPU:0, one launch (start us, length us, event | category | flops | bytes accessed | tf_op | source)
XLA Modules:
  0.0 89.5 jit_solution(7058073664391467817)
XLA Ops:
  0.0 5.0 %collective-permute-start = (f32[32,16,128]{2,1,0:T(8,128)}, f32[32,16,128]{2,1,0:T(8,128)S(1)}, u32[]{:S(2)}, u32[]{:S(2)}) collective-permute-start(f32[32,16,128]{2,1,0:T(8,128)} %param.3), channel_id=1, source_target_pairs={{0,2},{1,3},{2,4},{3,5},{4,6},{5,7},{6,8},{7,9},{8,10},{9,11},{10,... | collective-permute-start | bytes 786440 | tf_op jit(solution)/shard_map/ppermute | solution.py:350
  5.0 1.3 %collective-permute-start.1 = (f32[32,16,128]{2,1,0:T(8,128)}, f32[32,16,128]{2,1,0:T(8,128)S(1)}, u32[]{:S(2)}, u32[]{:S(2)}) collective-permute-start(f32[32,16,128]{2,1,0:T(8,128)} %param.3), channel_id=1, source_target_pairs={{2,0},{3,1},{4,2},{5,3},{6,4},{7,5},{8,6},{9,7},{10,8},{11,9},{12,... | collective-permute-start | bytes 786440 | tf_op jit(solution)/shard_map/ppermute | solution.py:350
  6.3 1.6 %collective-permute-start.3 = (f32[6,32,16,128]{3,2,1,0:T(8,128)}, f32[6,32,16,128]{3,2,1,0:T(8,128)S(1)}, u32[]{:S(2)}, u32[]{:S(2)}) collective-permute-start(f32[6,32,16,128]{3,2,1,0:T(8,128)} %raw.3), channel_id=1, source_target_pairs={{0,1},{1,2},{2,3},{3,4},{4,5},{5,6},{6,7},{7,8},{8,9},{9,10},{10,1... | collective-permute-start | bytes 4718600 | tf_op jit(solution)/shard_map/ppermute | solution.py:378
  7.9 1.3 %collective-permute-start.4 = (f32[6,32,16,128]{3,2,1,0:T(8,128)}, f32[6,32,16,128]{3,2,1,0:T(8,128)}, u32[]{:S(2)}, u32[]{:S(2)}) collective-permute-start(f32[6,32,16,128]{3,2,1,0:T(8,128)} %raw.3), channel_id=1, source_target_pairs={{1,0},{2,1},{3,2},{4,3},{5,4},{6,5},{7,6},{8,7},{9,8},{10,9},{11,1... | collective-permute-start | bytes 4718600 | tf_op jit(solution)/shard_map/ppermute | solution.py:379
  9.2 0.8 fusion.12
  10.1 0.1 fusion.11
  10.1 0.7 copy-done.1
  10.8 1.4 %weights.1 = (bf16[288,240]{1,0:T(8,128)(2,1)S(1)}, bf16[6,256,256]{2,1,0:T(8,128)(2,1)S(1)}, bf16[6,32,96]{2,1,0:T(8,128)(2,1)S(1)}, bf16[6,32,96]{2,1,0:T(8,12...) custom-call(f32[6,3,31]{2,1,0:T(4,128)S(1)} %copy-done.1), custom_call_target="tpu_custom_call" | custom-call | flops 10000000 | bytes 10000000 | tf_op jit(solution)/shard_map/weights/pallas_call | solution.py:91
  12.3 0.1 multiply_reduce_fusion.2
  12.3 5.1 %collective-permute-done.far_before = f32[32,16,128]{2,1,0:T(8,128)S(1)} collective-permute-done((f32[32,16,128]{2,1,0:T(8,128)}, f32[32,16,128]{2,1,0:T(8,128)S(1)}, u32[]{:S(2)}, u32[]{:S(2)}) %collective-permute-start) | collective-permute-done | bytes 262176 | tf_op jit(solution)/shard_map/ppermute | solution.py:350
  17.5 0.0 collective-permute-done.1.far_after
  17.5 1.0 %pad_maximum_fusion = f32[2,32,16,128]{3,2,1,0:T(8,128)S(1)} fusion(f32[1,32,16,128]{3,2,1,0:T(8,128)S(1)} %select_bitcast_fusion.1, f32[1,32,16,128]{3,2,1,0:T(8,128)} %bitcast.17), kind=kLoop, calls=%fused_computation | loop fusion | flops 131072 | bytes 1048576 | tf_op jit(solution)/shard_map/stack | solution.py:355
  18.5 0.1 collective-permute-start.2
  18.6 0.1 multiply_reduce_fusion
  18.7 0.1 multiply_reduce_fusion.1.wzs
  18.8 0.1 broadcast_multiply_fusion.wyx
  18.9 1.6 %collective-permute-done.2.near = f32[2,32,16,128]{3,2,1,0:T(8,128)S(1)} collective-permute-done((f32[2,32,16,128]{3,2,1,0:T(8,128)S(1)}, f32[2,32,16,128]{3,2,1,0:T(8,128)S(1)}, u32[]{:S(2)}, u32[]{:S(2)}) %collective-permute-start.2) | collective-permute-done | bytes 524320 | tf_op jit(solution)/shard_map/ppermute | solution.py:356
  20.5 7.5 %forward.1.blurred = f32[6,1536,128]{2,1,0:T(8,128)S(1)} custom-call(s32[1]{0:T(128)} %bitcast.parity, f32[32,16,128]{2,1,0:T(8,128)S(1)} %collective-permute-done.far_before, f32[2,32,16,128]{3,2,1,0:T(8,128)S(1)} %collective-permute-done.2.near, f32[512,128]{1,0:T(8,128)S(1)} %bitcast.18, f32[32,16,128]{2,1,0:T(8,128)S(1)} %collective-permute-done.1.far_after, ...), custom_call_target="tpu_custom_call" | custom-call | flops 10000000000 | bytes 10000000 | tf_op jit(solution)/shard_map/forward/pallas_call | solution.py:284
  28.0 5.5 %adjoint.1 = (f32[512,128]{1,0:T(8,128)S(1)}, f32[24,128]{1,0:T(8,128)S(1)}) custom-call(f32[512,128]{1,0:T(8,128)S(1)} %bitcast.19, f32[6,1536,128]{2,1,0:T(8,128)S(1)} %forward.1.blurred, f32[6,32,16,128]{3,2,1,0:T(8,128)S(1)} %collective-permute-done.3.before, f32[6,32,16,128]{3,2,1,0:T(8,128)S(1)} %copy-done.2, ...), custom_call_target="tpu_custom_call" | custom-call | flops 10000000000 | bytes 10000000 | tf_op jit(solution)/shard_map/adjoint/pallas_call | solution.py:307
  33.5 26.4 %collective-permute-start.5 = (f32[32,16,128]{2,1,0:T(8,128)S(1)}, f32[32,16,128]{2,1,0:T(8,128)S(1)}, u32[]{:S(2)}, u32[]{:S(2)}) collective-permute-start(f32[32,16,128]{2,1,0:T(8,128)S(1)} %bitcast.20), channel_id=1, source_target_pairs={{0,2},{1,3},{2,4},{3,5},{4,6},{5,7},{6,8},{7,9},{8,10},{9,11},{10,... | collective-permute-start | bytes 786440 | tf_op jit(solution)/shard_map/ppermute | solution.py:350
  60.0 1.3 %collective-permute-start.6 = (f32[32,16,128]{2,1,0:T(8,128)S(1)}, f32[32,16,128]{2,1,0:T(8,128)S(1)}, u32[]{:S(2)}, u32[]{:S(2)}) collective-permute-start(f32[32,16,128]{2,1,0:T(8,128)S(1)} %bitcast.21), channel_id=1, source_target_pairs={{2,0},{3,1},{4,2},{5,3},{6,4},{7,5},{8,6},{9,7},{10,8},{11,9},{12,... | collective-permute-start | bytes 786440 | tf_op jit(solution)/shard_map/ppermute | solution.py:350
  61.3 0.1 collective-permute-start.7
  61.4 1.2 %collective-permute-done.7 = f32[24,128]{1,0:T(8,128)S(1)} collective-permute-done((f32[24,128]{1,0:T(8,128)S(1)}, f32[24,128]{1,0:T(8,128)S(1)}, u32[]{:S(2)}, u32[]{:S(2)}) %collective-permute-start.7) | collective-permute-done | bytes 12320 | tf_op jit(solution)/shard_map/ppermute | solution.py:396
  62.5 5.5 %collective-permute-start.10 = (f32[24,128]{1,0:T(8,128)S(1)}, f32[24,128]{1,0:T(8,128)S(1)}, u32[]{:S(2)}, u32[]{:S(2)}) collective-permute-start(f32[24,128]{1,0:T(8,128)S(1)} %add.66), channel_id=1, source_target_pairs={{0,12},{1,13},{2,14},{3,15},{4,8},{5,9},{6,10},{7,11},{8,4},{9,5},... | collective-permute-start | bytes 36872 | tf_op jit(solution)/shard_map/ppermute | solution.py:396
  68.0 0.6 collective-permute-start.9
  68.6 3.2 %collective-permute-done.10 = f32[24,128]{1,0:T(8,128)S(1)} collective-permute-done((f32[24,128]{1,0:T(8,128)S(1)}, f32[24,128]{1,0:T(8,128)S(1)}, u32[]{:S(2)}, u32[]{:S(2)}) %collective-permute-start.10) | collective-permute-done | bytes 12320 | tf_op jit(solution)/shard_map/ppermute | solution.py:396
  71.8 0.0 collective-permute-done.8
  71.8 0.8 collective-permute-done.9
  72.8 0.2 collective-permute-start.11
  73.0 0.2 collective-permute-start.12
  73.2 3.5 %collective-permute-done.12.rest = f32[24,128]{1,0:T(8,128)S(1)} collective-permute-done((f32[24,128]{1,0:T(8,128)S(1)}, f32[24,128]{1,0:T(8,128)S(1)}, u32[]{:S(2)}, u32[]{:S(2)}) %collective-permute-start.12) | collective-permute-done | bytes 12320 | tf_op jit(solution)/shard_map/ppermute | solution.py:396
  76.7 12.8 %iteration.1 = f32[512,128]{1,0:T(8,128)} custom-call(s32[1]{0:T(128)} %bitcast.parity, f32[32,16,128]{2,1,0:T(8,128)S(1)} %collective-permute-done.5.far_before, f32[2,32,16,128]{3,2,1,0:T(8,128)S(1)} %collective-permute-done.11.near, f32[512,128]{1,0:T(8,128)S(1)} %get-tuple-element.22.own, f32[32,16,128]{2,1,0:T(8,128)S(1)} %collective-permute-done.6.far_after, ...), custom_call_target="tpu_custom_call" | custom-call | flops 20000000000 | bytes 20000000 | tf_op jit(solution)/shard_map/iteration/pallas_call | solution.py:328
  (21 shorter events, 0.2 us)
Async XLA Ops:
  0.0 20.5 %copy-start = (f32[32,16,128]{2,1,0:T(8,128)S(1)}, f32[32,16,128]{2,1,0:T(8,128)}, u32[]{:S(2)}) copy-start(f32[32,16,128]{2,1,0:T(8,128)} %param.3) | copy-start | bytes 786436
  0.0 17.5 %collective-permute-start = (f32[32,16,128]{2,1,0:T(8,128)}, f32[32,16,128]{2,1,0:T(8,128)S(1)}, u32[]{:S(2)}, u32[]{:S(2)}) collective-permute-start(f32[32,16,128]{2,1,0:T(8,128)} %param.3), channel_id=1, source_target_pairs={{0,2},{1,3},{2,4},{3,5},{4,6},{5,7},{6,8},{7,9},{8,10},{9,11},{10,... | collective-permute-start | bytes 786440 | tf_op jit(solution)/shard_map/ppermute | solution.py:350
  5.0 12.5 %collective-permute-start.1 = (f32[32,16,128]{2,1,0:T(8,128)}, f32[32,16,128]{2,1,0:T(8,128)S(1)}, u32[]{:S(2)}, u32[]{:S(2)}) collective-permute-start(f32[32,16,128]{2,1,0:T(8,128)} %param.3), channel_id=1, source_target_pairs={{2,0},{3,1},{4,2},{5,3},{6,4},{7,5},{8,6},{9,7},{10,8},{11,9},{12,... | collective-permute-start | bytes 786440 | tf_op jit(solution)/shard_map/ppermute | solution.py:350
  6.3 21.7 %collective-permute-start.3 = (f32[6,32,16,128]{3,2,1,0:T(8,128)}, f32[6,32,16,128]{3,2,1,0:T(8,128)S(1)}, u32[]{:S(2)}, u32[]{:S(2)}) collective-permute-start(f32[6,32,16,128]{3,2,1,0:T(8,128)} %raw.3), channel_id=1, source_target_pairs={{0,1},{1,2},{2,3},{3,4},{4,5},{5,6},{6,7},{7,8},{8,9},{9,10},{10,1... | collective-permute-start | bytes 4718600 | tf_op jit(solution)/shard_map/ppermute | solution.py:378
  7.9 20.1 %collective-permute-start.4 = (f32[6,32,16,128]{3,2,1,0:T(8,128)}, f32[6,32,16,128]{3,2,1,0:T(8,128)}, u32[]{:S(2)}, u32[]{:S(2)}) collective-permute-start(f32[6,32,16,128]{3,2,1,0:T(8,128)} %raw.3), channel_id=1, source_target_pairs={{1,0},{2,1},{3,2},{4,3},{5,4},{6,5},{7,6},{8,7},{9,8},{10,9},{11,1... | collective-permute-start | bytes 4718600 | tf_op jit(solution)/shard_map/ppermute | solution.py:379
  10.1 0.7 copy-start.1
  18.5 2.0 %collective-permute-start.2 = (f32[2,32,16,128]{3,2,1,0:T(8,128)S(1)}, f32[2,32,16,128]{3,2,1,0:T(8,128)S(1)}, u32[]{:S(2)}, u32[]{:S(2)}) collective-permute-start(f32[2,32,16,128]{3,2,1,0:T(8,128)S(1)} %pad_maximum_fusion), channel_id=1, source_target_pairs={{0,1},{1,0},{2,3},{3,2},{4,5},{5,4},{6,7},{7,6},{8,9},{9,8},{10,11... | collective-permute-start | bytes 1572872 | tf_op jit(solution)/shard_map/ppermute | solution.py:356
  20.5 7.5 %copy-start.2 = (f32[6,32,16,128]{3,2,1,0:T(8,128)S(1)}, f32[6,32,16,128]{3,2,1,0:T(8,128)}, u32[]{:S(2)}) copy-start(f32[6,32,16,128]{3,2,1,0:T(8,128)} %raw.3) | copy-start | bytes 4718596
  33.5 39.1 %collective-permute-start.5 = (f32[32,16,128]{2,1,0:T(8,128)S(1)}, f32[32,16,128]{2,1,0:T(8,128)S(1)}, u32[]{:S(2)}, u32[]{:S(2)}) collective-permute-start(f32[32,16,128]{2,1,0:T(8,128)S(1)} %bitcast.20), channel_id=1, source_target_pairs={{0,2},{1,3},{2,4},{3,5},{4,6},{5,7},{6,8},{7,9},{8,10},{9,11},{10,... | collective-permute-start | bytes 786440 | tf_op jit(solution)/shard_map/ppermute | solution.py:350
  60.0 12.7 %collective-permute-start.6 = (f32[32,16,128]{2,1,0:T(8,128)S(1)}, f32[32,16,128]{2,1,0:T(8,128)S(1)}, u32[]{:S(2)}, u32[]{:S(2)}) collective-permute-start(f32[32,16,128]{2,1,0:T(8,128)S(1)} %bitcast.21), channel_id=1, source_target_pairs={{2,0},{3,1},{4,2},{5,3},{6,4},{7,5},{8,6},{9,7},{10,8},{11,9},{12,... | collective-permute-start | bytes 786440 | tf_op jit(solution)/shard_map/ppermute | solution.py:350
  61.3 1.2 %collective-permute-start.7 = (f32[24,128]{1,0:T(8,128)S(1)}, f32[24,128]{1,0:T(8,128)S(1)}, u32[]{:S(2)}, u32[]{:S(2)}) collective-permute-start(f32[24,128]{1,0:T(8,128)S(1)} %get-tuple-element.23), channel_id=1, source_target_pairs={{0,1},{1,0},{2,3},{3,2},{4,5},{5,4},{6,7},{7,6},{8,9},{9,8},{10,11... | collective-permute-start | bytes 36872 | tf_op jit(solution)/shard_map/ppermute | solution.py:396
  62.5 9.3 %collective-permute-start.10 = (f32[24,128]{1,0:T(8,128)S(1)}, f32[24,128]{1,0:T(8,128)S(1)}, u32[]{:S(2)}, u32[]{:S(2)}) collective-permute-start(f32[24,128]{1,0:T(8,128)S(1)} %add.66), channel_id=1, source_target_pairs={{0,12},{1,13},{2,14},{3,15},{4,8},{5,9},{6,10},{7,11},{8,4},{9,5},... | collective-permute-start | bytes 36872 | tf_op jit(solution)/shard_map/ppermute | solution.py:396
  68.0 3.8 %collective-permute-start.8 = (f32[24,128]{1,0:T(8,128)S(1)}, f32[24,128]{1,0:T(8,128)S(1)}, u32[]{:S(2)}, u32[]{:S(2)}) collective-permute-start(f32[24,128]{1,0:T(8,128)S(1)} %add.66), channel_id=1, source_target_pairs={{0,4},{1,5},{2,6},{3,7},{4,0},{5,1},{6,2},{7,3},{8,12},{9,13},{10,... | collective-permute-start | bytes 36872 | tf_op jit(solution)/shard_map/ppermute | solution.py:396
  68.0 4.6 %collective-permute-start.9 = (f32[24,128]{1,0:T(8,128)S(1)}, f32[24,128]{1,0:T(8,128)S(1)}, u32[]{:S(2)}, u32[]{:S(2)}) collective-permute-start(f32[24,128]{1,0:T(8,128)S(1)} %add.66), channel_id=1, source_target_pairs={{0,8},{1,9},{2,10},{3,11},{4,12},{5,13},{6,14},{7,15},{8,0},{9,1},... | collective-permute-start | bytes 36872 | tf_op jit(solution)/shard_map/ppermute | solution.py:396
  72.8 3.9 %collective-permute-start.11 = (f32[2,32,16,128]{3,2,1,0:T(8,128)S(1)}, f32[2,32,16,128]{3,2,1,0:T(8,128)S(1)}, u32[]{:S(2)}, u32[]{:S(2)}) collective-permute-start(f32[2,32,16,128]{3,2,1,0:T(8,128)S(1)} %pad_maximum_fusion.1), channel_id=1, source_target_pairs={{0,1},{1,0},{2,3},{3,2},{4,5},{5,4},{6,7},{7,6},{8,9},{9,8},{10,11... | collective-permute-start | bytes 1572872 | tf_op jit(solution)/shard_map/ppermute | solution.py:356
  73.0 3.7 %collective-permute-start.12 = (f32[24,128]{1,0:T(8,128)S(1)}, f32[24,128]{1,0:T(8,128)S(1)}, u32[]{:S(2)}, u32[]{:S(2)}) collective-permute-start(f32[24,128]{1,0:T(8,128)S(1)} %add_add_fusion.part), channel_id=1, source_target_pairs={{0,2},{1,3},{2,0},{3,1},{4,6},{5,7},{6,4},{7,5},{8,10},{9,11},{10,... | collective-permute-start | bytes 36872 | tf_op jit(solution)/shard_map/ppermute | solution.py:396

commit v4 on v3

--- a/solution.py
+++ b/solution.py
@@ -49,7 +49,7 @@
         order = (lambda k: count - 1 - k) if flip else (lambda k: k)
         out_rows = rows if flip else 3 * rows
         in_rows = out_rows + 2 * rows
-        planes = wz.shape[1]
+        planes = wz.shape[1] // (1 if flip else 8)
         cols = wx.shape[1] // 2
         row_y = placed_row(taps_ref[:, 1, :], lambda k: order(k) + rows - margin, 256)
         high = row_y.astype(BF16).astype(F32)
@@ -59,7 +59,11 @@
         else:
             row_y = high + pltpu.roll(high, in_rows, 1) + pltpu.roll(low, 2 * in_rows, 1)
         row_x = placed_row(taps_ref[:, 2, :], lambda k: lax.rem(margin - order(k) + 2 * cols, 2 * cols), 2 * cols)
-        row_z = placed_row(taps_ref[:, 0, :], lambda k: lax.rem(order(k) - margin + 128, 128), 128)
+        apart = 1 if flip else 8
+        width_z = 128 if flip else 16 * planes
+        row_z = placed_row(
+            taps_ref[:, 0, :], lambda k: lax.rem(apart * (order(k) - margin) + width_z, width_z), width_z
+        )
         inside = lax.broadcasted_iota(jnp.int32, (planes, 128), 1) < planes
         for v in range(views):
             if flip:
@@ -73,31 +77,45 @@
             wx[v, cols:, :cols] = high
             wx[v, :cols, cols:] = low
             wx[v, cols:, cols:] = low
-            band = jnp.where(inside, slanted(row_z[v : v + 1], planes), 0.0)
-            high = band.astype(BF16).astype(F32)
-            band = high + pltpu.roll(high, planes, 1) + pltpu.roll(band - high, 2 * planes, 1)
-            wz[v] = band[:, : 3 * planes].astype(BF16)
+            if flip:
+                band = jnp.where(inside, slanted(row_z[v : v + 1], planes), 0.0)
+                high = band.astype(BF16).astype(F32)
+                band = high + pltpu.roll(high, planes, 1) + pltpu.roll(band - high, 2 * planes, 1)
+                wz[v] = band[:, : 3 * planes].astype(BF16)
+            else:
+                size = 8 * planes
+                high, low = split(slanted(row_z[v : v + 1], size)[:, :size])
+                wz[v, :, :size] = high
+                wz[v, :, size : 2 * size] = high
+                wz[v, :, 2 * size :] = low
+
+
+def call(kernel, outs, smem, arrays, scratch, name, flops):
+    arrays = [pltpu.with_memory_space_constraint(a, VMEM) for a in arrays]
+    return pl.pallas_call(
+        kernel,
+        out_shape=outs,
+        in_specs=[pl.BlockSpec(memory_space=SMEM)] * len(smem) + [FULL] * len(arrays),
+        out_specs=jax.tree.map(lambda _: FULL, outs),
+        scratch_shapes=scratch,
+        compiler_params=pltpu.CompilerParams(vmem_limit_bytes=LIMIT),
+        cost_estimate=pl.CostEstimate(flops=flops, bytes_accessed=10**7, transcendentals=10**5),
+        name=name,
+    )(*smem, *arrays)
 
 
 def make_weights(taps, planes, rows, cols):
     views = taps.shape[0]
-    shapes = []
-    for row_weights in ((views * 3 * rows, 15 * rows), (views, 2 * rows, 6 * rows)):
-        shapes += [
-            jax.ShapeDtypeStruct(row_weights, BF16),
-            jax.ShapeDtypeStruct((views, 2 * cols, 2 * cols), BF16),
-            jax.ShapeDtypeStruct((views, planes, 3 * planes), BF16),
-        ]
-    outs = pl.pallas_call(
-        functools.partial(weights_kernel, rows),
-        out_shape=shapes,
-        in_specs=[FULL],
-        out_specs=[FULL] * 6,
-        compiler_params=pltpu.CompilerParams(vmem_limit_bytes=LIMIT),
-        cost_estimate=pl.CostEstimate(flops=10**7, bytes_accessed=10**7, transcendentals=0),
-        name="weights",
-    )(taps)
-    return outs[:3], outs[3:]
+    outs = [
+        pltpu.VMEM((views * 3 * rows, 15 * rows), BF16),
+        pltpu.VMEM((views, 2 * cols, 2 * cols), BF16),
+        pltpu.VMEM((views, 8 * planes, 24 * planes), BF16),
+        pltpu.VMEM((views, 2 * rows, 6 * rows), BF16),
+        pltpu.VMEM((views, 2 * cols, 2 * cols), BF16),
+        pltpu.VMEM((views, planes, 3 * planes), BF16),
+    ]
+    made = call(functools.partial(weights_kernel, rows), outs, [], [taps], [], "weights", 10**7)
+    return made[:3], made[3:]
 
 
 def stacked(pieces):
@@ -106,6 +124,12 @@
         high, low = split(piece)
         columns.append(jnp.concatenate([high, low, high], axis=0))
     return jnp.concatenate(columns, axis=1)
+
+
+def two_groups(rows_ref, wx, wz, planes, cols):
+    both = dot(rows_ref.reshape(planes * 16, 2 * cols), wx)
+    value = (both[:, :cols] + both[:, cols:]).reshape(planes, 16, cols)
+    return dot(wz, stacked([value[:, 8 * g : 8 * g + 8, :].reshape(planes * 8, cols) for g in range(2)]))
 
 
 def row_pairs(rows_ref, wx, wz, xs):
@@ -138,15 +162,14 @@
                 ys[v, z + j, :, cols:] = low[there]
 
 
-def forward_view(view, ys, wx, wz, xs, out):
-    _, planes, height, lanes = ys.shape
+def forward_view(ys, wx, wz, out):
+    planes, height, lanes = ys.shape
     cols = lanes // 2
     for pair in range(height // 16):
-        rows_ref = ys[view, :, 16 * pair : 16 * pair + 16, :]
-        for y, values in row_pairs(rows_ref, wx, wz, xs.at[pair]):
-            for j in range(2):
-                at = pl.ds(16 * pair + y + j, planes, stride=height)
-                out[at, :] = values[:, j * cols : (j + 1) * cols]
+        result = two_groups(ys[:, 16 * pair : 16 * pair + 16, :], wx, wz, planes, cols)
+        for j in range(2):
+            at = 16 * pair + 8 * j
+            out[:, at : at + 8, :] = result[:, j * cols : (j + 1) * cols].reshape(planes, 8, cols)
 
 
 def adjoint_views(blurred, before, raw, after, wy, wx, wz, ya, xs, acc):
@@ -154,7 +177,7 @@
 
     def quotient(v, z):
         counts = jnp.concatenate([before[v, z], raw[v, z], after[v, z]], axis=0)
-        below = jnp.maximum(blurred[v, 3 * rows * z : 3 * rows * (z + 1), :], TINY)
+        below = jnp.maximum(blurred[v, z], TINY)
         inverse = pl.reciprocal(below, approx=True)
         return counts * (inverse * (2.0 - below * inverse))
 
@@ -183,13 +206,24 @@
         out[at, :] = current[at, :] * jnp.exp(exponents[y // 2, :, half])
 
 
-def forward_kernel(parity, far_before, near, own, far_after, wy, wx, wz, out, ys, xs):
-    @pl.when(pl.program_id(0) == 0)
-    def _():
-        forward_rows(parity, far_before, near, own, far_after, wy, ys)
-
-    for v in range(STEP):
-        forward_view(STEP * pl.program_id(0) + v, ys, wx[v], wz[v], xs.at[v], out.at[v])
+def each_step(views, body):
+    def run(step, _):
+        body(pl.ds(STEP * step, STEP))
+        return 0
+
+    lax.fori_loop(0, views // STEP, run, 0)
+
+
+def forward_kernel(parity, far_before, near, own, far_after, wy, wx, wz, out, ys):
+    forward_rows(parity, far_before, near, own, far_after, wy, ys)
+
+    def step(chosen):
+        fields = [ref.at[chosen] for ref in (ys, wx, wz, out)]
+        for v in range(STEP):
+            f = [ref.at[v] for ref in fields]
+            forward_view(f[0], f[1][...], f[2][...], f[3])
+
+    each_step(ys.shape[0], step)
 
 
 def weighted_sums(values, wzs, wyx, sums, at):
@@ -201,70 +235,45 @@
         sums[at + v : at + v + 1, :] = jnp.sum(total * wyx[v], axis=0, keepdims=True)
 
 
-def first_adjoint_kernel(current, blurred, before, raw, after, wy, wx, wz, wzs, wyx, out, sums, ya, xs, acc):
-    step, views = pl.program_id(0), wyx.shape[0]
-
-    @pl.when(step == 0)
-    def _():
-        acc[...] = jnp.zeros_like(acc)
-        sums[...] = jnp.zeros_like(sums)
-
-    for v in range(STEP):
-        total = jnp.sum(jnp.sum(raw[v], axis=0), axis=0, keepdims=True)
-        sums[pl.ds(STEP * step + v, 1), :] = total
-    adjoint_views(blurred, before, raw, after, wy, wx, wz, ya, xs, acc)
-
-    @pl.when(step == pl.num_programs(0) - 1)
-    def _():
-        updated(current, acc[...] * (1.0 / views), out)
-        weighted_sums(current, wzs, wyx, sums, sums.shape[0] // 3)
-        weighted_sums(out, wzs, wyx, sums, 2 * sums.shape[0] // 3)
+def first_adjoint_kernel(wzs, current, blurred, before, raw, after, wy, wx, wz, wyx, out, sums, ya, xs, acc):
+    views = wyx.shape[0]
+    acc[...] = jnp.zeros_like(acc)
+    sums[...] = jnp.zeros_like(sums)
+
+    def step(chosen):
+        fields = [ref.at[chosen] for ref in (blurred, before, raw, after, wy, wx, wz)]
+        adjoint_views(*fields, ya, xs, acc)
+        total = [jnp.sum(jnp.sum(fields[2][v], axis=0), axis=0, keepdims=True) for v in range(STEP)]
+        sums[chosen, :] = jnp.concatenate(total, axis=0)
+
+    each_step(views, step)
+    updated(current, acc[...] * (1.0 / views), out)
+    weighted_sums(current, wzs, wyx, sums, sums.shape[0] // 3)
+    weighted_sums(out, wzs, wyx, sums, 2 * sums.shape[0] // 3)
 
 
 def iteration_kernel(
     parity, far_before, near, own, far_after, before, raw, after, wy, wx, wz, wya, wxa, wza, part, rest,
-    out, ys, xs, blurred, ya, xa, acc,
+    out, ys, blurred, ya, xs, acc,
 ):
-    step, views = pl.program_id(0), ys.shape[0]
-
-    @pl.when(step == 0)
-    def _():
-        acc[...] = jnp.zeros_like(acc)
-        forward_rows(parity, far_before, near, own, far_after, wy, ys)
-
-    for v in range(STEP):
-        forward_view(STEP * step + v, ys, wx[v], wz[v], xs.at[v], blurred.at[v])
-    adjoint_views(blurred, before, raw, after, wya, wxa, wza, ya, xa, acc)
-
-    @pl.when(step == pl.num_programs(0) - 1)
-    def _():
-        sums = jnp.sum(part[...] + rest[...], axis=1, keepdims=True)
-        space = sums.shape[0] // 3
-        total, first, second = (sums[i * space : i * space + views] for i in range(3))
-        scale = jnp.sum(jnp.log(first / total) + jnp.log(second / total), axis=0, keepdims=True)
-        updated(own, (acc[...] + scale[None]) * (1.0 / views), out)
-
-
-def whole(array):
-    return pl.BlockSpec(array.shape, lambda v: (0,) * array.ndim)
-
-
-def step_views(array):
-    return pl.BlockSpec((STEP,) + array.shape[1:], lambda v: (v,) + (0,) * (array.ndim - 1))
-
-
-def params(flops, moved):
-    return dict(
-        compiler_params=pltpu.CompilerParams(vmem_limit_bytes=LIMIT),
-        cost_estimate=pl.CostEstimate(flops=flops, bytes_accessed=moved, transcendentals=10**5),
-    )
-
-
-def forward_scratch(views, planes, rows, cols):
-    return [
-        pltpu.VMEM((views, planes, 3 * rows, 2 * cols), BF16),
-        pltpu.VMEM((STEP, 3 * rows // 16, planes * 16, cols), F32),
-    ]
+    views = ys.shape[0]
+    acc[...] = jnp.zeros_like(acc)
+    forward_rows(parity, far_before, near, own, far_after, wy, ys)
+
+    def step(chosen):
+        fields = [ref.at[chosen] for ref in (ys, wx, wz)]
+        for v in range(STEP):
+            f = [ref.at[v] for ref in fields]
+            forward_view(f[0], f[1][...], f[2][...], blurred.at[v])
+        fields = [ref.at[chosen] for ref in (before, raw, after, wya, wxa, wza)]
+        adjoint_views(blurred, *fields, ya, xs, acc)
+
+    each_step(views, step)
+    sums = jnp.sum(part[...] + rest[...], axis=1, keepdims=True)
+    space = sums.shape[0] // 3
+    total, first, second = (sums[i * space : i * space + views] for i in range(3))
+    scale = jnp.sum(jnp.log(first / total) + jnp.log(second / total), axis=0, keepdims=True)
+    updated(own, (acc[...] + scale[None]) * (1.0 / views), out)
 
 
 def adjoint_scratch(planes, rows, cols):
@@ -277,71 +286,47 @@
 
 def forward(parity, slabs, weights):
     planes, rows, cols = slabs[0].shape
-    wy, wx, wz = weights
-    views = wx.shape[0]
+    views = weights[1].shape[0]
     slabs = [s.reshape(-1, cols) if i == 2 else s for i, s in enumerate(slabs)]
-    out = jax.ShapeDtypeStruct((views, planes * 3 * rows, cols), F32)
-    return pl.pallas_call(
-        forward_kernel,
-        grid=(views // STEP,),
-        out_shape=out,
-        in_specs=[pl.BlockSpec(memory_space=SMEM)]
-        + [whole(s) for s in slabs]
-        + [whole(wy), step_views(wx), step_views(wz)],
-        out_specs=step_views(out),
-        scratch_shapes=forward_scratch(views, planes, rows, cols),
-        name="forward",
-        **params(10**10, 10**7),
-    )(parity, *slabs, *weights)
+    out = pltpu.VMEM((views, planes, 3 * rows, cols), F32)
+    scratch = [pltpu.VMEM((views, planes, 3 * rows, 2 * cols), BF16)]
+    return call(forward_kernel, out, [parity], [*slabs, *weights], scratch, "forward", 10**10)
 
 
 def first_adjoint(current, blurred, before, raw, after, weights, wzs, wyx):
-    wy, wx, wz = weights
+    planes, rows, cols = current.shape
     views = raw.shape[0]
-    planes, rows, cols = current.shape
     current = current.reshape(planes * rows, cols)
-    shapes = [
-        jax.ShapeDtypeStruct(current.shape, F32),
-        jax.ShapeDtypeStruct((24 * -(-views // 8), cols), F32),
-    ]
-    out, sums = pl.pallas_call(
+    outs = [pltpu.VMEM(current.shape, F32), pltpu.VMEM((24 * -(-views // 8), cols), F32)]
+    out, sums = call(
         first_adjoint_kernel,
-        grid=(views // STEP,),
-        out_shape=shapes,
-        in_specs=[whole(current)]
-        + [step_views(a) for a in (blurred, before, raw, after, wy, wx, wz)]
-        + [pl.BlockSpec(memory_space=SMEM), whole(wyx)],
-        out_specs=[whole(s) for s in shapes],
-        scratch_shapes=adjoint_scratch(planes, rows, cols),
-        name="adjoint",
-        **params(10**10, 10**7),
-    )(current, blurred, before, raw, after, wy, wx, wz, wzs, wyx)
+        outs,
+        [wzs],
+        [current, blurred, before, raw, after, *weights, wyx],
+        adjoint_scratch(planes, rows, cols),
+        "adjoint",
+        10**10,
+    )
     return out.reshape(planes, rows, cols), sums
 
 
 def full_iteration(parity, slabs, before, raw, after, weights, adjoint_weights, part, rest):
     planes, rows, cols = slabs[0].shape
     views = raw.shape[0]
-    wy, wx, wz = weights
     slabs = [s.reshape(-1, cols) if i == 2 else s for i, s in enumerate(slabs)]
-    out = jax.ShapeDtypeStruct((planes * rows, cols), F32)
-    return pl.pallas_call(
+    scratch = [
+        pltpu.VMEM((views, planes, 3 * rows, 2 * cols), BF16),
+        pltpu.VMEM((STEP, planes, 3 * rows, cols), F32),
+    ]
+    return call(
         iteration_kernel,
-        grid=(views // STEP,),
-        out_shape=out,
-        in_specs=[pl.BlockSpec(memory_space=SMEM)]
-        + [whole(s) for s in slabs]
-        + [step_views(a) for a in (before, raw, after)]
-        + [whole(wy), step_views(wx), step_views(wz)]
-        + [step_views(a) for a in adjoint_weights]
-        + [whole(part), whole(rest)],
-        out_specs=whole(out),
-        scratch_shapes=forward_scratch(views, planes, rows, cols)
-        + [pltpu.VMEM((STEP, planes * 3 * rows, cols), F32)]
-        + adjoint_scratch(planes, rows, cols),
-        name="iteration",
-        **params(2 * 10**10, 2 * 10**7),
-    )(parity, *slabs, before, raw, after, *weights, *adjoint_weights, part, rest).reshape(planes, rows, cols)
+        jax.ShapeDtypeStruct((planes * rows, cols), F32),
+        [parity],
+        [*slabs, before, raw, after, *weights, *adjoint_weights, part, rest],
+        scratch + adjoint_scratch(planes, rows, cols),
+        "iteration",
+        2 * 10**10,
+    ).reshape(planes, rows, cols)
 
 
 def two_slabs_away(value, count):

time: 89.9 us -> 89.2 us (level)
  Pallas kernels: 27.2 us -> 26 us
    pallas_call x4, Pallas kernels: 27.2 us -> 26 us  [call(): pl.pallas_call(kernel, out_shape=outs, in_specs=[pl.BlockSpec(memory_spac...]
  transfers between devices with their start and end apart: 13 -> 13, of which waited for: 6 -> 7; matrix products, arithmetic and copies ran while one was open for 3% -> 3% of each run, Pallas kernels for 10% -> 9%
where the time goes in v4:
time: 89.2 us; the launch traced here: 88.8 us
  starting transfers between devices  44.2 us (50%)
  Pallas kernels  26 us (29%)
  waiting for transfers between devices  15.3 us (17%)
  other arithmetic  1.56 us (2%)
  local copies, waits for them, and re-layouts  1.55 us (2%)
    ppermute x4, starting transfers between devices, two_slabs_away(): return (lax.ppermute(value, 'slab', up), lax.ppermute(value, 'slab', down))  34.7 us
    pallas_call x4, Pallas kernels, call(): pl.pallas_call(kernel, out_shape=outs, in_specs=[pl.BlockSpec(memory_spac...  26 us
    ppermute x5, waiting for transfers between devices, per_device(): lax.ppermute(sums, 'slab', [(i, i ^ d) for i in range(count)])  8.71 us
    ppermute x5, starting transfers between devices, per_device(): lax.ppermute(sums, 'slab', [(i, i ^ d) for i in range(count)])  6.36 us
    ppermute x4, waiting for transfers between devices, two_slabs_away(): return (lax.ppermute(value, 'slab', up), lax.ppermute(value, 'slab', down))  4.95 us
  transfers between devices with their start and end apart: 13, of which 7 were waited for; matrix products, arithmetic and copies ran while one was open for 3% of the time, Pallas kernels for 9%

profile of v4, /device:TPU:0, one launch (start us, length us, event | category | flops | bytes accessed | tf_op | source)
XLA Modules:
  0.0 88.8 jit_solution(17153895867053191238)
XLA Ops:
  0.0 5.0 %collective-permute-start = (f32[32,16,128]{2,1,0:T(8,128)}, f32[32,16,128]{2,1,0:T(8,128)S(1)}, u32[]{:S(2)}, u32[]{:S(2)}) collective-permute-start(f32[32,16,128]{2,1,0:T(8,128)} %param.3), channel_id=1, source_target_pairs={{0,2},{1,3},{2,4},{3,5},{4,6},{5,7},{6,8},{7,9},{8,10},{9,11},{10,... | collective-permute-start | bytes 786440 | tf_op jit(solution)/shard_map/ppermute | solution.py:335
  5.0 1.3 %collective-permute-start.1 = (f32[32,16,128]{2,1,0:T(8,128)}, f32[32,16,128]{2,1,0:T(8,128)S(1)}, u32[]{:S(2)}, u32[]{:S(2)}) collective-permute-start(f32[32,16,128]{2,1,0:T(8,128)} %param.3), channel_id=1, source_target_pairs={{2,0},{3,1},{4,2},{5,3},{6,4},{7,5},{8,6},{9,7},{10,8},{11,9},{12,... | collective-permute-start | bytes 786440 | tf_op jit(solution)/shard_map/ppermute | solution.py:335
  6.3 1.6 %collective-permute-start.3 = (f32[6,32,16,128]{3,2,1,0:T(8,128)}, f32[6,32,16,128]{3,2,1,0:T(8,128)S(1)}, u32[]{:S(2)}, u32[]{:S(2)}) collective-permute-start(f32[6,32,16,128]{3,2,1,0:T(8,128)} %raw.3), channel_id=1, source_target_pairs={{0,1},{1,2},{2,3},{3,4},{4,5},{5,6},{6,7},{7,8},{8,9},{9,10},{10,1... | collective-permute-start | bytes 4718600 | tf_op jit(solution)/shard_map/ppermute | solution.py:363
  7.9 1.3 %collective-permute-start.4 = (f32[6,32,16,128]{3,2,1,0:T(8,128)}, f32[6,32,16,128]{3,2,1,0:T(8,128)}, u32[]{:S(2)}, u32[]{:S(2)}) collective-permute-start(f32[6,32,16,128]{3,2,1,0:T(8,128)} %raw.3), channel_id=1, source_target_pairs={{1,0},{2,1},{3,2},{4,3},{5,4},{6,5},{7,6},{8,7},{9,8},{10,9},{11,1... | collective-permute-start | bytes 4718600 | tf_op jit(solution)/shard_map/ppermute | solution.py:364
  9.2 0.8 fusion.12
  10.1 0.1 fusion.11
  10.1 0.7 copy-done.1
  10.8 1.6 %weights.1 = (bf16[288,240]{1,0:T(8,128)(2,1)S(1)}, bf16[6,256,256]{2,1,0:T(8,128)(2,1)S(1)}, bf16[6,256,768]{2,1,0:T(8,128)(2,1)S(1)}, bf16[6,32,96]{2,1,0:T(8,...) custom-call(f32[6,3,31]{2,1,0:T(4,128)S(1)} %copy-done.1), custom_call_target="tpu_custom_call" | custom-call | flops 10000000 | bytes 10000000 | tf_op jit(solution)/shard_map/weights/pallas_call | solution.py:95
  12.5 0.1 multiply_reduce_fusion.2
  12.6 4.9 %collective-permute-done.far_before = f32[32,16,128]{2,1,0:T(8,128)S(1)} collective-permute-done((f32[32,16,128]{2,1,0:T(8,128)}, f32[32,16,128]{2,1,0:T(8,128)S(1)}, u32[]{:S(2)}, u32[]{:S(2)}) %collective-permute-start) | collective-permute-done | bytes 262176 | tf_op jit(solution)/shard_map/ppermute | solution.py:335
  17.5 0.0 collective-permute-done.1.far_after
  17.5 1.0 %pad_maximum_fusion = f32[2,32,16,128]{3,2,1,0:T(8,128)S(1)} fusion(f32[1,32,16,128]{3,2,1,0:T(8,128)S(1)} %select_bitcast_fusion.1, f32[1,32,16,128]{3,2,1,0:T(8,128)} %bitcast.17), kind=kLoop, calls=%fused_computation | loop fusion | flops 131072 | bytes 1048576 | tf_op jit(solution)/shard_map/stack | solution.py:340
  18.5 0.1 collective-permute-start.2
  18.6 0.1 multiply_reduce_fusion
  18.7 0.1 multiply_reduce_fusion.1.wzs
  18.8 0.1 broadcast_multiply_fusion.wyx
  18.9 1.6 %collective-permute-done.2.near = f32[2,32,16,128]{3,2,1,0:T(8,128)S(1)} collective-permute-done((f32[2,32,16,128]{3,2,1,0:T(8,128)S(1)}, f32[2,32,16,128]{3,2,1,0:T(8,128)S(1)}, u32[]{:S(2)}, u32[]{:S(2)}) %collective-permute-start.2) | collective-permute-done | bytes 524320 | tf_op jit(solution)/shard_map/ppermute | solution.py:341
  20.5 6.8 %forward.1.blurred = f32[6,32,48,128]{3,2,1,0:T(8,128)S(1)} custom-call(s32[1]{0:T(128)} %bitcast.parity, f32[32,16,128]{2,1,0:T(8,128)S(1)} %collective-permute-done.far_before, f32[2,32,16,128]{3,2,1,0:T(8,128)S(1)} %collective-permute-done.2.near, f32[512,128]{1,0:T(8,128)S(1)} %bitcast.18, f32[32,16,128]{2,1,0:T(8,128)S(1)} %collective-permute-done.1.far_after, ...), custom_call_target="tpu_custom_call" | custom-call | flops 10000000000 | bytes 10000000 | tf_op jit(solution)/shard_map/forward/pallas_call | solution.py:95
  27.3 5.7 %adjoint.1 = (f32[512,128]{1,0:T(8,128)S(1)}, f32[24,128]{1,0:T(8,128)S(1)}) custom-call(f32[6,32]{1,0:T(8,128)S(1)} %multiply_reduce_fusion.1.wzs, f32[512,128]{1,0:T(8,128)S(1)} %bitcast.19, f32[6,32,48,128]{3,2,1,0:T(8,128)S(1)} %forward.1.blurred, f32[6,32,16,128]{3,2,1,0:T(8,128)S(1)} %collective-permute-done.3.before, ...), custom_call_target="tpu_custom_call" | custom-call | flops 10000000000 | bytes 10000000 | tf_op jit(solution)/shard_map/adjoint/pallas_call | solution.py:95
  33.1 27.2 %collective-permute-start.5 = (f32[32,16,128]{2,1,0:T(8,128)S(1)}, f32[32,16,128]{2,1,0:T(8,128)S(1)}, u32[]{:S(2)}, u32[]{:S(2)}) collective-permute-start(f32[32,16,128]{2,1,0:T(8,128)S(1)} %bitcast.20), channel_id=1, source_target_pairs={{0,2},{1,3},{2,4},{3,5},{4,6},{5,7},{6,8},{7,9},{8,10},{9,11},{10,... | collective-permute-start | bytes 786440 | tf_op jit(solution)/shard_map/ppermute | solution.py:335
  60.2 1.3 %collective-permute-start.6 = (f32[32,16,128]{2,1,0:T(8,128)S(1)}, f32[32,16,128]{2,1,0:T(8,128)S(1)}, u32[]{:S(2)}, u32[]{:S(2)}) collective-permute-start(f32[32,16,128]{2,1,0:T(8,128)S(1)} %bitcast.21), channel_id=1, source_target_pairs={{2,0},{3,1},{4,2},{5,3},{6,4},{7,5},{8,6},{9,7},{10,8},{11,9},{12,... | collective-permute-start | bytes 786440 | tf_op jit(solution)/shard_map/ppermute | solution.py:335
  61.5 0.1 collective-permute-start.7
  61.6 1.2 %collective-permute-done.7 = f32[24,128]{1,0:T(8,128)S(1)} collective-permute-done((f32[24,128]{1,0:T(8,128)S(1)}, f32[24,128]{1,0:T(8,128)S(1)}, u32[]{:S(2)}, u32[]{:S(2)}) %collective-permute-start.7) | collective-permute-done | bytes 12320 | tf_op jit(solution)/shard_map/ppermute | solution.py:381
  62.8 5.5 %collective-permute-start.10 = (f32[24,128]{1,0:T(8,128)S(1)}, f32[24,128]{1,0:T(8,128)S(1)}, u32[]{:S(2)}, u32[]{:S(2)}) collective-permute-start(f32[24,128]{1,0:T(8,128)S(1)} %add.66), channel_id=1, source_target_pairs={{0,12},{1,13},{2,14},{3,15},{4,8},{5,9},{6,10},{7,11},{8,4},{9,5},... | collective-permute-start | bytes 36872 | tf_op jit(solution)/shard_map/ppermute | solution.py:381
  68.3 0.6 collective-permute-start.9
  68.9 3.2 %collective-permute-done.10 = f32[24,128]{1,0:T(8,128)S(1)} collective-permute-done((f32[24,128]{1,0:T(8,128)S(1)}, f32[24,128]{1,0:T(8,128)S(1)}, u32[]{:S(2)}, u32[]{:S(2)}) %collective-permute-start.10) | collective-permute-done | bytes 12320 | tf_op jit(solution)/shard_map/ppermute | solution.py:381
  72.0 0.1 collective-permute-done.8
  72.1 0.8 collective-permute-done.9
  73.0 0.2 collective-permute-start.11
  73.2 0.2 collective-permute-start.12
  73.4 3.5 %collective-permute-done.12.rest = f32[24,128]{1,0:T(8,128)S(1)} collective-permute-done((f32[24,128]{1,0:T(8,128)S(1)}, f32[24,128]{1,0:T(8,128)S(1)}, u32[]{:S(2)}, u32[]{:S(2)}) %collective-permute-start.12) | collective-permute-done | bytes 12320 | tf_op jit(solution)/shard_map/ppermute | solution.py:381
  76.9 11.8 %iteration.1 = f32[512,128]{1,0:T(8,128)} custom-call(s32[1]{0:T(128)} %bitcast.parity, f32[32,16,128]{2,1,0:T(8,128)S(1)} %collective-permute-done.5.far_before, f32[2,32,16,128]{3,2,1,0:T(8,128)S(1)} %collective-permute-done.11.near, f32[512,128]{1,0:T(8,128)S(1)} %get-tuple-element.22.own, f32[32,16,128]{2,1,0:T(8,128)S(1)} %collective-permute-done.6.far_after, ...), custom_call_target="tpu_custom_call" | custom-call | flops 20000000000 | bytes 10000000 | tf_op jit(solution)/shard_map/iteration/pallas_call | solution.py:95
  (21 shorter events, 0.2 us)
Async XLA Ops:
  0.0 20.5 %copy-start = (f32[32,16,128]{2,1,0:T(8,128)S(1)}, f32[32,16,128]{2,1,0:T(8,128)}, u32[]{:S(2)}) copy-start(f32[32,16,128]{2,1,0:T(8,128)} %param.3) | copy-start | bytes 786436
  0.0 17.5 %collective-permute-start = (f32[32,16,128]{2,1,0:T(8,128)}, f32[32,16,128]{2,1,0:T(8,128)S(1)}, u32[]{:S(2)}, u32[]{:S(2)}) collective-permute-start(f32[32,16,128]{2,1,0:T(8,128)} %param.3), channel_id=1, source_target_pairs={{0,2},{1,3},{2,4},{3,5},{4,6},{5,7},{6,8},{7,9},{8,10},{9,11},{10,... | collective-permute-start | bytes 786440 | tf_op jit(solution)/shard_map/ppermute | solution.py:335
  5.0 12.5 %collective-permute-start.1 = (f32[32,16,128]{2,1,0:T(8,128)}, f32[32,16,128]{2,1,0:T(8,128)S(1)}, u32[]{:S(2)}, u32[]{:S(2)}) collective-permute-start(f32[32,16,128]{2,1,0:T(8,128)} %param.3), channel_id=1, source_target_pairs={{2,0},{3,1},{4,2},{5,3},{6,4},{7,5},{8,6},{9,7},{10,8},{11,9},{12,... | collective-permute-start | bytes 786440 | tf_op jit(solution)/shard_map/ppermute | solution.py:335
  6.3 21.0 %collective-permute-start.3 = (f32[6,32,16,128]{3,2,1,0:T(8,128)}, f32[6,32,16,128]{3,2,1,0:T(8,128)S(1)}, u32[]{:S(2)}, u32[]{:S(2)}) collective-permute-start(f32[6,32,16,128]{3,2,1,0:T(8,128)} %raw.3), channel_id=1, source_target_pairs={{0,1},{1,2},{2,3},{3,4},{4,5},{5,6},{6,7},{7,8},{8,9},{9,10},{10,1... | collective-permute-start | bytes 4718600 | tf_op jit(solution)/shard_map/ppermute | solution.py:363
  7.9 19.4 %collective-permute-start.4 = (f32[6,32,16,128]{3,2,1,0:T(8,128)}, f32[6,32,16,128]{3,2,1,0:T(8,128)}, u32[]{:S(2)}, u32[]{:S(2)}) collective-permute-start(f32[6,32,16,128]{3,2,1,0:T(8,128)} %raw.3), channel_id=1, source_target_pairs={{1,0},{2,1},{3,2},{4,3},{5,4},{6,5},{7,6},{8,7},{9,8},{10,9},{11,1... | collective-permute-start | bytes 4718600 | tf_op jit(solution)/shard_map/ppermute | solution.py:364
  10.1 0.7 copy-start.1
  18.5 2.0 %collective-permute-start.2 = (f32[2,32,16,128]{3,2,1,0:T(8,128)S(1)}, f32[2,32,16,128]{3,2,1,0:T(8,128)S(1)}, u32[]{:S(2)}, u32[]{:S(2)}) collective-permute-start(f32[2,32,16,128]{3,2,1,0:T(8,128)S(1)} %pad_maximum_fusion), channel_id=1, source_target_pairs={{0,1},{1,0},{2,3},{3,2},{4,5},{5,4},{6,7},{7,6},{8,9},{9,8},{10,11... | collective-permute-start | bytes 1572872 | tf_op jit(solution)/shard_map/ppermute | solution.py:341
  20.5 6.8 %copy-start.2 = (f32[6,32,16,128]{3,2,1,0:T(8,128)S(1)}, f32[6,32,16,128]{3,2,1,0:T(8,128)}, u32[]{:S(2)}) copy-start(f32[6,32,16,128]{3,2,1,0:T(8,128)} %raw.3) | copy-start | bytes 4718596
  33.1 39.8 %collective-permute-start.5 = (f32[32,16,128]{2,1,0:T(8,128)S(1)}, f32[32,16,128]{2,1,0:T(8,128)S(1)}, u32[]{:S(2)}, u32[]{:S(2)}) collective-permute-start(f32[32,16,128]{2,1,0:T(8,128)S(1)} %bitcast.20), channel_id=1, source_target_pairs={{0,2},{1,3},{2,4},{3,5},{4,6},{5,7},{6,8},{7,9},{8,10},{9,11},{10,... | collective-permute-start | bytes 786440 | tf_op jit(solution)/shard_map/ppermute | solution.py:335
  60.2 12.7 %collective-permute-start.6 = (f32[32,16,128]{2,1,0:T(8,128)S(1)}, f32[32,16,128]{2,1,0:T(8,128)S(1)}, u32[]{:S(2)}, u32[]{:S(2)}) collective-permute-start(f32[32,16,128]{2,1,0:T(8,128)S(1)} %bitcast.21), channel_id=1, source_target_pairs={{2,0},{3,1},{4,2},{5,3},{6,4},{7,5},{8,6},{9,7},{10,8},{11,9},{12,... | collective-permute-start | bytes 786440 | tf_op jit(solution)/shard_map/ppermute | solution.py:335
  61.5 1.2 %collective-permute-start.7 = (f32[24,128]{1,0:T(8,128)S(1)}, f32[24,128]{1,0:T(8,128)S(1)}, u32[]{:S(2)}, u32[]{:S(2)}) collective-permute-start(f32[24,128]{1,0:T(8,128)S(1)} %get-tuple-element.23), channel_id=1, source_target_pairs={{0,1},{1,0},{2,3},{3,2},{4,5},{5,4},{6,7},{7,6},{8,9},{9,8},{10,11... | collective-permute-start | bytes 36872 | tf_op jit(solution)/shard_map/ppermute | solution.py:381
  62.8 9.2 %collective-permute-start.10 = (f32[24,128]{1,0:T(8,128)S(1)}, f32[24,128]{1,0:T(8,128)S(1)}, u32[]{:S(2)}, u32[]{:S(2)}) collective-permute-start(f32[24,128]{1,0:T(8,128)S(1)} %add.66), channel_id=1, source_target_pairs={{0,12},{1,13},{2,14},{3,15},{4,8},{5,9},{6,10},{7,11},{8,4},{9,5},... | collective-permute-start | bytes 36872 | tf_op jit(solution)/shard_map/ppermute | solution.py:381
  68.3 3.8 %collective-permute-start.8 = (f32[24,128]{1,0:T(8,128)S(1)}, f32[24,128]{1,0:T(8,128)S(1)}, u32[]{:S(2)}, u32[]{:S(2)}) collective-permute-start(f32[24,128]{1,0:T(8,128)S(1)} %add.66), channel_id=1, source_target_pairs={{0,4},{1,5},{2,6},{3,7},{4,0},{5,1},{6,2},{7,3},{8,12},{9,13},{10,... | collective-permute-start | bytes 36872 | tf_op jit(solution)/shard_map/ppermute | solution.py:381
  68.3 4.6 %collective-permute-start.9 = (f32[24,128]{1,0:T(8,128)S(1)}, f32[24,128]{1,0:T(8,128)S(1)}, u32[]{:S(2)}, u32[]{:S(2)}) collective-permute-start(f32[24,128]{1,0:T(8,128)S(1)} %add.66), channel_id=1, source_target_pairs={{0,8},{1,9},{2,10},{3,11},{4,12},{5,13},{6,14},{7,15},{8,0},{9,1},... | collective-permute-start | bytes 36872 | tf_op jit(solution)/shard_map/ppermute | solution.py:381
  73.0 3.9 %collective-permute-start.11 = (f32[2,32,16,128]{3,2,1,0:T(8,128)S(1)}, f32[2,32,16,128]{3,2,1,0:T(8,128)S(1)}, u32[]{:S(2)}, u32[]{:S(2)}) collective-permute-start(f32[2,32,16,128]{3,2,1,0:T(8,128)S(1)} %pad_maximum_fusion.1), channel_id=1, source_target_pairs={{0,1},{1,0},{2,3},{3,2},{4,5},{5,4},{6,7},{7,6},{8,9},{9,8},{10,11... | collective-permute-start | bytes 1572872 | tf_op jit(solution)/shard_map/ppermute | solution.py:341
  73.2 3.7 %collective-permute-start.12 = (f32[24,128]{1,0:T(8,128)S(1)}, f32[24,128]{1,0:T(8,128)S(1)}, u32[]{:S(2)}, u32[]{:S(2)}) collective-permute-start(f32[24,128]{1,0:T(8,128)S(1)} %add_add_fusion.part), channel_id=1, source_target_pairs={{0,2},{1,3},{2,0},{3,1},{4,6},{5,7},{6,4},{7,5},{8,10},{9,11},{10,... | collective-permute-start | bytes 36872 | tf_op jit(solution)/shard_map/ppermute | solution.py:381

commit v5 on v4

--- a/solution.py
+++ b/solution.py
@@ -56,6 +56,7 @@
         low = row_y - high
         if flip:
             row_y = [part + pltpu.roll(part, in_rows, 1) for part in (high, low)]
+            row_y = [part if j == 0 else pltpu.roll(part, 2 * in_rows, 1) for part in row_y for j in range(2)]
         else:
             row_y = high + pltpu.roll(high, in_rows, 1) + pltpu.roll(low, 2 * in_rows, 1)
         row_x = placed_row(taps_ref[:, 2, :], lambda k: lax.rem(margin - order(k) + 2 * cols, 2 * cols), 2 * cols)
@@ -68,7 +69,7 @@
         for v in range(views):
             if flip:
                 for j, row in enumerate(row_y):
-                    wy[v, j * rows : (j + 1) * rows, :] = slanted(row[v : v + 1], rows)[:, : 2 * in_rows].astype(BF16)
+                    wy[v, j * rows : (j + 1) * rows, :] = slanted(row[v : v + 1], rows)[:, : 4 * in_rows].astype(BF16)
             else:
                 band = slanted(row_y[v : v + 1], out_rows)
                 wy[v * out_rows : (v + 1) * out_rows, :] = band[:, : 3 * in_rows].astype(BF16)
@@ -110,7 +111,7 @@
         pltpu.VMEM((views * 3 * rows, 15 * rows), BF16),
         pltpu.VMEM((views, 2 * cols, 2 * cols), BF16),
         pltpu.VMEM((views, 8 * planes, 24 * planes), BF16),
-        pltpu.VMEM((views, 2 * rows, 6 * rows), BF16),
+        pltpu.VMEM((views, 4 * rows, 12 * rows), BF16),
         pltpu.VMEM((views, 2 * cols, 2 * cols), BF16),
         pltpu.VMEM((views, planes, 3 * planes), BF16),
     ]
@@ -182,13 +183,16 @@
         return counts * (inverse * (2.0 - below * inverse))
 
     for v in range(STEP):
-        for z in range(0, planes, 2):
-            high, low = split(jnp.concatenate([quotient(v, z), quotient(v, z + 1)], axis=1))
-            both = dot(wy[v], jnp.concatenate([high, low], axis=0))
-            high, low = split(both[:rows] + both[rows:])
-            for j in range(2):
-                ya[v, z + j, :, :cols] = high[:, j * cols : (j + 1) * cols]
-                ya[v, z + j, :, cols:] = low[:, j * cols : (j + 1) * cols]
+        for z in range(0, planes, 4):
+            parts = []
+            for first in (z, z + 2):
+                parts += split(jnp.concatenate([quotient(v, first), quotient(v, first + 1)], axis=1))
+            both = dot(wy[v], jnp.concatenate(parts, axis=0))
+            high, low = split(both[: 2 * rows] + both[2 * rows :])
+            for j in range(4):
+                here = (slice(j // 2 * rows, (j // 2 + 1) * rows), slice(j % 2 * cols, (j % 2 + 1) * cols))
+                ya[v, z + j, :, :cols] = high[here]
+                ya[v, z + j, :, cols:] = low[here]
     for pair in range(rows // 16):
         chosen = slice(16 * pair, 16 * pair + 16)
         found = [row_pairs(ya[v, :, chosen, :], wx[v], wz[v], xs.at[v]) for v in range(STEP)]
@@ -206,24 +210,22 @@
         out[at, :] = current[at, :] * jnp.exp(exponents[y // 2, :, half])
 
 
-def each_step(views, body):
+def each_step(steps, body):
     def run(step, _):
-        body(pl.ds(STEP * step, STEP))
+        body(step)
         return 0
 
-    lax.fori_loop(0, views // STEP, run, 0)
-
-
-def forward_kernel(parity, far_before, near, own, far_after, wy, wx, wz, out, ys):
+    lax.fori_loop(0, steps, run, 0)
+
+
+def forward_kernel(parity, wzs, far_before, near, own, far_after, wy, wx, wz, raw, wyx, out, sums, ys):
+    views = ys.shape[0]
     forward_rows(parity, far_before, near, own, far_after, wy, ys)
-
-    def step(chosen):
-        fields = [ref.at[chosen] for ref in (ys, wx, wz, out)]
-        for v in range(STEP):
-            f = [ref.at[v] for ref in fields]
-            forward_view(f[0], f[1][...], f[2][...], f[3])
-
-    each_step(ys.shape[0], step)
+    each_step(views, lambda v: forward_view(ys.at[v], wx[v], wz[v], out.at[v]))
+    sums[...] = jnp.zeros_like(sums)
+    for v in range(views):
+        sums[v : v + 1, :] = jnp.sum(jnp.sum(raw[v], axis=0), axis=0, keepdims=True)
+    weighted_sums(own, wzs, wyx, sums, sums.shape[0] // 3)
 
 
 def weighted_sums(values, wzs, wyx, sums, at):
@@ -235,20 +237,18 @@
         sums[at + v : at + v + 1, :] = jnp.sum(total * wyx[v], axis=0, keepdims=True)
 
 
-def first_adjoint_kernel(wzs, current, blurred, before, raw, after, wy, wx, wz, wyx, out, sums, ya, xs, acc):
+def first_adjoint_kernel(wzs, current, blurred, before, raw, after, wy, wx, wz, wyx, known, out, sums, ya, xs, acc):
     views = wyx.shape[0]
     acc[...] = jnp.zeros_like(acc)
-    sums[...] = jnp.zeros_like(sums)
-
-    def step(chosen):
+
+    def step(i):
+        chosen = pl.ds(STEP * i, STEP)
         fields = [ref.at[chosen] for ref in (blurred, before, raw, after, wy, wx, wz)]
         adjoint_views(*fields, ya, xs, acc)
-        total = [jnp.sum(jnp.sum(fields[2][v], axis=0), axis=0, keepdims=True) for v in range(STEP)]
-        sums[chosen, :] = jnp.concatenate(total, axis=0)
-
-    each_step(views, step)
+
+    each_step(views // STEP, step)
     updated(current, acc[...] * (1.0 / views), out)
-    weighted_sums(current, wzs, wyx, sums, sums.shape[0] // 3)
+    sums[...] = known[...]
     weighted_sums(out, wzs, wyx, sums, 2 * sums.shape[0] // 3)
 
 
@@ -260,15 +260,17 @@
     acc[...] = jnp.zeros_like(acc)
     forward_rows(parity, far_before, near, own, far_after, wy, ys)
 
-    def step(chosen):
-        fields = [ref.at[chosen] for ref in (ys, wx, wz)]
-        for v in range(STEP):
-            f = [ref.at[v] for ref in fields]
-            forward_view(f[0], f[1][...], f[2][...], blurred.at[v])
+    def step(i):
+        def one_view(j):
+            v = STEP * i + j
+            forward_view(ys.at[v], wx[v], wz[v], blurred.at[j])
+
+        each_step(STEP, one_view)
+        chosen = pl.ds(STEP * i, STEP)
         fields = [ref.at[chosen] for ref in (before, raw, after, wya, wxa, wza)]
         adjoint_views(blurred, *fields, ya, xs, acc)
 
-    each_step(views, step)
+    each_step(views // STEP, step)
     sums = jnp.sum(part[...] + rest[...], axis=1, keepdims=True)
     space = sums.shape[0] // 3
     total, first, second = (sums[i * space : i * space + views] for i in range(3))
@@ -284,25 +286,23 @@
     ]
 
 
-def forward(parity, slabs, weights):
+def forward(parity, slabs, weights, raw, wzs, wyx):
     planes, rows, cols = slabs[0].shape
-    views = weights[1].shape[0]
+    views = raw.shape[0]
     slabs = [s.reshape(-1, cols) if i == 2 else s for i, s in enumerate(slabs)]
-    out = pltpu.VMEM((views, planes, 3 * rows, cols), F32)
+    outs = [pltpu.VMEM((views, planes, 3 * rows, cols), F32), pltpu.VMEM((24 * -(-views // 8), cols), F32)]
     scratch = [pltpu.VMEM((views, planes, 3 * rows, 2 * cols), BF16)]
-    return call(forward_kernel, out, [parity], [*slabs, *weights], scratch, "forward", 10**10)
-
-
-def first_adjoint(current, blurred, before, raw, after, weights, wzs, wyx):
+    return call(forward_kernel, outs, [parity, wzs], [*slabs, *weights, raw, wyx], scratch, "forward", 10**10)
+
+
+def first_adjoint(current, blurred, before, raw, after, weights, wzs, wyx, known):
     planes, rows, cols = current.shape
-    views = raw.shape[0]
     current = current.reshape(planes * rows, cols)
-    outs = [pltpu.VMEM(current.shape, F32), pltpu.VMEM((24 * -(-views // 8), cols), F32)]
     out, sums = call(
         first_adjoint_kernel,
-        outs,
+        [pltpu.VMEM(current.shape, F32), pltpu.VMEM(known.shape, F32)],
         [wzs],
-        [current, blurred, before, raw, after, *weights, wyx],
+        [current, blurred, before, raw, after, *weights, wyx, known],
         adjoint_scratch(planes, rows, cols),
         "adjoint",
         10**10,
@@ -371,8 +371,8 @@
     forward_weights, adjoint_weights = make_weights(taps, planes, rows, cols)
 
     slabs = with_near(estimate, *far, parity, count)
-    blurred = forward(parity, slabs, forward_weights)
-    current, sums = first_adjoint(estimate, blurred, before, raw, after, adjoint_weights, wzs, wyx)
+    blurred, known = forward(parity, slabs, forward_weights, raw, wzs, wyx)
+    current, sums = first_adjoint(estimate, blurred, before, raw, after, adjoint_weights, wzs, wyx, known)
 
     far = two_slabs_away(current, count)
     bits = [1 << b for b in range(count.bit_length() - 1)]

time: 89.2 us -> 89.4 us (level)
  transfers between devices with their start and end apart: 13 -> 13, of which waited for: 7 -> 6; matrix products, arithmetic and copies ran while one was open for 3% -> 3% of each run, Pallas kernels for 9% -> 10%
where the time goes in v5:
time: 89.4 us; the launch traced here: 89 us
  starting transfers between devices  44.2 us (49%)
  Pallas kernels  26.3 us (29%)
  waiting for transfers between devices  15.2 us (17%)
  other arithmetic  1.56 us (2%)
  local copies, waits for them, and re-layouts  1.55 us (2%)
    ppermute x4, starting transfers between devices, two_slabs_away(): return (lax.ppermute(value, 'slab', up), lax.ppermute(value, 'slab', down))  34.8 us
    pallas_call x4, Pallas kernels, call(): pl.pallas_call(kernel, out_shape=outs, in_specs=[pl.BlockSpec(memory_spac...  26.3 us
    ppermute x5, waiting for transfers between devices, per_device(): lax.ppermute(sums, 'slab', [(i, i ^ d) for i in range(count)])  8.71 us
    ppermute x5, starting transfers between devices, per_device(): lax.ppermute(sums, 'slab', [(i, i ^ d) for i in range(count)])  6.36 us
    ppermute x4, waiting for transfers between devices, two_slabs_away(): return (lax.ppermute(value, 'slab', up), lax.ppermute(value, 'slab', down))  4.85 us
  transfers between devices with their start and end apart: 13, of which 6 were waited for; matrix products, arithmetic and copies ran while one was open for 3% of the time, Pallas kernels for 10%

profile of v5, /device:TPU:0, one launch (start us, length us, event | category | flops | bytes accessed | tf_op | source)
XLA Modules:
  0.0 89.0 jit_solution(8165491672586675167)
XLA Ops:
  0.0 5.0 %collective-permute-start = (f32[32,16,128]{2,1,0:T(8,128)}, f32[32,16,128]{2,1,0:T(8,128)S(1)}, u32[]{:S(2)}, u32[]{:S(2)}) collective-permute-start(f32[32,16,128]{2,1,0:T(8,128)} %param.3), channel_id=1, source_target_pairs={{0,2},{1,3},{2,4},{3,5},{4,6},{5,7},{6,8},{7,9},{8,10},{9,11},{10,... | collective-permute-start | bytes 786440 | tf_op jit(solution)/shard_map/ppermute | solution.py:335
  5.0 1.3 %collective-permute-start.1 = (f32[32,16,128]{2,1,0:T(8,128)}, f32[32,16,128]{2,1,0:T(8,128)S(1)}, u32[]{:S(2)}, u32[]{:S(2)}) collective-permute-start(f32[32,16,128]{2,1,0:T(8,128)} %param.3), channel_id=1, source_target_pairs={{2,0},{3,1},{4,2},{5,3},{6,4},{7,5},{8,6},{9,7},{10,8},{11,9},{12,... | collective-permute-start | bytes 786440 | tf_op jit(solution)/shard_map/ppermute | solution.py:335
  6.3 1.6 %collective-permute-start.3 = (f32[6,32,16,128]{3,2,1,0:T(8,128)}, f32[6,32,16,128]{3,2,1,0:T(8,128)S(1)}, u32[]{:S(2)}, u32[]{:S(2)}) collective-permute-start(f32[6,32,16,128]{3,2,1,0:T(8,128)} %raw.5), channel_id=1, source_target_pairs={{0,1},{1,2},{2,3},{3,4},{4,5},{5,6},{6,7},{7,8},{8,9},{9,10},{10,1... | collective-permute-start | bytes 4718600 | tf_op jit(solution)/shard_map/ppermute | solution.py:363
  7.9 1.3 %collective-permute-start.4 = (f32[6,32,16,128]{3,2,1,0:T(8,128)}, f32[6,32,16,128]{3,2,1,0:T(8,128)}, u32[]{:S(2)}, u32[]{:S(2)}) collective-permute-start(f32[6,32,16,128]{3,2,1,0:T(8,128)} %raw.5), channel_id=1, source_target_pairs={{1,0},{2,1},{3,2},{4,3},{5,4},{6,5},{7,6},{8,7},{9,8},{10,9},{11,1... | collective-permute-start | bytes 4718600 | tf_op jit(solution)/shard_map/ppermute | solution.py:364
  9.2 0.8 fusion.12
  10.1 0.1 fusion.11
  10.1 0.7 copy-done.1
  10.8 1.7 %weights.1 = (bf16[288,240]{1,0:T(8,128)(2,1)S(1)}, bf16[6,256,256]{2,1,0:T(8,128)(2,1)S(1)}, bf16[6,256,768]{2,1,0:T(8,128)(2,1)S(1)}, bf16[6,64,192]{2,1,0:T(8...) custom-call(f32[6,3,31]{2,1,0:T(4,128)S(1)} %copy-done.1), custom_call_target="tpu_custom_call" | custom-call | flops 10000000 | bytes 10000000 | tf_op jit(solution)/shard_map/weights/pallas_call | solution.py:96
  12.6 0.1 multiply_reduce_fusion.2
  12.7 4.8 %collective-permute-done.far_before = f32[32,16,128]{2,1,0:T(8,128)S(1)} collective-permute-done((f32[32,16,128]{2,1,0:T(8,128)}, f32[32,16,128]{2,1,0:T(8,128)S(1)}, u32[]{:S(2)}, u32[]{:S(2)}) %collective-permute-start) | collective-permute-done | bytes 262176 | tf_op jit(solution)/shard_map/ppermute | solution.py:335
  17.5 0.0 collective-permute-done.1.far_after
  17.5 1.0 %pad_maximum_fusion = f32[2,32,16,128]{3,2,1,0:T(8,128)S(1)} fusion(f32[1,32,16,128]{3,2,1,0:T(8,128)S(1)} %select_bitcast_fusion.1, f32[1,32,16,128]{3,2,1,0:T(8,128)} %bitcast.17), kind=kLoop, calls=%fused_computation | loop fusion | flops 131072 | bytes 1048576 | tf_op jit(solution)/shard_map/stack | solution.py:340
  18.5 0.1 collective-permute-start.2
  18.6 0.1 multiply_reduce_fusion
  18.7 0.1 multiply_reduce_fusion.1.wzs
  18.8 0.1 broadcast_multiply_fusion.wyx
  18.9 1.6 %collective-permute-done.2.near = f32[2,32,16,128]{3,2,1,0:T(8,128)S(1)} collective-permute-done((f32[2,32,16,128]{3,2,1,0:T(8,128)S(1)}, f32[2,32,16,128]{3,2,1,0:T(8,128)S(1)}, u32[]{:S(2)}, u32[]{:S(2)}) %collective-permute-start.2) | collective-permute-done | bytes 524320 | tf_op jit(solution)/shard_map/ppermute | solution.py:341
  20.5 6.8 %forward.1 = (f32[6,32,48,128]{3,2,1,0:T(8,128)S(1)}, f32[24,128]{1,0:T(8,128)S(1)}) custom-call(s32[1]{0:T(128)} %bitcast.parity, f32[6,32]{1,0:T(8,128)S(1)} %multiply_reduce_fusion.1.wzs, f32[32,16,128]{2,1,0:T(8,128)S(1)} %collective-permute-done.far_before, f32[2,32,16,128]{3,2,1,0:T(8,128)S(1)} %collective-permute-done.2.near, ...), custom_call_target="tpu_custom_call" | custom-call | flops 10000000000 | bytes 10000000 | tf_op jit(solution)/shard_map/forward/pallas_call | solution.py:96
  27.3 5.7 %adjoint.1 = (f32[512,128]{1,0:T(8,128)S(1)}, f32[24,128]{1,0:T(8,128)S(1)}) custom-call(f32[6,32]{1,0:T(8,128)S(1)} %multiply_reduce_fusion.1.wzs, f32[512,128]{1,0:T(8,128)S(1)} %bitcast.19, f32[6,32,48,128]{3,2,1,0:T(8,128)S(1)} %get-tuple-element.21.blurred, f32[6,32,16,128]{3,2,1,0:T(8,128)S(1)} %collective-permute-done.3.before, ...), custom_call_target="tpu_custom_call" | custom-call | flops 10000000000 | bytes 10000000 | tf_op jit(solution)/shard_map/adjoint/pallas_call | solution.py:96
  33.0 27.2 %collective-permute-start.5 = (f32[32,16,128]{2,1,0:T(8,128)S(1)}, f32[32,16,128]{2,1,0:T(8,128)S(1)}, u32[]{:S(2)}, u32[]{:S(2)}) collective-permute-start(f32[32,16,128]{2,1,0:T(8,128)S(1)} %bitcast.20), channel_id=1, source_target_pairs={{0,2},{1,3},{2,4},{3,5},{4,6},{5,7},{6,8},{7,9},{8,10},{9,11},{10,... | collective-permute-start | bytes 786440 | tf_op jit(solution)/shard_map/ppermute | solution.py:335
  60.2 1.3 %collective-permute-start.6 = (f32[32,16,128]{2,1,0:T(8,128)S(1)}, f32[32,16,128]{2,1,0:T(8,128)S(1)}, u32[]{:S(2)}, u32[]{:S(2)}) collective-permute-start(f32[32,16,128]{2,1,0:T(8,128)S(1)} %bitcast.21), channel_id=1, source_target_pairs={{2,0},{3,1},{4,2},{5,3},{6,4},{7,5},{8,6},{9,7},{10,8},{11,9},{12,... | collective-permute-start | bytes 786440 | tf_op jit(solution)/shard_map/ppermute | solution.py:335
  61.5 0.1 collective-permute-start.7
  61.6 1.2 %collective-permute-done.7 = f32[24,128]{1,0:T(8,128)S(1)} collective-permute-done((f32[24,128]{1,0:T(8,128)S(1)}, f32[24,128]{1,0:T(8,128)S(1)}, u32[]{:S(2)}, u32[]{:S(2)}) %collective-permute-start.7) | collective-permute-done | bytes 12320 | tf_op jit(solution)/shard_map/ppermute | solution.py:381
  62.7 5.5 %collective-permute-start.10 = (f32[24,128]{1,0:T(8,128)S(1)}, f32[24,128]{1,0:T(8,128)S(1)}, u32[]{:S(2)}, u32[]{:S(2)}) collective-permute-start(f32[24,128]{1,0:T(8,128)S(1)} %add.66), channel_id=1, source_target_pairs={{0,12},{1,13},{2,14},{3,15},{4,8},{5,9},{6,10},{7,11},{8,4},{9,5},... | collective-permute-start | bytes 36872 | tf_op jit(solution)/shard_map/ppermute | solution.py:381
  68.3 0.6 collective-permute-start.9
  68.8 3.2 %collective-permute-done.10 = f32[24,128]{1,0:T(8,128)S(1)} collective-permute-done((f32[24,128]{1,0:T(8,128)S(1)}, f32[24,128]{1,0:T(8,128)S(1)}, u32[]{:S(2)}, u32[]{:S(2)}) %collective-permute-start.10) | collective-permute-done | bytes 12320 | tf_op jit(solution)/shard_map/ppermute | solution.py:381
  72.0 0.0 collective-permute-done.8
  72.0 0.8 collective-permute-done.9
  73.0 0.2 collective-permute-start.11
  73.2 0.2 collective-permute-start.12
  73.4 3.5 %collective-permute-done.12.rest = f32[24,128]{1,0:T(8,128)S(1)} collective-permute-done((f32[24,128]{1,0:T(8,128)S(1)}, f32[24,128]{1,0:T(8,128)S(1)}, u32[]{:S(2)}, u32[]{:S(2)}) %collective-permute-start.12) | collective-permute-done | bytes 12320 | tf_op jit(solution)/shard_map/ppermute | solution.py:381
  76.9 12.1 %iteration.1 = f32[512,128]{1,0:T(8,128)} custom-call(s32[1]{0:T(128)} %bitcast.parity, f32[32,16,128]{2,1,0:T(8,128)S(1)} %collective-permute-done.5.far_before, f32[2,32,16,128]{3,2,1,0:T(8,128)S(1)} %collective-permute-done.11.near, f32[512,128]{1,0:T(8,128)S(1)} %get-tuple-element.26.own, f32[32,16,128]{2,1,0:T(8,128)S(1)} %collective-permute-done.6.far_after, ...), custom_call_target="tpu_custom_call" | custom-call | flops 20000000000 | bytes 10000000 | tf_op jit(solution)/shard_map/iteration/pallas_call | solution.py:96
  (21 shorter events, 0.2 us)
Async XLA Ops:
  0.0 20.5 %copy-start = (f32[32,16,128]{2,1,0:T(8,128)S(1)}, f32[32,16,128]{2,1,0:T(8,128)}, u32[]{:S(2)}) copy-start(f32[32,16,128]{2,1,0:T(8,128)} %param.3) | copy-start | bytes 786436
  0.0 17.5 %collective-permute-start = (f32[32,16,128]{2,1,0:T(8,128)}, f32[32,16,128]{2,1,0:T(8,128)S(1)}, u32[]{:S(2)}, u32[]{:S(2)}) collective-permute-start(f32[32,16,128]{2,1,0:T(8,128)} %param.3), channel_id=1, source_target_pairs={{0,2},{1,3},{2,4},{3,5},{4,6},{5,7},{6,8},{7,9},{8,10},{9,11},{10,... | collective-permute-start | bytes 786440 | tf_op jit(solution)/shard_map/ppermute | solution.py:335
  5.0 12.5 %collective-permute-start.1 = (f32[32,16,128]{2,1,0:T(8,128)}, f32[32,16,128]{2,1,0:T(8,128)S(1)}, u32[]{:S(2)}, u32[]{:S(2)}) collective-permute-start(f32[32,16,128]{2,1,0:T(8,128)} %param.3), channel_id=1, source_target_pairs={{2,0},{3,1},{4,2},{5,3},{6,4},{7,5},{8,6},{9,7},{10,8},{11,9},{12,... | collective-permute-start | bytes 786440 | tf_op jit(solution)/shard_map/ppermute | solution.py:335
  6.3 21.0 %collective-permute-start.3 = (f32[6,32,16,128]{3,2,1,0:T(8,128)}, f32[6,32,16,128]{3,2,1,0:T(8,128)S(1)}, u32[]{:S(2)}, u32[]{:S(2)}) collective-permute-start(f32[6,32,16,128]{3,2,1,0:T(8,128)} %raw.5), channel_id=1, source_target_pairs={{0,1},{1,2},{2,3},{3,4},{4,5},{5,6},{6,7},{7,8},{8,9},{9,10},{10,1... | collective-permute-start | bytes 4718600 | tf_op jit(solution)/shard_map/ppermute | solution.py:363
  7.9 19.4 %collective-permute-start.4 = (f32[6,32,16,128]{3,2,1,0:T(8,128)}, f32[6,32,16,128]{3,2,1,0:T(8,128)}, u32[]{:S(2)}, u32[]{:S(2)}) collective-permute-start(f32[6,32,16,128]{3,2,1,0:T(8,128)} %raw.5), channel_id=1, source_target_pairs={{1,0},{2,1},{3,2},{4,3},{5,4},{6,5},{7,6},{8,7},{9,8},{10,9},{11,1... | collective-permute-start | bytes 4718600 | tf_op jit(solution)/shard_map/ppermute | solution.py:364
  10.1 0.7 copy-start.1
  10.8 9.7 %copy-start.2 = (f32[6,32,16,128]{3,2,1,0:T(8,128)S(1)}, f32[6,32,16,128]{3,2,1,0:T(8,128)}, u32[]{:S(2)}) copy-start(f32[6,32,16,128]{3,2,1,0:T(8,128)} %raw.5) | copy-start | bytes 4718596
  18.5 2.0 %collective-permute-start.2 = (f32[2,32,16,128]{3,2,1,0:T(8,128)S(1)}, f32[2,32,16,128]{3,2,1,0:T(8,128)S(1)}, u32[]{:S(2)}, u32[]{:S(2)}) collective-permute-start(f32[2,32,16,128]{3,2,1,0:T(8,128)S(1)} %pad_maximum_fusion), channel_id=1, source_target_pairs={{0,1},{1,0},{2,3},{3,2},{4,5},{5,4},{6,7},{7,6},{8,9},{9,8},{10,11... | collective-permute-start | bytes 1572872 | tf_op jit(solution)/shard_map/ppermute | solution.py:341
  33.0 39.8 %collective-permute-start.5 = (f32[32,16,128]{2,1,0:T(8,128)S(1)}, f32[32,16,128]{2,1,0:T(8,128)S(1)}, u32[]{:S(2)}, u32[]{:S(2)}) collective-permute-start(f32[32,16,128]{2,1,0:T(8,128)S(1)} %bitcast.20), channel_id=1, source_target_pairs={{0,2},{1,3},{2,4},{3,5},{4,6},{5,7},{6,8},{7,9},{8,10},{9,11},{10,... | collective-permute-start | bytes 786440 | tf_op jit(solution)/shard_map/ppermute | solution.py:335
  60.2 12.7 %collective-permute-start.6 = (f32[32,16,128]{2,1,0:T(8,128)S(1)}, f32[32,16,128]{2,1,0:T(8,128)S(1)}, u32[]{:S(2)}, u32[]{:S(2)}) collective-permute-start(f32[32,16,128]{2,1,0:T(8,128)S(1)} %bitcast.21), channel_id=1, source_target_pairs={{2,0},{3,1},{4,2},{5,3},{6,4},{7,5},{8,6},{9,7},{10,8},{11,9},{12,... | collective-permute-start | bytes 786440 | tf_op jit(solution)/shard_map/ppermute | solution.py:335
  61.5 1.2 %collective-permute-start.7 = (f32[24,128]{1,0:T(8,128)S(1)}, f32[24,128]{1,0:T(8,128)S(1)}, u32[]{:S(2)}, u32[]{:S(2)}) collective-permute-start(f32[24,128]{1,0:T(8,128)S(1)} %get-tuple-element.27), channel_id=1, source_target_pairs={{0,1},{1,0},{2,3},{3,2},{4,5},{5,4},{6,7},{7,6},{8,9},{9,8},{10,11... | collective-permute-start | bytes 36872 | tf_op jit(solution)/shard_map/ppermute | solution.py:381
  62.7 9.3 %collective-permute-start.10 = (f32[24,128]{1,0:T(8,128)S(1)}, f32[24,128]{1,0:T(8,128)S(1)}, u32[]{:S(2)}, u32[]{:S(2)}) collective-permute-start(f32[24,128]{1,0:T(8,128)S(1)} %add.66), channel_id=1, source_target_pairs={{0,12},{1,13},{2,14},{3,15},{4,8},{5,9},{6,10},{7,11},{8,4},{9,5},... | collective-permute-start | bytes 36872 | tf_op jit(solution)/shard_map/ppermute | solution.py:381
  68.2 3.8 %collective-permute-start.8 = (f32[24,128]{1,0:T(8,128)S(1)}, f32[24,128]{1,0:T(8,128)S(1)}, u32[]{:S(2)}, u32[]{:S(2)}) collective-permute-start(f32[24,128]{1,0:T(8,128)S(1)} %add.66), channel_id=1, source_target_pairs={{0,4},{1,5},{2,6},{3,7},{4,0},{5,1},{6,2},{7,3},{8,12},{9,13},{10,... | collective-permute-start | bytes 36872 | tf_op jit(solution)/shard_map/ppermute | solution.py:381
  68.3 4.6 %collective-permute-start.9 = (f32[24,128]{1,0:T(8,128)S(1)}, f32[24,128]{1,0:T(8,128)S(1)}, u32[]{:S(2)}, u32[]{:S(2)}) collective-permute-start(f32[24,128]{1,0:T(8,128)S(1)} %add.66), channel_id=1, source_target_pairs={{0,8},{1,9},{2,10},{3,11},{4,12},{5,13},{6,14},{7,15},{8,0},{9,1},... | collective-permute-start | bytes 36872 | tf_op jit(solution)/shard_map/ppermute | solution.py:381
  73.0 3.9 %collective-permute-start.11 = (f32[2,32,16,128]{3,2,1,0:T(8,128)S(1)}, f32[2,32,16,128]{3,2,1,0:T(8,128)S(1)}, u32[]{:S(2)}, u32[]{:S(2)}) collective-permute-start(f32[2,32,16,128]{3,2,1,0:T(8,128)S(1)} %pad_maximum_fusion.1), channel_id=1, source_target_pairs={{0,1},{1,0},{2,3},{3,2},{4,5},{5,4},{6,7},{7,6},{8,9},{9,8},{10,11... | collective-permute-start | bytes 1572872 | tf_op jit(solution)/shard_map/ppermute | solution.py:341
  73.2 3.7 %collective-permute-start.12 = (f32[24,128]{1,0:T(8,128)S(1)}, f32[24,128]{1,0:T(8,128)S(1)}, u32[]{:S(2)}, u32[]{:S(2)}) collective-permute-start(f32[24,128]{1,0:T(8,128)S(1)} %add_add_fusion.part), channel_id=1, source_target_pairs={{0,2},{1,3},{2,0},{3,1},{4,6},{5,7},{6,4},{7,5},{8,10},{9,11},{10,... | collective-permute-start | bytes 36872 | tf_op jit(solution)/shard_map/ppermute | solution.py:381

commit v6 on v5

--- a/solution.py
+++ b/solution.py
@@ -14,7 +14,6 @@
 SMEM = pltpu.MemorySpace.SMEM
 FULL = pl.BlockSpec(memory_space=VMEM)
 LIMIT = 30 * 1024 * 1024
-STEP = 2
 TINY = float(np.finfo(np.float32).tiny)
 
 
@@ -56,7 +55,6 @@
         low = row_y - high
         if flip:
             row_y = [part + pltpu.roll(part, in_rows, 1) for part in (high, low)]
-            row_y = [part if j == 0 else pltpu.roll(part, 2 * in_rows, 1) for part in row_y for j in range(2)]
         else:
             row_y = high + pltpu.roll(high, in_rows, 1) + pltpu.roll(low, 2 * in_rows, 1)
         row_x = placed_row(taps_ref[:, 2, :], lambda k: lax.rem(margin - order(k) + 2 * cols, 2 * cols), 2 * cols)
@@ -69,7 +67,7 @@
         for v in range(views):
             if flip:
                 for j, row in enumerate(row_y):
-                    wy[v, j * rows : (j + 1) * rows, :] = slanted(row[v : v + 1], rows)[:, : 4 * in_rows].astype(BF16)
+                    wy[v, j * rows : (j + 1) * rows, :] = slanted(row[v : v + 1], rows)[:, : 2 * in_rows].astype(BF16)
             else:
                 band = slanted(row_y[v : v + 1], out_rows)
                 wy[v * out_rows : (v + 1) * out_rows, :] = band[:, : 3 * in_rows].astype(BF16)
@@ -111,7 +109,7 @@
         pltpu.VMEM((views * 3 * rows, 15 * rows), BF16),
         pltpu.VMEM((views, 2 * cols, 2 * cols), BF16),
         pltpu.VMEM((views, 8 * planes, 24 * planes), BF16),
-        pltpu.VMEM((views, 4 * rows, 12 * rows), BF16),
+        pltpu.VMEM((views, 2 * rows, 6 * rows), BF16),
         pltpu.VMEM((views, 2 * cols, 2 * cols), BF16),
         pltpu.VMEM((views, planes, 3 * planes), BF16),
     ]
@@ -133,13 +131,21 @@
     return dot(wz, stacked([value[:, 8 * g : 8 * g + 8, :].reshape(planes * 8, cols) for g in range(2)]))
 
 
-def row_pairs(rows_ref, wx, wz, xs):
+def interleaved(*streams):
+    keyed = [((i + 0.5) / len(s), n, piece) for n, s in enumerate(streams) for i, piece in enumerate(s)]
+    for _, _, piece in sorted(keyed, key=lambda k: k[:2]):
+        piece()
+
+
+def along_x(rows_ref, wx, out):
     planes, height, lanes = rows_ref.shape
-    cols = lanes // 2
-    both = dot(rows_ref.reshape(planes * height, lanes), wx)
-    xs[...] = both[:, :cols] + both[:, cols:]
-    for y in range(0, height, 2):
-        yield y, dot(wz, stacked([xs[pl.ds(y + j, planes, stride=height), :] for j in range(2)]))
+    cols, part = lanes // 2, planes // 4
+
+    def piece(z):
+        both = dot(rows_ref[z : z + part].reshape(part * height, lanes), wx[...])
+        out[z * height : (z + part) * height, :] = both[:, :cols] + both[:, cols:]
+
+    return [functools.partial(piece, z) for z in range(0, planes, part)]
 
 
 def forward_rows(parity, far_before, near, own, far_after, wy, ys):
@@ -173,32 +179,51 @@
             out[:, at : at + 8, :] = result[:, j * cols : (j + 1) * cols].reshape(planes, 8, cols)
 
 
-def adjoint_views(blurred, before, raw, after, wy, wx, wz, ya, xs, acc):
-    _, planes, rows, cols = raw.shape
-
-    def quotient(v, z):
-        counts = jnp.concatenate([before[v, z], raw[v, z], after[v, z]], axis=0)
-        below = jnp.maximum(blurred[v, z], TINY)
-        inverse = pl.reciprocal(below, approx=True)
-        return counts * (inverse * (2.0 - below * inverse))
-
-    for v in range(STEP):
-        for z in range(0, planes, 4):
-            parts = []
-            for first in (z, z + 2):
-                parts += split(jnp.concatenate([quotient(v, first), quotient(v, first + 1)], axis=1))
-            both = dot(wy[v], jnp.concatenate(parts, axis=0))
-            high, low = split(both[: 2 * rows] + both[2 * rows :])
-            for j in range(4):
-                here = (slice(j // 2 * rows, (j // 2 + 1) * rows), slice(j % 2 * cols, (j % 2 + 1) * cols))
-                ya[v, z + j, :, :cols] = high[here]
-                ya[v, z + j, :, cols:] = low[here]
-    for pair in range(rows // 16):
-        chosen = slice(16 * pair, 16 * pair + 16)
-        found = [row_pairs(ya[v, :, chosen, :], wx[v], wz[v], xs.at[v]) for v in range(STEP)]
-        for results in zip(*found):
-            at = 8 * pair + results[0][0] // 2
-            acc[at] += sum(jnp.log(values) for _, values in results)
+def forward_pieces(ys, wx, wz, xs, out):
+    planes, height, lanes = ys.shape
+    cols = lanes // 2
+
+    def along_z(pair):
+        value = xs[pair].reshape(planes, 16, cols)
+        groups = [value[:, 8 * g : 8 * g + 8, :].reshape(planes * 8, cols) for g in range(2)]
+        result = dot(wz[...], stacked(groups))
+        for j in range(2):
+            at = 16 * pair + 8 * j
+            out[:, at : at + 8, :] = result[:, j * cols : (j + 1) * cols].reshape(planes, 8, cols)
+
+    pieces = []
+    for pair in range(height // 16):
+        pieces += along_x(ys.at[:, 16 * pair : 16 * pair + 16, :], wx, xs.at[pair])
+        pieces.append(functools.partial(along_z, pair))
+    return pieces
+
+
+def adjoint_rows(blurred, before, raw, after, wy, ya):
+    planes, rows, cols = raw.shape
+
+    def quotient(z):
+        counts = jnp.concatenate([before[z], raw[z], after[z]], axis=0)
+        return counts * pl.reciprocal(jnp.maximum(blurred[z], TINY), approx=True)
+
+    def piece(z):
+        high, low = split(jnp.concatenate([quotient(z), quotient(z + 1)], axis=1))
+        both = dot(wy[...], jnp.concatenate([high, low], axis=0))
+        high, low = split(both[:rows] + both[rows:])
+        for j in range(2):
+            ya[z + j, :, :cols] = high[:, j * cols : (j + 1) * cols]
+            ya[z + j, :, cols:] = low[:, j * cols : (j + 1) * cols]
+
+    return [functools.partial(piece, z) for z in range(0, planes, 2)]
+
+
+def adjoint_logs(first, ya, wx, wz, xs, acc):
+    planes, rows, lanes = ya.shape
+
+    def piece(y):
+        result = jnp.log(dot(wz[...], stacked([xs[pl.ds(y + j, planes, stride=rows), :] for j in range(2)])))
+        acc[y // 2] = result if first else acc[y // 2] + result
+
+    return along_x(ya, wx, xs) + [functools.partial(piece, y) for y in range(0, rows, 2)]
 
 
 def updated(current, exponents, out):
@@ -237,16 +262,19 @@
         sums[at + v : at + v + 1, :] = jnp.sum(total * wyx[v], axis=0, keepdims=True)
 
 
-def first_adjoint_kernel(wzs, current, blurred, before, raw, after, wy, wx, wz, wyx, known, out, sums, ya, xs, acc):
+def first_adjoint_kernel(
+    wzs, current, blurred, before, raw, after, wy, wx, wz, wyx, known, out, sums, ya, yb, xs, acc
+):
     views = wyx.shape[0]
-    acc[...] = jnp.zeros_like(acc)
-
-    def step(i):
-        chosen = pl.ds(STEP * i, STEP)
-        fields = [ref.at[chosen] for ref in (blurred, before, raw, after, wy, wx, wz)]
-        adjoint_views(*fields, ya, xs, acc)
-
-    each_step(views // STEP, step)
+
+    def rows_of(v):
+        fields = [ref.at[v] for ref in (blurred, before, raw, after, wy)] if v < views else None
+        return adjoint_rows(*fields, (ya, yb)[v % 2]) if fields else []
+
+    interleaved(rows_of(0))
+    for v in range(views):
+        logs = adjoint_logs(v == 0, (ya, yb)[v % 2], wx.at[v], wz.at[v], xs.at[v % 2], acc)
+        interleaved(logs, rows_of(v + 1))
     updated(current, acc[...] * (1.0 / views), out)
     sums[...] = known[...]
     weighted_sums(out, wzs, wyx, sums, 2 * sums.shape[0] // 3)
@@ -254,23 +282,22 @@
 
 def iteration_kernel(
     parity, far_before, near, own, far_after, before, raw, after, wy, wx, wz, wya, wxa, wza, part, rest,
-    out, ys, blurred, ya, xs, acc,
+    out, ys, xf, blurred_a, blurred_b, ya, yb, xs, acc,
 ):
     views = ys.shape[0]
-    acc[...] = jnp.zeros_like(acc)
+    blurred = (blurred_a, blurred_b)
     forward_rows(parity, far_before, near, own, far_after, wy, ys)
 
-    def step(i):
-        def one_view(j):
-            v = STEP * i + j
-            forward_view(ys.at[v], wx[v], wz[v], blurred.at[j])
-
-        each_step(STEP, one_view)
-        chosen = pl.ds(STEP * i, STEP)
-        fields = [ref.at[chosen] for ref in (before, raw, after, wya, wxa, wza)]
-        adjoint_views(blurred, *fields, ya, xs, acc)
-
-    each_step(views // STEP, step)
+    def forward_of(v):
+        return forward_pieces(ys.at[v], wx.at[v], wz.at[v], xf, blurred[v % 2]) if v < views else []
+
+    interleaved(forward_of(0))
+    for v in range(views):
+        fields = [ref.at[v] for ref in (before, raw, after, wya)]
+        y = (ya, yb)[v % 2]
+        steps = adjoint_rows(blurred[v % 2], *fields, y)
+        steps += adjoint_logs(v == 0, y, wxa.at[v], wza.at[v], xs.at[v % 2], acc)
+        interleaved(steps, forward_of(v + 1))
     sums = jnp.sum(part[...] + rest[...], axis=1, keepdims=True)
     space = sums.shape[0] // 3
     total, first, second = (sums[i * space : i * space + views] for i in range(3))
@@ -280,8 +307,9 @@
 
 def adjoint_scratch(planes, rows, cols):
     return [
-        pltpu.VMEM((STEP, planes, rows, 2 * cols), BF16),
-        pltpu.VMEM((STEP, planes * 16, cols), F32),
+        pltpu.VMEM((planes, rows, 2 * cols), BF16),
+        pltpu.VMEM((planes, rows, 2 * cols), BF16),
+        pltpu.VMEM((2, planes * 16, cols), F32),
         pltpu.VMEM((rows // 2, planes, 2 * cols), F32),
     ]
 
@@ -316,7 +344,9 @@
     slabs = [s.reshape(-1, cols) if i == 2 else s for i, s in enumerate(slabs)]
     scratch = [
         pltpu.VMEM((views, planes, 3 * rows, 2 * cols), BF16),
-        pltpu.VMEM((STEP, planes, 3 * rows, cols), F32),
+        pltpu.VMEM((3 * rows // 16, planes * 16, cols), F32),
+        pltpu.VMEM((planes, 3 * rows, cols), F32),
+        pltpu.VMEM((planes, 3 * rows, cols), F32),
     ]
     return call(
         iteration_kernel,
@@ -353,7 +383,7 @@
     views = raw.shape[0]
     planes, rows, cols = estimate.shape
     count = lax.axis_size("slab")
-    assert rows >= taps.shape[2] // 2 and count & (count - 1) == 0
+    assert 16 == rows >= taps.shape[2] // 2 and count & (count - 1) == 0
     up = [(i, i + 1) for i in range(count - 1)]
     down = [(j, i) for i, j in up]
     place = lax.axis_index("slab")

time: 89.4 us -> 88.4 us (0.989)
  Pallas kernels: 26.3 us -> 25.1 us
    pallas_call x4, Pallas kernels: 26.3 us -> 25.1 us  [call(): pl.pallas_call(kernel, out_shape=outs, in_specs=[pl.BlockSpec(memory_spac...]
  transfers between devices with their start and end apart: 13 -> 13, of which waited for: 6 -> 7; matrix products, arithmetic and copies ran while one was open for 3% -> 3% of each run, Pallas kernels for 10% -> 10%
where the time goes in v6:
time: 88.4 us; the launch traced here: 88 us
  starting transfers between devices  44.3 us (50%)
  Pallas kernels  25.1 us (28%)
  waiting for transfers between devices  15.2 us (17%)
  other arithmetic  1.56 us (2%)
  local copies, waits for them, and re-layouts  1.55 us (2%)
    ppermute x4, starting transfers between devices, two_slabs_away(): return (lax.ppermute(value, 'slab', up), lax.ppermute(value, 'slab', down))  34.9 us
    pallas_call x4, Pallas kernels, call(): pl.pallas_call(kernel, out_shape=outs, in_specs=[pl.BlockSpec(memory_spac...  25.1 us
    ppermute x5, waiting for transfers between devices, per_device(): lax.ppermute(sums, 'slab', [(i, i ^ d) for i in range(count)])  8.66 us
    ppermute x5, starting transfers between devices, per_device(): lax.ppermute(sums, 'slab', [(i, i ^ d) for i in range(count)])  6.47 us
    ppermute x4, waiting for transfers between devices, two_slabs_away(): return (lax.ppermute(value, 'slab', up), lax.ppermute(value, 'slab', down))  4.94 us
  transfers between devices with their start and end apart: 13, of which 7 were waited for; matrix products, arithmetic and copies ran while one was open for 3% of the time, Pallas kernels for 10%

profile of v6, /device:TPU:0, one launch (start us, length us, event | category | flops | bytes accessed | tf_op | source)
XLA Modules:
  0.0 88.0 jit_solution(2732825917181660905)
XLA Ops:
  0.0 5.0 %collective-permute-start = (f32[32,16,128]{2,1,0:T(8,128)}, f32[32,16,128]{2,1,0:T(8,128)S(1)}, u32[]{:S(2)}, u32[]{:S(2)}) collective-permute-start(f32[32,16,128]{2,1,0:T(8,128)} %param.3), channel_id=1, source_target_pairs={{0,2},{1,3},{2,4},{3,5},{4,6},{5,7},{6,8},{7,9},{8,10},{9,11},{10,... | collective-permute-start | bytes 786440 | tf_op jit(solution)/shard_map/ppermute | solution.py:365
  5.0 1.3 %collective-permute-start.1 = (f32[32,16,128]{2,1,0:T(8,128)}, f32[32,16,128]{2,1,0:T(8,128)S(1)}, u32[]{:S(2)}, u32[]{:S(2)}) collective-permute-start(f32[32,16,128]{2,1,0:T(8,128)} %param.3), channel_id=1, source_target_pairs={{2,0},{3,1},{4,2},{5,3},{6,4},{7,5},{8,6},{9,7},{10,8},{11,9},{12,... | collective-permute-start | bytes 786440 | tf_op jit(solution)/shard_map/ppermute | solution.py:365
  6.3 1.6 %collective-permute-start.3 = (f32[6,32,16,128]{3,2,1,0:T(8,128)}, f32[6,32,16,128]{3,2,1,0:T(8,128)S(1)}, u32[]{:S(2)}, u32[]{:S(2)}) collective-permute-start(f32[6,32,16,128]{3,2,1,0:T(8,128)} %raw.5), channel_id=1, source_target_pairs={{0,1},{1,2},{2,3},{3,4},{4,5},{5,6},{6,7},{7,8},{8,9},{9,10},{10,1... | collective-permute-start | bytes 4718600 | tf_op jit(solution)/shard_map/ppermute | solution.py:393
  7.9 1.3 %collective-permute-start.4 = (f32[6,32,16,128]{3,2,1,0:T(8,128)}, f32[6,32,16,128]{3,2,1,0:T(8,128)}, u32[]{:S(2)}, u32[]{:S(2)}) collective-permute-start(f32[6,32,16,128]{3,2,1,0:T(8,128)} %raw.5), channel_id=1, source_target_pairs={{1,0},{2,1},{3,2},{4,3},{5,4},{6,5},{7,6},{8,7},{9,8},{10,9},{11,1... | collective-permute-start | bytes 4718600 | tf_op jit(solution)/shard_map/ppermute | solution.py:394
  9.2 0.8 fusion.12
  10.1 0.1 fusion.11
  10.1 0.7 copy-done.1
  10.8 1.6 %weights.1 = (bf16[288,240]{1,0:T(8,128)(2,1)S(1)}, bf16[6,256,256]{2,1,0:T(8,128)(2,1)S(1)}, bf16[6,256,768]{2,1,0:T(8,128)(2,1)S(1)}, bf16[6,32,96]{2,1,0:T(8,...) custom-call(f32[6,3,31]{2,1,0:T(4,128)S(1)} %copy-done.1), custom_call_target="tpu_custom_call" | custom-call | flops 10000000 | bytes 10000000 | tf_op jit(solution)/shard_map/weights/pallas_call | solution.py:94
  12.5 0.1 multiply_reduce_fusion.2
  12.6 4.9 %collective-permute-done.far_before = f32[32,16,128]{2,1,0:T(8,128)S(1)} collective-permute-done((f32[32,16,128]{2,1,0:T(8,128)}, f32[32,16,128]{2,1,0:T(8,128)S(1)}, u32[]{:S(2)}, u32[]{:S(2)}) %collective-permute-start) | collective-permute-done | bytes 262176 | tf_op jit(solution)/shard_map/ppermute | solution.py:365
  17.5 1.0 %pad_maximum_fusion = f32[2,32,16,128]{3,2,1,0:T(8,128)S(1)} fusion(f32[1,32,16,128]{3,2,1,0:T(8,128)S(1)} %select_bitcast_fusion.1, f32[1,32,16,128]{3,2,1,0:T(8,128)} %bitcast.17), kind=kLoop, calls=%fused_computation | loop fusion | flops 131072 | bytes 1048576 | tf_op jit(solution)/shard_map/stack | solution.py:370
  18.5 0.1 collective-permute-start.2
  18.6 0.1 multiply_reduce_fusion
  18.7 0.1 multiply_reduce_fusion.1.wzs
  18.8 0.1 broadcast_multiply_fusion.wyx
  18.9 1.6 %collective-permute-done.2.near = f32[2,32,16,128]{3,2,1,0:T(8,128)S(1)} collective-permute-done((f32[2,32,16,128]{3,2,1,0:T(8,128)S(1)}, f32[2,32,16,128]{3,2,1,0:T(8,128)S(1)}, u32[]{:S(2)}, u32[]{:S(2)}) %collective-permute-start.2) | collective-permute-done | bytes 524320 | tf_op jit(solution)/shard_map/ppermute | solution.py:371
  20.5 6.8 %forward.1 = (f32[6,32,48,128]{3,2,1,0:T(8,128)S(1)}, f32[24,128]{1,0:T(8,128)S(1)}) custom-call(s32[1]{0:T(128)} %bitcast.parity, f32[6,32]{1,0:T(8,128)S(1)} %multiply_reduce_fusion.1.wzs, f32[32,16,128]{2,1,0:T(8,128)S(1)} %collective-permute-done.far_before, f32[2,32,16,128]{3,2,1,0:T(8,128)S(1)} %collective-permute-done.2.near, ...), custom_call_target="tpu_custom_call" | custom-call | flops 10000000000 | bytes 10000000 | tf_op jit(solution)/shard_map/forward/pallas_call | solution.py:94
  27.4 0.0 collective-permute-done.3.before
  27.4 4.7 %adjoint.1 = (f32[512,128]{1,0:T(8,128)S(1)}, f32[24,128]{1,0:T(8,128)S(1)}) custom-call(f32[6,32]{1,0:T(8,128)S(1)} %multiply_reduce_fusion.1.wzs, f32[512,128]{1,0:T(8,128)S(1)} %bitcast.19, f32[6,32,48,128]{3,2,1,0:T(8,128)S(1)} %get-tuple-element.21.blurred, f32[6,32,16,128]{3,2,1,0:T(8,128)S(1)} %collective-permute-done.3.before, ...), custom_call_target="tpu_custom_call" | custom-call | flops 10000000000 | bytes 10000000 | tf_op jit(solution)/shard_map/adjoint/pallas_call | solution.py:94
  32.1 27.1 %collective-permute-start.5 = (f32[32,16,128]{2,1,0:T(8,128)S(1)}, f32[32,16,128]{2,1,0:T(8,128)S(1)}, u32[]{:S(2)}, u32[]{:S(2)}) collective-permute-start(f32[32,16,128]{2,1,0:T(8,128)S(1)} %bitcast.20), channel_id=1, source_target_pairs={{0,2},{1,3},{2,4},{3,5},{4,6},{5,7},{6,8},{7,9},{8,10},{9,11},{10,... | collective-permute-start | bytes 786440 | tf_op jit(solution)/shard_map/ppermute | solution.py:365
  59.2 1.5 %collective-permute-start.6 = (f32[32,16,128]{2,1,0:T(8,128)S(1)}, f32[32,16,128]{2,1,0:T(8,128)S(1)}, u32[]{:S(2)}, u32[]{:S(2)}) collective-permute-start(f32[32,16,128]{2,1,0:T(8,128)S(1)} %bitcast.21), channel_id=1, source_target_pairs={{2,0},{3,1},{4,2},{5,3},{6,4},{7,5},{8,6},{9,7},{10,8},{11,9},{12,... | collective-permute-start | bytes 786440 | tf_op jit(solution)/shard_map/ppermute | solution.py:365
  60.7 0.1 collective-permute-start.7
  60.8 1.2 %collective-permute-done.7 = f32[24,128]{1,0:T(8,128)S(1)} collective-permute-done((f32[24,128]{1,0:T(8,128)S(1)}, f32[24,128]{1,0:T(8,128)S(1)}, u32[]{:S(2)}, u32[]{:S(2)}) %collective-permute-start.7) | collective-permute-done | bytes 12320 | tf_op jit(solution)/shard_map/ppermute | solution.py:411
  61.9 5.5 %collective-permute-start.10 = (f32[24,128]{1,0:T(8,128)S(1)}, f32[24,128]{1,0:T(8,128)S(1)}, u32[]{:S(2)}, u32[]{:S(2)}) collective-permute-start(f32[24,128]{1,0:T(8,128)S(1)} %add.66), channel_id=1, source_target_pairs={{0,12},{1,13},{2,14},{3,15},{4,8},{5,9},{6,10},{7,11},{8,4},{9,5},... | collective-permute-start | bytes 36872 | tf_op jit(solution)/shard_map/ppermute | solution.py:411
  67.5 0.6 collective-permute-start.9
  68.0 3.0 %collective-permute-done.10 = f32[24,128]{1,0:T(8,128)S(1)} collective-permute-done((f32[24,128]{1,0:T(8,128)S(1)}, f32[24,128]{1,0:T(8,128)S(1)}, u32[]{:S(2)}, u32[]{:S(2)}) %collective-permute-start.10) | collective-permute-done | bytes 12320 | tf_op jit(solution)/shard_map/ppermute | solution.py:411
  71.0 0.1 collective-permute-done.8
  71.1 0.9 %collective-permute-done.9 = f32[24,128]{1,0:T(8,128)S(1)} collective-permute-done((f32[24,128]{1,0:T(8,128)S(1)}, f32[24,128]{1,0:T(8,128)S(1)}, u32[]{:S(2)}, u32[]{:S(2)}) %collective-permute-start.9) | collective-permute-done | bytes 12320 | tf_op jit(solution)/shard_map/ppermute | solution.py:411
  72.2 0.1 collective-permute-start.11
  72.2 0.3 collective-permute-start.12
  72.6 3.5 %collective-permute-done.12.rest = f32[24,128]{1,0:T(8,128)S(1)} collective-permute-done((f32[24,128]{1,0:T(8,128)S(1)}, f32[24,128]{1,0:T(8,128)S(1)}, u32[]{:S(2)}, u32[]{:S(2)}) %collective-permute-start.12) | collective-permute-done | bytes 12320 | tf_op jit(solution)/shard_map/ppermute | solution.py:411
  76.0 12.0 %iteration.1 = f32[512,128]{1,0:T(8,128)} custom-call(s32[1]{0:T(128)} %bitcast.parity, f32[32,16,128]{2,1,0:T(8,128)S(1)} %collective-permute-done.5.far_before, f32[2,32,16,128]{3,2,1,0:T(8,128)S(1)} %collective-permute-done.11.near, f32[512,128]{1,0:T(8,128)S(1)} %get-tuple-element.26.own, f32[32,16,128]{2,1,0:T(8,128)S(1)} %collective-permute-done.6.far_after, ...), custom_call_target="tpu_custom_call" | custom-call | flops 20000000000 | bytes 10000000 | tf_op jit(solution)/shard_map/iteration/pallas_call | solution.py:94
  (21 shorter events, 0.2 us)
Async XLA Ops:
  0.0 20.5 %copy-start = (f32[32,16,128]{2,1,0:T(8,128)S(1)}, f32[32,16,128]{2,1,0:T(8,128)}, u32[]{:S(2)}) copy-start(f32[32,16,128]{2,1,0:T(8,128)} %param.3) | copy-start | bytes 786436
  0.0 17.5 %collective-permute-start = (f32[32,16,128]{2,1,0:T(8,128)}, f32[32,16,128]{2,1,0:T(8,128)S(1)}, u32[]{:S(2)}, u32[]{:S(2)}) collective-permute-start(f32[32,16,128]{2,1,0:T(8,128)} %param.3), channel_id=1, source_target_pairs={{0,2},{1,3},{2,4},{3,5},{4,6},{5,7},{6,8},{7,9},{8,10},{9,11},{10,... | collective-permute-start | bytes 786440 | tf_op jit(solution)/shard_map/ppermute | solution.py:365
  5.0 12.5 %collective-permute-start.1 = (f32[32,16,128]{2,1,0:T(8,128)}, f32[32,16,128]{2,1,0:T(8,128)S(1)}, u32[]{:S(2)}, u32[]{:S(2)}) collective-permute-start(f32[32,16,128]{2,1,0:T(8,128)} %param.3), channel_id=1, source_target_pairs={{2,0},{3,1},{4,2},{5,3},{6,4},{7,5},{8,6},{9,7},{10,8},{11,9},{12,... | collective-permute-start | bytes 786440 | tf_op jit(solution)/shard_map/ppermute | solution.py:365
  6.3 21.0 %collective-permute-start.3 = (f32[6,32,16,128]{3,2,1,0:T(8,128)}, f32[6,32,16,128]{3,2,1,0:T(8,128)S(1)}, u32[]{:S(2)}, u32[]{:S(2)}) collective-permute-start(f32[6,32,16,128]{3,2,1,0:T(8,128)} %raw.5), channel_id=1, source_target_pairs={{0,1},{1,2},{2,3},{3,4},{4,5},{5,6},{6,7},{7,8},{8,9},{9,10},{10,1... | collective-permute-start | bytes 4718600 | tf_op jit(solution)/shard_map/ppermute | solution.py:393
  7.9 19.5 %collective-permute-start.4 = (f32[6,32,16,128]{3,2,1,0:T(8,128)}, f32[6,32,16,128]{3,2,1,0:T(8,128)}, u32[]{:S(2)}, u32[]{:S(2)}) collective-permute-start(f32[6,32,16,128]{3,2,1,0:T(8,128)} %raw.5), channel_id=1, source_target_pairs={{1,0},{2,1},{3,2},{4,3},{5,4},{6,5},{7,6},{8,7},{9,8},{10,9},{11,1... | collective-permute-start | bytes 4718600 | tf_op jit(solution)/shard_map/ppermute | solution.py:394
  10.1 0.7 copy-start.1
  10.8 9.7 %copy-start.2 = (f32[6,32,16,128]{3,2,1,0:T(8,128)S(1)}, f32[6,32,16,128]{3,2,1,0:T(8,128)}, u32[]{:S(2)}) copy-start(f32[6,32,16,128]{3,2,1,0:T(8,128)} %raw.5) | copy-start | bytes 4718596
  18.5 2.0 %collective-permute-start.2 = (f32[2,32,16,128]{3,2,1,0:T(8,128)S(1)}, f32[2,32,16,128]{3,2,1,0:T(8,128)S(1)}, u32[]{:S(2)}, u32[]{:S(2)}) collective-permute-start(f32[2,32,16,128]{3,2,1,0:T(8,128)S(1)} %pad_maximum_fusion), channel_id=1, source_target_pairs={{0,1},{1,0},{2,3},{3,2},{4,5},{5,4},{6,7},{7,6},{8,9},{9,8},{10,11... | collective-permute-start | bytes 1572872 | tf_op jit(solution)/shard_map/ppermute | solution.py:371
  32.1 40.0 %collective-permute-start.5 = (f32[32,16,128]{2,1,0:T(8,128)S(1)}, f32[32,16,128]{2,1,0:T(8,128)S(1)}, u32[]{:S(2)}, u32[]{:S(2)}) collective-permute-start(f32[32,16,128]{2,1,0:T(8,128)S(1)} %bitcast.20), channel_id=1, source_target_pairs={{0,2},{1,3},{2,4},{3,5},{4,6},{5,7},{6,8},{7,9},{8,10},{9,11},{10,... | collective-permute-start | bytes 786440 | tf_op jit(solution)/shard_map/ppermute | solution.py:365
  59.2 12.9 %collective-permute-start.6 = (f32[32,16,128]{2,1,0:T(8,128)S(1)}, f32[32,16,128]{2,1,0:T(8,128)S(1)}, u32[]{:S(2)}, u32[]{:S(2)}) collective-permute-start(f32[32,16,128]{2,1,0:T(8,128)S(1)} %bitcast.21), channel_id=1, source_target_pairs={{2,0},{3,1},{4,2},{5,3},{6,4},{7,5},{8,6},{9,7},{10,8},{11,9},{12,... | collective-permute-start | bytes 786440 | tf_op jit(solution)/shard_map/ppermute | solution.py:365
  60.7 1.2 %collective-permute-start.7 = (f32[24,128]{1,0:T(8,128)S(1)}, f32[24,128]{1,0:T(8,128)S(1)}, u32[]{:S(2)}, u32[]{:S(2)}) collective-permute-start(f32[24,128]{1,0:T(8,128)S(1)} %get-tuple-element.27), channel_id=1, source_target_pairs={{0,1},{1,0},{2,3},{3,2},{4,5},{5,4},{6,7},{7,6},{8,9},{9,8},{10,11... | collective-permute-start | bytes 36872 | tf_op jit(solution)/shard_map/ppermute | solution.py:411
  61.9 9.1 %collective-permute-start.10 = (f32[24,128]{1,0:T(8,128)S(1)}, f32[24,128]{1,0:T(8,128)S(1)}, u32[]{:S(2)}, u32[]{:S(2)}) collective-permute-start(f32[24,128]{1,0:T(8,128)S(1)} %add.66), channel_id=1, source_target_pairs={{0,12},{1,13},{2,14},{3,15},{4,8},{5,9},{6,10},{7,11},{8,4},{9,5},... | collective-permute-start | bytes 36872 | tf_op jit(solution)/shard_map/ppermute | solution.py:411
  67.5 3.7 %collective-permute-start.8 = (f32[24,128]{1,0:T(8,128)S(1)}, f32[24,128]{1,0:T(8,128)S(1)}, u32[]{:S(2)}, u32[]{:S(2)}) collective-permute-start(f32[24,128]{1,0:T(8,128)S(1)} %add.66), channel_id=1, source_target_pairs={{0,4},{1,5},{2,6},{3,7},{4,0},{5,1},{6,2},{7,3},{8,12},{9,13},{10,... | collective-permute-start | bytes 36872 | tf_op jit(solution)/shard_map/ppermute | solution.py:411
  67.5 4.6 %collective-permute-start.9 = (f32[24,128]{1,0:T(8,128)S(1)}, f32[24,128]{1,0:T(8,128)S(1)}, u32[]{:S(2)}, u32[]{:S(2)}) collective-permute-start(f32[24,128]{1,0:T(8,128)S(1)} %add.66), channel_id=1, source_target_pairs={{0,8},{1,9},{2,10},{3,11},{4,12},{5,13},{6,14},{7,15},{8,0},{9,1},... | collective-permute-start | bytes 36872 | tf_op jit(solution)/shard_map/ppermute | solution.py:411
  72.2 3.8 %collective-permute-start.11 = (f32[2,32,16,128]{3,2,1,0:T(8,128)S(1)}, f32[2,32,16,128]{3,2,1,0:T(8,128)S(1)}, u32[]{:S(2)}, u32[]{:S(2)}) collective-permute-start(f32[2,32,16,128]{3,2,1,0:T(8,128)S(1)} %pad_maximum_fusion.1), channel_id=1, source_target_pairs={{0,1},{1,0},{2,3},{3,2},{4,5},{5,4},{6,7},{7,6},{8,9},{9,8},{10,11... | collective-permute-start | bytes 1572872 | tf_op jit(solution)/shard_map/ppermute | solution.py:371
  72.2 3.8 %collective-permute-start.12 = (f32[24,128]{1,0:T(8,128)S(1)}, f32[24,128]{1,0:T(8,128)S(1)}, u32[]{:S(2)}, u32[]{:S(2)}) collective-permute-start(f32[24,128]{1,0:T(8,128)S(1)} %add_add_fusion.part), channel_id=1, source_target_pairs={{0,2},{1,3},{2,0},{3,1},{4,6},{5,7},{6,4},{7,5},{8,10},{9,11},{10,... | collective-permute-start | bytes 36872 | tf_op jit(solution)/shard_map/ppermute | solution.py:411

commit v7 on v6

--- a/solution.py
+++ b/solution.py
@@ -156,17 +156,21 @@
 
     def plane(z):
         return jnp.concatenate(
-            [far_before[z], near[1 - side, z], own[z * rows : (z + 1) * rows, :], near[side, z], far_after[z]], axis=0
+            [far_before[z], near[1 - side, z], own[pl.ds(z * rows, rows), :], near[side, z], far_after[z]], axis=0
         )
 
-    for z in range(0, planes, 2):
-        result = dot(wy[...], stacked([plane(z), plane(z + 1)]))
-        high, low = split(result)
-        for j in range(2):
-            for v in range(views):
-                there = (slice(v * height, (v + 1) * height), slice(j * cols, (j + 1) * cols))
-                ys[v, z + j, :, :cols] = high[there]
-                ys[v, z + j, :, cols:] = low[there]
+    def some_planes(start, _):
+        for z in range(0, 8, 2):
+            at = 8 * start + z
+            high, low = split(dot(wy[...], stacked([plane(at), plane(at + 1)])))
+            for j in range(2):
+                for v in range(views):
+                    there = (slice(v * height, (v + 1) * height), slice(j * cols, (j + 1) * cols))
+                    ys[v, at + j, :, :cols] = high[there]
+                    ys[v, at + j, :, cols:] = low[there]
+        return 0
+
+    lax.fori_loop(0, planes // 8, some_planes, 0)
 
 
 def forward_view(ys, wx, wz, out):
@@ -179,25 +183,6 @@
             out[:, at : at + 8, :] = result[:, j * cols : (j + 1) * cols].reshape(planes, 8, cols)
 
 
-def forward_pieces(ys, wx, wz, xs, out):
-    planes, height, lanes = ys.shape
-    cols = lanes // 2
-
-    def along_z(pair):
-        value = xs[pair].reshape(planes, 16, cols)
-        groups = [value[:, 8 * g : 8 * g + 8, :].reshape(planes * 8, cols) for g in range(2)]
-        result = dot(wz[...], stacked(groups))
-        for j in range(2):
-            at = 16 * pair + 8 * j
-            out[:, at : at + 8, :] = result[:, j * cols : (j + 1) * cols].reshape(planes, 8, cols)
-
-    pieces = []
-    for pair in range(height // 16):
-        pieces += along_x(ys.at[:, 16 * pair : 16 * pair + 16, :], wx, xs.at[pair])
-        pieces.append(functools.partial(along_z, pair))
-    return pieces
-
-
 def adjoint_rows(blurred, before, raw, after, wy, ya):
     planes, rows, cols = raw.shape
 
@@ -262,10 +247,8 @@
         sums[at + v : at + v + 1, :] = jnp.sum(total * wyx[v], axis=0, keepdims=True)
 
 
-def first_adjoint_kernel(
-    wzs, current, blurred, before, raw, after, wy, wx, wz, wyx, known, out, sums, ya, yb, xs, acc
-):
-    views = wyx.shape[0]
+def adjoint_all(blurred, before, raw, after, wy, wx, wz, ya, yb, xs, acc):
+    views = raw.shape[0]
 
     def rows_of(v):
         fields = [ref.at[v] for ref in (blurred, before, raw, after, wy)] if v < views else None
@@ -275,29 +258,25 @@
     for v in range(views):
         logs = adjoint_logs(v == 0, (ya, yb)[v % 2], wx.at[v], wz.at[v], xs.at[v % 2], acc)
         interleaved(logs, rows_of(v + 1))
-    updated(current, acc[...] * (1.0 / views), out)
+
+
+def first_adjoint_kernel(
+    wzs, current, blurred, before, raw, after, wy, wx, wz, wyx, known, out, sums, ya, yb, xs, acc
+):
+    adjoint_all(blurred, before, raw, after, wy, wx, wz, ya, yb, xs, acc)
+    updated(current, acc[...] * (1.0 / raw.shape[0]), out)
     sums[...] = known[...]
     weighted_sums(out, wzs, wyx, sums, 2 * sums.shape[0] // 3)
 
 
 def iteration_kernel(
     parity, far_before, near, own, far_after, before, raw, after, wy, wx, wz, wya, wxa, wza, part, rest,
-    out, ys, xf, blurred_a, blurred_b, ya, yb, xs, acc,
+    out, ys, blurred, ya, yb, xs, acc,
 ):
     views = ys.shape[0]
-    blurred = (blurred_a, blurred_b)
     forward_rows(parity, far_before, near, own, far_after, wy, ys)
-
-    def forward_of(v):
-        return forward_pieces(ys.at[v], wx.at[v], wz.at[v], xf, blurred[v % 2]) if v < views else []
-
-    interleaved(forward_of(0))
-    for v in range(views):
-        fields = [ref.at[v] for ref in (before, raw, after, wya)]
-        y = (ya, yb)[v % 2]
-        steps = adjoint_rows(blurred[v % 2], *fields, y)
-        steps += adjoint_logs(v == 0, y, wxa.at[v], wza.at[v], xs.at[v % 2], acc)
-        interleaved(steps, forward_of(v + 1))
+    each_step(views, lambda v: forward_view(ys.at[v], wx[v], wz[v], blurred.at[v]))
+    adjoint_all(blurred, before, raw, after, wya, wxa, wza, ya, yb, xs, acc)
     sums = jnp.sum(part[...] + rest[...], axis=1, keepdims=True)
     space = sums.shape[0] // 3
     total, first, second = (sums[i * space : i * space + views] for i in range(3))
@@ -344,9 +323,7 @@
     slabs = [s.reshape(-1, cols) if i == 2 else s for i, s in enumerate(slabs)]
     scratch = [
         pltpu.VMEM((views, planes, 3 * rows, 2 * cols), BF16),
-        pltpu.VMEM((3 * rows // 16, planes * 16, cols), F32),
-        pltpu.VMEM((planes, 3 * rows, cols), F32),
-        pltpu.VMEM((planes, 3 * rows, cols), F32),
+        pltpu.VMEM((views, planes, 3 * rows, cols), F32),
     ]
     return call(
         iteration_kernel,

time: 88.4 us -> 87.8 us (level)
  no operation moved by 1% of the time
where the time goes in v7:
time: 87.8 us; the launch traced here: 87.4 us
  starting transfers between devices  43.9 us (50%)
  Pallas kernels  24.9 us (28%)
  waiting for transfers between devices  15.2 us (17%)
  other arithmetic  1.56 us (2%)
  local copies, waits for them, and re-layouts  1.55 us (2%)
    ppermute x4, starting transfers between devices, two_slabs_away(): return (lax.ppermute(value, 'slab', up), lax.ppermute(value, 'slab', down))  34.4 us
    pallas_call x4, Pallas kernels, call(): pl.pallas_call(kernel, out_shape=outs, in_specs=[pl.BlockSpec(memory_spac...  24.9 us
    ppermute x5, waiting for transfers between devices, per_device(): lax.ppermute(sums, 'slab', [(i, i ^ d) for i in range(count)])  8.71 us
    ppermute x5, starting transfers between devices, per_device(): lax.ppermute(sums, 'slab', [(i, i ^ d) for i in range(count)])  6.36 us
    ppermute x4, waiting for transfers between devices, two_slabs_away(): return (lax.ppermute(value, 'slab', up), lax.ppermute(value, 'slab', down))  4.94 us
  transfers between devices with their start and end apart: 13, of which 7 were waited for; matrix products, arithmetic and copies ran while one was open for 3% of the time, Pallas kernels for 10%

profile of v7, /device:TPU:0, one launch (start us, length us, event | category | flops | bytes accessed | tf_op | source)
XLA Modules:
  0.0 87.4 jit_solution(2268602206511343335)
XLA Ops:
  0.0 5.0 %collective-permute-start = (f32[32,16,128]{2,1,0:T(8,128)}, f32[32,16,128]{2,1,0:T(8,128)S(1)}, u32[]{:S(2)}, u32[]{:S(2)}) collective-permute-start(f32[32,16,128]{2,1,0:T(8,128)} %param.3), channel_id=1, source_target_pairs={{0,2},{1,3},{2,4},{3,5},{4,6},{5,7},{6,8},{7,9},{8,10},{9,11},{10,... | collective-permute-start | bytes 786440 | tf_op jit(solution)/shard_map/ppermute | solution.py:342
  5.0 1.3 %collective-permute-start.1 = (f32[32,16,128]{2,1,0:T(8,128)}, f32[32,16,128]{2,1,0:T(8,128)S(1)}, u32[]{:S(2)}, u32[]{:S(2)}) collective-permute-start(f32[32,16,128]{2,1,0:T(8,128)} %param.3), channel_id=1, source_target_pairs={{2,0},{3,1},{4,2},{5,3},{6,4},{7,5},{8,6},{9,7},{10,8},{11,9},{12,... | collective-permute-start | bytes 786440 | tf_op jit(solution)/shard_map/ppermute | solution.py:342
  6.3 1.6 %collective-permute-start.3 = (f32[6,32,16,128]{3,2,1,0:T(8,128)}, f32[6,32,16,128]{3,2,1,0:T(8,128)S(1)}, u32[]{:S(2)}, u32[]{:S(2)}) collective-permute-start(f32[6,32,16,128]{3,2,1,0:T(8,128)} %raw.5), channel_id=1, source_target_pairs={{0,1},{1,2},{2,3},{3,4},{4,5},{5,6},{6,7},{7,8},{8,9},{9,10},{10,1... | collective-permute-start | bytes 4718600 | tf_op jit(solution)/shard_map/ppermute | solution.py:370
  7.9 1.3 %collective-permute-start.4 = (f32[6,32,16,128]{3,2,1,0:T(8,128)}, f32[6,32,16,128]{3,2,1,0:T(8,128)}, u32[]{:S(2)}, u32[]{:S(2)}) collective-permute-start(f32[6,32,16,128]{3,2,1,0:T(8,128)} %raw.5), channel_id=1, source_target_pairs={{1,0},{2,1},{3,2},{4,3},{5,4},{6,5},{7,6},{8,7},{9,8},{10,9},{11,1... | collective-permute-start | bytes 4718600 | tf_op jit(solution)/shard_map/ppermute | solution.py:371
  9.2 0.8 fusion.12
  10.1 0.1 fusion.11
  10.1 0.7 copy-done.1
  10.8 1.6 %weights.1 = (bf16[288,240]{1,0:T(8,128)(2,1)S(1)}, bf16[6,256,256]{2,1,0:T(8,128)(2,1)S(1)}, bf16[6,256,768]{2,1,0:T(8,128)(2,1)S(1)}, bf16[6,32,96]{2,1,0:T(8,...) custom-call(f32[6,3,31]{2,1,0:T(4,128)S(1)} %copy-done.1), custom_call_target="tpu_custom_call" | custom-call | flops 10000000 | bytes 10000000 | tf_op jit(solution)/shard_map/weights/pallas_call | solution.py:94
  12.5 0.1 multiply_reduce_fusion.2
  12.6 4.9 %collective-permute-done.far_before = f32[32,16,128]{2,1,0:T(8,128)S(1)} collective-permute-done((f32[32,16,128]{2,1,0:T(8,128)}, f32[32,16,128]{2,1,0:T(8,128)S(1)}, u32[]{:S(2)}, u32[]{:S(2)}) %collective-permute-start) | collective-permute-done | bytes 262176 | tf_op jit(solution)/shard_map/ppermute | solution.py:342
  17.5 0.0 collective-permute-done.1.far_after
  17.5 1.0 %pad_maximum_fusion = f32[2,32,16,128]{3,2,1,0:T(8,128)S(1)} fusion(f32[1,32,16,128]{3,2,1,0:T(8,128)S(1)} %select_bitcast_fusion.1, f32[1,32,16,128]{3,2,1,0:T(8,128)} %bitcast.17), kind=kLoop, calls=%fused_computation | loop fusion | flops 131072 | bytes 1048576 | tf_op jit(solution)/shard_map/stack | solution.py:347
  18.5 0.1 collective-permute-start.2
  18.6 0.1 multiply_reduce_fusion
  18.7 0.1 multiply_reduce_fusion.1.wzs
  18.8 0.1 broadcast_multiply_fusion.wyx
  18.9 1.6 %collective-permute-done.2.near = f32[2,32,16,128]{3,2,1,0:T(8,128)S(1)} collective-permute-done((f32[2,32,16,128]{3,2,1,0:T(8,128)S(1)}, f32[2,32,16,128]{3,2,1,0:T(8,128)S(1)}, u32[]{:S(2)}, u32[]{:S(2)}) %collective-permute-start.2) | collective-permute-done | bytes 524320 | tf_op jit(solution)/shard_map/ppermute | solution.py:348
  20.5 7.2 %forward.1 = (f32[6,32,48,128]{3,2,1,0:T(8,128)S(1)}, f32[24,128]{1,0:T(8,128)S(1)}) custom-call(s32[1]{0:T(128)} %bitcast.parity, f32[6,32]{1,0:T(8,128)S(1)} %multiply_reduce_fusion.1.wzs, f32[32,16,128]{2,1,0:T(8,128)S(1)} %collective-permute-done.far_before, f32[2,32,16,128]{3,2,1,0:T(8,128)S(1)} %collective-permute-done.2.near, ...), custom_call_target="tpu_custom_call" | custom-call | flops 10000000000 | bytes 10000000 | tf_op jit(solution)/shard_map/forward/pallas_call | solution.py:94
  27.7 4.7 %adjoint.1 = (f32[512,128]{1,0:T(8,128)S(1)}, f32[24,128]{1,0:T(8,128)S(1)}) custom-call(f32[6,32]{1,0:T(8,128)S(1)} %multiply_reduce_fusion.1.wzs, f32[512,128]{1,0:T(8,128)S(1)} %bitcast.19, f32[6,32,48,128]{3,2,1,0:T(8,128)S(1)} %get-tuple-element.21.blurred, f32[6,32,16,128]{3,2,1,0:T(8,128)S(1)} %collective-permute-done.3.before, ...), custom_call_target="tpu_custom_call" | custom-call | flops 10000000000 | bytes 10000000 | tf_op jit(solution)/shard_map/adjoint/pallas_call | solution.py:94
  32.4 26.8 %collective-permute-start.5 = (f32[32,16,128]{2,1,0:T(8,128)S(1)}, f32[32,16,128]{2,1,0:T(8,128)S(1)}, u32[]{:S(2)}, u32[]{:S(2)}) collective-permute-start(f32[32,16,128]{2,1,0:T(8,128)S(1)} %bitcast.20), channel_id=1, source_target_pairs={{0,2},{1,3},{2,4},{3,5},{4,6},{5,7},{6,8},{7,9},{8,10},{9,11},{10,... | collective-permute-start | bytes 786440 | tf_op jit(solution)/shard_map/ppermute | solution.py:342
  59.2 1.3 %collective-permute-start.6 = (f32[32,16,128]{2,1,0:T(8,128)S(1)}, f32[32,16,128]{2,1,0:T(8,128)S(1)}, u32[]{:S(2)}, u32[]{:S(2)}) collective-permute-start(f32[32,16,128]{2,1,0:T(8,128)S(1)} %bitcast.21), channel_id=1, source_target_pairs={{2,0},{3,1},{4,2},{5,3},{6,4},{7,5},{8,6},{9,7},{10,8},{11,9},{12,... | collective-permute-start | bytes 786440 | tf_op jit(solution)/shard_map/ppermute | solution.py:342
  60.5 0.1 collective-permute-start.7
  60.6 1.2 %collective-permute-done.7 = f32[24,128]{1,0:T(8,128)S(1)} collective-permute-done((f32[24,128]{1,0:T(8,128)S(1)}, f32[24,128]{1,0:T(8,128)S(1)}, u32[]{:S(2)}, u32[]{:S(2)}) %collective-permute-start.7) | collective-permute-done | bytes 12320 | tf_op jit(solution)/shard_map/ppermute | solution.py:388
  61.7 5.5 %collective-permute-start.10 = (f32[24,128]{1,0:T(8,128)S(1)}, f32[24,128]{1,0:T(8,128)S(1)}, u32[]{:S(2)}, u32[]{:S(2)}) collective-permute-start(f32[24,128]{1,0:T(8,128)S(1)} %add.66), channel_id=1, source_target_pairs={{0,12},{1,13},{2,14},{3,15},{4,8},{5,9},{6,10},{7,11},{8,4},{9,5},... | collective-permute-start | bytes 36872 | tf_op jit(solution)/shard_map/ppermute | solution.py:388
  67.3 0.6 collective-permute-start.9
  67.8 3.2 %collective-permute-done.10 = f32[24,128]{1,0:T(8,128)S(1)} collective-permute-done((f32[24,128]{1,0:T(8,128)S(1)}, f32[24,128]{1,0:T(8,128)S(1)}, u32[]{:S(2)}, u32[]{:S(2)}) %collective-permute-start.10) | collective-permute-done | bytes 12320 | tf_op jit(solution)/shard_map/ppermute | solution.py:388
  71.0 0.1 collective-permute-done.8
  71.0 0.8 collective-permute-done.9
  72.0 0.2 collective-permute-start.11
  72.2 0.2 collective-permute-start.12
  72.4 3.5 %collective-permute-done.12.rest = f32[24,128]{1,0:T(8,128)S(1)} collective-permute-done((f32[24,128]{1,0:T(8,128)S(1)}, f32[24,128]{1,0:T(8,128)S(1)}, u32[]{:S(2)}, u32[]{:S(2)}) %collective-permute-start.12) | collective-permute-done | bytes 12320 | tf_op jit(solution)/shard_map/ppermute | solution.py:388
  75.9 11.5 %iteration.1 = f32[512,128]{1,0:T(8,128)} custom-call(s32[1]{0:T(128)} %bitcast.parity, f32[32,16,128]{2,1,0:T(8,128)S(1)} %collective-permute-done.5.far_before, f32[2,32,16,128]{3,2,1,0:T(8,128)S(1)} %collective-permute-done.11.near, f32[512,128]{1,0:T(8,128)S(1)} %get-tuple-element.26.own, f32[32,16,128]{2,1,0:T(8,128)S(1)} %collective-permute-done.6.far_after, ...), custom_call_target="tpu_custom_call" | custom-call | flops 20000000000 | bytes 10000000 | tf_op jit(solution)/shard_map/iteration/pallas_call | solution.py:94
  (21 shorter events, 0.2 us)
Async XLA Ops:
  0.0 20.5 %copy-start = (f32[32,16,128]{2,1,0:T(8,128)S(1)}, f32[32,16,128]{2,1,0:T(8,128)}, u32[]{:S(2)}) copy-start(f32[32,16,128]{2,1,0:T(8,128)} %param.3) | copy-start | bytes 786436
  0.0 17.5 %collective-permute-start = (f32[32,16,128]{2,1,0:T(8,128)}, f32[32,16,128]{2,1,0:T(8,128)S(1)}, u32[]{:S(2)}, u32[]{:S(2)}) collective-permute-start(f32[32,16,128]{2,1,0:T(8,128)} %param.3), channel_id=1, source_target_pairs={{0,2},{1,3},{2,4},{3,5},{4,6},{5,7},{6,8},{7,9},{8,10},{9,11},{10,... | collective-permute-start | bytes 786440 | tf_op jit(solution)/shard_map/ppermute | solution.py:342
  5.0 12.5 %collective-permute-start.1 = (f32[32,16,128]{2,1,0:T(8,128)}, f32[32,16,128]{2,1,0:T(8,128)S(1)}, u32[]{:S(2)}, u32[]{:S(2)}) collective-permute-start(f32[32,16,128]{2,1,0:T(8,128)} %param.3), channel_id=1, source_target_pairs={{2,0},{3,1},{4,2},{5,3},{6,4},{7,5},{8,6},{9,7},{10,8},{11,9},{12,... | collective-permute-start | bytes 786440 | tf_op jit(solution)/shard_map/ppermute | solution.py:342
  6.3 21.4 %collective-permute-start.3 = (f32[6,32,16,128]{3,2,1,0:T(8,128)}, f32[6,32,16,128]{3,2,1,0:T(8,128)S(1)}, u32[]{:S(2)}, u32[]{:S(2)}) collective-permute-start(f32[6,32,16,128]{3,2,1,0:T(8,128)} %raw.5), channel_id=1, source_target_pairs={{0,1},{1,2},{2,3},{3,4},{4,5},{5,6},{6,7},{7,8},{8,9},{9,10},{10,1... | collective-permute-start | bytes 4718600 | tf_op jit(solution)/shard_map/ppermute | solution.py:370
  7.9 19.8 %collective-permute-start.4 = (f32[6,32,16,128]{3,2,1,0:T(8,128)}, f32[6,32,16,128]{3,2,1,0:T(8,128)}, u32[]{:S(2)}, u32[]{:S(2)}) collective-permute-start(f32[6,32,16,128]{3,2,1,0:T(8,128)} %raw.5), channel_id=1, source_target_pairs={{1,0},{2,1},{3,2},{4,3},{5,4},{6,5},{7,6},{8,7},{9,8},{10,9},{11,1... | collective-permute-start | bytes 4718600 | tf_op jit(solution)/shard_map/ppermute | solution.py:371
  10.1 0.7 copy-start.1
  10.8 9.7 %copy-start.2 = (f32[6,32,16,128]{3,2,1,0:T(8,128)S(1)}, f32[6,32,16,128]{3,2,1,0:T(8,128)}, u32[]{:S(2)}) copy-start(f32[6,32,16,128]{3,2,1,0:T(8,128)} %raw.5) | copy-start | bytes 4718596
  18.5 2.0 %collective-permute-start.2 = (f32[2,32,16,128]{3,2,1,0:T(8,128)S(1)}, f32[2,32,16,128]{3,2,1,0:T(8,128)S(1)}, u32[]{:S(2)}, u32[]{:S(2)}) collective-permute-start(f32[2,32,16,128]{3,2,1,0:T(8,128)S(1)} %pad_maximum_fusion), channel_id=1, source_target_pairs={{0,1},{1,0},{2,3},{3,2},{4,5},{5,4},{6,7},{7,6},{8,9},{9,8},{10,11... | collective-permute-start | bytes 1572872 | tf_op jit(solution)/shard_map/ppermute | solution.py:348
  32.4 39.5 %collective-permute-start.5 = (f32[32,16,128]{2,1,0:T(8,128)S(1)}, f32[32,16,128]{2,1,0:T(8,128)S(1)}, u32[]{:S(2)}, u32[]{:S(2)}) collective-permute-start(f32[32,16,128]{2,1,0:T(8,128)S(1)} %bitcast.20), channel_id=1, source_target_pairs={{0,2},{1,3},{2,4},{3,5},{4,6},{5,7},{6,8},{7,9},{8,10},{9,11},{10,... | collective-permute-start | bytes 786440 | tf_op jit(solution)/shard_map/ppermute | solution.py:342
  59.2 12.7 %collective-permute-start.6 = (f32[32,16,128]{2,1,0:T(8,128)S(1)}, f32[32,16,128]{2,1,0:T(8,128)S(1)}, u32[]{:S(2)}, u32[]{:S(2)}) collective-permute-start(f32[32,16,128]{2,1,0:T(8,128)S(1)} %bitcast.21), channel_id=1, source_target_pairs={{2,0},{3,1},{4,2},{5,3},{6,4},{7,5},{8,6},{9,7},{10,8},{11,9},{12,... | collective-permute-start | bytes 786440 | tf_op jit(solution)/shard_map/ppermute | solution.py:342
  60.5 1.2 %collective-permute-start.7 = (f32[24,128]{1,0:T(8,128)S(1)}, f32[24,128]{1,0:T(8,128)S(1)}, u32[]{:S(2)}, u32[]{:S(2)}) collective-permute-start(f32[24,128]{1,0:T(8,128)S(1)} %get-tuple-element.27), channel_id=1, source_target_pairs={{0,1},{1,0},{2,3},{3,2},{4,5},{5,4},{6,7},{7,6},{8,9},{9,8},{10,11... | collective-permute-start | bytes 36872 | tf_op jit(solution)/shard_map/ppermute | solution.py:388
  61.7 9.2 %collective-permute-start.10 = (f32[24,128]{1,0:T(8,128)S(1)}, f32[24,128]{1,0:T(8,128)S(1)}, u32[]{:S(2)}, u32[]{:S(2)}) collective-permute-start(f32[24,128]{1,0:T(8,128)S(1)} %add.66), channel_id=1, source_target_pairs={{0,12},{1,13},{2,14},{3,15},{4,8},{5,9},{6,10},{7,11},{8,4},{9,5},... | collective-permute-start | bytes 36872 | tf_op jit(solution)/shard_map/ppermute | solution.py:388
  67.3 3.8 %collective-permute-start.8 = (f32[24,128]{1,0:T(8,128)S(1)}, f32[24,128]{1,0:T(8,128)S(1)}, u32[]{:S(2)}, u32[]{:S(2)}) collective-permute-start(f32[24,128]{1,0:T(8,128)S(1)} %add.66), channel_id=1, source_target_pairs={{0,4},{1,5},{2,6},{3,7},{4,0},{5,1},{6,2},{7,3},{8,12},{9,13},{10,... | collective-permute-start | bytes 36872 | tf_op jit(solution)/shard_map/ppermute | solution.py:388
  67.3 4.6 %collective-permute-start.9 = (f32[24,128]{1,0:T(8,128)S(1)}, f32[24,128]{1,0:T(8,128)S(1)}, u32[]{:S(2)}, u32[]{:S(2)}) collective-permute-start(f32[24,128]{1,0:T(8,128)S(1)} %add.66), channel_id=1, source_target_pairs={{0,8},{1,9},{2,10},{3,11},{4,12},{5,13},{6,14},{7,15},{8,0},{9,1},... | collective-permute-start | bytes 36872 | tf_op jit(solution)/shard_map/ppermute | solution.py:388
  72.0 3.9 %collective-permute-start.11 = (f32[2,32,16,128]{3,2,1,0:T(8,128)S(1)}, f32[2,32,16,128]{3,2,1,0:T(8,128)S(1)}, u32[]{:S(2)}, u32[]{:S(2)}) collective-permute-start(f32[2,32,16,128]{3,2,1,0:T(8,128)S(1)} %pad_maximum_fusion.1), channel_id=1, source_target_pairs={{0,1},{1,0},{2,3},{3,2},{4,5},{5,4},{6,7},{7,6},{8,9},{9,8},{10,11... | collective-permute-start | bytes 1572872 | tf_op jit(solution)/shard_map/ppermute | solution.py:348
  72.2 3.7 %collective-permute-start.12 = (f32[24,128]{1,0:T(8,128)S(1)}, f32[24,128]{1,0:T(8,128)S(1)}, u32[]{:S(2)}, u32[]{:S(2)}) collective-permute-start(f32[24,128]{1,0:T(8,128)S(1)} %add_add_fusion.part), channel_id=1, source_target_pairs={{0,2},{1,3},{2,0},{3,1},{4,6},{5,7},{6,4},{7,5},{8,10},{9,11},{10,... | collective-permute-start | bytes 36872 | tf_op jit(solution)/shard_map/ppermute | solution.py:388

commit v8 on v7

--- a/solution.py
+++ b/solution.py
@@ -14,6 +14,7 @@
 SMEM = pltpu.MemorySpace.SMEM
 FULL = pl.BlockSpec(memory_space=VMEM)
 LIMIT = 30 * 1024 * 1024
+WIDE = 4
 TINY = float(np.finfo(np.float32).tiny)
 
 
@@ -125,12 +126,6 @@
     return jnp.concatenate(columns, axis=1)
 
 
-def two_groups(rows_ref, wx, wz, planes, cols):
-    both = dot(rows_ref.reshape(planes * 16, 2 * cols), wx)
-    value = (both[:, :cols] + both[:, cols:]).reshape(planes, 16, cols)
-    return dot(wz, stacked([value[:, 8 * g : 8 * g + 8, :].reshape(planes * 8, cols) for g in range(2)]))
-
-
 def interleaved(*streams):
     keyed = [((i + 0.5) / len(s), n, piece) for n, s in enumerate(streams) for i, piece in enumerate(s)]
     for _, _, piece in sorted(keyed, key=lambda k: k[:2]):
@@ -159,28 +154,27 @@
             [far_before[z], near[1 - side, z], own[pl.ds(z * rows, rows), :], near[side, z], far_after[z]], axis=0
         )
 
-    def some_planes(start, _):
-        for z in range(0, 8, 2):
-            at = 8 * start + z
-            high, low = split(dot(wy[...], stacked([plane(at), plane(at + 1)])))
-            for j in range(2):
-                for v in range(views):
-                    there = (slice(v * height, (v + 1) * height), slice(j * cols, (j + 1) * cols))
-                    ys[v, at + j, :, :cols] = high[there]
-                    ys[v, at + j, :, cols:] = low[there]
-        return 0
-
-    lax.fori_loop(0, planes // 8, some_planes, 0)
+    for z in range(0, planes, 2):
+        high, low = split(dot(wy[...], stacked([plane(z), plane(z + 1)])))
+        for j in range(2):
+            for v in range(views):
+                there = (slice(v * height, (v + 1) * height), slice(j * cols, (j + 1) * cols))
+                ys[v, z + j, :, :cols] = high[there]
+                ys[v, z + j, :, cols:] = low[there]
 
 
 def forward_view(ys, wx, wz, out):
     planes, height, lanes = ys.shape
     cols = lanes // 2
+    groups = []
     for pair in range(height // 16):
-        result = two_groups(ys[:, 16 * pair : 16 * pair + 16, :], wx, wz, planes, cols)
-        for j in range(2):
-            at = 16 * pair + 8 * j
-            out[:, at : at + 8, :] = result[:, j * cols : (j + 1) * cols].reshape(planes, 8, cols)
+        rows_in = ys[:, 16 * pair : 16 * pair + 16, :].reshape(planes * 16, lanes)
+        both = dot(rows_in, wx)
+        value = (both[:, :cols] + both[:, cols:]).reshape(planes, 16, cols)
+        groups += [value[:, 8 * g : 8 * g + 8, :].reshape(planes * 8, cols) for g in range(2)]
+    result = dot(wz, stacked(groups))
+    for g in range(len(groups)):
+        out[:, 8 * g : 8 * g + 8, :] = result[:, g * cols : (g + 1) * cols].reshape(planes, 8, cols)
 
 
 def adjoint_rows(blurred, before, raw, after, wy, ya):
@@ -191,33 +185,34 @@
         return counts * pl.reciprocal(jnp.maximum(blurred[z], TINY), approx=True)
 
     def piece(z):
-        high, low = split(jnp.concatenate([quotient(z), quotient(z + 1)], axis=1))
+        high, low = split(jnp.concatenate([quotient(z + j) for j in range(WIDE)], axis=1))
         both = dot(wy[...], jnp.concatenate([high, low], axis=0))
         high, low = split(both[:rows] + both[rows:])
-        for j in range(2):
+        for j in range(WIDE):
             ya[z + j, :, :cols] = high[:, j * cols : (j + 1) * cols]
             ya[z + j, :, cols:] = low[:, j * cols : (j + 1) * cols]
 
-    return [functools.partial(piece, z) for z in range(0, planes, 2)]
+    return [functools.partial(piece, z) for z in range(0, planes, WIDE)]
 
 
 def adjoint_logs(first, ya, wx, wz, xs, acc):
     planes, rows, lanes = ya.shape
 
     def piece(y):
-        result = jnp.log(dot(wz[...], stacked([xs[pl.ds(y + j, planes, stride=rows), :] for j in range(2)])))
-        acc[y // 2] = result if first else acc[y // 2] + result
-
-    return along_x(ya, wx, xs) + [functools.partial(piece, y) for y in range(0, rows, 2)]
+        values = stacked([xs[pl.ds(y + j, planes, stride=rows), :] for j in range(WIDE)])
+        result = jnp.log(dot(wz[...], values))
+        acc[y // WIDE] = result if first else acc[y // WIDE] + result
+
+    return along_x(ya, wx, xs) + [functools.partial(piece, y) for y in range(0, rows, WIDE)]
 
 
 def updated(current, exponents, out):
-    pairs, planes, lanes = exponents.shape
-    cols = lanes // 2
-    for y in range(2 * pairs):
-        at = pl.ds(y, planes, stride=2 * pairs)
-        half = slice((y % 2) * cols, (y % 2 + 1) * cols)
-        out[at, :] = current[at, :] * jnp.exp(exponents[y // 2, :, half])
+    count, planes, lanes = exponents.shape
+    cols, rows = lanes // WIDE, count * WIDE
+    for y in range(rows):
+        at = pl.ds(y, planes, stride=rows)
+        part = slice((y % WIDE) * cols, (y % WIDE + 1) * cols)
+        out[at, :] = current[at, :] * jnp.exp(exponents[y // WIDE, :, part])
 
 
 def each_step(steps, body):
@@ -289,7 +284,7 @@
         pltpu.VMEM((planes, rows, 2 * cols), BF16),
         pltpu.VMEM((planes, rows, 2 * cols), BF16),
         pltpu.VMEM((2, planes * 16, cols), F32),
-        pltpu.VMEM((rows // 2, planes, 2 * cols), F32),
+        pltpu.VMEM((rows // WIDE, planes, WIDE * cols), F32),
     ]
 
 

time: 87.8 us -> 87.5 us (level)
  no operation moved by 1% of the time
where the time goes in v8:
time: 87.5 us; the launch traced here: 87.1 us
  starting transfers between devices  44.3 us (51%)
  Pallas kernels  24.4 us (28%)
  waiting for transfers between devices  15.2 us (17%)
  other arithmetic  1.56 us (2%)
  local copies, waits for them, and re-layouts  1.55 us (2%)
    ppermute x4, starting transfers between devices, two_slabs_away(): return (lax.ppermute(value, 'slab', up), lax.ppermute(value, 'slab', down))  34.8 us
    pallas_call x4, Pallas kernels, call(): pl.pallas_call(kernel, out_shape=outs, in_specs=[pl.BlockSpec(memory_spac...  24.4 us
    ppermute x5, waiting for transfers between devices, per_device(): lax.ppermute(sums, 'slab', [(i, i ^ d) for i in range(count)])  8.63 us
    ppermute x5, starting transfers between devices, per_device(): lax.ppermute(sums, 'slab', [(i, i ^ d) for i in range(count)])  6.48 us
    ppermute x4, waiting for transfers between devices, two_slabs_away(): return (lax.ppermute(value, 'slab', up), lax.ppermute(value, 'slab', down))  4.94 us
  transfers between devices with their start and end apart: 13, of which 7 were waited for; matrix products, arithmetic and copies ran while one was open for 3% of the time, Pallas kernels for 10%

profile of v8, /device:TPU:0, one launch (start us, length us, event | category | flops | bytes accessed | tf_op | source)
XLA Modules:
  0.0 87.1 jit_solution(7959006083857596597)
XLA Ops:
  0.0 5.0 %collective-permute-start = (f32[32,16,128]{2,1,0:T(8,128)}, f32[32,16,128]{2,1,0:T(8,128)S(1)}, u32[]{:S(2)}, u32[]{:S(2)}) collective-permute-start(f32[32,16,128]{2,1,0:T(8,128)} %param.3), channel_id=1, source_target_pairs={{0,2},{1,3},{2,4},{3,5},{4,6},{5,7},{6,8},{7,9},{8,10},{9,11},{10,... | collective-permute-start | bytes 786440 | tf_op jit(solution)/shard_map/ppermute | solution.py:337
  5.0 1.3 %collective-permute-start.1 = (f32[32,16,128]{2,1,0:T(8,128)}, f32[32,16,128]{2,1,0:T(8,128)S(1)}, u32[]{:S(2)}, u32[]{:S(2)}) collective-permute-start(f32[32,16,128]{2,1,0:T(8,128)} %param.3), channel_id=1, source_target_pairs={{2,0},{3,1},{4,2},{5,3},{6,4},{7,5},{8,6},{9,7},{10,8},{11,9},{12,... | collective-permute-start | bytes 786440 | tf_op jit(solution)/shard_map/ppermute | solution.py:337
  6.3 1.6 %collective-permute-start.3 = (f32[6,32,16,128]{3,2,1,0:T(8,128)}, f32[6,32,16,128]{3,2,1,0:T(8,128)S(1)}, u32[]{:S(2)}, u32[]{:S(2)}) collective-permute-start(f32[6,32,16,128]{3,2,1,0:T(8,128)} %raw.5), channel_id=1, source_target_pairs={{0,1},{1,2},{2,3},{3,4},{4,5},{5,6},{6,7},{7,8},{8,9},{9,10},{10,1... | collective-permute-start | bytes 4718600 | tf_op jit(solution)/shard_map/ppermute | solution.py:365
  7.9 1.3 %collective-permute-start.4 = (f32[6,32,16,128]{3,2,1,0:T(8,128)}, f32[6,32,16,128]{3,2,1,0:T(8,128)}, u32[]{:S(2)}, u32[]{:S(2)}) collective-permute-start(f32[6,32,16,128]{3,2,1,0:T(8,128)} %raw.5), channel_id=1, source_target_pairs={{1,0},{2,1},{3,2},{4,3},{5,4},{6,5},{7,6},{8,7},{9,8},{10,9},{11,1... | collective-permute-start | bytes 4718600 | tf_op jit(solution)/shard_map/ppermute | solution.py:366
  9.2 0.8 fusion.12
  10.1 0.1 fusion.11
  10.1 0.7 copy-done.1
  10.8 1.6 %weights.1 = (bf16[288,240]{1,0:T(8,128)(2,1)S(1)}, bf16[6,256,256]{2,1,0:T(8,128)(2,1)S(1)}, bf16[6,256,768]{2,1,0:T(8,128)(2,1)S(1)}, bf16[6,32,96]{2,1,0:T(8,...) custom-call(f32[6,3,31]{2,1,0:T(4,128)S(1)} %copy-done.1), custom_call_target="tpu_custom_call" | custom-call | flops 10000000 | bytes 10000000 | tf_op jit(solution)/shard_map/weights/pallas_call | solution.py:95
  12.5 0.1 multiply_reduce_fusion.2
  12.6 4.9 %collective-permute-done.far_before = f32[32,16,128]{2,1,0:T(8,128)S(1)} collective-permute-done((f32[32,16,128]{2,1,0:T(8,128)}, f32[32,16,128]{2,1,0:T(8,128)S(1)}, u32[]{:S(2)}, u32[]{:S(2)}) %collective-permute-start) | collective-permute-done | bytes 262176 | tf_op jit(solution)/shard_map/ppermute | solution.py:337
  17.5 1.0 %pad_maximum_fusion = f32[2,32,16,128]{3,2,1,0:T(8,128)S(1)} fusion(f32[1,32,16,128]{3,2,1,0:T(8,128)S(1)} %select_bitcast_fusion.1, f32[1,32,16,128]{3,2,1,0:T(8,128)} %bitcast.17), kind=kLoop, calls=%fused_computation | loop fusion | flops 131072 | bytes 1048576 | tf_op jit(solution)/shard_map/stack | solution.py:342
  18.5 0.1 collective-permute-start.2
  18.6 0.1 multiply_reduce_fusion
  18.7 0.1 multiply_reduce_fusion.1.wzs
  18.8 0.1 broadcast_multiply_fusion.wyx
  18.9 1.6 %collective-permute-done.2.near = f32[2,32,16,128]{3,2,1,0:T(8,128)S(1)} collective-permute-done((f32[2,32,16,128]{3,2,1,0:T(8,128)S(1)}, f32[2,32,16,128]{3,2,1,0:T(8,128)S(1)}, u32[]{:S(2)}, u32[]{:S(2)}) %collective-permute-start.2) | collective-permute-done | bytes 524320 | tf_op jit(solution)/shard_map/ppermute | solution.py:343
  20.5 6.9 %forward.1 = (f32[6,32,48,128]{3,2,1,0:T(8,128)S(1)}, f32[24,128]{1,0:T(8,128)S(1)}) custom-call(s32[1]{0:T(128)} %bitcast.parity, f32[6,32]{1,0:T(8,128)S(1)} %multiply_reduce_fusion.1.wzs, f32[32,16,128]{2,1,0:T(8,128)S(1)} %collective-permute-done.far_before, f32[2,32,16,128]{3,2,1,0:T(8,128)S(1)} %collective-permute-done.2.near, ...), custom_call_target="tpu_custom_call" | custom-call | flops 10000000000 | bytes 10000000 | tf_op jit(solution)/shard_map/forward/pallas_call | solution.py:95
  27.4 0.0 collective-permute-done.3.before
  27.5 4.6 %adjoint.1 = (f32[512,128]{1,0:T(8,128)S(1)}, f32[24,128]{1,0:T(8,128)S(1)}) custom-call(f32[6,32]{1,0:T(8,128)S(1)} %multiply_reduce_fusion.1.wzs, f32[512,128]{1,0:T(8,128)S(1)} %bitcast.19, f32[6,32,48,128]{3,2,1,0:T(8,128)S(1)} %get-tuple-element.21.blurred, f32[6,32,16,128]{3,2,1,0:T(8,128)S(1)} %collective-permute-done.3.before, ...), custom_call_target="tpu_custom_call" | custom-call | flops 10000000000 | bytes 10000000 | tf_op jit(solution)/shard_map/adjoint/pallas_call | solution.py:95
  32.1 27.0 %collective-permute-start.5 = (f32[32,16,128]{2,1,0:T(8,128)S(1)}, f32[32,16,128]{2,1,0:T(8,128)S(1)}, u32[]{:S(2)}, u32[]{:S(2)}) collective-permute-start(f32[32,16,128]{2,1,0:T(8,128)S(1)} %bitcast.20), channel_id=1, source_target_pairs={{0,2},{1,3},{2,4},{3,5},{4,6},{5,7},{6,8},{7,9},{8,10},{9,11},{10,... | collective-permute-start | bytes 786440 | tf_op jit(solution)/shard_map/ppermute | solution.py:337
  59.1 1.5 %collective-permute-start.6 = (f32[32,16,128]{2,1,0:T(8,128)S(1)}, f32[32,16,128]{2,1,0:T(8,128)S(1)}, u32[]{:S(2)}, u32[]{:S(2)}) collective-permute-start(f32[32,16,128]{2,1,0:T(8,128)S(1)} %bitcast.21), channel_id=1, source_target_pairs={{2,0},{3,1},{4,2},{5,3},{6,4},{7,5},{8,6},{9,7},{10,8},{11,9},{12,... | collective-permute-start | bytes 786440 | tf_op jit(solution)/shard_map/ppermute | solution.py:337
  60.6 0.1 collective-permute-start.7
  60.7 1.2 %collective-permute-done.7 = f32[24,128]{1,0:T(8,128)S(1)} collective-permute-done((f32[24,128]{1,0:T(8,128)S(1)}, f32[24,128]{1,0:T(8,128)S(1)}, u32[]{:S(2)}, u32[]{:S(2)}) %collective-permute-start.7) | collective-permute-done | bytes 12320 | tf_op jit(solution)/shard_map/ppermute | solution.py:383
  61.9 5.5 %collective-permute-start.10 = (f32[24,128]{1,0:T(8,128)S(1)}, f32[24,128]{1,0:T(8,128)S(1)}, u32[]{:S(2)}, u32[]{:S(2)}) collective-permute-start(f32[24,128]{1,0:T(8,128)S(1)} %add.66), channel_id=1, source_target_pairs={{0,12},{1,13},{2,14},{3,15},{4,8},{5,9},{6,10},{7,11},{8,4},{9,5},... | collective-permute-start | bytes 36872 | tf_op jit(solution)/shard_map/ppermute | solution.py:383
  67.4 0.6 collective-permute-start.9
  68.0 3.0 %collective-permute-done.10 = f32[24,128]{1,0:T(8,128)S(1)} collective-permute-done((f32[24,128]{1,0:T(8,128)S(1)}, f32[24,128]{1,0:T(8,128)S(1)}, u32[]{:S(2)}, u32[]{:S(2)}) %collective-permute-start.10) | collective-permute-done | bytes 12320 | tf_op jit(solution)/shard_map/ppermute | solution.py:383
  70.9 0.1 collective-permute-done.8
  71.1 0.9 %collective-permute-done.9 = f32[24,128]{1,0:T(8,128)S(1)} collective-permute-done((f32[24,128]{1,0:T(8,128)S(1)}, f32[24,128]{1,0:T(8,128)S(1)}, u32[]{:S(2)}, u32[]{:S(2)}) %collective-permute-start.9) | collective-permute-done | bytes 12320 | tf_op jit(solution)/shard_map/ppermute | solution.py:383
  72.1 0.1 collective-permute-start.11
  72.2 0.3 collective-permute-start.12
  72.5 3.4 %collective-permute-done.12.rest = f32[24,128]{1,0:T(8,128)S(1)} collective-permute-done((f32[24,128]{1,0:T(8,128)S(1)}, f32[24,128]{1,0:T(8,128)S(1)}, u32[]{:S(2)}, u32[]{:S(2)}) %collective-permute-start.12) | collective-permute-done | bytes 12320 | tf_op jit(solution)/shard_map/ppermute | solution.py:383
  75.9 11.2 %iteration.1 = f32[512,128]{1,0:T(8,128)} custom-call(s32[1]{0:T(128)} %bitcast.parity, f32[32,16,128]{2,1,0:T(8,128)S(1)} %collective-permute-done.5.far_before, f32[2,32,16,128]{3,2,1,0:T(8,128)S(1)} %collective-permute-done.11.near, f32[512,128]{1,0:T(8,128)S(1)} %get-tuple-element.26.own, f32[32,16,128]{2,1,0:T(8,128)S(1)} %collective-permute-done.6.far_after, ...), custom_call_target="tpu_custom_call" | custom-call | flops 20000000000 | bytes 10000000 | tf_op jit(solution)/shard_map/iteration/pallas_call | solution.py:95
  (21 shorter events, 0.2 us)
Async XLA Ops:
  0.0 20.5 %copy-start = (f32[32,16,128]{2,1,0:T(8,128)S(1)}, f32[32,16,128]{2,1,0:T(8,128)}, u32[]{:S(2)}) copy-start(f32[32,16,128]{2,1,0:T(8,128)} %param.3) | copy-start | bytes 786436
  0.0 17.5 %collective-permute-start = (f32[32,16,128]{2,1,0:T(8,128)}, f32[32,16,128]{2,1,0:T(8,128)S(1)}, u32[]{:S(2)}, u32[]{:S(2)}) collective-permute-start(f32[32,16,128]{2,1,0:T(8,128)} %param.3), channel_id=1, source_target_pairs={{0,2},{1,3},{2,4},{3,5},{4,6},{5,7},{6,8},{7,9},{8,10},{9,11},{10,... | collective-permute-start | bytes 786440 | tf_op jit(solution)/shard_map/ppermute | solution.py:337
  5.0 12.5 %collective-permute-start.1 = (f32[32,16,128]{2,1,0:T(8,128)}, f32[32,16,128]{2,1,0:T(8,128)S(1)}, u32[]{:S(2)}, u32[]{:S(2)}) collective-permute-start(f32[32,16,128]{2,1,0:T(8,128)} %param.3), channel_id=1, source_target_pairs={{2,0},{3,1},{4,2},{5,3},{6,4},{7,5},{8,6},{9,7},{10,8},{11,9},{12,... | collective-permute-start | bytes 786440 | tf_op jit(solution)/shard_map/ppermute | solution.py:337
  6.3 21.1 %collective-permute-start.3 = (f32[6,32,16,128]{3,2,1,0:T(8,128)}, f32[6,32,16,128]{3,2,1,0:T(8,128)S(1)}, u32[]{:S(2)}, u32[]{:S(2)}) collective-permute-start(f32[6,32,16,128]{3,2,1,0:T(8,128)} %raw.5), channel_id=1, source_target_pairs={{0,1},{1,2},{2,3},{3,4},{4,5},{5,6},{6,7},{7,8},{8,9},{9,10},{10,1... | collective-permute-start | bytes 4718600 | tf_op jit(solution)/shard_map/ppermute | solution.py:365
  7.9 19.6 %collective-permute-start.4 = (f32[6,32,16,128]{3,2,1,0:T(8,128)}, f32[6,32,16,128]{3,2,1,0:T(8,128)}, u32[]{:S(2)}, u32[]{:S(2)}) collective-permute-start(f32[6,32,16,128]{3,2,1,0:T(8,128)} %raw.5), channel_id=1, source_target_pairs={{1,0},{2,1},{3,2},{4,3},{5,4},{6,5},{7,6},{8,7},{9,8},{10,9},{11,1... | collective-permute-start | bytes 4718600 | tf_op jit(solution)/shard_map/ppermute | solution.py:366
  10.1 0.7 copy-start.1
  10.8 9.7 %copy-start.2 = (f32[6,32,16,128]{3,2,1,0:T(8,128)S(1)}, f32[6,32,16,128]{3,2,1,0:T(8,128)}, u32[]{:S(2)}) copy-start(f32[6,32,16,128]{3,2,1,0:T(8,128)} %raw.5) | copy-start | bytes 4718596
  18.5 2.0 %collective-permute-start.2 = (f32[2,32,16,128]{3,2,1,0:T(8,128)S(1)}, f32[2,32,16,128]{3,2,1,0:T(8,128)S(1)}, u32[]{:S(2)}, u32[]{:S(2)}) collective-permute-start(f32[2,32,16,128]{3,2,1,0:T(8,128)S(1)} %pad_maximum_fusion), channel_id=1, source_target_pairs={{0,1},{1,0},{2,3},{3,2},{4,5},{5,4},{6,7},{7,6},{8,9},{9,8},{10,11... | collective-permute-start | bytes 1572872 | tf_op jit(solution)/shard_map/ppermute | solution.py:343
  32.1 39.9 %collective-permute-start.5 = (f32[32,16,128]{2,1,0:T(8,128)S(1)}, f32[32,16,128]{2,1,0:T(8,128)S(1)}, u32[]{:S(2)}, u32[]{:S(2)}) collective-permute-start(f32[32,16,128]{2,1,0:T(8,128)S(1)} %bitcast.20), channel_id=1, source_target_pairs={{0,2},{1,3},{2,4},{3,5},{4,6},{5,7},{6,8},{7,9},{8,10},{9,11},{10,... | collective-permute-start | bytes 786440 | tf_op jit(solution)/shard_map/ppermute | solution.py:337
  59.1 12.9 %collective-permute-start.6 = (f32[32,16,128]{2,1,0:T(8,128)S(1)}, f32[32,16,128]{2,1,0:T(8,128)S(1)}, u32[]{:S(2)}, u32[]{:S(2)}) collective-permute-start(f32[32,16,128]{2,1,0:T(8,128)S(1)} %bitcast.21), channel_id=1, source_target_pairs={{2,0},{3,1},{4,2},{5,3},{6,4},{7,5},{8,6},{9,7},{10,8},{11,9},{12,... | collective-permute-start | bytes 786440 | tf_op jit(solution)/shard_map/ppermute | solution.py:337
  60.6 1.2 %collective-permute-start.7 = (f32[24,128]{1,0:T(8,128)S(1)}, f32[24,128]{1,0:T(8,128)S(1)}, u32[]{:S(2)}, u32[]{:S(2)}) collective-permute-start(f32[24,128]{1,0:T(8,128)S(1)} %get-tuple-element.27), channel_id=1, source_target_pairs={{0,1},{1,0},{2,3},{3,2},{4,5},{5,4},{6,7},{7,6},{8,9},{9,8},{10,11... | collective-permute-start | bytes 36872 | tf_op jit(solution)/shard_map/ppermute | solution.py:383
  61.9 9.1 %collective-permute-start.10 = (f32[24,128]{1,0:T(8,128)S(1)}, f32[24,128]{1,0:T(8,128)S(1)}, u32[]{:S(2)}, u32[]{:S(2)}) collective-permute-start(f32[24,128]{1,0:T(8,128)S(1)} %add.66), channel_id=1, source_target_pairs={{0,12},{1,13},{2,14},{3,15},{4,8},{5,9},{6,10},{7,11},{8,4},{9,5},... | collective-permute-start | bytes 36872 | tf_op jit(solution)/shard_map/ppermute | solution.py:383
  67.4 3.7 %collective-permute-start.8 = (f32[24,128]{1,0:T(8,128)S(1)}, f32[24,128]{1,0:T(8,128)S(1)}, u32[]{:S(2)}, u32[]{:S(2)}) collective-permute-start(f32[24,128]{1,0:T(8,128)S(1)} %add.66), channel_id=1, source_target_pairs={{0,4},{1,5},{2,6},{3,7},{4,0},{5,1},{6,2},{7,3},{8,12},{9,13},{10,... | collective-permute-start | bytes 36872 | tf_op jit(solution)/shard_map/ppermute | solution.py:383
  67.4 4.6 %collective-permute-start.9 = (f32[24,128]{1,0:T(8,128)S(1)}, f32[24,128]{1,0:T(8,128)S(1)}, u32[]{:S(2)}, u32[]{:S(2)}) collective-permute-start(f32[24,128]{1,0:T(8,128)S(1)} %add.66), channel_id=1, source_target_pairs={{0,8},{1,9},{2,10},{3,11},{4,12},{5,13},{6,14},{7,15},{8,0},{9,1},... | collective-permute-start | bytes 36872 | tf_op jit(solution)/shard_map/ppermute | solution.py:383
  72.1 3.8 %collective-permute-start.11 = (f32[2,32,16,128]{3,2,1,0:T(8,128)S(1)}, f32[2,32,16,128]{3,2,1,0:T(8,128)S(1)}, u32[]{:S(2)}, u32[]{:S(2)}) collective-permute-start(f32[2,32,16,128]{3,2,1,0:T(8,128)S(1)} %pad_maximum_fusion.1), channel_id=1, source_target_pairs={{0,1},{1,0},{2,3},{3,2},{4,5},{5,4},{6,7},{7,6},{8,9},{9,8},{10,11... | collective-permute-start | bytes 1572872 | tf_op jit(solution)/shard_map/ppermute | solution.py:343
  72.2 3.8 %collective-permute-start.12 = (f32[24,128]{1,0:T(8,128)S(1)}, f32[24,128]{1,0:T(8,128)S(1)}, u32[]{:S(2)}, u32[]{:S(2)}) collective-permute-start(f32[24,128]{1,0:T(8,128)S(1)} %add_add_fusion.part), channel_id=1, source_target_pairs={{0,2},{1,3},{2,0},{3,1},{4,6},{5,7},{6,4},{7,5},{8,10},{9,11},{10,... | collective-permute-start | bytes 36872 | tf_op jit(solution)/shard_map/ppermute | solution.py:383

commit v9 on v8

--- a/solution.py
+++ b/solution.py
@@ -55,7 +55,7 @@
         high = row_y.astype(BF16).astype(F32)
         low = row_y - high
         if flip:
-            row_y = [part + pltpu.roll(part, in_rows, 1) for part in (high, low)]
+            row_y = (high, low)
         else:
             row_y = high + pltpu.roll(high, in_rows, 1) + pltpu.roll(low, 2 * in_rows, 1)
         row_x = placed_row(taps_ref[:, 2, :], lambda k: lax.rem(margin - order(k) + 2 * cols, 2 * cols), 2 * cols)
@@ -67,10 +67,18 @@
         inside = lax.broadcasted_iota(jnp.int32, (planes, 128), 1) < planes
         for v in range(views):
             if flip:
+                lane = lax.broadcasted_iota(jnp.int32, (rows, 256), 1)
                 for j, row in enumerate(row_y):
-                    wy[v, j * rows : (j + 1) * rows, :] = slanted(row[v : v + 1], rows)[:, : 2 * in_rows].astype(BF16)
+                    band = slanted(row[v : v + 1], rows)
+                    shifted = pltpu.roll(band, 256 - (rows - margin), 1)
+                    band = jnp.where(lane < margin, shifted, jnp.where(lane < rows, 0.0, band))
+                    band = band + pltpu.roll(band, in_rows, 1)
+                    wy[v, j * rows : (j + 1) * rows, :] = band[:, : 2 * in_rows].astype(BF16)
             else:
-                band = slanted(row_y[v : v + 1], out_rows)
+                row = row_y[v : v + 1]
+                band = jnp.concatenate(
+                    [slanted(pltpu.roll(row, rows - margin, 1), rows), slanted(pltpu.roll(row, rows, 1), 2 * rows)]
+                )
                 wy[v * out_rows : (v + 1) * out_rows, :] = band[:, : 3 * in_rows].astype(BF16)
             high, low = split(slanted(row_x[v : v + 1], cols)[:, :cols])
             wx[v, :cols, :cols] = high
@@ -177,11 +185,15 @@
         out[:, 8 * g : 8 * g + 8, :] = result[:, g * cols : (g + 1) * cols].reshape(planes, 8, cols)
 
 
-def adjoint_rows(blurred, before, raw, after, wy, ya):
-    planes, rows, cols = raw.shape
+def adjoint_rows(v, blurred, before, raw, after, wy, ya):
+    views, planes, rows, cols = raw.shape
+    blurred, raw, wy = blurred.at[v], raw.at[v], wy.at[v]
+    margin = before.shape[0] // (views * planes)
+    empty = jnp.zeros((rows - margin, cols), F32)
 
     def quotient(z):
-        counts = jnp.concatenate([before[z], raw[z], after[z]], axis=0)
+        at = pl.ds(v * planes + z, margin, stride=views * planes)
+        counts = jnp.concatenate([before[at, :], empty, raw[z], after[at, :], empty], axis=0)
         return counts * pl.reciprocal(jnp.maximum(blurred[z], TINY), approx=True)
 
     def piece(z):
@@ -246,8 +258,7 @@
     views = raw.shape[0]
 
     def rows_of(v):
-        fields = [ref.at[v] for ref in (blurred, before, raw, after, wy)] if v < views else None
-        return adjoint_rows(*fields, (ya, yb)[v % 2]) if fields else []
+        return adjoint_rows(v, blurred, before, raw, after, wy, (ya, yb)[v % 2]) if v < views else []
 
     interleaved(rows_of(0))
     for v in range(views):
@@ -265,18 +276,37 @@
 
 
 def iteration_kernel(
-    parity, far_before, near, own, far_after, before, raw, after, wy, wx, wz, wya, wxa, wza, part, rest,
+    parity, far_before, near, own, far_after, before, raw, after, wy, wx, wz, wya, wxa, wza,
     out, ys, blurred, ya, yb, xs, acc,
 ):
     views = ys.shape[0]
     forward_rows(parity, far_before, near, own, far_after, wy, ys)
     each_step(views, lambda v: forward_view(ys.at[v], wx[v], wz[v], blurred.at[v]))
     adjoint_all(blurred, before, raw, after, wya, wxa, wza, ya, yb, xs, acc)
+    updated(own, acc[...] * (1.0 / views), out)
+
+
+def pack_kernel(raw, last, leading):
+    count, rows = last.shape[0] // raw.shape[0], raw.shape[1]
+    flat = raw.reshape(raw.shape[0] * rows, raw.shape[2])
+    for y in range(count):
+        here = slice(y * raw.shape[0], (y + 1) * raw.shape[0])
+        last[here, :] = flat[pl.ds(rows - count + y, raw.shape[0], stride=rows), :]
+        leading[here, :] = flat[pl.ds(y, raw.shape[0], stride=rows), :]
+
+
+def packed(raw, count):
+    views, planes, rows, cols = raw.shape
+    outs = [pltpu.VMEM((count * views * planes, cols), F32)] * 2
+    return call(pack_kernel, outs, [], [raw.reshape(views * planes, rows, cols)], [], "pack", 10**6)
+
+
+def scaled_kernel(views, values, part, rest, out):
     sums = jnp.sum(part[...] + rest[...], axis=1, keepdims=True)
     space = sums.shape[0] // 3
     total, first, second = (sums[i * space : i * space + views] for i in range(3))
     scale = jnp.sum(jnp.log(first / total) + jnp.log(second / total), axis=0, keepdims=True)
-    updated(own, (acc[...] + scale[None]) * (1.0 / views), out)
+    out[...] = values[...] * jnp.exp(scale * (1.0 / views))
 
 
 def adjoint_scratch(planes, rows, cols):
@@ -312,7 +342,7 @@
     return out.reshape(planes, rows, cols), sums
 
 
-def full_iteration(parity, slabs, before, raw, after, weights, adjoint_weights, part, rest):
+def full_iteration(parity, slabs, before, raw, after, weights, adjoint_weights):
     planes, rows, cols = slabs[0].shape
     views = raw.shape[0]
     slabs = [s.reshape(-1, cols) if i == 2 else s for i, s in enumerate(slabs)]
@@ -322,13 +352,13 @@
     ]
     return call(
         iteration_kernel,
-        jax.ShapeDtypeStruct((planes * rows, cols), F32),
+        pltpu.VMEM((planes * rows, cols), F32),
         [parity],
-        [*slabs, before, raw, after, *weights, *adjoint_weights, part, rest],
+        [*slabs, before, raw, after, *weights, *adjoint_weights],
         scratch + adjoint_scratch(planes, rows, cols),
         "iteration",
         2 * 10**10,
-    ).reshape(planes, rows, cols)
+    )
 
 
 def two_slabs_away(value, count):
@@ -362,8 +392,9 @@
     parity = (place % 2).reshape(1)
 
     far = two_slabs_away(estimate, count)
-    before = lax.ppermute(raw, "slab", up)
-    after = lax.ppermute(raw, "slab", down)
+    last, leading = packed(raw, taps.shape[2] // 2)
+    before = lax.ppermute(last, "slab", up)
+    after = lax.ppermute(leading, "slab", down)
 
     wzs = tap_sums(taps[:, 0], 0, planes, planes)
     wy_sums = tap_sums(taps[:, 1], place * rows, rows, count * rows)
@@ -386,9 +417,10 @@
         elif r < len(rounds) - 1:
             sums = sums + sum(others)
     slabs = with_near(current, *far, parity, count)
-    return full_iteration(
-        parity, slabs, before, raw, after, forward_weights, adjoint_weights, sums, others[0]
-    )
+    current = full_iteration(parity, slabs, before, raw, after, forward_weights, adjoint_weights)
+    out = jax.ShapeDtypeStruct(current.shape, F32)
+    scaled = functools.partial(scaled_kernel, views)
+    return call(scaled, out, [], [current, sums, others[0]], [], "scaled", 10**5).reshape(estimate.shape)
 
 
 def solution(mesh):

time: 87.5 us -> 85.8 us (0.981)
  waiting for transfers between devices: 15.2 us -> 6.45 us
  Pallas kernels: 24.4 us -> 31.3 us
  starting transfers between devices: 44.3 us -> 45.4 us
  other arithmetic: 1.56 us -> 0.61 us
    pallas_call x4 -> x6, Pallas kernels: 24.4 us -> 31.3 us  [call(): pl.pallas_call(kernel, out_shape=outs, in_specs=[pl.BlockSpec(memory_spac...]
    ppermute x4, waiting for transfers between devices: 4.94 us -> 0.01 us  [two_slabs_away(): return (lax.ppermute(value, 'slab', up), lax.ppermute(value, 'slab', down))]
    ppermute x4, starting transfers between devices: 34.8 us -> 31.2 us  [two_slabs_away(): return (lax.ppermute(value, 'slab', up), lax.ppermute(value, 'slab', down))]
    ppermute x5, waiting for transfers between devices: 8.63 us -> 5.2 us  [per_device(): lax.ppermute(sums, 'slab', [(i, i ^ d) for i in range(count)])]
    ppermute x2, starting transfers between devices: 0.14 us -> 2.86 us  [with_near(): near = lax.ppermute(passed, 'slab', swap)]
    ppermute x2, starting transfers between devices: 2.85 us -> 3.99 us  [the longest x1 2.71 us: per_device(): before = lax.ppermute(last, 'slab', up)]
    another operation x4, other arithmetic: 1.09 us -> 0.14 us  [with_near(): jnp.stack([value, jnp.where(parity[0] == 0, far_after, far_before)])]
  transfers between devices with their start and end apart: 13 -> 13, of which waited for: 7 -> 4; matrix products, arithmetic and copies ran while one was open for 3% -> 1% of each run, Pallas kernels for 10% -> 29%
where the time goes in v9:
time: 85.8 us; the launch traced here: 85.5 us
  starting transfers between devices  45.4 us (53%)
  Pallas kernels  31.3 us (36%)
  waiting for transfers between devices  6.45 us (8%)
  local copies, waits for them, and re-layouts  1.43 us (2%)
    pallas_call x6, Pallas kernels, call(): pl.pallas_call(kernel, out_shape=outs, in_specs=[pl.BlockSpec(memory_spac...  31.3 us
    ppermute x4, starting transfers between devices, two_slabs_away(): return (lax.ppermute(value, 'slab', up), lax.ppermute(value, 'slab', down))  31.2 us
    ppermute x5, starting transfers between devices, per_device(): lax.ppermute(sums, 'slab', [(i, i ^ d) for i in range(count)])  7.34 us
    ppermute x5, waiting for transfers between devices, per_device(): lax.ppermute(sums, 'slab', [(i, i ^ d) for i in range(count)])  5.2 us
    ppermute x2, starting transfers between devices, with_near(): near = lax.ppermute(passed, 'slab', swap)  2.86 us
    ppermute x1, starting transfers between devices, per_device(): before = lax.ppermute(last, 'slab', up)  2.71 us
  transfers between devices with their start and end apart: 13, of which 4 were waited for; matrix products, arithmetic and copies ran while one was open for 1% of the time, Pallas kernels for 29%

profile of v9, /device:TPU:0, one launch (start us, length us, event | category | flops | bytes accessed | tf_op | source)
XLA Modules:
  0.0 85.5 jit_solution(16622278897313675016)
XLA Ops:
  0.0 4.9 %collective-permute-start = (f32[32,16,128]{2,1,0:T(8,128)}, f32[32,16,128]{2,1,0:T(8,128)S(1)}, u32[]{:S(2)}, u32[]{:S(2)}) collective-permute-start(f32[32,16,128]{2,1,0:T(8,128)} %param.3), channel_id=1, source_target_pairs={{0,2},{1,3},{2,4},{3,5},{4,6},{5,7},{6,8},{7,9},{8,10},{9,11},{10,... | collective-permute-start | bytes 786440 | tf_op jit(solution)/shard_map/ppermute | solution.py:367
  4.9 1.3 %collective-permute-start.1 = (f32[32,16,128]{2,1,0:T(8,128)}, f32[32,16,128]{2,1,0:T(8,128)S(1)}, u32[]{:S(2)}, u32[]{:S(2)}) collective-permute-start(f32[32,16,128]{2,1,0:T(8,128)} %param.3), channel_id=1, source_target_pairs={{2,0},{3,1},{4,2},{5,3},{6,4},{7,5},{8,6},{9,7},{10,8},{11,9},{12,... | collective-permute-start | bytes 786440 | tf_op jit(solution)/shard_map/ppermute | solution.py:367
  6.2 0.0 copy-start
  6.2 1.4 %copy-done = f32[6,32,16,128]{3,2,1,0:T(8,128)S(1)} copy-done((f32[6,32,16,128]{3,2,1,0:T(8,128)S(1)}, f32[6,32,16,128]{3,2,1,0:T(8,128)}, u32[]{:S(2)}) %copy-start) | copy-done | bytes 1572888
  7.6 2.7 %pack.1 = (f32[2880,128]{1,0:T(8,128)}, f32[2880,128]{1,0:T(8,128)}) custom-call(f32[192,16,128]{2,1,0:T(8,128)S(1)} %bitcast.18), custom_call_target="tpu_custom_call" | custom-call | flops 1000000 | bytes 10000000 | tf_op jit(solution)/shard_map/pack/pallas_call | solution.py:103
  10.3 2.7 %collective-permute-start.3 = (f32[2880,128]{1,0:T(8,128)}, f32[2880,128]{1,0:T(8,128)}, u32[]{:S(2)}, u32[]{:S(2)}) collective-permute-start(f32[2880,128]{1,0:T(8,128)} %get-tuple-element.24), channel_id=1, source_target_pairs={{0,1},{1,2},{2,3},{3,4},{4,5},{5,6},{6,7},{7,8},{8,9},{9,10},{10,1... | collective-permute-start | bytes 4423688 | tf_op jit(solution)/shard_map/ppermute | solution.py:396
  13.0 1.3 %collective-permute-start.4 = (f32[2880,128]{1,0:T(8,128)}, f32[2880,128]{1,0:T(8,128)}, u32[]{:S(2)}, u32[]{:S(2)}) collective-permute-start(f32[2880,128]{1,0:T(8,128)} %get-tuple-element.25), channel_id=1, source_target_pairs={{1,0},{2,1},{3,2},{4,3},{5,4},{6,5},{7,6},{8,7},{9,8},{10,9},{11,1... | collective-permute-start | bytes 4423688 | tf_op jit(solution)/shard_map/ppermute | solution.py:397
  14.4 0.1 fusion.11
  14.4 3.5 %weights.1 = (bf16[288,240]{1,0:T(8,128)(2,1)S(1)}, bf16[6,256,256]{2,1,0:T(8,128)(2,1)S(1)}, bf16[6,256,768]{2,1,0:T(8,128)(2,1)S(1)}, bf16[6,32,96]{2,1,0:T(8,...) custom-call(f32[6,3,31]{2,1,0:T(4,128)S(1)} %copy-done.3), custom_call_target="tpu_custom_call" | custom-call | flops 10000000 | bytes 10000000 | tf_op jit(solution)/shard_map/weights/pallas_call | solution.py:103
  17.9 0.1 multiply_reduce_fusion.2
  18.0 0.0 collective-permute-done.far_before
  18.1 2.8 %collective-permute-start.2 = (f32[2,32,16,128]{3,2,1,0:T(8,128)S(1)}, f32[2,32,16,128]{3,2,1,0:T(8,128)S(1)}, u32[]{:S(2)}, u32[]{:S(2)}) collective-permute-start(f32[2,32,16,128]{3,2,1,0:T(8,128)S(1)} %pad_maximum_fusion), channel_id=1, source_target_pairs={{0,1},{1,0},{2,3},{3,2},{4,5},{5,4},{6,7},{7,6},{8,9},{9,8},{10,11... | collective-permute-start | bytes 1572872 | tf_op jit(solution)/shard_map/ppermute | solution.py:373
  20.9 0.1 multiply_reduce_fusion
  21.0 0.1 multiply_reduce_fusion.1.wzs
  21.1 0.1 broadcast_multiply_fusion.wyx
  21.2 1.2 %collective-permute-done.2.near = f32[2,32,16,128]{3,2,1,0:T(8,128)S(1)} collective-permute-done((f32[2,32,16,128]{3,2,1,0:T(8,128)S(1)}, f32[2,32,16,128]{3,2,1,0:T(8,128)S(1)}, u32[]{:S(2)}, u32[]{:S(2)}) %collective-permute-start.2) | collective-permute-done | bytes 524320 | tf_op jit(solution)/shard_map/ppermute | solution.py:373
  22.5 6.9 %forward.1 = (f32[6,32,48,128]{3,2,1,0:T(8,128)S(1)}, f32[24,128]{1,0:T(8,128)S(1)}) custom-call(s32[1]{0:T(128)} %bitcast.parity, f32[6,32]{1,0:T(8,128)S(1)} %multiply_reduce_fusion.1.wzs, f32[32,16,128]{2,1,0:T(8,128)S(1)} %collective-permute-done.far_before, f32[2,32,16,128]{3,2,1,0:T(8,128)S(1)} %collective-permute-done.2.near, ...), custom_call_target="tpu_custom_call" | custom-call | flops 10000000000 | bytes 10000000 | tf_op jit(solution)/shard_map/forward/pallas_call | solution.py:103
  29.4 0.0 collective-permute-done.3.before
  29.4 0.0 collective-permute-done.4.after
  29.4 5.8 %adjoint.1 = (f32[512,128]{1,0:T(8,128)S(1)}, f32[24,128]{1,0:T(8,128)S(1)}) custom-call(f32[6,32]{1,0:T(8,128)S(1)} %multiply_reduce_fusion.1.wzs, f32[512,128]{1,0:T(8,128)S(1)} %bitcast.21, f32[6,32,48,128]{3,2,1,0:T(8,128)S(1)} %get-tuple-element.23.blurred, f32[2880,128]{1,0:T(8,128)} %collective-permute-done.3.before, ...), custom_call_target="tpu_custom_call" | custom-call | flops 10000000000 | bytes 10000000 | tf_op jit(solution)/shard_map/adjoint/pallas_call | solution.py:103
  35.3 1.3 %collective-permute-start.6 = (f32[32,16,128]{2,1,0:T(8,128)S(1)}, f32[32,16,128]{2,1,0:T(8,128)S(1)}, u32[]{:S(2)}, u32[]{:S(2)}) collective-permute-start(f32[32,16,128]{2,1,0:T(8,128)S(1)} %bitcast.22), channel_id=1, source_target_pairs={{2,0},{3,1},{4,2},{5,3},{6,4},{7,5},{8,6},{9,7},{10,8},{11,9},{12,... | collective-permute-start | bytes 786440 | tf_op jit(solution)/shard_map/ppermute | solution.py:367
  36.6 23.8 %collective-permute-start.5 = (f32[32,16,128]{2,1,0:T(8,128)S(1)}, f32[32,16,128]{2,1,0:T(8,128)S(1)}, u32[]{:S(2)}, u32[]{:S(2)}) collective-permute-start(f32[32,16,128]{2,1,0:T(8,128)S(1)} %bitcast.23), channel_id=1, source_target_pairs={{0,2},{1,3},{2,4},{3,5},{4,6},{5,7},{6,8},{7,9},{8,10},{9,11},{10,... | collective-permute-start | bytes 786440 | tf_op jit(solution)/shard_map/ppermute | solution.py:367
  60.3 0.1 collective-permute-start.7
  60.4 1.2 %collective-permute-done.7 = f32[24,128]{1,0:T(8,128)S(1)} collective-permute-done((f32[24,128]{1,0:T(8,128)S(1)}, f32[24,128]{1,0:T(8,128)S(1)}, u32[]{:S(2)}, u32[]{:S(2)}) %collective-permute-start.7) | collective-permute-done | bytes 12320 | tf_op jit(solution)/shard_map/ppermute | solution.py:414
  61.6 4.2 %collective-permute-start.10 = (f32[24,128]{1,0:T(8,128)S(1)}, f32[24,128]{1,0:T(8,128)S(1)}, u32[]{:S(2)}, u32[]{:S(2)}) collective-permute-start(f32[24,128]{1,0:T(8,128)S(1)} %add.66), channel_id=1, source_target_pairs={{0,12},{1,13},{2,14},{3,15},{4,8},{5,9},{6,10},{7,11},{8,4},{9,5},... | collective-permute-start | bytes 36872 | tf_op jit(solution)/shard_map/ppermute | solution.py:414
  65.8 0.6 collective-permute-start.8
  66.4 1.7 %collective-permute-done.10 = f32[24,128]{1,0:T(8,128)S(1)} collective-permute-done((f32[24,128]{1,0:T(8,128)S(1)}, f32[24,128]{1,0:T(8,128)S(1)}, u32[]{:S(2)}, u32[]{:S(2)}) %collective-permute-start.10) | collective-permute-done | bytes 12320 | tf_op jit(solution)/shard_map/ppermute | solution.py:414
  68.1 2.3 %collective-permute-done.9 = f32[24,128]{1,0:T(8,128)S(1)} collective-permute-done((f32[24,128]{1,0:T(8,128)S(1)}, f32[24,128]{1,0:T(8,128)S(1)}, u32[]{:S(2)}, u32[]{:S(2)}) %collective-permute-start.9) | collective-permute-done | bytes 12320 | tf_op jit(solution)/shard_map/ppermute | solution.py:414
  70.5 0.1 collective-permute-start.11
  70.6 2.5 %collective-permute-start.12 = (f32[24,128]{1,0:T(8,128)S(1)}, f32[24,128]{1,0:T(8,128)S(1)}, u32[]{:S(2)}, u32[]{:S(2)}) collective-permute-start(f32[24,128]{1,0:T(8,128)S(1)} %add_add_fusion.part), channel_id=1, source_target_pairs={{0,2},{1,3},{2,0},{3,1},{4,6},{5,7},{6,4},{7,5},{8,10},{9,11},{10,... | collective-permute-start | bytes 36872 | tf_op jit(solution)/shard_map/ppermute | solution.py:414
  73.1 11.6 %iteration.1.values = f32[512,128]{1,0:T(8,128)S(1)} custom-call(s32[1]{0:T(128)} %bitcast.parity, f32[32,16,128]{2,1,0:T(8,128)S(1)} %collective-permute-done.5.far_before, f32[2,32,16,128]{3,2,1,0:T(8,128)S(1)} %collective-permute-done.11.near, f32[512,128]{1,0:T(8,128)S(1)} %get-tuple-element.30.own, f32[32,16,128]{2,1,0:T(8,128)S(1)} %collective-permute-done.6.far_after, ...), custom_call_target="tpu_custom_call" | custom-call | flops 20000000000 | bytes 10000000 | tf_op jit(solution)/shard_map/iteration/pallas_call | solution.py:103
  84.7 0.8 scaled.1
  (25 shorter events, 0.2 us)
Async XLA Ops:
  0.0 18.0 %collective-permute-start = (f32[32,16,128]{2,1,0:T(8,128)}, f32[32,16,128]{2,1,0:T(8,128)S(1)}, u32[]{:S(2)}, u32[]{:S(2)}) collective-permute-start(f32[32,16,128]{2,1,0:T(8,128)} %param.3), channel_id=1, source_target_pairs={{0,2},{1,3},{2,4},{3,5},{4,6},{5,7},{6,8},{7,9},{8,10},{9,11},{10,... | collective-permute-start | bytes 786440 | tf_op jit(solution)/shard_map/ppermute | solution.py:367
  4.9 13.1 %collective-permute-start.1 = (f32[32,16,128]{2,1,0:T(8,128)}, f32[32,16,128]{2,1,0:T(8,128)S(1)}, u32[]{:S(2)}, u32[]{:S(2)}) collective-permute-start(f32[32,16,128]{2,1,0:T(8,128)} %param.3), channel_id=1, source_target_pairs={{2,0},{3,1},{4,2},{5,3},{6,4},{7,5},{8,6},{9,7},{10,8},{11,9},{12,... | collective-permute-start | bytes 786440 | tf_op jit(solution)/shard_map/ppermute | solution.py:367
  6.2 1.4 %copy-start = (f32[6,32,16,128]{3,2,1,0:T(8,128)S(1)}, f32[6,32,16,128]{3,2,1,0:T(8,128)}, u32[]{:S(2)}) copy-start(f32[6,32,16,128]{3,2,1,0:T(8,128)} %raw.5) | copy-start | bytes 4718596
  7.6 6.7 %copy-start.3 = (f32[6,3,31]{2,1,0:T(4,128)S(1)}, f32[6,3,31]{2,1,0:T(4,128)}, u32[]{:S(2)}) copy-start(f32[6,3,31]{2,1,0:T(4,128)} %taps_ref.1) | copy-start | bytes 6700
  7.6 10.5 %copy-start.2 = (f32[32,16,128]{2,1,0:T(8,128)S(1)}, f32[32,16,128]{2,1,0:T(8,128)}, u32[]{:S(2)}) copy-start(f32[32,16,128]{2,1,0:T(8,128)} %param.3) | copy-start | bytes 786436
  10.3 12.1 %copy-start.1 = (f32[6,32,16,128]{3,2,1,0:T(8,128)S(1)}, f32[6,32,16,128]{3,2,1,0:T(8,128)}, u32[]{:S(2)}) copy-start(f32[6,32,16,128]{3,2,1,0:T(8,128)} %raw.5) | copy-start | bytes 4718596
  10.3 19.1 %collective-permute-start.3 = (f32[2880,128]{1,0:T(8,128)}, f32[2880,128]{1,0:T(8,128)}, u32[]{:S(2)}, u32[]{:S(2)}) collective-permute-start(f32[2880,128]{1,0:T(8,128)} %get-tuple-element.24), channel_id=1, source_target_pairs={{0,1},{1,2},{2,3},{3,4},{4,5},{5,6},{6,7},{7,8},{8,9},{9,10},{10,1... | collective-permute-start | bytes 4423688 | tf_op jit(solution)/shard_map/ppermute | solution.py:396
  13.0 16.4 %collective-permute-start.4 = (f32[2880,128]{1,0:T(8,128)}, f32[2880,128]{1,0:T(8,128)}, u32[]{:S(2)}, u32[]{:S(2)}) collective-permute-start(f32[2880,128]{1,0:T(8,128)} %get-tuple-element.25), channel_id=1, source_target_pairs={{1,0},{2,1},{3,2},{4,3},{5,4},{6,5},{7,6},{8,7},{9,8},{10,9},{11,1... | collective-permute-start | bytes 4423688 | tf_op jit(solution)/shard_map/ppermute | solution.py:397
  18.1 4.3 %collective-permute-start.2 = (f32[2,32,16,128]{3,2,1,0:T(8,128)S(1)}, f32[2,32,16,128]{3,2,1,0:T(8,128)S(1)}, u32[]{:S(2)}, u32[]{:S(2)}) collective-permute-start(f32[2,32,16,128]{3,2,1,0:T(8,128)S(1)} %pad_maximum_fusion), channel_id=1, source_target_pairs={{0,1},{1,0},{2,3},{3,2},{4,5},{5,4},{6,7},{7,6},{8,9},{9,8},{10,11... | collective-permute-start | bytes 1572872 | tf_op jit(solution)/shard_map/ppermute | solution.py:373
  35.3 35.2 %collective-permute-start.6 = (f32[32,16,128]{2,1,0:T(8,128)S(1)}, f32[32,16,128]{2,1,0:T(8,128)S(1)}, u32[]{:S(2)}, u32[]{:S(2)}) collective-permute-start(f32[32,16,128]{2,1,0:T(8,128)S(1)} %bitcast.22), channel_id=1, source_target_pairs={{2,0},{3,1},{4,2},{5,3},{6,4},{7,5},{8,6},{9,7},{10,8},{11,9},{12,... | collective-permute-start | bytes 786440 | tf_op jit(solution)/shard_map/ppermute | solution.py:367
  36.6 33.9 %collective-permute-start.5 = (f32[32,16,128]{2,1,0:T(8,128)S(1)}, f32[32,16,128]{2,1,0:T(8,128)S(1)}, u32[]{:S(2)}, u32[]{:S(2)}) collective-permute-start(f32[32,16,128]{2,1,0:T(8,128)S(1)} %bitcast.23), channel_id=1, source_target_pairs={{0,2},{1,3},{2,4},{3,5},{4,6},{5,7},{6,8},{7,9},{8,10},{9,11},{10,... | collective-permute-start | bytes 786440 | tf_op jit(solution)/shard_map/ppermute | solution.py:367
  60.3 1.2 %collective-permute-start.7 = (f32[24,128]{1,0:T(8,128)S(1)}, f32[24,128]{1,0:T(8,128)S(1)}, u32[]{:S(2)}, u32[]{:S(2)}) collective-permute-start(f32[24,128]{1,0:T(8,128)S(1)} %get-tuple-element.31), channel_id=1, source_target_pairs={{0,1},{1,0},{2,3},{3,2},{4,5},{5,4},{6,7},{7,6},{8,9},{9,8},{10,11... | collective-permute-start | bytes 36872 | tf_op jit(solution)/shard_map/ppermute | solution.py:414
  61.6 6.5 %collective-permute-start.10 = (f32[24,128]{1,0:T(8,128)S(1)}, f32[24,128]{1,0:T(8,128)S(1)}, u32[]{:S(2)}, u32[]{:S(2)}) collective-permute-start(f32[24,128]{1,0:T(8,128)S(1)} %add.66), channel_id=1, source_target_pairs={{0,12},{1,13},{2,14},{3,15},{4,8},{5,9},{6,10},{7,11},{8,4},{9,5},... | collective-permute-start | bytes 36872 | tf_op jit(solution)/shard_map/ppermute | solution.py:414
  65.8 4.6 %collective-permute-start.9 = (f32[24,128]{1,0:T(8,128)S(1)}, f32[24,128]{1,0:T(8,128)S(1)}, u32[]{:S(2)}, u32[]{:S(2)}) collective-permute-start(f32[24,128]{1,0:T(8,128)S(1)} %add.66), channel_id=1, source_target_pairs={{0,8},{1,9},{2,10},{3,11},{4,12},{5,13},{6,14},{7,15},{8,0},{9,1},... | collective-permute-start | bytes 36872 | tf_op jit(solution)/shard_map/ppermute | solution.py:414
  65.8 4.6 %collective-permute-start.8 = (f32[24,128]{1,0:T(8,128)S(1)}, f32[24,128]{1,0:T(8,128)S(1)}, u32[]{:S(2)}, u32[]{:S(2)}) collective-permute-start(f32[24,128]{1,0:T(8,128)S(1)} %add.66), channel_id=1, source_target_pairs={{0,4},{1,5},{2,6},{3,7},{4,0},{5,1},{6,2},{7,3},{8,12},{9,13},{10,... | collective-permute-start | bytes 36872 | tf_op jit(solution)/shard_map/ppermute | solution.py:414
  70.5 2.5 %collective-permute-start.11 = (f32[2,32,16,128]{3,2,1,0:T(8,128)S(1)}, f32[2,32,16,128]{3,2,1,0:T(8,128)S(1)}, u32[]{:S(2)}, u32[]{:S(2)}) collective-permute-start(f32[2,32,16,128]{3,2,1,0:T(8,128)S(1)} %pad_maximum_fusion.1), channel_id=1, source_target_pairs={{0,1},{1,0},{2,3},{3,2},{4,5},{5,4},{6,7},{7,6},{8,9},{9,8},{10,11... | collective-permute-start | bytes 1572872 | tf_op jit(solution)/shard_map/ppermute | solution.py:373
  70.6 14.1 %collective-permute-start.12 = (f32[24,128]{1,0:T(8,128)S(1)}, f32[24,128]{1,0:T(8,128)S(1)}, u32[]{:S(2)}, u32[]{:S(2)}) collective-permute-start(f32[24,128]{1,0:T(8,128)S(1)} %add_add_fusion.part), channel_id=1, source_target_pairs={{0,2},{1,3},{2,0},{3,1},{4,6},{5,7},{6,4},{7,5},{8,10},{9,11},{10,... | collective-permute-start | bytes 36872 | tf_op jit(solution)/shard_map/ppermute | solution.py:414

commit v10 on v9

--- a/solution.py
+++ b/solution.py
@@ -49,7 +49,7 @@
         order = (lambda k: count - 1 - k) if flip else (lambda k: k)
         out_rows = rows if flip else 3 * rows
         in_rows = out_rows + 2 * rows
-        planes = wz.shape[1] // (1 if flip else 8)
+        planes = wz.shape[1] // 8
         cols = wx.shape[1] // 2
         row_y = placed_row(taps_ref[:, 1, :], lambda k: order(k) + rows - margin, 256)
         high = row_y.astype(BF16).astype(F32)
@@ -59,12 +59,10 @@
         else:
             row_y = high + pltpu.roll(high, in_rows, 1) + pltpu.roll(low, 2 * in_rows, 1)
         row_x = placed_row(taps_ref[:, 2, :], lambda k: lax.rem(margin - order(k) + 2 * cols, 2 * cols), 2 * cols)
-        apart = 1 if flip else 8
-        width_z = 128 if flip else 16 * planes
+        width_z = 16 * planes
         row_z = placed_row(
-            taps_ref[:, 0, :], lambda k: lax.rem(apart * (order(k) - margin) + width_z, width_z), width_z
+            taps_ref[:, 0, :], lambda k: lax.rem(8 * (order(k) - margin) + width_z, width_z), width_z
         )
-        inside = lax.broadcasted_iota(jnp.int32, (planes, 128), 1) < planes
         for v in range(views):
             if flip:
                 lane = lax.broadcasted_iota(jnp.int32, (rows, 256), 1)
@@ -85,17 +83,11 @@
             wx[v, cols:, :cols] = high
             wx[v, :cols, cols:] = low
             wx[v, cols:, cols:] = low
-            if flip:
-                band = jnp.where(inside, slanted(row_z[v : v + 1], planes), 0.0)
-                high = band.astype(BF16).astype(F32)
-                band = high + pltpu.roll(high, planes, 1) + pltpu.roll(band - high, 2 * planes, 1)
-                wz[v] = band[:, : 3 * planes].astype(BF16)
-            else:
-                size = 8 * planes
-                high, low = split(slanted(row_z[v : v + 1], size)[:, :size])
-                wz[v, :, :size] = high
-                wz[v, :, size : 2 * size] = high
-                wz[v, :, 2 * size :] = low
+            size = 8 * planes
+            high, low = split(slanted(row_z[v : v + 1], size)[:, :size])
+            wz[v, :, :size] = high
+            wz[v, :, size : 2 * size] = high
+            wz[v, :, 2 * size :] = low
 
 
 def call(kernel, outs, smem, arrays, scratch, name, flops):
@@ -120,7 +112,7 @@
         pltpu.VMEM((views, 8 * planes, 24 * planes), BF16),
         pltpu.VMEM((views, 2 * rows, 6 * rows), BF16),
         pltpu.VMEM((views, 2 * cols, 2 * cols), BF16),
-        pltpu.VMEM((views, planes, 3 * planes), BF16),
+        pltpu.VMEM((views, 8 * planes, 24 * planes), BF16),
     ]
     made = call(functools.partial(weights_kernel, rows), outs, [], [taps], [], "weights", 10**7)
     return made[:3], made[3:]
@@ -159,7 +151,7 @@
 
     def plane(z):
         return jnp.concatenate(
-            [far_before[z], near[1 - side, z], own[pl.ds(z * rows, rows), :], near[side, z], far_after[z]], axis=0
+            [far_before[z], near[1 - side, z], own[z], near[side, z], far_after[z]], axis=0
         )
 
     for z in range(0, planes, 2):
@@ -185,15 +177,12 @@
         out[:, 8 * g : 8 * g + 8, :] = result[:, g * cols : (g + 1) * cols].reshape(planes, 8, cols)
 
 
-def adjoint_rows(v, blurred, before, raw, after, wy, ya):
-    views, planes, rows, cols = raw.shape
-    blurred, raw, wy = blurred.at[v], raw.at[v], wy.at[v]
-    margin = before.shape[0] // (views * planes)
-    empty = jnp.zeros((rows - margin, cols), F32)
+def adjoint_rows(halo, raw, blurred, wy, ya):
+    planes, rows, cols = raw.shape
 
     def quotient(z):
-        at = pl.ds(v * planes + z, margin, stride=views * planes)
-        counts = jnp.concatenate([before[at, :], empty, raw[z], after[at, :], empty], axis=0)
+        around = halo(z)
+        counts = jnp.concatenate([around[:rows], raw[z], around[rows:]], axis=0)
         return counts * pl.reciprocal(jnp.maximum(blurred[z], TINY), approx=True)
 
     def piece(z):
@@ -209,22 +198,56 @@
 
 def adjoint_logs(first, ya, wx, wz, xs, acc):
     planes, rows, lanes = ya.shape
-
-    def piece(y):
-        values = stacked([xs[pl.ds(y + j, planes, stride=rows), :] for j in range(WIDE)])
-        result = jnp.log(dot(wz[...], values))
-        acc[y // WIDE] = result if first else acc[y // WIDE] + result
-
-    return along_x(ya, wx, xs) + [functools.partial(piece, y) for y in range(0, rows, WIDE)]
-
-
-def updated(current, exponents, out):
-    count, planes, lanes = exponents.shape
-    cols, rows = lanes // WIDE, count * WIDE
-    for y in range(rows):
-        at = pl.ds(y, planes, stride=rows)
-        part = slice((y % WIDE) * cols, (y % WIDE + 1) * cols)
-        out[at, :] = current[at, :] * jnp.exp(exponents[y // WIDE, :, part])
+    cols = lanes // 2
+
+    def piece():
+        value = xs[...].reshape(planes, rows, cols)
+        groups = [value[:, 8 * g : 8 * g + 8, :].reshape(planes * 8, cols) for g in range(2)]
+        result = jnp.log(dot(wz[...], stacked(groups)))
+        acc[...] = result if first else acc[...] + result
+
+    return along_x(ya, wx, xs) + [piece]
+
+
+def adjoint_of(chosen, begun, halo, raw, blurred, wy, wx, wz, ya, yb, xs, acc):
+    def rows_of(i):
+        if i == len(chosen):
+            return []
+        v = chosen[i]
+        return adjoint_rows(halo(v), raw.at[v], blurred.at[v], wy.at[v], (ya, yb)[i % 2])
+
+    interleaved(rows_of(0))
+    for i, v in enumerate(chosen):
+        logs = adjoint_logs(i == 0 and not begun, (ya, yb)[i % 2], wx.at[v], wz.at[v], xs.at[i % 2], acc)
+        interleaved(logs, rows_of(i + 1))
+
+
+def updated(current, acc, views, out):
+    planes, rows, cols = out.shape
+    for g in range(rows // 8):
+        here = slice(8 * g, 8 * g + 8)
+        exponent = acc[:, g * cols : (g + 1) * cols].reshape(planes, 8, cols) * (1.0 / views)
+        out[:, here, :] = current[:, here, :] * jnp.exp(exponent)
+
+
+def plane_halo(chosen, before, after, halos):
+    planes, rows = halos.shape[1], halos.shape[2] // 2
+    stride = len(chosen) * planes
+    count = before.shape[0] // stride
+    empty = jnp.zeros((rows - count, before.shape[1]), F32)
+
+    def of_view(v):
+        i = v - chosen[0]
+
+        def of_plane(z):
+            at = pl.ds(i * planes + z, count, stride=stride)
+            around = jnp.concatenate([before[at, :], empty, after[at, :], empty], axis=0)
+            halos[i, z] = around
+            return around
+
+        return of_plane
+
+    return of_view
 
 
 def each_step(steps, body):
@@ -246,44 +269,43 @@
 
 
 def weighted_sums(values, wzs, wyx, sums, at):
-    planes, (_, rows, cols) = wzs.shape[1], wyx.shape
+    planes, rows, cols = values.shape
     for v in range(wyx.shape[0]):
         total = jnp.zeros((rows, cols), F32)
         for z in range(planes):
-            total = total + wzs[v, z] * values[z * rows : (z + 1) * rows, :]
+            total = total + wzs[v, z] * values[z]
         sums[at + v : at + v + 1, :] = jnp.sum(total * wyx[v], axis=0, keepdims=True)
 
 
-def adjoint_all(blurred, before, raw, after, wy, wx, wz, ya, yb, xs, acc):
-    views = raw.shape[0]
-
-    def rows_of(v):
-        return adjoint_rows(v, blurred, before, raw, after, wy, (ya, yb)[v % 2]) if v < views else []
-
-    interleaved(rows_of(0))
-    for v in range(views):
-        logs = adjoint_logs(v == 0, (ya, yb)[v % 2], wx.at[v], wz.at[v], xs.at[v % 2], acc)
-        interleaved(logs, rows_of(v + 1))
-
-
-def first_adjoint_kernel(
-    wzs, current, blurred, before, raw, after, wy, wx, wz, wyx, known, out, sums, ya, yb, xs, acc
+def early_adjoint_kernel(chosen, before, after, raw, blurred, wy, wx, wz, acc, halos, ya, yb, xs):
+    halo = plane_halo(chosen, before, after, halos)
+    adjoint_of(chosen, False, halo, raw, blurred, wy, wx, wz, ya, yb, xs, acc)
+
+
+def late_adjoint_kernel(
+    chosen, wzs, before, after, raw, blurred, wy, wx, wz, known_acc, current, wyx, known, out, sums, halos, ya, yb, xs, acc
 ):
-    adjoint_all(blurred, before, raw, after, wy, wx, wz, ya, yb, xs, acc)
-    updated(current, acc[...] * (1.0 / raw.shape[0]), out)
+    acc[...] = known_acc[...]
+    halo = plane_halo(chosen, before, after, halos)
+    adjoint_of(chosen, True, halo, raw, blurred, wy, wx, wz, ya, yb, xs, acc)
+    updated(current, acc[...], raw.shape[0], out)
     sums[...] = known[...]
     weighted_sums(out, wzs, wyx, sums, 2 * sums.shape[0] // 3)
 
 
 def iteration_kernel(
-    parity, far_before, near, own, far_after, before, raw, after, wy, wx, wz, wya, wxa, wza,
+    parity, far_before, near, own, far_after, early, late, raw, wy, wx, wz, wya, wxa, wza,
     out, ys, blurred, ya, yb, xs, acc,
 ):
-    views = ys.shape[0]
+    views, split_at = ys.shape[0], early.shape[0]
     forward_rows(parity, far_before, near, own, far_after, wy, ys)
     each_step(views, lambda v: forward_view(ys.at[v], wx[v], wz[v], blurred.at[v]))
-    adjoint_all(blurred, before, raw, after, wya, wxa, wza, ya, yb, xs, acc)
-    updated(own, acc[...] * (1.0 / views), out)
+
+    def halo(v):
+        return lambda z: early[v, z] if v < split_at else late[v - split_at, z]
+
+    adjoint_of(range(views), False, halo, raw, blurred, wya, wxa, wza, ya, yb, xs, acc)
+    updated(own, acc[...], views, out)
 
 
 def pack_kernel(raw, last, leading):
@@ -295,10 +317,11 @@
         leading[here, :] = flat[pl.ds(y, raw.shape[0], stride=rows), :]
 
 
-def packed(raw, count):
-    views, planes, rows, cols = raw.shape
-    outs = [pltpu.VMEM((count * views * planes, cols), F32)] * 2
-    return call(pack_kernel, outs, [], [raw.reshape(views * planes, rows, cols)], [], "pack", 10**6)
+def packed(raw, chosen, count):
+    _, planes, rows, cols = raw.shape
+    part = raw[chosen[0] : chosen[-1] + 1].reshape(len(chosen) * planes, rows, cols)
+    outs = [pltpu.VMEM((count * part.shape[0], cols), F32)] * 2
+    return call(pack_kernel, outs, [], [part], [], "pack", 10**6)
 
 
 def scaled_kernel(views, values, part, rest, out):
@@ -306,56 +329,54 @@
     space = sums.shape[0] // 3
     total, first, second = (sums[i * space : i * space + views] for i in range(3))
     scale = jnp.sum(jnp.log(first / total) + jnp.log(second / total), axis=0, keepdims=True)
-    out[...] = values[...] * jnp.exp(scale * (1.0 / views))
+    out[...] = values[...] * jnp.exp(scale * (1.0 / views))[None]
 
 
 def adjoint_scratch(planes, rows, cols):
     return [
         pltpu.VMEM((planes, rows, 2 * cols), BF16),
         pltpu.VMEM((planes, rows, 2 * cols), BF16),
-        pltpu.VMEM((2, planes * 16, cols), F32),
-        pltpu.VMEM((rows // WIDE, planes, WIDE * cols), F32),
+        pltpu.VMEM((2, planes * rows, cols), F32),
     ]
 
 
 def forward(parity, slabs, weights, raw, wzs, wyx):
     planes, rows, cols = slabs[0].shape
     views = raw.shape[0]
-    slabs = [s.reshape(-1, cols) if i == 2 else s for i, s in enumerate(slabs)]
     outs = [pltpu.VMEM((views, planes, 3 * rows, cols), F32), pltpu.VMEM((24 * -(-views // 8), cols), F32)]
     scratch = [pltpu.VMEM((views, planes, 3 * rows, 2 * cols), BF16)]
     return call(forward_kernel, outs, [parity, wzs], [*slabs, *weights, raw, wyx], scratch, "forward", 10**10)
 
 
-def first_adjoint(current, blurred, before, raw, after, weights, wzs, wyx, known):
+def first_adjoint(groups, current, blurred, befores, raw, afters, weights, wzs, wyx, known):
     planes, rows, cols = current.shape
-    current = current.reshape(planes * rows, cols)
-    out, sums = call(
-        first_adjoint_kernel,
-        [pltpu.VMEM(current.shape, F32), pltpu.VMEM(known.shape, F32)],
-        [wzs],
-        [current, blurred, before, raw, after, *weights, wyx, known],
-        adjoint_scratch(planes, rows, cols),
-        "adjoint",
-        10**10,
-    )
-    return out.reshape(planes, rows, cols), sums
-
-
-def full_iteration(parity, slabs, before, raw, after, weights, adjoint_weights):
+    shared = (raw, blurred, *weights)
+    scratch = adjoint_scratch(planes, rows, cols)
+    acc = pltpu.VMEM((planes * 8, rows // 8 * cols), F32)
+    halos = [pltpu.VMEM((len(g), planes, 2 * rows, cols), F32) for g in groups]
+    kernel = functools.partial(early_adjoint_kernel, groups[0])
+    arrays = [befores[0], afters[0], *shared]
+    partial, early = call(kernel, [acc, halos[0]], [], arrays, scratch, "early_adjoint", 10**10)
+    kernel = functools.partial(late_adjoint_kernel, groups[1])
+    arrays = [befores[1], afters[1], *shared, partial, current, wyx, known]
+    outs = [pltpu.VMEM(current.shape, F32), pltpu.VMEM(known.shape, F32), halos[1]]
+    out, sums, late = call(kernel, outs, [wzs], arrays, scratch + [acc], "late_adjoint", 10**10)
+    return out, sums, (early, late)
+
+
+def full_iteration(parity, slabs, halos, raw, weights, adjoint_weights):
     planes, rows, cols = slabs[0].shape
     views = raw.shape[0]
-    slabs = [s.reshape(-1, cols) if i == 2 else s for i, s in enumerate(slabs)]
     scratch = [
         pltpu.VMEM((views, planes, 3 * rows, 2 * cols), BF16),
         pltpu.VMEM((views, planes, 3 * rows, cols), F32),
     ]
     return call(
         iteration_kernel,
-        pltpu.VMEM((planes * rows, cols), F32),
+        pltpu.VMEM((planes, rows, cols), F32),
         [parity],
-        [*slabs, before, raw, after, *weights, *adjoint_weights],
-        scratch + adjoint_scratch(planes, rows, cols),
+        [*slabs, *halos, raw, *weights, *adjoint_weights],
+        scratch + adjoint_scratch(planes, rows, cols) + [pltpu.VMEM((planes * 8, rows // 8 * cols), F32)],
         "iteration",
         2 * 10**10,
     )
@@ -392,9 +413,11 @@
     parity = (place % 2).reshape(1)
 
     far = two_slabs_away(estimate, count)
-    last, leading = packed(raw, taps.shape[2] // 2)
-    before = lax.ppermute(last, "slab", up)
-    after = lax.ppermute(leading, "slab", down)
+    margin = taps.shape[2] // 2
+    groups = (range(0, 2 * views // 3), range(2 * views // 3, views))
+    edges = [packed(raw, g, margin) for g in groups]
+    befores = [lax.ppermute(edges[0][0], "slab", up)]
+    afters = [lax.ppermute(edges[0][1], "slab", down)]
 
     wzs = tap_sums(taps[:, 0], 0, planes, planes)
     wy_sums = tap_sums(taps[:, 1], place * rows, rows, count * rows)
@@ -405,7 +428,12 @@
 
     slabs = with_near(estimate, *far, parity, count)
     blurred, known = forward(parity, slabs, forward_weights, raw, wzs, wyx)
-    current, sums = first_adjoint(estimate, blurred, before, raw, after, adjoint_weights, wzs, wyx, known)
+    last, leading, known = lax.optimization_barrier((*edges[1], known))
+    befores.append(lax.ppermute(last, "slab", up))
+    afters.append(lax.ppermute(leading, "slab", down))
+    current, sums, halos = first_adjoint(
+        groups, estimate, blurred, befores, raw, afters, adjoint_weights, wzs, wyx, known
+    )
 
     far = two_slabs_away(current, count)
     bits = [1 << b for b in range(count.bit_length() - 1)]
@@ -417,10 +445,10 @@
         elif r < len(rounds) - 1:
             sums = sums + sum(others)
     slabs = with_near(current, *far, parity, count)
-    current = full_iteration(parity, slabs, before, raw, after, forward_weights, adjoint_weights)
+    current = full_iteration(parity, slabs, halos, raw, forward_weights, adjoint_weights)
     out = jax.ShapeDtypeStruct(current.shape, F32)
     scaled = functools.partial(scaled_kernel, views)
-    return call(scaled, out, [], [current, sums, others[0]], [], "scaled", 10**5).reshape(estimate.shape)
+    return call(scaled, out, [], [current, sums, others[0]], [], "scaled", 10**5)
 
 
 def solution(mesh):

time: 85.8 us -> 87.9 us (1.024)
  waiting for transfers between devices: 6.45 us -> 13.5 us
  Pallas kernels: 31.3 us -> 28.8 us
  starting transfers between devices: 45.4 us -> 42.9 us
    ppermute x4, starting transfers between devices: 31.2 us -> 21.2 us  [two_slabs_away(): return (lax.ppermute(value, 'slab', up), lax.ppermute(value, 'slab', down))]
    ppermute x5, starting transfers between devices: 7.34 us -> 15.1 us  [per_device(): lax.ppermute(sums, 'slab', [(i, i ^ d) for i in range(count)])]
    ppermute x4, waiting for transfers between devices: 0.01 us -> 5.33 us  [two_slabs_away(): return (lax.ppermute(value, 'slab', up), lax.ppermute(value, 'slab', down))]
    ppermute x2, starting transfers between devices: 2.86 us -> 0.14 us  [with_near(): near = lax.ppermute(passed, 'slab', swap)]
    pallas_call x6 -> x8, Pallas kernels: 31.3 us -> 28.8 us  [call(): pl.pallas_call(kernel, out_shape=outs, in_specs=[pl.BlockSpec(memory_spac...]
    ppermute x2 -> x4, starting transfers between devices: 3.99 us -> 6.52 us  [the longest x1 2.43 us: per_device(): befores.append(lax.ppermute(last, 'slab', up))]
    unnamed x9 -> x7, local copies, waits for them, and re-layouts: 1.42 us -> 0.01 us
    slice x0 -> x2, local copies, waits for them, and re-layouts: none -> 1.34 us  [packed(): raw[chosen[0]:chosen[-1] + 1].reshape(len(chosen) * planes, rows, cols)]
  transfers between devices with their start and end apart: 13 -> 15, of which waited for: 4 -> 5; matrix products, arithmetic and copies ran while one was open for 1% -> 2% of each run, Pallas kernels for 29% -> 29%
where the time goes in v10:
time: 87.9 us; the launch traced here: 87.5 us
  starting transfers between devices  42.9 us (49%)
  Pallas kernels  28.8 us (33%)
  waiting for transfers between devices  13.5 us (15%)
  local copies, waits for them, and re-layouts  1.37 us (2%)
    pallas_call x8, Pallas kernels, call(): pl.pallas_call(kernel, out_shape=outs, in_specs=[pl.BlockSpec(memory_spac...  28.8 us
    ppermute x4, starting transfers between devices, two_slabs_away(): return (lax.ppermute(value, 'slab', up), lax.ppermute(value, 'slab', down))  21.2 us
    ppermute x5, starting transfers between devices, per_device(): lax.ppermute(sums, 'slab', [(i, i ^ d) for i in range(count)])  15.1 us
    ppermute x5, waiting for transfers between devices, per_device(): lax.ppermute(sums, 'slab', [(i, i ^ d) for i in range(count)])  6.33 us
    ppermute x4, waiting for transfers between devices, two_slabs_away(): return (lax.ppermute(value, 'slab', up), lax.ppermute(value, 'slab', down))  5.33 us
    ppermute x1, starting transfers between devices, per_device(): befores.append(lax.ppermute(last, 'slab', up))  2.43 us
    ppermute x2, waiting for transfers between devices, with_near(): near = lax.ppermute(passed, 'slab', swap)  1.82 us
  transfers between devices with their start and end apart: 15, of which 5 were waited for; matrix products, arithmetic and copies ran while one was open for 2% of the time, Pallas kernels for 29%

profile of v10, /device:TPU:0, one launch (start us, length us, event | category | flops | bytes accessed | tf_op | source)
XLA Modules:
  0.0 87.5 jit_solution(6323779197302741674)
XLA Ops:
  0.0 5.0 %collective-permute-start = (f32[32,16,128]{2,1,0:T(8,128)}, f32[32,16,128]{2,1,0:T(8,128)S(1)}, u32[]{:S(2)}, u32[]{:S(2)}) collective-permute-start(f32[32,16,128]{2,1,0:T(8,128)} %current.1), channel_id=1, source_target_pairs={{0,2},{1,3},{2,4},{3,5},{4,6},{5,7},{6,8},{7,9},{8,10},{9,11},{10,... | collective-permute-start | bytes 786440 | tf_op jit(solution)/shard_map/ppermute | solution.py:388
  5.0 1.3 %collective-permute-start.1 = (f32[32,16,128]{2,1,0:T(8,128)}, f32[32,16,128]{2,1,0:T(8,128)S(1)}, u32[]{:S(2)}, u32[]{:S(2)}) collective-permute-start(f32[32,16,128]{2,1,0:T(8,128)} %current.1), channel_id=1, source_target_pairs={{2,0},{3,1},{4,2},{5,3},{6,4},{7,5},{8,6},{9,7},{10,8},{11,9},{12,... | collective-permute-start | bytes 786440 | tf_op jit(solution)/shard_map/ppermute | solution.py:388
  6.3 1.3 %slice.19 = f32[4,32,16,128]{3,2,1,0:T(8,128)S(1)} slice(f32[6,32,16,128]{3,2,1,0:T(8,128)} %raw.7), slice={[0:4], [0:32], [0:16], [0:128]} | slice | bytes 2097152 | tf_op jit(solution)/shard_map/slice | solution.py:322
  7.6 1.6 %pack.3 = (f32[1920,128]{1,0:T(8,128)}, f32[1920,128]{1,0:T(8,128)}) custom-call(f32[128,16,128]{2,1,0:T(8,128)S(1)} %bitcast.16), custom_call_target="tpu_custom_call" | custom-call | flops 1000000 | bytes 10000000 | tf_op jit(solution)/shard_map/pack/pallas_call | solution.py:95
  9.3 1.5 %collective-permute-start.5 = (f32[1920,128]{1,0:T(8,128)}, f32[1920,128]{1,0:T(8,128)S(1)}, u32[]{:S(2)}, u32[]{:S(2)}) collective-permute-start(f32[1920,128]{1,0:T(8,128)} %get-tuple-element.40), channel_id=1, source_target_pairs={{0,1},{1,2},{2,3},{3,4},{4,5},{5,6},{6,7},{7,8},{8,9},{9,10},{10,1... | collective-permute-start | bytes 2949128 | tf_op jit(solution)/shard_map/ppermute | solution.py:419
  10.8 1.3 %collective-permute-start.6 = (f32[1920,128]{1,0:T(8,128)}, f32[1920,128]{1,0:T(8,128)}, u32[]{:S(2)}, u32[]{:S(2)}) collective-permute-start(f32[1920,128]{1,0:T(8,128)} %get-tuple-element.41), channel_id=1, source_target_pairs={{1,0},{2,1},{3,2},{4,3},{5,4},{6,5},{7,6},{8,7},{9,8},{10,9},{11,1... | collective-permute-start | bytes 2949128 | tf_op jit(solution)/shard_map/ppermute | solution.py:420
  12.2 0.1 fusion.11
  12.2 0.1 multiply_reduce_fusion.2
  12.3 5.3 %collective-permute-done.far_before = f32[32,16,128]{2,1,0:T(8,128)S(1)} collective-permute-done((f32[32,16,128]{2,1,0:T(8,128)}, f32[32,16,128]{2,1,0:T(8,128)S(1)}, u32[]{:S(2)}, u32[]{:S(2)}) %collective-permute-start) | collective-permute-done | bytes 262176 | tf_op jit(solution)/shard_map/ppermute | solution.py:388
  17.7 0.1 collective-permute-start.2
  17.8 0.1 multiply_reduce_fusion
  17.9 0.1 broadcast_multiply_fusion.wyx
  18.0 0.1 multiply_reduce_fusion.1.wzs
  18.2 0.2 pack.2
  18.4 3.7 %weights.1 = (bf16[288,240]{1,0:T(8,128)(2,1)S(1)}, bf16[6,256,256]{2,1,0:T(8,128)(2,1)S(1)}, bf16[6,256,768]{2,1,0:T(8,128)(2,1)S(1)}, bf16[6,32,96]{2,1,0:T(8,...) custom-call(f32[6,3,31]{2,1,0:T(4,128)S(1)} %copy-done.2), custom_call_target="tpu_custom_call" | custom-call | flops 10000000 | bytes 10000000 | tf_op jit(solution)/shard_map/weights/pallas_call | solution.py:95
  22.1 6.9 %forward.1 = (f32[6,32,48,128]{3,2,1,0:T(8,128)S(1)}, f32[24,128]{1,0:T(8,128)S(1)}) custom-call(s32[1]{0:T(128)} %bitcast.parity, f32[6,32]{1,0:T(8,128)S(1)} %multiply_reduce_fusion.1.wzs, f32[32,16,128]{2,1,0:T(8,128)S(1)} %collective-permute-done.far_before, f32[2,32,16,128]{3,2,1,0:T(8,128)S(1)} %collective-permute-done.2.near, ...), custom_call_target="tpu_custom_call" | custom-call | flops 10000000000 | bytes 10000000 | tf_op jit(solution)/shard_map/forward/pallas_call | solution.py:95
  29.0 2.4 %collective-permute-start.3 = (f32[960,128]{1,0:T(8,128)S(1)}, f32[960,128]{1,0:T(8,128)S(1)}, u32[]{:S(2)}, u32[]{:S(2)}) collective-permute-start(f32[960,128]{1,0:T(8,128)S(1)} %get-tuple-element.34), channel_id=1, source_target_pairs={{0,1},{1,2},{2,3},{3,4},{4,5},{5,6},{6,7},{7,8},{8,9},{9,10},{10,1... | collective-permute-start | bytes 1474568 | tf_op jit(solution)/shard_map/ppermute | solution.py:432
  31.4 1.3 %collective-permute-start.4 = (f32[960,128]{1,0:T(8,128)S(1)}, f32[960,128]{1,0:T(8,128)S(1)}, u32[]{:S(2)}, u32[]{:S(2)}) collective-permute-start(f32[960,128]{1,0:T(8,128)S(1)} %get-tuple-element.35), channel_id=1, source_target_pairs={{1,0},{2,1},{3,2},{4,3},{5,4},{6,5},{7,6},{8,7},{9,8},{10,9},{11,1... | collective-permute-start | bytes 1474568 | tf_op jit(solution)/shard_map/ppermute | solution.py:433
  32.7 4.2 %early_adjoint.1 = (f32[256,256]{1,0:T(8,128)S(1)}, f32[4,32,32,128]{3,2,1,0:T(8,128)S(1)}) custom-call(f32[1920,128]{1,0:T(8,128)S(1)} %collective-permute-done.5.before, f32[1920,128]{1,0:T(8,128)} %collective-permute-done.6.after, f32[6,32,16,128]{3,2,1,0:T(8,128)S(1)} %copy-done, f32[6,32,48,128]{3,2,1,0:T(8,128)S(1)} %get-tuple-element.36.blurred, ...), custom_call_target="tpu_custom_call" | custom-call | flops 10000000000 | bytes 10000000 | tf_op jit(solution)/shard_map/early_adjoint/pallas_call | solution.py:95
  37.0 2.2 %late_adjoint.1 = (f32[32,16,128]{2,1,0:T(8,128)S(1)}, f32[24,128]{1,0:T(8,128)S(1)}, f32[2,32,32,128]{3,2,1,0:T(8,128)S(1)}) custom-call(f32[6,32]{1,0:T(8,128)S(1)} %multiply_reduce_fusion.1.wzs, f32[960,128]{1,0:T(8,128)S(1)} %collective-permute-done.3.before, f32[960,128]{1,0:T(8,128)S(1)} %collective-permute-done.4.after, ...), custom_call_target="tpu_custom_call" | custom-call | flops 10000000000 | bytes 10000000 | tf_op jit(solution)/shard_map/late_adjoint/pallas_call | solution.py:95
  39.1 13.4 %collective-permute-start.7 = (f32[32,16,128]{2,1,0:T(8,128)S(1)}, f32[32,16,128]{2,1,0:T(8,128)S(1)}, u32[]{:S(2)}, u32[]{:S(2)}) collective-permute-start(f32[32,16,128]{2,1,0:T(8,128)S(1)} %get-tuple-element.44.own), channel_id=1, source_target_pairs={{0,2},{1,3},{2,4},{3,5},{4,6},{5,7},{6,8},{7,9},{8,10},{9,11},{10,... | collective-permute-start | bytes 786440 | tf_op jit(solution)/shard_map/ppermute | solution.py:388
  52.5 1.5 %collective-permute-start.8 = (f32[32,16,128]{2,1,0:T(8,128)S(1)}, f32[32,16,128]{2,1,0:T(8,128)S(1)}, u32[]{:S(2)}, u32[]{:S(2)}) collective-permute-start(f32[32,16,128]{2,1,0:T(8,128)S(1)} %get-tuple-element.44.own), channel_id=1, source_target_pairs={{2,0},{3,1},{4,2},{5,3},{6,4},{7,5},{8,6},{9,7},{10,8},{11,9},{12,... | collective-permute-start | bytes 786440 | tf_op jit(solution)/shard_map/ppermute | solution.py:388
  54.0 7.6 %collective-permute-start.9 = (f32[24,128]{1,0:T(8,128)S(1)}, f32[24,128]{1,0:T(8,128)S(1)}, u32[]{:S(2)}, u32[]{:S(2)}) collective-permute-start(f32[24,128]{1,0:T(8,128)S(1)} %get-tuple-element.45), channel_id=1, source_target_pairs={{0,1},{1,0},{2,3},{3,2},{4,5},{5,4},{6,7},{7,6},{8,9},{9,8},{10,11... | collective-permute-start | bytes 36872 | tf_op jit(solution)/shard_map/ppermute | solution.py:442
  61.6 0.8 collective-permute-done.9
  62.5 4.8 %collective-permute-start.10 = (f32[24,128]{1,0:T(8,128)S(1)}, f32[24,128]{1,0:T(8,128)S(1)}, u32[]{:S(2)}, u32[]{:S(2)}) collective-permute-start(f32[24,128]{1,0:T(8,128)S(1)} %add.66), channel_id=1, source_target_pairs={{0,4},{1,5},{2,6},{3,7},{4,0},{5,1},{6,2},{7,3},{8,12},{9,13},{10,... | collective-permute-start | bytes 36872 | tf_op jit(solution)/shard_map/ppermute | solution.py:442
  67.3 2.6 %collective-permute-start.11 = (f32[24,128]{1,0:T(8,128)S(1)}, f32[24,128]{1,0:T(8,128)S(1)}, u32[]{:S(2)}, u32[]{:S(2)}) collective-permute-start(f32[24,128]{1,0:T(8,128)S(1)} %add.66), channel_id=1, source_target_pairs={{0,8},{1,9},{2,10},{3,11},{4,12},{5,13},{6,14},{7,15},{8,0},{9,1},... | collective-permute-start | bytes 36872 | tf_op jit(solution)/shard_map/ppermute | solution.py:442
  69.9 2.3 %collective-permute-done.11 = f32[24,128]{1,0:T(8,128)S(1)} collective-permute-done((f32[24,128]{1,0:T(8,128)S(1)}, f32[24,128]{1,0:T(8,128)S(1)}, u32[]{:S(2)}, u32[]{:S(2)}) %collective-permute-start.11) | collective-permute-done | bytes 12320 | tf_op jit(solution)/shard_map/ppermute | solution.py:442
  72.2 3.2 %collective-permute-done.12 = f32[24,128]{1,0:T(8,128)S(1)} collective-permute-done((f32[24,128]{1,0:T(8,128)S(1)}, f32[24,128]{1,0:T(8,128)S(1)}, u32[]{:S(2)}, u32[]{:S(2)}) %collective-permute-start.12) | collective-permute-done | bytes 12320 | tf_op jit(solution)/shard_map/ppermute | solution.py:442
  75.6 0.1 collective-permute-start.14
  75.6 1.8 %collective-permute-done.13.near = f32[2,32,16,128]{3,2,1,0:T(8,128)S(1)} collective-permute-done((f32[2,32,16,128]{3,2,1,0:T(8,128)S(1)}, f32[2,32,16,128]{3,2,1,0:T(8,128)S(1)}, u32[]{:S(2)}, u32[]{:S(2)}) %collective-permute-start.13) | collective-permute-done | bytes 524320 | tf_op jit(solution)/shard_map/ppermute | solution.py:394
  77.5 9.2 %iteration.1.values = f32[32,16,128]{2,1,0:T(8,128)S(1)} custom-call(s32[1]{0:T(128)} %bitcast.parity, f32[32,16,128]{2,1,0:T(8,128)S(1)} %collective-permute-done.7.far_before, f32[2,32,16,128]{3,2,1,0:T(8,128)S(1)} %collective-permute-done.13.near, f32[32,16,128]{2,1,0:T(8,128)S(1)} %get-tuple-element.44.own, ...), custom_call_target="tpu_custom_call" | custom-call | flops 20000000000 | bytes 10000000 | tf_op jit(solution)/shard_map/iteration/pallas_call | solution.py:95
  86.7 0.8 scaled.1
  (31 shorter events, 0.3 us)
Async XLA Ops:
  0.0 17.7 %copy-start.1 = (f32[32,16,128]{2,1,0:T(8,128)S(1)}, f32[32,16,128]{2,1,0:T(8,128)}, u32[]{:S(2)}) copy-start(f32[32,16,128]{2,1,0:T(8,128)} %current.1) | copy-start | bytes 786436
  0.0 18.1 %copy-start = (f32[6,32,16,128]{3,2,1,0:T(8,128)S(1)}, f32[6,32,16,128]{3,2,1,0:T(8,128)}, u32[]{:S(2)}) copy-start(f32[6,32,16,128]{3,2,1,0:T(8,128)} %raw.7) | copy-start | bytes 4718596
  0.0 12.1 %copy-start.2 = (f32[6,3,31]{2,1,0:T(4,128)S(1)}, f32[6,3,31]{2,1,0:T(4,128)}, u32[]{:S(2)}) copy-start(f32[6,3,31]{2,1,0:T(4,128)} %taps_ref.1) | copy-start | bytes 6700
  0.0 17.6 %collective-permute-start = (f32[32,16,128]{2,1,0:T(8,128)}, f32[32,16,128]{2,1,0:T(8,128)S(1)}, u32[]{:S(2)}, u32[]{:S(2)}) collective-permute-start(f32[32,16,128]{2,1,0:T(8,128)} %current.1), channel_id=1, source_target_pairs={{0,2},{1,3},{2,4},{3,5},{4,6},{5,7},{6,8},{7,9},{8,10},{9,11},{10,... | collective-permute-start | bytes 786440 | tf_op jit(solution)/shard_map/ppermute | solution.py:388
  5.0 12.6 %collective-permute-start.1 = (f32[32,16,128]{2,1,0:T(8,128)}, f32[32,16,128]{2,1,0:T(8,128)S(1)}, u32[]{:S(2)}, u32[]{:S(2)}) collective-permute-start(f32[32,16,128]{2,1,0:T(8,128)} %current.1), channel_id=1, source_target_pairs={{2,0},{3,1},{4,2},{5,3},{6,4},{7,5},{8,6},{9,7},{10,8},{11,9},{12,... | collective-permute-start | bytes 786440 | tf_op jit(solution)/shard_map/ppermute | solution.py:388
  9.3 23.4 %collective-permute-start.5 = (f32[1920,128]{1,0:T(8,128)}, f32[1920,128]{1,0:T(8,128)S(1)}, u32[]{:S(2)}, u32[]{:S(2)}) collective-permute-start(f32[1920,128]{1,0:T(8,128)} %get-tuple-element.40), channel_id=1, source_target_pairs={{0,1},{1,2},{2,3},{3,4},{4,5},{5,6},{6,7},{7,8},{8,9},{9,10},{10,1... | collective-permute-start | bytes 2949128 | tf_op jit(solution)/shard_map/ppermute | solution.py:419
  10.8 21.9 %collective-permute-start.6 = (f32[1920,128]{1,0:T(8,128)}, f32[1920,128]{1,0:T(8,128)}, u32[]{:S(2)}, u32[]{:S(2)}) collective-permute-start(f32[1920,128]{1,0:T(8,128)} %get-tuple-element.41), channel_id=1, source_target_pairs={{1,0},{2,1},{3,2},{4,3},{5,4},{6,5},{7,6},{8,7},{9,8},{10,9},{11,1... | collective-permute-start | bytes 2949128 | tf_op jit(solution)/shard_map/ppermute | solution.py:420
  17.7 4.3 %collective-permute-start.2 = (f32[2,32,16,128]{3,2,1,0:T(8,128)S(1)}, f32[2,32,16,128]{3,2,1,0:T(8,128)S(1)}, u32[]{:S(2)}, u32[]{:S(2)}) collective-permute-start(f32[2,32,16,128]{3,2,1,0:T(8,128)S(1)} %pad_maximum_fusion), channel_id=1, source_target_pairs={{0,1},{1,0},{2,3},{3,2},{4,5},{5,4},{6,7},{7,6},{8,9},{9,8},{10,11... | collective-permute-start | bytes 1572872 | tf_op jit(solution)/shard_map/ppermute | solution.py:394
  29.0 8.0 %collective-permute-start.3 = (f32[960,128]{1,0:T(8,128)S(1)}, f32[960,128]{1,0:T(8,128)S(1)}, u32[]{:S(2)}, u32[]{:S(2)}) collective-permute-start(f32[960,128]{1,0:T(8,128)S(1)} %get-tuple-element.34), channel_id=1, source_target_pairs={{0,1},{1,2},{2,3},{3,4},{4,5},{5,6},{6,7},{7,8},{8,9},{9,10},{10,1... | collective-permute-start | bytes 1474568 | tf_op jit(solution)/shard_map/ppermute | solution.py:432
  31.4 5.5 %collective-permute-start.4 = (f32[960,128]{1,0:T(8,128)S(1)}, f32[960,128]{1,0:T(8,128)S(1)}, u32[]{:S(2)}, u32[]{:S(2)}) collective-permute-start(f32[960,128]{1,0:T(8,128)S(1)} %get-tuple-element.35), channel_id=1, source_target_pairs={{1,0},{2,1},{3,2},{4,3},{5,4},{6,5},{7,6},{8,7},{9,8},{10,9},{11,1... | collective-permute-start | bytes 1474568 | tf_op jit(solution)/shard_map/ppermute | solution.py:433
  39.1 36.2 %collective-permute-start.7 = (f32[32,16,128]{2,1,0:T(8,128)S(1)}, f32[32,16,128]{2,1,0:T(8,128)S(1)}, u32[]{:S(2)}, u32[]{:S(2)}) collective-permute-start(f32[32,16,128]{2,1,0:T(8,128)S(1)} %get-tuple-element.44.own), channel_id=1, source_target_pairs={{0,2},{1,3},{2,4},{3,5},{4,6},{5,7},{6,8},{7,9},{8,10},{9,11},{10,... | collective-permute-start | bytes 786440 | tf_op jit(solution)/shard_map/ppermute | solution.py:388
  52.5 22.8 %collective-permute-start.8 = (f32[32,16,128]{2,1,0:T(8,128)S(1)}, f32[32,16,128]{2,1,0:T(8,128)S(1)}, u32[]{:S(2)}, u32[]{:S(2)}) collective-permute-start(f32[32,16,128]{2,1,0:T(8,128)S(1)} %get-tuple-element.44.own), channel_id=1, source_target_pairs={{2,0},{3,1},{4,2},{5,3},{6,4},{7,5},{8,6},{9,7},{10,8},{11,9},{12,... | collective-permute-start | bytes 786440 | tf_op jit(solution)/shard_map/ppermute | solution.py:388
  54.0 8.4 %collective-permute-start.9 = (f32[24,128]{1,0:T(8,128)S(1)}, f32[24,128]{1,0:T(8,128)S(1)}, u32[]{:S(2)}, u32[]{:S(2)}) collective-permute-start(f32[24,128]{1,0:T(8,128)S(1)} %get-tuple-element.45), channel_id=1, source_target_pairs={{0,1},{1,0},{2,3},{3,2},{4,5},{5,4},{6,7},{7,6},{8,9},{9,8},{10,11... | collective-permute-start | bytes 36872 | tf_op jit(solution)/shard_map/ppermute | solution.py:442
  62.5 7.4 %collective-permute-start.10 = (f32[24,128]{1,0:T(8,128)S(1)}, f32[24,128]{1,0:T(8,128)S(1)}, u32[]{:S(2)}, u32[]{:S(2)}) collective-permute-start(f32[24,128]{1,0:T(8,128)S(1)} %add.66), channel_id=1, source_target_pairs={{0,4},{1,5},{2,6},{3,7},{4,0},{5,1},{6,2},{7,3},{8,12},{9,13},{10,... | collective-permute-start | bytes 36872 | tf_op jit(solution)/shard_map/ppermute | solution.py:442
  67.3 4.9 %collective-permute-start.11 = (f32[24,128]{1,0:T(8,128)S(1)}, f32[24,128]{1,0:T(8,128)S(1)}, u32[]{:S(2)}, u32[]{:S(2)}) collective-permute-start(f32[24,128]{1,0:T(8,128)S(1)} %add.66), channel_id=1, source_target_pairs={{0,8},{1,9},{2,10},{3,11},{4,12},{5,13},{6,14},{7,15},{8,0},{9,1},... | collective-permute-start | bytes 36872 | tf_op jit(solution)/shard_map/ppermute | solution.py:442
  69.9 5.5 %collective-permute-start.12 = (f32[24,128]{1,0:T(8,128)S(1)}, f32[24,128]{1,0:T(8,128)S(1)}, u32[]{:S(2)}, u32[]{:S(2)}) collective-permute-start(f32[24,128]{1,0:T(8,128)S(1)} %add.66), channel_id=1, source_target_pairs={{0,12},{1,13},{2,14},{3,15},{4,8},{5,9},{6,10},{7,11},{8,4},{9,5},... | collective-permute-start | bytes 36872 | tf_op jit(solution)/shard_map/ppermute | solution.py:442
  75.5 2.0 %collective-permute-start.13 = (f32[2,32,16,128]{3,2,1,0:T(8,128)S(1)}, f32[2,32,16,128]{3,2,1,0:T(8,128)S(1)}, u32[]{:S(2)}, u32[]{:S(2)}) collective-permute-start(f32[2,32,16,128]{3,2,1,0:T(8,128)S(1)} %pad_maximum_fusion.1), channel_id=1, source_target_pairs={{0,1},{1,0},{2,3},{3,2},{4,5},{5,4},{6,7},{7,6},{8,9},{9,8},{10,11... | collective-permute-start | bytes 1572872 | tf_op jit(solution)/shard_map/ppermute | solution.py:394
  75.6 11.1 %collective-permute-start.14 = (f32[24,128]{1,0:T(8,128)S(1)}, f32[24,128]{1,0:T(8,128)S(1)}, u32[]{:S(2)}, u32[]{:S(2)}) collective-permute-start(f32[24,128]{1,0:T(8,128)S(1)} %add_add_fusion.part), channel_id=1, source_target_pairs={{0,2},{1,3},{2,0},{3,1},{4,6},{5,7},{6,4},{7,5},{8,10},{9,11},{10,... | collective-permute-start | bytes 36872 | tf_op jit(solution)/shard_map/ppermute | solution.py:442

commit v11 on v10

--- a/solution.py
+++ b/solution.py
@@ -416,21 +416,24 @@
     margin = taps.shape[2] // 2
     groups = (range(0, 2 * views // 3), range(2 * views // 3, views))
     edges = [packed(raw, g, margin) for g in groups]
-    befores = [lax.ppermute(edges[0][0], "slab", up)]
-    afters = [lax.ppermute(edges[0][1], "slab", down)]
+    forward_weights, adjoint_weights = make_weights(taps, planes, rows, cols)
+    first_edges, forward_weights, adjoint_weights = lax.optimization_barrier(
+        (edges[0], forward_weights, adjoint_weights)
+    )
+    befores = [lax.ppermute(first_edges[0], "slab", up)]
+    afters = [lax.ppermute(first_edges[1], "slab", down)]
 
     wzs = tap_sums(taps[:, 0], 0, planes, planes)
     wy_sums = tap_sums(taps[:, 1], place * rows, rows, count * rows)
     wx_sums = tap_sums(taps[:, 2], 0, cols, cols)
     wyx = wy_sums[:, :, None] * wx_sums[:, None, :]
 
-    forward_weights, adjoint_weights = make_weights(taps, planes, rows, cols)
-
-    slabs = with_near(estimate, *far, parity, count)
-    blurred, known = forward(parity, slabs, forward_weights, raw, wzs, wyx)
-    last, leading, known = lax.optimization_barrier((*edges[1], known))
+    far_before, near, own, far_after = with_near(estimate, *far, parity, count)
+    near, last, leading = lax.optimization_barrier((near, *edges[1]))
     befores.append(lax.ppermute(last, "slab", up))
     afters.append(lax.ppermute(leading, "slab", down))
+    slabs = (far_before, near, own, far_after)
+    blurred, known = forward(parity, slabs, forward_weights, raw, wzs, wyx)
     current, sums, halos = first_adjoint(
         groups, estimate, blurred, befores, raw, afters, adjoint_weights, wzs, wyx, known
     )

time: 87.9 us -> 86.8 us (0.987)
  waiting for transfers between devices: 13.5 us -> 6.22 us
  local copies, waits for them, and re-layouts: 1.37 us -> 7.61 us
    ppermute x5, starting transfers between devices: 15.1 us -> 7.8 us  [per_device(): lax.ppermute(sums, 'slab', [(i, i ^ d) for i in range(count)])]
    unnamed x7 -> x23, local copies, waits for them, and re-layouts: 0.01 us -> 5.69 us
    ppermute x4, waiting for transfers between devices: 5.33 us -> 0.01 us  [two_slabs_away(): return (lax.ppermute(value, 'slab', up), lax.ppermute(value, 'slab', down))]
    ppermute x4, starting transfers between devices: 21.2 us -> 24.7 us  [two_slabs_away(): return (lax.ppermute(value, 'slab', up), lax.ppermute(value, 'slab', down))]
    ppermute x2, starting transfers between devices: 0.14 us -> 3.04 us  [with_near(): near = lax.ppermute(passed, 'slab', swap)]
    ppermute x5, waiting for transfers between devices: 6.33 us -> 5.2 us  [per_device(): lax.ppermute(sums, 'slab', [(i, i ^ d) for i in range(count)])]
    ppermute x2, starting transfers between devices: 2.8 us -> 3.68 us  [the longest x1 2.4 us: per_device(): befores = [lax.ppermute(first_edges[0], 'slab', up)]]
  transfers between devices with their start and end apart: 15 -> 15, of which waited for: 5 -> 4; matrix products, arithmetic and copies ran while one was open for 2% -> 4% of each run, Pallas kernels for 29% -> 30%
where the time goes in v11:
time: 86.8 us; the launch traced here: 86.4 us
  starting transfers between devices  42.8 us (49%)
  Pallas kernels  28.8 us (33%)
  local copies, waits for them, and re-layouts  7.61 us (9%)
  waiting for transfers between devices  6.22 us (7%)
    pallas_call x8, Pallas kernels, call(): pl.pallas_call(kernel, out_shape=outs, in_specs=[pl.BlockSpec(memory_spac...  28.8 us
    ppermute x4, starting transfers between devices, two_slabs_away(): return (lax.ppermute(value, 'slab', up), lax.ppermute(value, 'slab', down))  24.7 us
    ppermute x5, starting transfers between devices, per_device(): lax.ppermute(sums, 'slab', [(i, i ^ d) for i in range(count)])  7.8 us
    unnamed x23, local copies, waits for them, and re-layouts  5.69 us
    ppermute x5, waiting for transfers between devices, per_device(): lax.ppermute(sums, 'slab', [(i, i ^ d) for i in range(count)])  5.2 us
    ppermute x2, starting transfers between devices, with_near(): near = lax.ppermute(passed, 'slab', swap)  3.04 us
    ppermute x1, starting transfers between devices, per_device(): befores = [lax.ppermute(first_edges[0], 'slab', up)]  2.4 us
    ppermute x1, starting transfers between devices, per_device(): befores.append(lax.ppermute(last, 'slab', up))  2.3 us
  transfers between devices with their start and end apart: 15, of which 4 were waited for; matrix products, arithmetic and copies ran while one was open for 4% of the time, Pallas kernels for 30%

profile of v11, /device:TPU:0, one launch (start us, length us, event | category | flops | bytes accessed | tf_op | source)
XLA Modules:
  0.0 86.4 jit_solution(6441279321976602157)
XLA Ops:
  0.0 5.0 %collective-permute-start.1 = (f32[32,16,128]{2,1,0:T(8,128)}, f32[32,16,128]{2,1,0:T(8,128)S(1)}, u32[]{:S(2)}, u32[]{:S(2)}) collective-permute-start(f32[32,16,128]{2,1,0:T(8,128)} %current.1), channel_id=1, source_target_pairs={{0,2},{1,3},{2,4},{3,5},{4,6},{5,7},{6,8},{7,9},{8,10},{9,11},{10,... | collective-permute-start | bytes 786440 | tf_op jit(solution)/shard_map/ppermute | solution.py:388
  5.0 1.3 %collective-permute-start = (f32[32,16,128]{2,1,0:T(8,128)}, f32[32,16,128]{2,1,0:T(8,128)S(1)}, u32[]{:S(2)}, u32[]{:S(2)}) collective-permute-start(f32[32,16,128]{2,1,0:T(8,128)} %current.1), channel_id=1, source_target_pairs={{2,0},{3,1},{4,2},{5,3},{6,4},{7,5},{8,6},{9,7},{10,8},{11,9},{12,... | collective-permute-start | bytes 786440 | tf_op jit(solution)/shard_map/ppermute | solution.py:388
  6.3 1.3 %slice.17 = f32[4,32,16,128]{3,2,1,0:T(8,128)S(1)} slice(f32[6,32,16,128]{3,2,1,0:T(8,128)} %raw.7), slice={[0:4], [0:32], [0:16], [0:128]} | slice | bytes 2097152 | tf_op jit(solution)/shard_map/slice | solution.py:322
  7.6 1.6 %pack.3 = (f32[1920,128]{1,0:T(8,128)}, f32[1920,128]{1,0:T(8,128)S(1)}) custom-call(f32[128,16,128]{2,1,0:T(8,128)S(1)} %bitcast.16), custom_call_target="tpu_custom_call" | custom-call | flops 1000000 | bytes 10000000 | tf_op jit(solution)/shard_map/pack/pallas_call | solution.py:95
  9.2 3.7 %weights.1 = (bf16[288,240]{1,0:T(8,128)(2,1)S(1)}, bf16[6,256,256]{2,1,0:T(8,128)(2,1)S(1)}, bf16[6,256,768]{2,1,0:T(8,128)(2,1)S(1)}, bf16[6,32,96]{2,1,0:T(8,...) custom-call(f32[6,3,31]{2,1,0:T(4,128)S(1)} %copy-done.2), custom_call_target="tpu_custom_call" | custom-call | flops 10000000 | bytes 10000000 | tf_op jit(solution)/shard_map/weights/pallas_call | solution.py:95
  13.0 1.4 %copy-done.3 = bf16[6,256,768]{2,1,0:T(8,128)(2,1)} copy-done((bf16[6,256,768]{2,1,0:T(8,128)(2,1)}, bf16[6,256,768]{2,1,0:T(8,128)(2,1)S(1)}, u32[]{:S(2)}) %copy-start.3) | copy-done | bytes 2359320
  14.4 1.4 %copy-done.5 = bf16[6,256,768]{2,1,0:T(8,128)(2,1)} copy-done((bf16[6,256,768]{2,1,0:T(8,128)(2,1)}, bf16[6,256,768]{2,1,0:T(8,128)(2,1)S(1)}, u32[]{:S(2)}) %copy-start.5) | copy-done | bytes 2359320
  15.8 1.0 %copy-done.7 = bf16[6,256,256]{2,1,0:T(8,128)(2,1)} copy-done((bf16[6,256,256]{2,1,0:T(8,128)(2,1)}, bf16[6,256,256]{2,1,0:T(8,128)(2,1)S(1)}, u32[]{:S(2)}) %copy-start.7) | copy-done | bytes 786456
  16.8 1.0 %copy-done.9 = bf16[6,256,256]{2,1,0:T(8,128)(2,1)} copy-done((bf16[6,256,256]{2,1,0:T(8,128)(2,1)}, bf16[6,256,256]{2,1,0:T(8,128)(2,1)S(1)}, u32[]{:S(2)}) %copy-start.9) | copy-done | bytes 786456
  17.8 2.4 %collective-permute-start.5 = (f32[1920,128]{1,0:T(8,128)}, f32[1920,128]{1,0:T(8,128)}, u32[]{:S(2)}, u32[]{:S(2)}) collective-permute-start(f32[1920,128]{1,0:T(8,128)} %get-tuple-element.56), channel_id=1, source_target_pairs={{0,1},{1,2},{2,3},{3,4},{4,5},{5,6},{6,7},{7,8},{8,9},{9,10},{10,1... | collective-permute-start | bytes 2949128 | tf_op jit(solution)/shard_map/ppermute | solution.py:423
  20.2 1.3 %collective-permute-start.6 = (f32[1920,128]{1,0:T(8,128)S(1)}, f32[1920,128]{1,0:T(8,128)}, u32[]{:S(2)}, u32[]{:S(2)}) collective-permute-start(f32[1920,128]{1,0:T(8,128)S(1)} %get-tuple-element.57), channel_id=1, source_target_pairs={{1,0},{2,1},{3,2},{4,3},{5,4},{6,5},{7,6},{8,7},{9,8},{10,9},{11,1... | collective-permute-start | bytes 2949128 | tf_op jit(solution)/shard_map/ppermute | solution.py:424
  21.5 0.6 fusion.12
  22.1 0.8 copy.16
  23.2 3.0 %collective-permute-start.2 = (f32[2,32,16,128]{3,2,1,0:T(8,128)S(1)}, f32[2,32,16,128]{3,2,1,0:T(8,128)S(1)}, u32[]{:S(2)}, u32[]{:S(2)}) collective-permute-start(f32[2,32,16,128]{3,2,1,0:T(8,128)S(1)} %pad_maximum_fusion), channel_id=1, source_target_pairs={{0,1},{1,0},{2,3},{3,2},{4,5},{5,4},{6,7},{7,6},{8,9},{9,8},{10,11... | collective-permute-start | bytes 1572872 | tf_op jit(solution)/shard_map/ppermute | solution.py:394
  26.4 0.1 multiply_reduce_fusion.1.wzs
  26.5 0.2 pack.2
  26.7 1.0 %collective-permute-done.2.near = f32[2,32,16,128]{3,2,1,0:T(8,128)S(1)} collective-permute-done((f32[2,32,16,128]{3,2,1,0:T(8,128)S(1)}, f32[2,32,16,128]{3,2,1,0:T(8,128)S(1)}, u32[]{:S(2)}, u32[]{:S(2)}) %collective-permute-start.2) | collective-permute-done | bytes 524320 | tf_op jit(solution)/shard_map/ppermute | solution.py:394
  27.7 2.3 %collective-permute-start.3 = (f32[960,128]{1,0:T(8,128)S(1)}, f32[960,128]{1,0:T(8,128)S(1)}, u32[]{:S(2)}, u32[]{:S(2)}) collective-permute-start(f32[960,128]{1,0:T(8,128)S(1)} %get-tuple-element.38), channel_id=1, source_target_pairs={{0,1},{1,2},{2,3},{3,4},{4,5},{5,6},{6,7},{7,8},{8,9},{9,10},{10,1... | collective-permute-start | bytes 1474568 | tf_op jit(solution)/shard_map/ppermute | solution.py:433
  30.0 1.3 %collective-permute-start.4 = (f32[960,128]{1,0:T(8,128)S(1)}, f32[960,128]{1,0:T(8,128)S(1)}, u32[]{:S(2)}, u32[]{:S(2)}) collective-permute-start(f32[960,128]{1,0:T(8,128)S(1)} %get-tuple-element.39), channel_id=1, source_target_pairs={{1,0},{2,1},{3,2},{4,3},{5,4},{6,5},{7,6},{8,7},{9,8},{10,9},{11,1... | collective-permute-start | bytes 1474568 | tf_op jit(solution)/shard_map/ppermute | solution.py:434
  31.3 6.9 %forward.1 = (f32[6,32,48,128]{3,2,1,0:T(8,128)S(1)}, f32[24,128]{1,0:T(8,128)S(1)}) custom-call(s32[1]{0:T(128)} %bitcast.parity, f32[6,32]{1,0:T(8,128)S(1)} %multiply_reduce_fusion.1.wzs, f32[32,16,128]{2,1,0:T(8,128)S(1)} %collective-permute-done.1.far_before, f32[2,32,16,128]{3,2,1,0:T(8,128)S(1)} %collective-permute-done.2.near, ...), custom_call_target="tpu_custom_call" | custom-call | flops 10000000000 | bytes 10000000 | tf_op jit(solution)/shard_map/forward/pallas_call | solution.py:95
  38.3 4.4 %early_adjoint.1 = (f32[256,256]{1,0:T(8,128)S(1)}, f32[4,32,32,128]{3,2,1,0:T(8,128)S(1)}) custom-call(f32[1920,128]{1,0:T(8,128)} %collective-permute-done.5.before, f32[1920,128]{1,0:T(8,128)} %collective-permute-done.6.after, f32[6,32,16,128]{3,2,1,0:T(8,128)S(1)} %copy-done, f32[6,32,48,128]{3,2,1,0:T(8,128)S(1)} %get-tuple-element.52.blurred, ...), custom_call_target="tpu_custom_call" | custom-call | flops 10000000000 | bytes 10000000 | tf_op jit(solution)/shard_map/early_adjoint/pallas_call | solution.py:95
  42.7 2.2 %late_adjoint.1 = (f32[32,16,128]{2,1,0:T(8,128)S(1)}, f32[24,128]{1,0:T(8,128)S(1)}, f32[2,32,32,128]{3,2,1,0:T(8,128)S(1)}) custom-call(f32[6,32]{1,0:T(8,128)S(1)} %multiply_reduce_fusion.1.wzs, f32[960,128]{1,0:T(8,128)S(1)} %collective-permute-done.3.before, f32[960,128]{1,0:T(8,128)S(1)} %collective-permute-done.4.after, ...), custom_call_target="tpu_custom_call" | custom-call | flops 10000000000 | bytes 10000000 | tf_op jit(solution)/shard_map/late_adjoint/pallas_call | solution.py:95
  44.9 1.3 %collective-permute-start.8 = (f32[32,16,128]{2,1,0:T(8,128)S(1)}, f32[32,16,128]{2,1,0:T(8,128)S(1)}, u32[]{:S(2)}, u32[]{:S(2)}) collective-permute-start(f32[32,16,128]{2,1,0:T(8,128)S(1)} %get-tuple-element.60.own), channel_id=1, source_target_pairs={{2,0},{3,1},{4,2},{5,3},{6,4},{7,5},{8,6},{9,7},{10,8},{11,9},{12,... | collective-permute-start | bytes 786440 | tf_op jit(solution)/shard_map/ppermute | solution.py:388
  46.2 17.1 %collective-permute-start.7 = (f32[32,16,128]{2,1,0:T(8,128)S(1)}, f32[32,16,128]{2,1,0:T(8,128)S(1)}, u32[]{:S(2)}, u32[]{:S(2)}) collective-permute-start(f32[32,16,128]{2,1,0:T(8,128)S(1)} %get-tuple-element.60.own), channel_id=1, source_target_pairs={{0,2},{1,3},{2,4},{3,5},{4,6},{5,7},{6,8},{7,9},{8,10},{9,11},{10,... | collective-permute-start | bytes 786440 | tf_op jit(solution)/shard_map/ppermute | solution.py:388
  63.4 1.2 %collective-permute-done.9 = f32[24,128]{1,0:T(8,128)S(1)} collective-permute-done((f32[24,128]{1,0:T(8,128)S(1)}, f32[24,128]{1,0:T(8,128)S(1)}, u32[]{:S(2)}, u32[]{:S(2)}) %collective-permute-start.9) | collective-permute-done | bytes 12320 | tf_op jit(solution)/shard_map/ppermute | solution.py:445
  64.6 4.8 %collective-permute-start.12 = (f32[24,128]{1,0:T(8,128)S(1)}, f32[24,128]{1,0:T(8,128)S(1)}, u32[]{:S(2)}, u32[]{:S(2)}) collective-permute-start(f32[24,128]{1,0:T(8,128)S(1)} %add.66), channel_id=1, source_target_pairs={{0,12},{1,13},{2,14},{3,15},{4,8},{5,9},{6,10},{7,11},{8,4},{9,5},... | collective-permute-start | bytes 36872 | tf_op jit(solution)/shard_map/ppermute | solution.py:445
  69.3 0.6 collective-permute-start.10
  69.9 1.7 %collective-permute-done.12 = f32[24,128]{1,0:T(8,128)S(1)} collective-permute-done((f32[24,128]{1,0:T(8,128)S(1)}, f32[24,128]{1,0:T(8,128)S(1)}, u32[]{:S(2)}, u32[]{:S(2)}) %collective-permute-start.12) | collective-permute-done | bytes 12320 | tf_op jit(solution)/shard_map/ppermute | solution.py:445
  71.6 2.3 %collective-permute-done.11 = f32[24,128]{1,0:T(8,128)S(1)} collective-permute-done((f32[24,128]{1,0:T(8,128)S(1)}, f32[24,128]{1,0:T(8,128)S(1)}, u32[]{:S(2)}, u32[]{:S(2)}) %collective-permute-start.11) | collective-permute-done | bytes 12320 | tf_op jit(solution)/shard_map/ppermute | solution.py:445
  74.1 2.4 %collective-permute-start.14 = (f32[24,128]{1,0:T(8,128)S(1)}, f32[24,128]{1,0:T(8,128)S(1)}, u32[]{:S(2)}, u32[]{:S(2)}) collective-permute-start(f32[24,128]{1,0:T(8,128)S(1)} %add_add_fusion.part), channel_id=1, source_target_pairs={{0,2},{1,3},{2,0},{3,1},{4,6},{5,7},{6,4},{7,5},{8,10},{9,11},{10,... | collective-permute-start | bytes 36872 | tf_op jit(solution)/shard_map/ppermute | solution.py:445
  76.5 9.0 %iteration.1.values = f32[32,16,128]{2,1,0:T(8,128)S(1)} custom-call(s32[1]{0:T(128)} %bitcast.parity, f32[32,16,128]{2,1,0:T(8,128)S(1)} %collective-permute-done.7.far_before, f32[2,32,16,128]{3,2,1,0:T(8,128)S(1)} %collective-permute-done.13.near, f32[32,16,128]{2,1,0:T(8,128)S(1)} %get-tuple-element.60.own, ...), custom_call_target="tpu_custom_call" | custom-call | flops 20000000000 | bytes 10000000 | tf_op jit(solution)/shard_map/iteration/pallas_call | solution.py:95
  85.6 0.8 scaled.1
  (47 shorter events, 0.8 us)
Async XLA Ops:
  0.0 23.1 %copy-start.1 = (f32[32,16,128]{2,1,0:T(8,128)S(1)}, f32[32,16,128]{2,1,0:T(8,128)}, u32[]{:S(2)}) copy-start(f32[32,16,128]{2,1,0:T(8,128)} %current.1) | copy-start | bytes 786436
  0.0 26.5 %copy-start = (f32[6,32,16,128]{3,2,1,0:T(8,128)S(1)}, f32[6,32,16,128]{3,2,1,0:T(8,128)}, u32[]{:S(2)}) copy-start(f32[6,32,16,128]{3,2,1,0:T(8,128)} %raw.7) | copy-start | bytes 4718596
  0.0 9.2 %copy-start.2 = (f32[6,3,31]{2,1,0:T(4,128)S(1)}, f32[6,3,31]{2,1,0:T(4,128)}, u32[]{:S(2)}) copy-start(f32[6,3,31]{2,1,0:T(4,128)} %taps_ref.1) | copy-start | bytes 6700
  0.0 23.1 %collective-permute-start.1 = (f32[32,16,128]{2,1,0:T(8,128)}, f32[32,16,128]{2,1,0:T(8,128)S(1)}, u32[]{:S(2)}, u32[]{:S(2)}) collective-permute-start(f32[32,16,128]{2,1,0:T(8,128)} %current.1), channel_id=1, source_target_pairs={{0,2},{1,3},{2,4},{3,5},{4,6},{5,7},{6,8},{7,9},{8,10},{9,11},{10,... | collective-permute-start | bytes 786440 | tf_op jit(solution)/shard_map/ppermute | solution.py:388
  5.0 18.1 %collective-permute-start = (f32[32,16,128]{2,1,0:T(8,128)}, f32[32,16,128]{2,1,0:T(8,128)S(1)}, u32[]{:S(2)}, u32[]{:S(2)}) collective-permute-start(f32[32,16,128]{2,1,0:T(8,128)} %current.1), channel_id=1, source_target_pairs={{2,0},{3,1},{4,2},{5,3},{6,4},{7,5},{8,6},{9,7},{10,8},{11,9},{12,... | collective-permute-start | bytes 786440 | tf_op jit(solution)/shard_map/ppermute | solution.py:388
  12.9 1.4 %copy-start.3 = (bf16[6,256,768]{2,1,0:T(8,128)(2,1)}, bf16[6,256,768]{2,1,0:T(8,128)(2,1)S(1)}, u32[]{:S(2)}) copy-start(bf16[6,256,768]{2,1,0:T(8,128)(2,1)S(1)} %get-tuple-element.51.wz) | copy-start | bytes 7077892
  14.4 1.4 %copy-start.5 = (bf16[6,256,768]{2,1,0:T(8,128)(2,1)}, bf16[6,256,768]{2,1,0:T(8,128)(2,1)S(1)}, u32[]{:S(2)}) copy-start(bf16[6,256,768]{2,1,0:T(8,128)(2,1)S(1)} %get-tuple-element.55.wz.wza) | copy-start | bytes 7077892
  15.8 1.0 %copy-start.7 = (bf16[6,256,256]{2,1,0:T(8,128)(2,1)}, bf16[6,256,256]{2,1,0:T(8,128)(2,1)S(1)}, u32[]{:S(2)}) copy-start(bf16[6,256,256]{2,1,0:T(8,128)(2,1)S(1)} %get-tuple-element.50.wx) | copy-start | bytes 2359300
  16.8 1.0 %copy-start.9 = (bf16[6,256,256]{2,1,0:T(8,128)(2,1)}, bf16[6,256,256]{2,1,0:T(8,128)(2,1)S(1)}, u32[]{:S(2)}) copy-start(bf16[6,256,256]{2,1,0:T(8,128)(2,1)S(1)} %get-tuple-element.54.wx.wxa) | copy-start | bytes 2359300
  17.8 20.5 %collective-permute-start.5 = (f32[1920,128]{1,0:T(8,128)}, f32[1920,128]{1,0:T(8,128)}, u32[]{:S(2)}, u32[]{:S(2)}) collective-permute-start(f32[1920,128]{1,0:T(8,128)} %get-tuple-element.56), channel_id=1, source_target_pairs={{0,1},{1,2},{2,3},{3,4},{4,5},{5,6},{6,7},{7,8},{8,9},{9,10},{10,1... | collective-permute-start | bytes 2949128 | tf_op jit(solution)/shard_map/ppermute | solution.py:423
  20.2 18.1 %collective-permute-start.6 = (f32[1920,128]{1,0:T(8,128)S(1)}, f32[1920,128]{1,0:T(8,128)}, u32[]{:S(2)}, u32[]{:S(2)}) collective-permute-start(f32[1920,128]{1,0:T(8,128)S(1)} %get-tuple-element.57), channel_id=1, source_target_pairs={{1,0},{2,1},{3,2},{4,3},{5,4},{6,5},{7,6},{8,7},{9,8},{10,9},{11,1... | collective-permute-start | bytes 2949128 | tf_op jit(solution)/shard_map/ppermute | solution.py:424
  22.1 9.2 %copy-start.4 = (bf16[6,256,768]{2,1,0:T(8,128)(2,1)S(1)}, bf16[6,256,768]{2,1,0:T(8,128)(2,1)}, u32[]{:S(2)}) copy-start(bf16[6,256,768]{2,1,0:T(8,128)(2,1)} %copy-done.3) | copy-start | bytes 7077892
  22.1 9.2 %copy-start.8 = (bf16[6,256,256]{2,1,0:T(8,128)(2,1)S(1)}, bf16[6,256,256]{2,1,0:T(8,128)(2,1)}, u32[]{:S(2)}) copy-start(bf16[6,256,256]{2,1,0:T(8,128)(2,1)} %copy-done.7) | copy-start | bytes 2359300
  23.2 4.5 %collective-permute-start.2 = (f32[2,32,16,128]{3,2,1,0:T(8,128)S(1)}, f32[2,32,16,128]{3,2,1,0:T(8,128)S(1)}, u32[]{:S(2)}, u32[]{:S(2)}) collective-permute-start(f32[2,32,16,128]{3,2,1,0:T(8,128)S(1)} %pad_maximum_fusion), channel_id=1, source_target_pairs={{0,1},{1,0},{2,3},{3,2},{4,5},{5,4},{6,7},{7,6},{8,9},{9,8},{10,11... | collective-permute-start | bytes 1572872 | tf_op jit(solution)/shard_map/ppermute | solution.py:394
  27.7 15.0 %collective-permute-start.3 = (f32[960,128]{1,0:T(8,128)S(1)}, f32[960,128]{1,0:T(8,128)S(1)}, u32[]{:S(2)}, u32[]{:S(2)}) collective-permute-start(f32[960,128]{1,0:T(8,128)S(1)} %get-tuple-element.38), channel_id=1, source_target_pairs={{0,1},{1,2},{2,3},{3,4},{4,5},{5,6},{6,7},{7,8},{8,9},{9,10},{10,1... | collective-permute-start | bytes 1474568 | tf_op jit(solution)/shard_map/ppermute | solution.py:433
  30.0 12.7 %collective-permute-start.4 = (f32[960,128]{1,0:T(8,128)S(1)}, f32[960,128]{1,0:T(8,128)S(1)}, u32[]{:S(2)}, u32[]{:S(2)}) collective-permute-start(f32[960,128]{1,0:T(8,128)S(1)} %get-tuple-element.39), channel_id=1, source_target_pairs={{1,0},{2,1},{3,2},{4,3},{5,4},{6,5},{7,6},{8,7},{9,8},{10,9},{11,1... | collective-permute-start | bytes 1474568 | tf_op jit(solution)/shard_map/ppermute | solution.py:434
  31.3 6.9 %copy-start.6 = (bf16[6,256,768]{2,1,0:T(8,128)(2,1)S(1)}, bf16[6,256,768]{2,1,0:T(8,128)(2,1)}, u32[]{:S(2)}) copy-start(bf16[6,256,768]{2,1,0:T(8,128)(2,1)} %copy-done.5) | copy-start | bytes 7077892
  31.3 6.9 %copy-start.10 = (bf16[6,256,256]{2,1,0:T(8,128)(2,1)S(1)}, bf16[6,256,256]{2,1,0:T(8,128)(2,1)}, u32[]{:S(2)}) copy-start(bf16[6,256,256]{2,1,0:T(8,128)(2,1)} %copy-done.9) | copy-start | bytes 2359300
  44.9 29.0 %collective-permute-start.8 = (f32[32,16,128]{2,1,0:T(8,128)S(1)}, f32[32,16,128]{2,1,0:T(8,128)S(1)}, u32[]{:S(2)}, u32[]{:S(2)}) collective-permute-start(f32[32,16,128]{2,1,0:T(8,128)S(1)} %get-tuple-element.60.own), channel_id=1, source_target_pairs={{2,0},{3,1},{4,2},{5,3},{6,4},{7,5},{8,6},{9,7},{10,8},{11,9},{12,... | collective-permute-start | bytes 786440 | tf_op jit(solution)/shard_map/ppermute | solution.py:388
  46.2 27.8 %collective-permute-start.7 = (f32[32,16,128]{2,1,0:T(8,128)S(1)}, f32[32,16,128]{2,1,0:T(8,128)S(1)}, u32[]{:S(2)}, u32[]{:S(2)}) collective-permute-start(f32[32,16,128]{2,1,0:T(8,128)S(1)} %get-tuple-element.60.own), channel_id=1, source_target_pairs={{0,2},{1,3},{2,4},{3,5},{4,6},{5,7},{6,8},{7,9},{8,10},{9,11},{10,... | collective-permute-start | bytes 786440 | tf_op jit(solution)/shard_map/ppermute | solution.py:388
  63.3 1.2 %collective-permute-start.9 = (f32[24,128]{1,0:T(8,128)S(1)}, f32[24,128]{1,0:T(8,128)S(1)}, u32[]{:S(2)}, u32[]{:S(2)}) collective-permute-start(f32[24,128]{1,0:T(8,128)S(1)} %get-tuple-element.61), channel_id=1, source_target_pairs={{0,1},{1,0},{2,3},{3,2},{4,5},{5,4},{6,7},{7,6},{8,9},{9,8},{10,11... | collective-permute-start | bytes 36872 | tf_op jit(solution)/shard_map/ppermute | solution.py:445
  64.6 7.1 %collective-permute-start.12 = (f32[24,128]{1,0:T(8,128)S(1)}, f32[24,128]{1,0:T(8,128)S(1)}, u32[]{:S(2)}, u32[]{:S(2)}) collective-permute-start(f32[24,128]{1,0:T(8,128)S(1)} %add.66), channel_id=1, source_target_pairs={{0,12},{1,13},{2,14},{3,15},{4,8},{5,9},{6,10},{7,11},{8,4},{9,5},... | collective-permute-start | bytes 36872 | tf_op jit(solution)/shard_map/ppermute | solution.py:445
  69.3 4.6 %collective-permute-start.11 = (f32[24,128]{1,0:T(8,128)S(1)}, f32[24,128]{1,0:T(8,128)S(1)}, u32[]{:S(2)}, u32[]{:S(2)}) collective-permute-start(f32[24,128]{1,0:T(8,128)S(1)} %add.66), channel_id=1, source_target_pairs={{0,8},{1,9},{2,10},{3,11},{4,12},{5,13},{6,14},{7,15},{8,0},{9,1},... | collective-permute-start | bytes 36872 | tf_op jit(solution)/shard_map/ppermute | solution.py:445
  69.3 4.6 %collective-permute-start.10 = (f32[24,128]{1,0:T(8,128)S(1)}, f32[24,128]{1,0:T(8,128)S(1)}, u32[]{:S(2)}, u32[]{:S(2)}) collective-permute-start(f32[24,128]{1,0:T(8,128)S(1)} %add.66), channel_id=1, source_target_pairs={{0,4},{1,5},{2,6},{3,7},{4,0},{5,1},{6,2},{7,3},{8,12},{9,13},{10,... | collective-permute-start | bytes 36872 | tf_op jit(solution)/shard_map/ppermute | solution.py:445
  74.1 2.5 %collective-permute-start.13 = (f32[2,32,16,128]{3,2,1,0:T(8,128)S(1)}, f32[2,32,16,128]{3,2,1,0:T(8,128)S(1)}, u32[]{:S(2)}, u32[]{:S(2)}) collective-permute-start(f32[2,32,16,128]{3,2,1,0:T(8,128)S(1)} %pad_maximum_fusion.1), channel_id=1, source_target_pairs={{0,1},{1,0},{2,3},{3,2},{4,5},{5,4},{6,7},{7,6},{8,9},{9,8},{10,11... | collective-permute-start | bytes 1572872 | tf_op jit(solution)/shard_map/ppermute | solution.py:394
  74.1 11.4 %collective-permute-start.14 = (f32[24,128]{1,0:T(8,128)S(1)}, f32[24,128]{1,0:T(8,128)S(1)}, u32[]{:S(2)}, u32[]{:S(2)}) collective-permute-start(f32[24,128]{1,0:T(8,128)S(1)} %add_add_fusion.part), channel_id=1, source_target_pairs={{0,2},{1,3},{2,0},{3,1},{4,6},{5,7},{6,4},{7,5},{8,10},{9,11},{10,... | collective-permute-start | bytes 36872 | tf_op jit(solution)/shard_map/ppermute | solution.py:445

commit v12 on v11

--- a/solution.py
+++ b/solution.py
@@ -114,7 +114,7 @@
         pltpu.VMEM((views, 2 * cols, 2 * cols), BF16),
         pltpu.VMEM((views, 8 * planes, 24 * planes), BF16),
     ]
-    made = call(functools.partial(weights_kernel, rows), outs, [], [taps], [], "weights", 10**7)
+    made = call(functools.partial(weights_kernel, rows), outs, [], [taps], [], "weights", 10**10)
     return made[:3], made[3:]
 
 
@@ -308,7 +308,8 @@
     updated(own, acc[...], views, out)
 
 
-def pack_kernel(raw, last, leading):
+def pack_kernel(raw, *refs):
+    last, leading = refs[-2:]
     count, rows = last.shape[0] // raw.shape[0], raw.shape[1]
     flat = raw.reshape(raw.shape[0] * rows, raw.shape[2])
     for y in range(count):
@@ -317,11 +318,11 @@
         leading[here, :] = flat[pl.ds(y, raw.shape[0], stride=rows), :]
 
 
-def packed(raw, chosen, count):
+def packed(raw, chosen, count, *awaited):
     _, planes, rows, cols = raw.shape
     part = raw[chosen[0] : chosen[-1] + 1].reshape(len(chosen) * planes, rows, cols)
     outs = [pltpu.VMEM((count * part.shape[0], cols), F32)] * 2
-    return call(pack_kernel, outs, [], [part], [], "pack", 10**6)
+    return call(pack_kernel, outs, [], [part, *awaited], [], "pack", 10**6)
 
 
 def scaled_kernel(views, values, part, rest, out):
@@ -415,13 +416,10 @@
     far = two_slabs_away(estimate, count)
     margin = taps.shape[2] // 2
     groups = (range(0, 2 * views // 3), range(2 * views // 3, views))
-    edges = [packed(raw, g, margin) for g in groups]
+    edges = packed(raw, groups[0], margin)
     forward_weights, adjoint_weights = make_weights(taps, planes, rows, cols)
-    first_edges, forward_weights, adjoint_weights = lax.optimization_barrier(
-        (edges[0], forward_weights, adjoint_weights)
-    )
-    befores = [lax.ppermute(first_edges[0], "slab", up)]
-    afters = [lax.ppermute(first_edges[1], "slab", down)]
+    befores = [lax.ppermute(edges[0], "slab", up)]
+    afters = [lax.ppermute(edges[1], "slab", down)]
 
     wzs = tap_sums(taps[:, 0], 0, planes, planes)
     wy_sums = tap_sums(taps[:, 1], place * rows, rows, count * rows)
@@ -429,9 +427,9 @@
     wyx = wy_sums[:, :, None] * wx_sums[:, None, :]
 
     far_before, near, own, far_after = with_near(estimate, *far, parity, count)
-    near, last, leading = lax.optimization_barrier((near, *edges[1]))
-    befores.append(lax.ppermute(last, "slab", up))
-    afters.append(lax.ppermute(leading, "slab", down))
+    edges = packed(raw, groups[1], margin, near)
+    befores.append(lax.ppermute(edges[0], "slab", up))
+    afters.append(lax.ppermute(edges[1], "slab", down))
     slabs = (far_before, near, own, far_after)
     blurred, known = forward(parity, slabs, forward_weights, raw, wzs, wyx)
     current, sums, halos = first_adjoint(

time: 86.8 us -> 81.4 us (0.938)
  starting transfers between devices: 42.8 us -> 33 us
  waiting for transfers between devices: 6.22 us -> 9.59 us
  local copies, waits for them, and re-layouts: 7.61 us -> 8.73 us
    ppermute x4, starting transfers between devices: 24.7 us -> 17.1 us  [two_slabs_away(): return (lax.ppermute(value, 'slab', up), lax.ppermute(value, 'slab', down))]
    ppermute x5, starting transfers between devices: 7.8 us -> 5.36 us  [per_device(): lax.ppermute(sums, 'slab', [(i, i ^ d) for i in range(count)])]
    ppermute x2, waiting for transfers between devices: 1 us -> 2.91 us  [with_near(): near = lax.ppermute(passed, 'slab', swap)]
    ppermute x5, waiting for transfers between devices: 5.2 us -> 6.66 us  [per_device(): lax.ppermute(sums, 'slab', [(i, i ^ d) for i in range(count)])]
    ppermute x2, starting transfers between devices: 3.04 us -> 4.17 us  [with_near(): near = lax.ppermute(passed, 'slab', swap)]
    unnamed x23 -> x25, local copies, waits for them, and re-layouts: 5.69 us -> 6.8 us
    ppermute x4, starting transfers between devices: 7.27 us -> 6.4 us  [the longest x1 2.31 us: per_device(): befores.append(lax.ppermute(edges[0], 'slab', up))]
  transfers between devices with their start and end apart: 15 -> 15, of which waited for: 4 -> 6; matrix products, arithmetic and copies ran while one was open for 4% -> 4% of each run, Pallas kernels for 30% -> 32%
where the time goes in v12:
time: 81.4 us; the launch traced here: 81 us
  starting transfers between devices  33 us (41%)
  Pallas kernels  28.7 us (35%)
  waiting for transfers between devices  9.59 us (12%)
  local copies, waits for them, and re-layouts  8.73 us (11%)
    pallas_call x8, Pallas kernels, call(): pl.pallas_call(kernel, out_shape=outs, in_specs=[pl.BlockSpec(memory_spac...  28.7 us
    ppermute x4, starting transfers between devices, two_slabs_away(): return (lax.ppermute(value, 'slab', up), lax.ppermute(value, 'slab', down))  17.1 us
    unnamed x25, local copies, waits for them, and re-layouts  6.8 us
    ppermute x5, waiting for transfers between devices, per_device(): lax.ppermute(sums, 'slab', [(i, i ^ d) for i in range(count)])  6.66 us
    ppermute x5, starting transfers between devices, per_device(): lax.ppermute(sums, 'slab', [(i, i ^ d) for i in range(count)])  5.36 us
    ppermute x2, starting transfers between devices, with_near(): near = lax.ppermute(passed, 'slab', swap)  4.17 us
    ppermute x2, waiting for transfers between devices, with_near(): near = lax.ppermute(passed, 'slab', swap)  2.91 us
    ppermute x1, starting transfers between devices, per_device(): befores.append(lax.ppermute(edges[0], 'slab', up))  2.31 us
  transfers between devices with their start and end apart: 15, of which 6 were waited for; matrix products, arithmetic and copies ran while one was open for 4% of the time, Pallas kernels for 32%

profile of v12, /device:TPU:0, one launch (start us, length us, event | category | flops | bytes accessed | tf_op | source)
XLA Modules:
  0.0 81.0 jit_solution(10869311398671017629)
XLA Ops:
  0.0 1.4 %collective-permute-start = (f32[32,16,128]{2,1,0:T(8,128)}, f32[32,16,128]{2,1,0:T(8,128)S(1)}, u32[]{:S(2)}, u32[]{:S(2)}) collective-permute-start(f32[32,16,128]{2,1,0:T(8,128)} %current.1), channel_id=1, source_target_pairs={{2,0},{3,1},{4,2},{5,3},{6,4},{7,5},{8,6},{9,7},{10,8},{11,9},{12,... | collective-permute-start | bytes 786440 | tf_op jit(solution)/shard_map/ppermute | solution.py:389
  1.4 5.5 %collective-permute-start.1 = (f32[32,16,128]{2,1,0:T(8,128)}, f32[32,16,128]{2,1,0:T(8,128)S(1)}, u32[]{:S(2)}, u32[]{:S(2)}) collective-permute-start(f32[32,16,128]{2,1,0:T(8,128)} %current.1), channel_id=1, source_target_pairs={{0,2},{1,3},{2,4},{3,5},{4,6},{5,7},{6,8},{7,9},{8,10},{9,11},{10,... | collective-permute-start | bytes 786440 | tf_op jit(solution)/shard_map/ppermute | solution.py:389
  6.9 1.3 %slice.19 = f32[4,32,16,128]{3,2,1,0:T(8,128)S(1)} slice(f32[6,32,16,128]{3,2,1,0:T(8,128)} %raw.7), slice={[0:4], [0:32], [0:16], [0:128]} | slice | bytes 2097152 | tf_op jit(solution)/shard_map/slice | solution.py:323
  8.3 1.6 %pack.3 = (f32[1920,128]{1,0:T(8,128)}, f32[1920,128]{1,0:T(8,128)}) custom-call(f32[128,16,128]{2,1,0:T(8,128)S(1)} %bitcast.16), custom_call_target="tpu_custom_call" | custom-call | flops 1000000 | bytes 10000000 | tf_op jit(solution)/shard_map/pack/pallas_call | solution.py:95
  9.9 1.5 %collective-permute-start.5 = (f32[1920,128]{1,0:T(8,128)}, f32[1920,128]{1,0:T(8,128)S(1)}, u32[]{:S(2)}, u32[]{:S(2)}) collective-permute-start(f32[1920,128]{1,0:T(8,128)} %get-tuple-element.34), channel_id=1, source_target_pairs={{0,1},{1,2},{2,3},{3,4},{4,5},{5,6},{6,7},{7,8},{8,9},{9,10},{10,1... | collective-permute-start | bytes 2949128 | tf_op jit(solution)/shard_map/ppermute | solution.py:421
  11.4 1.3 %collective-permute-start.6 = (f32[1920,128]{1,0:T(8,128)}, f32[1920,128]{1,0:T(8,128)}, u32[]{:S(2)}, u32[]{:S(2)}) collective-permute-start(f32[1920,128]{1,0:T(8,128)} %get-tuple-element.35), channel_id=1, source_target_pairs={{1,0},{2,1},{3,2},{4,3},{5,4},{6,5},{7,6},{8,7},{9,8},{10,9},{11,1... | collective-permute-start | bytes 2949128 | tf_op jit(solution)/shard_map/ppermute | solution.py:422
  12.7 0.6 fusion.12
  13.3 3.7 %weights.1 = (bf16[288,240]{1,0:T(8,128)(2,1)S(1)}, bf16[6,256,256]{2,1,0:T(8,128)(2,1)S(1)}, bf16[6,256,768]{2,1,0:T(8,128)(2,1)S(1)}, bf16[6,32,96]{2,1,0:T(8,...) custom-call(f32[6,3,31]{2,1,0:T(4,128)S(1)} %copy-done.2), custom_call_target="tpu_custom_call" | custom-call | flops 10000000000 | bytes 10000000 | tf_op jit(solution)/shard_map/weights/pallas_call | solution.py:95
  17.0 1.4 %copy-done.3 = bf16[6,256,768]{2,1,0:T(8,128)(2,1)} copy-done((bf16[6,256,768]{2,1,0:T(8,128)(2,1)}, bf16[6,256,768]{2,1,0:T(8,128)(2,1)S(1)}, u32[]{:S(2)}) %copy-start.3) | copy-done | bytes 2359320
  18.5 1.4 %copy-done.5 = bf16[6,256,768]{2,1,0:T(8,128)(2,1)} copy-done((bf16[6,256,768]{2,1,0:T(8,128)(2,1)}, bf16[6,256,768]{2,1,0:T(8,128)(2,1)S(1)}, u32[]{:S(2)}) %copy-start.5) | copy-done | bytes 2359320
  19.9 1.0 %copy-done.7 = bf16[6,256,256]{2,1,0:T(8,128)(2,1)} copy-done((bf16[6,256,256]{2,1,0:T(8,128)(2,1)}, bf16[6,256,256]{2,1,0:T(8,128)(2,1)S(1)}, u32[]{:S(2)}) %copy-start.7) | copy-done | bytes 786456
  20.9 1.0 %copy-done.9 = bf16[6,256,256]{2,1,0:T(8,128)(2,1)} copy-done((bf16[6,256,256]{2,1,0:T(8,128)(2,1)}, bf16[6,256,256]{2,1,0:T(8,128)(2,1)S(1)}, u32[]{:S(2)}) %copy-start.9) | copy-done | bytes 786456
  21.9 0.8 %copy.16 = f32[6,1,31]{2,0,1:T(8,128)S(1)} copy(f32[6,1,31]{2,1,0:T(1,128)} %get-tuple-element.46) | data formatting | bytes 1488
  23.0 4.1 %collective-permute-start.2 = (f32[2,32,16,128]{3,2,1,0:T(8,128)S(1)}, f32[2,32,16,128]{3,2,1,0:T(8,128)S(1)}, u32[]{:S(2)}, u32[]{:S(2)}) collective-permute-start(f32[2,32,16,128]{3,2,1,0:T(8,128)S(1)} %pad_maximum_fusion), channel_id=1, source_target_pairs={{0,1},{1,0},{2,3},{3,2},{4,5},{5,4},{6,7},{7,6},{8,9},{9,8},{10,11... | collective-permute-start | bytes 1572872 | tf_op jit(solution)/shard_map/ppermute | solution.py:395
  27.4 1.2 %collective-permute-done.2.refs_0_.near = f32[2,32,16,128]{3,2,1,0:T(8,128)S(1)} collective-permute-done((f32[2,32,16,128]{3,2,1,0:T(8,128)S(1)}, f32[2,32,16,128]{3,2,1,0:T(8,128)S(1)}, u32[]{:S(2)}, u32[]{:S(2)}) %collective-permute-start.2) | collective-permute-done | bytes 524320 | tf_op jit(solution)/shard_map/ppermute | solution.py:395
  28.8 2.3 %collective-permute-start.3 = (f32[960,128]{1,0:T(8,128)S(1)}, f32[960,128]{1,0:T(8,128)S(1)}, u32[]{:S(2)}, u32[]{:S(2)}) collective-permute-start(f32[960,128]{1,0:T(8,128)S(1)} %get-tuple-element.25), channel_id=1, source_target_pairs={{0,1},{1,2},{2,3},{3,4},{4,5},{5,6},{6,7},{7,8},{8,9},{9,10},{10,1... | collective-permute-start | bytes 1474568 | tf_op jit(solution)/shard_map/ppermute | solution.py:431
  31.1 1.3 %collective-permute-start.4 = (f32[960,128]{1,0:T(8,128)S(1)}, f32[960,128]{1,0:T(8,128)S(1)}, u32[]{:S(2)}, u32[]{:S(2)}) collective-permute-start(f32[960,128]{1,0:T(8,128)S(1)} %get-tuple-element.26), channel_id=1, source_target_pairs={{1,0},{2,1},{3,2},{4,3},{5,4},{6,5},{7,6},{8,7},{9,8},{10,9},{11,1... | collective-permute-start | bytes 1474568 | tf_op jit(solution)/shard_map/ppermute | solution.py:432
  32.4 1.1 %copy-done.10 = bf16[6,256,256]{2,1,0:T(8,128)(2,1)S(1)} copy-done((bf16[6,256,256]{2,1,0:T(8,128)(2,1)S(1)}, bf16[6,256,256]{2,1,0:T(8,128)(2,1)}, u32[]{:S(2)}) %copy-start.10) | copy-done | bytes 786456
  33.5 6.9 %forward.1 = (f32[6,32,48,128]{3,2,1,0:T(8,128)S(1)}, f32[24,128]{1,0:T(8,128)S(1)}) custom-call(s32[1]{0:T(128)} %bitcast.parity, f32[6,32]{1,0:T(8,128)S(1)} %multiply_reduce_fusion.1.wzs, f32[32,16,128]{2,1,0:T(8,128)S(1)} %collective-permute-done.1.far_before, f32[2,32,16,128]{3,2,1,0:T(8,128)S(1)} %collective-permute-done.2.refs_0_.near, ...), custom_call_target="tpu_custom_call" | custom-call | flops 10000000000 | bytes 10000000 | tf_op jit(solution)/shard_map/forward/pallas_call | solution.py:95
  40.5 4.1 %early_adjoint.1 = (f32[256,256]{1,0:T(8,128)S(1)}, f32[4,32,32,128]{3,2,1,0:T(8,128)S(1)}) custom-call(f32[1920,128]{1,0:T(8,128)S(1)} %collective-permute-done.5.before, f32[1920,128]{1,0:T(8,128)} %collective-permute-done.6.after, f32[6,32,16,128]{3,2,1,0:T(8,128)S(1)} %copy-done, f32[6,32,48,128]{3,2,1,0:T(8,128)S(1)} %get-tuple-element.30.blurred, ...), custom_call_target="tpu_custom_call" | custom-call | flops 10000000000 | bytes 10000000 | tf_op jit(solution)/shard_map/early_adjoint/pallas_call | solution.py:95
  44.6 2.2 %late_adjoint.1 = (f32[32,16,128]{2,1,0:T(8,128)S(1)}, f32[24,128]{1,0:T(8,128)S(1)}, f32[2,32,32,128]{3,2,1,0:T(8,128)S(1)}) custom-call(f32[6,32]{1,0:T(8,128)S(1)} %multiply_reduce_fusion.1.wzs, f32[960,128]{1,0:T(8,128)S(1)} %collective-permute-done.3.before, f32[960,128]{1,0:T(8,128)S(1)} %collective-permute-done.4.after, ...), custom_call_target="tpu_custom_call" | custom-call | flops 10000000000 | bytes 10000000 | tf_op jit(solution)/shard_map/late_adjoint/pallas_call | solution.py:95
  46.8 8.7 %collective-permute-start.7 = (f32[32,16,128]{2,1,0:T(8,128)S(1)}, f32[32,16,128]{2,1,0:T(8,128)S(1)}, u32[]{:S(2)}, u32[]{:S(2)}) collective-permute-start(f32[32,16,128]{2,1,0:T(8,128)S(1)} %get-tuple-element.38.own), channel_id=1, source_target_pairs={{0,2},{1,3},{2,4},{3,5},{4,6},{5,7},{6,8},{7,9},{8,10},{9,11},{10,... | collective-permute-start | bytes 786440 | tf_op jit(solution)/shard_map/ppermute | solution.py:389
  55.5 1.5 %collective-permute-start.8 = (f32[32,16,128]{2,1,0:T(8,128)S(1)}, f32[32,16,128]{2,1,0:T(8,128)S(1)}, u32[]{:S(2)}, u32[]{:S(2)}) collective-permute-start(f32[32,16,128]{2,1,0:T(8,128)S(1)} %get-tuple-element.38.own), channel_id=1, source_target_pairs={{2,0},{3,1},{4,2},{5,3},{6,4},{7,5},{8,6},{9,7},{10,8},{11,9},{12,... | collective-permute-start | bytes 786440 | tf_op jit(solution)/shard_map/ppermute | solution.py:389
  57.0 1.2 %collective-permute-done.9 = f32[24,128]{1,0:T(8,128)S(1)} collective-permute-done((f32[24,128]{1,0:T(8,128)S(1)}, f32[24,128]{1,0:T(8,128)S(1)}, u32[]{:S(2)}, u32[]{:S(2)}) %collective-permute-start.9) | collective-permute-done | bytes 12320 | tf_op jit(solution)/shard_map/ppermute | solution.py:443
  58.2 2.5 %collective-permute-start.10 = (f32[24,128]{1,0:T(8,128)S(1)}, f32[24,128]{1,0:T(8,128)S(1)}, u32[]{:S(2)}, u32[]{:S(2)}) collective-permute-start(f32[24,128]{1,0:T(8,128)S(1)} %add.66), channel_id=1, source_target_pairs={{0,4},{1,5},{2,6},{3,7},{4,0},{5,1},{6,2},{7,3},{8,12},{9,13},{10,... | collective-permute-start | bytes 36872 | tf_op jit(solution)/shard_map/ppermute | solution.py:443
  60.7 2.6 %collective-permute-start.11 = (f32[24,128]{1,0:T(8,128)S(1)}, f32[24,128]{1,0:T(8,128)S(1)}, u32[]{:S(2)}, u32[]{:S(2)}) collective-permute-start(f32[24,128]{1,0:T(8,128)S(1)} %add.66), channel_id=1, source_target_pairs={{0,8},{1,9},{2,10},{3,11},{4,12},{5,13},{6,14},{7,15},{8,0},{9,1},... | collective-permute-start | bytes 36872 | tf_op jit(solution)/shard_map/ppermute | solution.py:443
  63.3 2.5 %collective-permute-done.10 = f32[24,128]{1,0:T(8,128)S(1)} collective-permute-done((f32[24,128]{1,0:T(8,128)S(1)}, f32[24,128]{1,0:T(8,128)S(1)}, u32[]{:S(2)}, u32[]{:S(2)}) %collective-permute-start.10) | collective-permute-done | bytes 12320 | tf_op jit(solution)/shard_map/ppermute | solution.py:443
  65.8 1.1 %collective-permute-done.11 = f32[24,128]{1,0:T(8,128)S(1)} collective-permute-done((f32[24,128]{1,0:T(8,128)S(1)}, f32[24,128]{1,0:T(8,128)S(1)}, u32[]{:S(2)}, u32[]{:S(2)}) %collective-permute-start.11) | collective-permute-done | bytes 12320 | tf_op jit(solution)/shard_map/ppermute | solution.py:443
  67.0 1.8 %collective-permute-done.12 = f32[24,128]{1,0:T(8,128)S(1)} collective-permute-done((f32[24,128]{1,0:T(8,128)S(1)}, f32[24,128]{1,0:T(8,128)S(1)}, u32[]{:S(2)}, u32[]{:S(2)}) %collective-permute-start.12) | collective-permute-done | bytes 12320 | tf_op jit(solution)/shard_map/ppermute | solution.py:443
  69.2 1.7 %collective-permute-done.13.near = f32[2,32,16,128]{3,2,1,0:T(8,128)S(1)} collective-permute-done((f32[2,32,16,128]{3,2,1,0:T(8,128)S(1)}, f32[2,32,16,128]{3,2,1,0:T(8,128)S(1)}, u32[]{:S(2)}, u32[]{:S(2)}) %collective-permute-start.13) | collective-permute-done | bytes 524320 | tf_op jit(solution)/shard_map/ppermute | solution.py:395
  70.9 9.2 %iteration.1.values = f32[32,16,128]{2,1,0:T(8,128)S(1)} custom-call(s32[1]{0:T(128)} %bitcast.parity, f32[32,16,128]{2,1,0:T(8,128)S(1)} %collective-permute-done.7.far_before, f32[2,32,16,128]{3,2,1,0:T(8,128)S(1)} %collective-permute-done.13.near, f32[32,16,128]{2,1,0:T(8,128)S(1)} %get-tuple-element.38.own, ...), custom_call_target="tpu_custom_call" | custom-call | flops 20000000000 | bytes 10000000 | tf_op jit(solution)/shard_map/iteration/pallas_call | solution.py:95
  80.1 0.8 %scaled.1 = f32[32,16,128]{2,1,0:T(8,128)} custom-call(f32[32,16,128]{2,1,0:T(8,128)S(1)} %iteration.1.values, f32[24,128]{1,0:T(8,128)S(1)} %add_add_fusion.part, f32[24,128]{1,0:T(8,128)S(1)} %collective-permute-done.14.rest), custom_call_target="tpu_custom_call" | custom-call | flops 100000 | bytes 10000000 | tf_op jit(solution)/shard_map/scaled/pallas_call | solution.py:95
  (49 shorter events, 1.2 us)
Async XLA Ops:
  0.0 12.7 %copy-start.2 = (f32[6,3,31]{2,1,0:T(4,128)S(1)}, f32[6,3,31]{2,1,0:T(4,128)}, u32[]{:S(2)}) copy-start(f32[6,3,31]{2,1,0:T(4,128)} %taps_ref.1) | copy-start | bytes 6700
  0.0 22.8 %collective-permute-start = (f32[32,16,128]{2,1,0:T(8,128)}, f32[32,16,128]{2,1,0:T(8,128)S(1)}, u32[]{:S(2)}, u32[]{:S(2)}) collective-permute-start(f32[32,16,128]{2,1,0:T(8,128)} %current.1), channel_id=1, source_target_pairs={{2,0},{3,1},{4,2},{5,3},{6,4},{7,5},{8,6},{9,7},{10,8},{11,9},{12,... | collective-permute-start | bytes 786440 | tf_op jit(solution)/shard_map/ppermute | solution.py:389
  1.4 21.4 %collective-permute-start.1 = (f32[32,16,128]{2,1,0:T(8,128)}, f32[32,16,128]{2,1,0:T(8,128)S(1)}, u32[]{:S(2)}, u32[]{:S(2)}) collective-permute-start(f32[32,16,128]{2,1,0:T(8,128)} %current.1), channel_id=1, source_target_pairs={{0,2},{1,3},{2,4},{3,5},{4,6},{5,7},{6,8},{7,9},{8,10},{9,11},{10,... | collective-permute-start | bytes 786440 | tf_op jit(solution)/shard_map/ppermute | solution.py:389
  9.9 30.6 %collective-permute-start.5 = (f32[1920,128]{1,0:T(8,128)}, f32[1920,128]{1,0:T(8,128)S(1)}, u32[]{:S(2)}, u32[]{:S(2)}) collective-permute-start(f32[1920,128]{1,0:T(8,128)} %get-tuple-element.34), channel_id=1, source_target_pairs={{0,1},{1,2},{2,3},{3,4},{4,5},{5,6},{6,7},{7,8},{8,9},{9,10},{10,1... | collective-permute-start | bytes 2949128 | tf_op jit(solution)/shard_map/ppermute | solution.py:421
  11.4 29.1 %collective-permute-start.6 = (f32[1920,128]{1,0:T(8,128)}, f32[1920,128]{1,0:T(8,128)}, u32[]{:S(2)}, u32[]{:S(2)}) collective-permute-start(f32[1920,128]{1,0:T(8,128)} %get-tuple-element.35), channel_id=1, source_target_pairs={{1,0},{2,1},{3,2},{4,3},{5,4},{6,5},{7,6},{8,7},{9,8},{10,9},{11,1... | collective-permute-start | bytes 2949128 | tf_op jit(solution)/shard_map/ppermute | solution.py:422
  13.3 9.6 %copy-start.1 = (f32[32,16,128]{2,1,0:T(8,128)S(1)}, f32[32,16,128]{2,1,0:T(8,128)}, u32[]{:S(2)}) copy-start(f32[32,16,128]{2,1,0:T(8,128)} %current.1) | copy-start | bytes 786436
  17.0 1.4 %copy-start.3 = (bf16[6,256,768]{2,1,0:T(8,128)(2,1)}, bf16[6,256,768]{2,1,0:T(8,128)(2,1)S(1)}, u32[]{:S(2)}) copy-start(bf16[6,256,768]{2,1,0:T(8,128)(2,1)S(1)} %get-tuple-element.33.wz.wza) | copy-start | bytes 7077892
  18.5 1.4 %copy-start.5 = (bf16[6,256,768]{2,1,0:T(8,128)(2,1)}, bf16[6,256,768]{2,1,0:T(8,128)(2,1)S(1)}, u32[]{:S(2)}) copy-start(bf16[6,256,768]{2,1,0:T(8,128)(2,1)S(1)} %get-tuple-element.29.wz) | copy-start | bytes 7077892
  19.9 1.0 %copy-start.7 = (bf16[6,256,256]{2,1,0:T(8,128)(2,1)}, bf16[6,256,256]{2,1,0:T(8,128)(2,1)S(1)}, u32[]{:S(2)}) copy-start(bf16[6,256,256]{2,1,0:T(8,128)(2,1)S(1)} %get-tuple-element.32.wx.wxa) | copy-start | bytes 2359300
  20.9 1.0 %copy-start.9 = (bf16[6,256,256]{2,1,0:T(8,128)(2,1)}, bf16[6,256,256]{2,1,0:T(8,128)(2,1)S(1)}, u32[]{:S(2)}) copy-start(bf16[6,256,256]{2,1,0:T(8,128)(2,1)S(1)} %get-tuple-element.28.wx) | copy-start | bytes 2359300
  21.8 5.5 %copy-start = (f32[6,32,16,128]{3,2,1,0:T(8,128)S(1)}, f32[6,32,16,128]{3,2,1,0:T(8,128)}, u32[]{:S(2)}) copy-start(f32[6,32,16,128]{3,2,1,0:T(8,128)} %raw.7) | copy-start | bytes 4718596
  21.9 10.5 %copy-start.6 = (bf16[6,256,768]{2,1,0:T(8,128)(2,1)S(1)}, bf16[6,256,768]{2,1,0:T(8,128)(2,1)}, u32[]{:S(2)}) copy-start(bf16[6,256,768]{2,1,0:T(8,128)(2,1)} %copy-done.5) | copy-start | bytes 7077892
  23.0 5.6 %collective-permute-start.2 = (f32[2,32,16,128]{3,2,1,0:T(8,128)S(1)}, f32[2,32,16,128]{3,2,1,0:T(8,128)S(1)}, u32[]{:S(2)}, u32[]{:S(2)}) collective-permute-start(f32[2,32,16,128]{3,2,1,0:T(8,128)S(1)} %pad_maximum_fusion), channel_id=1, source_target_pairs={{0,1},{1,0},{2,3},{3,2},{4,5},{5,4},{6,7},{7,6},{8,9},{9,8},{10,11... | collective-permute-start | bytes 1572872 | tf_op jit(solution)/shard_map/ppermute | solution.py:395
  28.8 15.8 %collective-permute-start.3 = (f32[960,128]{1,0:T(8,128)S(1)}, f32[960,128]{1,0:T(8,128)S(1)}, u32[]{:S(2)}, u32[]{:S(2)}) collective-permute-start(f32[960,128]{1,0:T(8,128)S(1)} %get-tuple-element.25), channel_id=1, source_target_pairs={{0,1},{1,2},{2,3},{3,4},{4,5},{5,6},{6,7},{7,8},{8,9},{9,10},{10,1... | collective-permute-start | bytes 1474568 | tf_op jit(solution)/shard_map/ppermute | solution.py:431
  31.1 13.5 %collective-permute-start.4 = (f32[960,128]{1,0:T(8,128)S(1)}, f32[960,128]{1,0:T(8,128)S(1)}, u32[]{:S(2)}, u32[]{:S(2)}) collective-permute-start(f32[960,128]{1,0:T(8,128)S(1)} %get-tuple-element.26), channel_id=1, source_target_pairs={{1,0},{2,1},{3,2},{4,3},{5,4},{6,5},{7,6},{8,7},{9,8},{10,9},{11,1... | collective-permute-start | bytes 1474568 | tf_op jit(solution)/shard_map/ppermute | solution.py:432
  32.4 1.1 %copy-start.10 = (bf16[6,256,256]{2,1,0:T(8,128)(2,1)S(1)}, bf16[6,256,256]{2,1,0:T(8,128)(2,1)}, u32[]{:S(2)}) copy-start(bf16[6,256,256]{2,1,0:T(8,128)(2,1)} %copy-done.9) | copy-start | bytes 2359300
  33.5 6.9 %copy-start.4 = (bf16[6,256,768]{2,1,0:T(8,128)(2,1)S(1)}, bf16[6,256,768]{2,1,0:T(8,128)(2,1)}, u32[]{:S(2)}) copy-start(bf16[6,256,768]{2,1,0:T(8,128)(2,1)} %copy-done.3) | copy-start | bytes 7077892
  33.5 6.9 %copy-start.8 = (bf16[6,256,256]{2,1,0:T(8,128)(2,1)S(1)}, bf16[6,256,256]{2,1,0:T(8,128)(2,1)}, u32[]{:S(2)}) copy-start(bf16[6,256,256]{2,1,0:T(8,128)(2,1)} %copy-done.7) | copy-start | bytes 2359300
  44.6 26.3 %copy-start.11 = (bf16[6,256,256]{2,1,0:T(8,128)(2,1)S(1)}, bf16[6,256,256]{2,1,0:T(8,128)(2,1)}, u32[]{:S(2)}) copy-start(bf16[6,256,256]{2,1,0:T(8,128)(2,1)} %copy-done.9) | copy-start | bytes 2359300
  46.8 22.1 %collective-permute-start.7 = (f32[32,16,128]{2,1,0:T(8,128)S(1)}, f32[32,16,128]{2,1,0:T(8,128)S(1)}, u32[]{:S(2)}, u32[]{:S(2)}) collective-permute-start(f32[32,16,128]{2,1,0:T(8,128)S(1)} %get-tuple-element.38.own), channel_id=1, source_target_pairs={{0,2},{1,3},{2,4},{3,5},{4,6},{5,7},{6,8},{7,9},{8,10},{9,11},{10,... | collective-permute-start | bytes 786440 | tf_op jit(solution)/shard_map/ppermute | solution.py:389
  55.5 13.4 %collective-permute-start.8 = (f32[32,16,128]{2,1,0:T(8,128)S(1)}, f32[32,16,128]{2,1,0:T(8,128)S(1)}, u32[]{:S(2)}, u32[]{:S(2)}) collective-permute-start(f32[32,16,128]{2,1,0:T(8,128)S(1)} %get-tuple-element.38.own), channel_id=1, source_target_pairs={{2,0},{3,1},{4,2},{5,3},{6,4},{7,5},{8,6},{9,7},{10,8},{11,9},{12,... | collective-permute-start | bytes 786440 | tf_op jit(solution)/shard_map/ppermute | solution.py:389
  56.9 1.2 %collective-permute-start.9 = (f32[24,128]{1,0:T(8,128)S(1)}, f32[24,128]{1,0:T(8,128)S(1)}, u32[]{:S(2)}, u32[]{:S(2)}) collective-permute-start(f32[24,128]{1,0:T(8,128)S(1)} %get-tuple-element.39), channel_id=1, source_target_pairs={{0,1},{1,0},{2,3},{3,2},{4,5},{5,4},{6,7},{7,6},{8,9},{9,8},{10,11... | collective-permute-start | bytes 36872 | tf_op jit(solution)/shard_map/ppermute | solution.py:443
  58.2 7.6 %collective-permute-start.10 = (f32[24,128]{1,0:T(8,128)S(1)}, f32[24,128]{1,0:T(8,128)S(1)}, u32[]{:S(2)}, u32[]{:S(2)}) collective-permute-start(f32[24,128]{1,0:T(8,128)S(1)} %add.66), channel_id=1, source_target_pairs={{0,4},{1,5},{2,6},{3,7},{4,0},{5,1},{6,2},{7,3},{8,12},{9,13},{10,... | collective-permute-start | bytes 36872 | tf_op jit(solution)/shard_map/ppermute | solution.py:443
  60.7 6.2 %collective-permute-start.11 = (f32[24,128]{1,0:T(8,128)S(1)}, f32[24,128]{1,0:T(8,128)S(1)}, u32[]{:S(2)}, u32[]{:S(2)}) collective-permute-start(f32[24,128]{1,0:T(8,128)S(1)} %add.66), channel_id=1, source_target_pairs={{0,8},{1,9},{2,10},{3,11},{4,12},{5,13},{6,14},{7,15},{8,0},{9,1},... | collective-permute-start | bytes 36872 | tf_op jit(solution)/shard_map/ppermute | solution.py:443
  63.3 5.5 %collective-permute-start.12 = (f32[24,128]{1,0:T(8,128)S(1)}, f32[24,128]{1,0:T(8,128)S(1)}, u32[]{:S(2)}, u32[]{:S(2)}) collective-permute-start(f32[24,128]{1,0:T(8,128)S(1)} %add.66), channel_id=1, source_target_pairs={{0,12},{1,13},{2,14},{3,15},{4,8},{5,9},{6,10},{7,11},{8,4},{9,5},... | collective-permute-start | bytes 36872 | tf_op jit(solution)/shard_map/ppermute | solution.py:443
  68.9 2.0 %collective-permute-start.13 = (f32[2,32,16,128]{3,2,1,0:T(8,128)S(1)}, f32[2,32,16,128]{3,2,1,0:T(8,128)S(1)}, u32[]{:S(2)}, u32[]{:S(2)}) collective-permute-start(f32[2,32,16,128]{3,2,1,0:T(8,128)S(1)} %pad_maximum_fusion.1), channel_id=1, source_target_pairs={{0,1},{1,0},{2,3},{3,2},{4,5},{5,4},{6,7},{7,6},{8,9},{9,8},{10,11... | collective-permute-start | bytes 1572872 | tf_op jit(solution)/shard_map/ppermute | solution.py:395
  69.0 11.1 %collective-permute-start.14 = (f32[24,128]{1,0:T(8,128)S(1)}, f32[24,128]{1,0:T(8,128)S(1)}, u32[]{:S(2)}, u32[]{:S(2)}) collective-permute-start(f32[24,128]{1,0:T(8,128)S(1)} %add_add_fusion.part), channel_id=1, source_target_pairs={{0,2},{1,3},{2,0},{3,1},{4,6},{5,7},{6,4},{7,5},{8,10},{9,11},{10,... | collective-permute-start | bytes 36872 | tf_op jit(solution)/shard_map/ppermute | solution.py:443

commit v13 on v12

--- a/solution.py
+++ b/solution.py
@@ -13,7 +13,7 @@
 VMEM = pltpu.MemorySpace.VMEM
 SMEM = pltpu.MemorySpace.SMEM
 FULL = pl.BlockSpec(memory_space=VMEM)
-LIMIT = 30 * 1024 * 1024
+LIMIT = 20 * 1024 * 1024
 WIDE = 4
 TINY = float(np.finfo(np.float32).tiny)
 

time: 81.4 us -> 81.4 us (level)
  no operation moved by 1% of the time
where the time goes in v13:
time: 81.4 us; the launch traced here: 81 us
  starting transfers between devices  33 us (41%)
  Pallas kernels  28.7 us (35%)
  waiting for transfers between devices  9.59 us (12%)
  local copies, waits for them, and re-layouts  8.73 us (11%)
    pallas_call x8, Pallas kernels, call(): pl.pallas_call(kernel, out_shape=outs, in_specs=[pl.BlockSpec(memory_spac...  28.7 us
    ppermute x4, starting transfers between devices, two_slabs_away(): return (lax.ppermute(value, 'slab', up), lax.ppermute(value, 'slab', down))  17.1 us
    unnamed x25, local copies, waits for them, and re-layouts  6.8 us
    ppermute x5, waiting for transfers between devices, per_device(): lax.ppermute(sums, 'slab', [(i, i ^ d) for i in range(count)])  6.66 us
    ppermute x5, starting transfers between devices, per_device(): lax.ppermute(sums, 'slab', [(i, i ^ d) for i in range(count)])  5.36 us
    ppermute x2, starting transfers between devices, with_near(): near = lax.ppermute(passed, 'slab', swap)  4.17 us
    ppermute x2, waiting for transfers between devices, with_near(): near = lax.ppermute(passed, 'slab', swap)  2.91 us
    ppermute x1, starting transfers between devices, per_device(): befores.append(lax.ppermute(edges[0], 'slab', up))  2.31 us
  transfers between devices with their start and end apart: 15, of which 6 were waited for; matrix products, arithmetic and copies ran while one was open for 4% of the time, Pallas kernels for 32%

profile of v13, /device:TPU:0, one launch (start us, length us, event | category | flops | bytes accessed | tf_op | source)
XLA Modules:
  0.0 81.0 jit_solution(6415280746201705863)
XLA Ops:
  0.0 1.4 %collective-permute-start = (f32[32,16,128]{2,1,0:T(8,128)}, f32[32,16,128]{2,1,0:T(8,128)S(1)}, u32[]{:S(2)}, u32[]{:S(2)}) collective-permute-start(f32[32,16,128]{2,1,0:T(8,128)} %current.1), channel_id=1, source_target_pairs={{2,0},{3,1},{4,2},{5,3},{6,4},{7,5},{8,6},{9,7},{10,8},{11,9},{12,... | collective-permute-start | bytes 786440 | tf_op jit(solution)/shard_map/ppermute | solution.py:389
  1.4 5.5 %collective-permute-start.1 = (f32[32,16,128]{2,1,0:T(8,128)}, f32[32,16,128]{2,1,0:T(8,128)S(1)}, u32[]{:S(2)}, u32[]{:S(2)}) collective-permute-start(f32[32,16,128]{2,1,0:T(8,128)} %current.1), channel_id=1, source_target_pairs={{0,2},{1,3},{2,4},{3,5},{4,6},{5,7},{6,8},{7,9},{8,10},{9,11},{10,... | collective-permute-start | bytes 786440 | tf_op jit(solution)/shard_map/ppermute | solution.py:389
  6.9 1.3 %slice.19 = f32[4,32,16,128]{3,2,1,0:T(8,128)S(1)} slice(f32[6,32,16,128]{3,2,1,0:T(8,128)} %raw.7), slice={[0:4], [0:32], [0:16], [0:128]} | slice | bytes 2097152 | tf_op jit(solution)/shard_map/slice | solution.py:323
  8.3 1.6 %pack.3 = (f32[1920,128]{1,0:T(8,128)}, f32[1920,128]{1,0:T(8,128)}) custom-call(f32[128,16,128]{2,1,0:T(8,128)S(1)} %bitcast.16), custom_call_target="tpu_custom_call" | custom-call | flops 1000000 | bytes 10000000 | tf_op jit(solution)/shard_map/pack/pallas_call | solution.py:95
  9.9 1.5 %collective-permute-start.5 = (f32[1920,128]{1,0:T(8,128)}, f32[1920,128]{1,0:T(8,128)S(1)}, u32[]{:S(2)}, u32[]{:S(2)}) collective-permute-start(f32[1920,128]{1,0:T(8,128)} %get-tuple-element.34), channel_id=1, source_target_pairs={{0,1},{1,2},{2,3},{3,4},{4,5},{5,6},{6,7},{7,8},{8,9},{9,10},{10,1... | collective-permute-start | bytes 2949128 | tf_op jit(solution)/shard_map/ppermute | solution.py:421
  11.4 1.3 %collective-permute-start.6 = (f32[1920,128]{1,0:T(8,128)}, f32[1920,128]{1,0:T(8,128)}, u32[]{:S(2)}, u32[]{:S(2)}) collective-permute-start(f32[1920,128]{1,0:T(8,128)} %get-tuple-element.35), channel_id=1, source_target_pairs={{1,0},{2,1},{3,2},{4,3},{5,4},{6,5},{7,6},{8,7},{9,8},{10,9},{11,1... | collective-permute-start | bytes 2949128 | tf_op jit(solution)/shard_map/ppermute | solution.py:422
  12.7 0.6 fusion.12
  13.3 3.7 %weights.1 = (bf16[288,240]{1,0:T(8,128)(2,1)S(1)}, bf16[6,256,256]{2,1,0:T(8,128)(2,1)S(1)}, bf16[6,256,768]{2,1,0:T(8,128)(2,1)S(1)}, bf16[6,32,96]{2,1,0:T(8,...) custom-call(f32[6,3,31]{2,1,0:T(4,128)S(1)} %copy-done.2), custom_call_target="tpu_custom_call" | custom-call | flops 10000000000 | bytes 10000000 | tf_op jit(solution)/shard_map/weights/pallas_call | solution.py:95
  17.0 1.4 %copy-done.3 = bf16[6,256,768]{2,1,0:T(8,128)(2,1)} copy-done((bf16[6,256,768]{2,1,0:T(8,128)(2,1)}, bf16[6,256,768]{2,1,0:T(8,128)(2,1)S(1)}, u32[]{:S(2)}) %copy-start.3) | copy-done | bytes 2359320
  18.5 1.4 %copy-done.5 = bf16[6,256,768]{2,1,0:T(8,128)(2,1)} copy-done((bf16[6,256,768]{2,1,0:T(8,128)(2,1)}, bf16[6,256,768]{2,1,0:T(8,128)(2,1)S(1)}, u32[]{:S(2)}) %copy-start.5) | copy-done | bytes 2359320
  19.9 1.0 %copy-done.7 = bf16[6,256,256]{2,1,0:T(8,128)(2,1)} copy-done((bf16[6,256,256]{2,1,0:T(8,128)(2,1)}, bf16[6,256,256]{2,1,0:T(8,128)(2,1)S(1)}, u32[]{:S(2)}) %copy-start.7) | copy-done | bytes 786456
  20.9 1.0 %copy-done.9 = bf16[6,256,256]{2,1,0:T(8,128)(2,1)} copy-done((bf16[6,256,256]{2,1,0:T(8,128)(2,1)}, bf16[6,256,256]{2,1,0:T(8,128)(2,1)S(1)}, u32[]{:S(2)}) %copy-start.9) | copy-done | bytes 786456
  21.9 0.8 %copy.16 = f32[6,1,31]{2,0,1:T(8,128)S(1)} copy(f32[6,1,31]{2,1,0:T(1,128)} %get-tuple-element.46) | data formatting | bytes 1488
  23.0 4.1 %collective-permute-start.2 = (f32[2,32,16,128]{3,2,1,0:T(8,128)S(1)}, f32[2,32,16,128]{3,2,1,0:T(8,128)S(1)}, u32[]{:S(2)}, u32[]{:S(2)}) collective-permute-start(f32[2,32,16,128]{3,2,1,0:T(8,128)S(1)} %pad_maximum_fusion), channel_id=1, source_target_pairs={{0,1},{1,0},{2,3},{3,2},{4,5},{5,4},{6,7},{7,6},{8,9},{9,8},{10,11... | collective-permute-start | bytes 1572872 | tf_op jit(solution)/shard_map/ppermute | solution.py:395
  27.4 1.2 %collective-permute-done.2.refs_0_.near = f32[2,32,16,128]{3,2,1,0:T(8,128)S(1)} collective-permute-done((f32[2,32,16,128]{3,2,1,0:T(8,128)S(1)}, f32[2,32,16,128]{3,2,1,0:T(8,128)S(1)}, u32[]{:S(2)}, u32[]{:S(2)}) %collective-permute-start.2) | collective-permute-done | bytes 524320 | tf_op jit(solution)/shard_map/ppermute | solution.py:395
  28.8 2.3 %collective-permute-start.3 = (f32[960,128]{1,0:T(8,128)S(1)}, f32[960,128]{1,0:T(8,128)S(1)}, u32[]{:S(2)}, u32[]{:S(2)}) collective-permute-start(f32[960,128]{1,0:T(8,128)S(1)} %get-tuple-element.25), channel_id=1, source_target_pairs={{0,1},{1,2},{2,3},{3,4},{4,5},{5,6},{6,7},{7,8},{8,9},{9,10},{10,1... | collective-permute-start | bytes 1474568 | tf_op jit(solution)/shard_map/ppermute | solution.py:431
  31.1 1.3 %collective-permute-start.4 = (f32[960,128]{1,0:T(8,128)S(1)}, f32[960,128]{1,0:T(8,128)S(1)}, u32[]{:S(2)}, u32[]{:S(2)}) collective-permute-start(f32[960,128]{1,0:T(8,128)S(1)} %get-tuple-element.26), channel_id=1, source_target_pairs={{1,0},{2,1},{3,2},{4,3},{5,4},{6,5},{7,6},{8,7},{9,8},{10,9},{11,1... | collective-permute-start | bytes 1474568 | tf_op jit(solution)/shard_map/ppermute | solution.py:432
  32.4 1.1 %copy-done.10 = bf16[6,256,256]{2,1,0:T(8,128)(2,1)S(1)} copy-done((bf16[6,256,256]{2,1,0:T(8,128)(2,1)S(1)}, bf16[6,256,256]{2,1,0:T(8,128)(2,1)}, u32[]{:S(2)}) %copy-start.10) | copy-done | bytes 786456
  33.5 6.9 %forward.1 = (f32[6,32,48,128]{3,2,1,0:T(8,128)S(1)}, f32[24,128]{1,0:T(8,128)S(1)}) custom-call(s32[1]{0:T(128)} %bitcast.parity, f32[6,32]{1,0:T(8,128)S(1)} %multiply_reduce_fusion.1.wzs, f32[32,16,128]{2,1,0:T(8,128)S(1)} %collective-permute-done.1.far_before, f32[2,32,16,128]{3,2,1,0:T(8,128)S(1)} %collective-permute-done.2.refs_0_.near, ...), custom_call_target="tpu_custom_call" | custom-call | flops 10000000000 | bytes 10000000 | tf_op jit(solution)/shard_map/forward/pallas_call | solution.py:95
  40.5 4.1 %early_adjoint.1 = (f32[256,256]{1,0:T(8,128)S(1)}, f32[4,32,32,128]{3,2,1,0:T(8,128)S(1)}) custom-call(f32[1920,128]{1,0:T(8,128)S(1)} %collective-permute-done.5.before, f32[1920,128]{1,0:T(8,128)} %collective-permute-done.6.after, f32[6,32,16,128]{3,2,1,0:T(8,128)S(1)} %copy-done, f32[6,32,48,128]{3,2,1,0:T(8,128)S(1)} %get-tuple-element.30.blurred, ...), custom_call_target="tpu_custom_call" | custom-call | flops 10000000000 | bytes 10000000 | tf_op jit(solution)/shard_map/early_adjoint/pallas_call | solution.py:95
  44.6 2.2 %late_adjoint.1 = (f32[32,16,128]{2,1,0:T(8,128)S(1)}, f32[24,128]{1,0:T(8,128)S(1)}, f32[2,32,32,128]{3,2,1,0:T(8,128)S(1)}) custom-call(f32[6,32]{1,0:T(8,128)S(1)} %multiply_reduce_fusion.1.wzs, f32[960,128]{1,0:T(8,128)S(1)} %collective-permute-done.3.before, f32[960,128]{1,0:T(8,128)S(1)} %collective-permute-done.4.after, ...), custom_call_target="tpu_custom_call" | custom-call | flops 10000000000 | bytes 10000000 | tf_op jit(solution)/shard_map/late_adjoint/pallas_call | solution.py:95
  46.8 8.7 %collective-permute-start.7 = (f32[32,16,128]{2,1,0:T(8,128)S(1)}, f32[32,16,128]{2,1,0:T(8,128)S(1)}, u32[]{:S(2)}, u32[]{:S(2)}) collective-permute-start(f32[32,16,128]{2,1,0:T(8,128)S(1)} %get-tuple-element.38.own), channel_id=1, source_target_pairs={{0,2},{1,3},{2,4},{3,5},{4,6},{5,7},{6,8},{7,9},{8,10},{9,11},{10,... | collective-permute-start | bytes 786440 | tf_op jit(solution)/shard_map/ppermute | solution.py:389
  55.5 1.5 %collective-permute-start.8 = (f32[32,16,128]{2,1,0:T(8,128)S(1)}, f32[32,16,128]{2,1,0:T(8,128)S(1)}, u32[]{:S(2)}, u32[]{:S(2)}) collective-permute-start(f32[32,16,128]{2,1,0:T(8,128)S(1)} %get-tuple-element.38.own), channel_id=1, source_target_pairs={{2,0},{3,1},{4,2},{5,3},{6,4},{7,5},{8,6},{9,7},{10,8},{11,9},{12,... | collective-permute-start | bytes 786440 | tf_op jit(solution)/shard_map/ppermute | solution.py:389
  57.0 1.2 %collective-permute-done.9 = f32[24,128]{1,0:T(8,128)S(1)} collective-permute-done((f32[24,128]{1,0:T(8,128)S(1)}, f32[24,128]{1,0:T(8,128)S(1)}, u32[]{:S(2)}, u32[]{:S(2)}) %collective-permute-start.9) | collective-permute-done | bytes 12320 | tf_op jit(solution)/shard_map/ppermute | solution.py:443
  58.2 2.5 %collective-permute-start.10 = (f32[24,128]{1,0:T(8,128)S(1)}, f32[24,128]{1,0:T(8,128)S(1)}, u32[]{:S(2)}, u32[]{:S(2)}) collective-permute-start(f32[24,128]{1,0:T(8,128)S(1)} %add.66), channel_id=1, source_target_pairs={{0,4},{1,5},{2,6},{3,7},{4,0},{5,1},{6,2},{7,3},{8,12},{9,13},{10,... | collective-permute-start | bytes 36872 | tf_op jit(solution)/shard_map/ppermute | solution.py:443
  60.7 2.6 %collective-permute-start.11 = (f32[24,128]{1,0:T(8,128)S(1)}, f32[24,128]{1,0:T(8,128)S(1)}, u32[]{:S(2)}, u32[]{:S(2)}) collective-permute-start(f32[24,128]{1,0:T(8,128)S(1)} %add.66), channel_id=1, source_target_pairs={{0,8},{1,9},{2,10},{3,11},{4,12},{5,13},{6,14},{7,15},{8,0},{9,1},... | collective-permute-start | bytes 36872 | tf_op jit(solution)/shard_map/ppermute | solution.py:443
  63.3 2.5 %collective-permute-done.10 = f32[24,128]{1,0:T(8,128)S(1)} collective-permute-done((f32[24,128]{1,0:T(8,128)S(1)}, f32[24,128]{1,0:T(8,128)S(1)}, u32[]{:S(2)}, u32[]{:S(2)}) %collective-permute-start.10) | collective-permute-done | bytes 12320 | tf_op jit(solution)/shard_map/ppermute | solution.py:443
  65.8 1.1 %collective-permute-done.11 = f32[24,128]{1,0:T(8,128)S(1)} collective-permute-done((f32[24,128]{1,0:T(8,128)S(1)}, f32[24,128]{1,0:T(8,128)S(1)}, u32[]{:S(2)}, u32[]{:S(2)}) %collective-permute-start.11) | collective-permute-done | bytes 12320 | tf_op jit(solution)/shard_map/ppermute | solution.py:443
  67.0 1.8 %collective-permute-done.12 = f32[24,128]{1,0:T(8,128)S(1)} collective-permute-done((f32[24,128]{1,0:T(8,128)S(1)}, f32[24,128]{1,0:T(8,128)S(1)}, u32[]{:S(2)}, u32[]{:S(2)}) %collective-permute-start.12) | collective-permute-done | bytes 12320 | tf_op jit(solution)/shard_map/ppermute | solution.py:443
  69.2 1.7 %collective-permute-done.13.near = f32[2,32,16,128]{3,2,1,0:T(8,128)S(1)} collective-permute-done((f32[2,32,16,128]{3,2,1,0:T(8,128)S(1)}, f32[2,32,16,128]{3,2,1,0:T(8,128)S(1)}, u32[]{:S(2)}, u32[]{:S(2)}) %collective-permute-start.13) | collective-permute-done | bytes 524320 | tf_op jit(solution)/shard_map/ppermute | solution.py:395
  70.9 9.2 %iteration.1.values = f32[32,16,128]{2,1,0:T(8,128)S(1)} custom-call(s32[1]{0:T(128)} %bitcast.parity, f32[32,16,128]{2,1,0:T(8,128)S(1)} %collective-permute-done.7.far_before, f32[2,32,16,128]{3,2,1,0:T(8,128)S(1)} %collective-permute-done.13.near, f32[32,16,128]{2,1,0:T(8,128)S(1)} %get-tuple-element.38.own, ...), custom_call_target="tpu_custom_call" | custom-call | flops 20000000000 | bytes 10000000 | tf_op jit(solution)/shard_map/iteration/pallas_call | solution.py:95
  80.1 0.8 %scaled.1 = f32[32,16,128]{2,1,0:T(8,128)} custom-call(f32[32,16,128]{2,1,0:T(8,128)S(1)} %iteration.1.values, f32[24,128]{1,0:T(8,128)S(1)} %add_add_fusion.part, f32[24,128]{1,0:T(8,128)S(1)} %collective-permute-done.14.rest), custom_call_target="tpu_custom_call" | custom-call | flops 100000 | bytes 10000000 | tf_op jit(solution)/shard_map/scaled/pallas_call | solution.py:95
  (49 shorter events, 1.2 us)
Async XLA Ops:
  0.0 12.7 %copy-start.2 = (f32[6,3,31]{2,1,0:T(4,128)S(1)}, f32[6,3,31]{2,1,0:T(4,128)}, u32[]{:S(2)}) copy-start(f32[6,3,31]{2,1,0:T(4,128)} %taps_ref.1) | copy-start | bytes 6700
  0.0 22.8 %collective-permute-start = (f32[32,16,128]{2,1,0:T(8,128)}, f32[32,16,128]{2,1,0:T(8,128)S(1)}, u32[]{:S(2)}, u32[]{:S(2)}) collective-permute-start(f32[32,16,128]{2,1,0:T(8,128)} %current.1), channel_id=1, source_target_pairs={{2,0},{3,1},{4,2},{5,3},{6,4},{7,5},{8,6},{9,7},{10,8},{11,9},{12,... | collective-permute-start | bytes 786440 | tf_op jit(solution)/shard_map/ppermute | solution.py:389
  1.4 21.4 %collective-permute-start.1 = (f32[32,16,128]{2,1,0:T(8,128)}, f32[32,16,128]{2,1,0:T(8,128)S(1)}, u32[]{:S(2)}, u32[]{:S(2)}) collective-permute-start(f32[32,16,128]{2,1,0:T(8,128)} %current.1), channel_id=1, source_target_pairs={{0,2},{1,3},{2,4},{3,5},{4,6},{5,7},{6,8},{7,9},{8,10},{9,11},{10,... | collective-permute-start | bytes 786440 | tf_op jit(solution)/shard_map/ppermute | solution.py:389
  9.9 30.6 %collective-permute-start.5 = (f32[1920,128]{1,0:T(8,128)}, f32[1920,128]{1,0:T(8,128)S(1)}, u32[]{:S(2)}, u32[]{:S(2)}) collective-permute-start(f32[1920,128]{1,0:T(8,128)} %get-tuple-element.34), channel_id=1, source_target_pairs={{0,1},{1,2},{2,3},{3,4},{4,5},{5,6},{6,7},{7,8},{8,9},{9,10},{10,1... | collective-permute-start | bytes 2949128 | tf_op jit(solution)/shard_map/ppermute | solution.py:421
  11.4 29.1 %collective-permute-start.6 = (f32[1920,128]{1,0:T(8,128)}, f32[1920,128]{1,0:T(8,128)}, u32[]{:S(2)}, u32[]{:S(2)}) collective-permute-start(f32[1920,128]{1,0:T(8,128)} %get-tuple-element.35), channel_id=1, source_target_pairs={{1,0},{2,1},{3,2},{4,3},{5,4},{6,5},{7,6},{8,7},{9,8},{10,9},{11,1... | collective-permute-start | bytes 2949128 | tf_op jit(solution)/shard_map/ppermute | solution.py:422
  13.3 9.6 %copy-start.1 = (f32[32,16,128]{2,1,0:T(8,128)S(1)}, f32[32,16,128]{2,1,0:T(8,128)}, u32[]{:S(2)}) copy-start(f32[32,16,128]{2,1,0:T(8,128)} %current.1) | copy-start | bytes 786436
  17.0 1.4 %copy-start.3 = (bf16[6,256,768]{2,1,0:T(8,128)(2,1)}, bf16[6,256,768]{2,1,0:T(8,128)(2,1)S(1)}, u32[]{:S(2)}) copy-start(bf16[6,256,768]{2,1,0:T(8,128)(2,1)S(1)} %get-tuple-element.33.wz.wza) | copy-start | bytes 7077892
  18.5 1.4 %copy-start.5 = (bf16[6,256,768]{2,1,0:T(8,128)(2,1)}, bf16[6,256,768]{2,1,0:T(8,128)(2,1)S(1)}, u32[]{:S(2)}) copy-start(bf16[6,256,768]{2,1,0:T(8,128)(2,1)S(1)} %get-tuple-element.29.wz) | copy-start | bytes 7077892
  19.9 1.0 %copy-start.7 = (bf16[6,256,256]{2,1,0:T(8,128)(2,1)}, bf16[6,256,256]{2,1,0:T(8,128)(2,1)S(1)}, u32[]{:S(2)}) copy-start(bf16[6,256,256]{2,1,0:T(8,128)(2,1)S(1)} %get-tuple-element.32.wx.wxa) | copy-start | bytes 2359300
  20.9 1.0 %copy-start.9 = (bf16[6,256,256]{2,1,0:T(8,128)(2,1)}, bf16[6,256,256]{2,1,0:T(8,128)(2,1)S(1)}, u32[]{:S(2)}) copy-start(bf16[6,256,256]{2,1,0:T(8,128)(2,1)S(1)} %get-tuple-element.28.wx) | copy-start | bytes 2359300
  21.8 5.5 %copy-start = (f32[6,32,16,128]{3,2,1,0:T(8,128)S(1)}, f32[6,32,16,128]{3,2,1,0:T(8,128)}, u32[]{:S(2)}) copy-start(f32[6,32,16,128]{3,2,1,0:T(8,128)} %raw.7) | copy-start | bytes 4718596
  21.9 10.5 %copy-start.6 = (bf16[6,256,768]{2,1,0:T(8,128)(2,1)S(1)}, bf16[6,256,768]{2,1,0:T(8,128)(2,1)}, u32[]{:S(2)}) copy-start(bf16[6,256,768]{2,1,0:T(8,128)(2,1)} %copy-done.5) | copy-start | bytes 7077892
  23.0 5.6 %collective-permute-start.2 = (f32[2,32,16,128]{3,2,1,0:T(8,128)S(1)}, f32[2,32,16,128]{3,2,1,0:T(8,128)S(1)}, u32[]{:S(2)}, u32[]{:S(2)}) collective-permute-start(f32[2,32,16,128]{3,2,1,0:T(8,128)S(1)} %pad_maximum_fusion), channel_id=1, source_target_pairs={{0,1},{1,0},{2,3},{3,2},{4,5},{5,4},{6,7},{7,6},{8,9},{9,8},{10,11... | collective-permute-start | bytes 1572872 | tf_op jit(solution)/shard_map/ppermute | solution.py:395
  28.8 15.8 %collective-permute-start.3 = (f32[960,128]{1,0:T(8,128)S(1)}, f32[960,128]{1,0:T(8,128)S(1)}, u32[]{:S(2)}, u32[]{:S(2)}) collective-permute-start(f32[960,128]{1,0:T(8,128)S(1)} %get-tuple-element.25), channel_id=1, source_target_pairs={{0,1},{1,2},{2,3},{3,4},{4,5},{5,6},{6,7},{7,8},{8,9},{9,10},{10,1... | collective-permute-start | bytes 1474568 | tf_op jit(solution)/shard_map/ppermute | solution.py:431
  31.1 13.5 %collective-permute-start.4 = (f32[960,128]{1,0:T(8,128)S(1)}, f32[960,128]{1,0:T(8,128)S(1)}, u32[]{:S(2)}, u32[]{:S(2)}) collective-permute-start(f32[960,128]{1,0:T(8,128)S(1)} %get-tuple-element.26), channel_id=1, source_target_pairs={{1,0},{2,1},{3,2},{4,3},{5,4},{6,5},{7,6},{8,7},{9,8},{10,9},{11,1... | collective-permute-start | bytes 1474568 | tf_op jit(solution)/shard_map/ppermute | solution.py:432
  32.4 1.1 %copy-start.10 = (bf16[6,256,256]{2,1,0:T(8,128)(2,1)S(1)}, bf16[6,256,256]{2,1,0:T(8,128)(2,1)}, u32[]{:S(2)}) copy-start(bf16[6,256,256]{2,1,0:T(8,128)(2,1)} %copy-done.9) | copy-start | bytes 2359300
  33.5 6.9 %copy-start.4 = (bf16[6,256,768]{2,1,0:T(8,128)(2,1)S(1)}, bf16[6,256,768]{2,1,0:T(8,128)(2,1)}, u32[]{:S(2)}) copy-start(bf16[6,256,768]{2,1,0:T(8,128)(2,1)} %copy-done.3) | copy-start | bytes 7077892
  33.5 6.9 %copy-start.8 = (bf16[6,256,256]{2,1,0:T(8,128)(2,1)S(1)}, bf16[6,256,256]{2,1,0:T(8,128)(2,1)}, u32[]{:S(2)}) copy-start(bf16[6,256,256]{2,1,0:T(8,128)(2,1)} %copy-done.7) | copy-start | bytes 2359300
  44.6 26.3 %copy-start.11 = (bf16[6,256,256]{2,1,0:T(8,128)(2,1)S(1)}, bf16[6,256,256]{2,1,0:T(8,128)(2,1)}, u32[]{:S(2)}) copy-start(bf16[6,256,256]{2,1,0:T(8,128)(2,1)} %copy-done.9) | copy-start | bytes 2359300
  46.8 22.1 %collective-permute-start.7 = (f32[32,16,128]{2,1,0:T(8,128)S(1)}, f32[32,16,128]{2,1,0:T(8,128)S(1)}, u32[]{:S(2)}, u32[]{:S(2)}) collective-permute-start(f32[32,16,128]{2,1,0:T(8,128)S(1)} %get-tuple-element.38.own), channel_id=1, source_target_pairs={{0,2},{1,3},{2,4},{3,5},{4,6},{5,7},{6,8},{7,9},{8,10},{9,11},{10,... | collective-permute-start | bytes 786440 | tf_op jit(solution)/shard_map/ppermute | solution.py:389
  55.5 13.4 %collective-permute-start.8 = (f32[32,16,128]{2,1,0:T(8,128)S(1)}, f32[32,16,128]{2,1,0:T(8,128)S(1)}, u32[]{:S(2)}, u32[]{:S(2)}) collective-permute-start(f32[32,16,128]{2,1,0:T(8,128)S(1)} %get-tuple-element.38.own), channel_id=1, source_target_pairs={{2,0},{3,1},{4,2},{5,3},{6,4},{7,5},{8,6},{9,7},{10,8},{11,9},{12,... | collective-permute-start | bytes 786440 | tf_op jit(solution)/shard_map/ppermute | solution.py:389
  56.9 1.2 %collective-permute-start.9 = (f32[24,128]{1,0:T(8,128)S(1)}, f32[24,128]{1,0:T(8,128)S(1)}, u32[]{:S(2)}, u32[]{:S(2)}) collective-permute-start(f32[24,128]{1,0:T(8,128)S(1)} %get-tuple-element.39), channel_id=1, source_target_pairs={{0,1},{1,0},{2,3},{3,2},{4,5},{5,4},{6,7},{7,6},{8,9},{9,8},{10,11... | collective-permute-start | bytes 36872 | tf_op jit(solution)/shard_map/ppermute | solution.py:443
  58.2 7.6 %collective-permute-start.10 = (f32[24,128]{1,0:T(8,128)S(1)}, f32[24,128]{1,0:T(8,128)S(1)}, u32[]{:S(2)}, u32[]{:S(2)}) collective-permute-start(f32[24,128]{1,0:T(8,128)S(1)} %add.66), channel_id=1, source_target_pairs={{0,4},{1,5},{2,6},{3,7},{4,0},{5,1},{6,2},{7,3},{8,12},{9,13},{10,... | collective-permute-start | bytes 36872 | tf_op jit(solution)/shard_map/ppermute | solution.py:443
  60.7 6.2 %collective-permute-start.11 = (f32[24,128]{1,0:T(8,128)S(1)}, f32[24,128]{1,0:T(8,128)S(1)}, u32[]{:S(2)}, u32[]{:S(2)}) collective-permute-start(f32[24,128]{1,0:T(8,128)S(1)} %add.66), channel_id=1, source_target_pairs={{0,8},{1,9},{2,10},{3,11},{4,12},{5,13},{6,14},{7,15},{8,0},{9,1},... | collective-permute-start | bytes 36872 | tf_op jit(solution)/shard_map/ppermute | solution.py:443
  63.3 5.5 %collective-permute-start.12 = (f32[24,128]{1,0:T(8,128)S(1)}, f32[24,128]{1,0:T(8,128)S(1)}, u32[]{:S(2)}, u32[]{:S(2)}) collective-permute-start(f32[24,128]{1,0:T(8,128)S(1)} %add.66), channel_id=1, source_target_pairs={{0,12},{1,13},{2,14},{3,15},{4,8},{5,9},{6,10},{7,11},{8,4},{9,5},... | collective-permute-start | bytes 36872 | tf_op jit(solution)/shard_map/ppermute | solution.py:443
  68.9 2.0 %collective-permute-start.13 = (f32[2,32,16,128]{3,2,1,0:T(8,128)S(1)}, f32[2,32,16,128]{3,2,1,0:T(8,128)S(1)}, u32[]{:S(2)}, u32[]{:S(2)}) collective-permute-start(f32[2,32,16,128]{3,2,1,0:T(8,128)S(1)} %pad_maximum_fusion.1), channel_id=1, source_target_pairs={{0,1},{1,0},{2,3},{3,2},{4,5},{5,4},{6,7},{7,6},{8,9},{9,8},{10,11... | collective-permute-start | bytes 1572872 | tf_op jit(solution)/shard_map/ppermute | solution.py:395
  69.0 11.1 %collective-permute-start.14 = (f32[24,128]{1,0:T(8,128)S(1)}, f32[24,128]{1,0:T(8,128)S(1)}, u32[]{:S(2)}, u32[]{:S(2)}) collective-permute-start(f32[24,128]{1,0:T(8,128)S(1)} %add_add_fusion.part), channel_id=1, source_target_pairs={{0,2},{1,3},{2,0},{3,1},{4,6},{5,7},{6,4},{7,5},{8,10},{9,11},{10,... | collective-permute-start | bytes 36872 | tf_op jit(solution)/shard_map/ppermute | solution.py:443

commit v14 on v13

--- a/solution.py
+++ b/solution.py
@@ -438,7 +438,7 @@
 
     far = two_slabs_away(current, count)
     bits = [1 << b for b in range(count.bit_length() - 1)]
-    rounds = [bits[:1], bits[2:4] + [sum(bits[2:4])], *([b] for b in bits[4:]), bits[1:2]]
+    rounds = [bits[:1], [sum(bits[2:4])] + bits[3:1:-1], *([b] for b in bits[4:]), bits[1:2]]
     for r, distances in enumerate(rounds):
         others = [lax.ppermute(sums, "slab", [(i, i ^ d) for i in range(count)]) for d in distances]
         if r == 1:

time: 81.4 us -> 80.3 us (0.986)
  waiting for transfers between devices: 9.59 us -> 8.62 us
    ppermute x5, waiting for transfers between devices: 6.66 us -> 5.6 us  [per_device(): lax.ppermute(sums, 'slab', [(i, i ^ d) for i in range(count)])]
  transfers between devices with their start and end apart: 15 -> 15, of which waited for: 6 -> 4; matrix products, arithmetic and copies ran while one was open for 4% -> 4% of each run, Pallas kernels for 32% -> 32%
where the time goes in v14:
time: 80.3 us; the launch traced here: 79.9 us
  starting transfers between devices  32.9 us (41%)
  Pallas kernels  28.7 us (36%)
  local copies, waits for them, and re-layouts  8.73 us (11%)
  waiting for transfers between devices  8.62 us (11%)
    pallas_call x8, Pallas kernels, call(): pl.pallas_call(kernel, out_shape=outs, in_specs=[pl.BlockSpec(memory_spac...  28.7 us
    ppermute x4, starting transfers between devices, two_slabs_away(): return (lax.ppermute(value, 'slab', up), lax.ppermute(value, 'slab', down))  17.1 us
    unnamed x25, local copies, waits for them, and re-layouts  6.8 us
    ppermute x5, waiting for transfers between devices, per_device(): lax.ppermute(sums, 'slab', [(i, i ^ d) for i in range(count)])  5.6 us
    ppermute x5, starting transfers between devices, per_device(): lax.ppermute(sums, 'slab', [(i, i ^ d) for i in range(count)])  5.27 us
    ppermute x2, starting transfers between devices, with_near(): near = lax.ppermute(passed, 'slab', swap)  4.17 us
    ppermute x2, waiting for transfers between devices, with_near(): near = lax.ppermute(passed, 'slab', swap)  3 us
    ppermute x1, starting transfers between devices, per_device(): befores.append(lax.ppermute(edges[0], 'slab', up))  2.31 us
  transfers between devices with their start and end apart: 15, of which 4 were waited for; matrix products, arithmetic and copies ran while one was open for 4% of the time, Pallas kernels for 32%

profile of v14, /device:TPU:0, one launch (start us, length us, event | category | flops | bytes accessed | tf_op | source)
XLA Modules:
  0.0 79.9 jit_solution(3197235655816501425)
XLA Ops:
  0.0 1.4 %collective-permute-start = (f32[32,16,128]{2,1,0:T(8,128)}, f32[32,16,128]{2,1,0:T(8,128)S(1)}, u32[]{:S(2)}, u32[]{:S(2)}) collective-permute-start(f32[32,16,128]{2,1,0:T(8,128)} %current.1), channel_id=1, source_target_pairs={{2,0},{3,1},{4,2},{5,3},{6,4},{7,5},{8,6},{9,7},{10,8},{11,9},{12,... | collective-permute-start | bytes 786440 | tf_op jit(solution)/shard_map/ppermute | solution.py:389
  1.4 5.5 %collective-permute-start.1 = (f32[32,16,128]{2,1,0:T(8,128)}, f32[32,16,128]{2,1,0:T(8,128)S(1)}, u32[]{:S(2)}, u32[]{:S(2)}) collective-permute-start(f32[32,16,128]{2,1,0:T(8,128)} %current.1), channel_id=1, source_target_pairs={{0,2},{1,3},{2,4},{3,5},{4,6},{5,7},{6,8},{7,9},{8,10},{9,11},{10,... | collective-permute-start | bytes 786440 | tf_op jit(solution)/shard_map/ppermute | solution.py:389
  6.9 1.3 %slice.19 = f32[4,32,16,128]{3,2,1,0:T(8,128)S(1)} slice(f32[6,32,16,128]{3,2,1,0:T(8,128)} %raw.7), slice={[0:4], [0:32], [0:16], [0:128]} | slice | bytes 2097152 | tf_op jit(solution)/shard_map/slice | solution.py:323
  8.3 1.6 %pack.3 = (f32[1920,128]{1,0:T(8,128)}, f32[1920,128]{1,0:T(8,128)}) custom-call(f32[128,16,128]{2,1,0:T(8,128)S(1)} %bitcast.16), custom_call_target="tpu_custom_call" | custom-call | flops 1000000 | bytes 10000000 | tf_op jit(solution)/shard_map/pack/pallas_call | solution.py:95
  9.9 1.5 %collective-permute-start.5 = (f32[1920,128]{1,0:T(8,128)}, f32[1920,128]{1,0:T(8,128)S(1)}, u32[]{:S(2)}, u32[]{:S(2)}) collective-permute-start(f32[1920,128]{1,0:T(8,128)} %get-tuple-element.34), channel_id=1, source_target_pairs={{0,1},{1,2},{2,3},{3,4},{4,5},{5,6},{6,7},{7,8},{8,9},{9,10},{10,1... | collective-permute-start | bytes 2949128 | tf_op jit(solution)/shard_map/ppermute | solution.py:421
  11.4 1.3 %collective-permute-start.6 = (f32[1920,128]{1,0:T(8,128)}, f32[1920,128]{1,0:T(8,128)}, u32[]{:S(2)}, u32[]{:S(2)}) collective-permute-start(f32[1920,128]{1,0:T(8,128)} %get-tuple-element.35), channel_id=1, source_target_pairs={{1,0},{2,1},{3,2},{4,3},{5,4},{6,5},{7,6},{8,7},{9,8},{10,9},{11,1... | collective-permute-start | bytes 2949128 | tf_op jit(solution)/shard_map/ppermute | solution.py:422
  12.7 0.6 fusion.12
  13.3 3.7 %weights.1 = (bf16[288,240]{1,0:T(8,128)(2,1)S(1)}, bf16[6,256,256]{2,1,0:T(8,128)(2,1)S(1)}, bf16[6,256,768]{2,1,0:T(8,128)(2,1)S(1)}, bf16[6,32,96]{2,1,0:T(8,...) custom-call(f32[6,3,31]{2,1,0:T(4,128)S(1)} %copy-done.2), custom_call_target="tpu_custom_call" | custom-call | flops 10000000000 | bytes 10000000 | tf_op jit(solution)/shard_map/weights/pallas_call | solution.py:95
  17.0 1.4 %copy-done.3 = bf16[6,256,768]{2,1,0:T(8,128)(2,1)} copy-done((bf16[6,256,768]{2,1,0:T(8,128)(2,1)}, bf16[6,256,768]{2,1,0:T(8,128)(2,1)S(1)}, u32[]{:S(2)}) %copy-start.3) | copy-done | bytes 2359320
  18.5 1.4 %copy-done.5 = bf16[6,256,768]{2,1,0:T(8,128)(2,1)} copy-done((bf16[6,256,768]{2,1,0:T(8,128)(2,1)}, bf16[6,256,768]{2,1,0:T(8,128)(2,1)S(1)}, u32[]{:S(2)}) %copy-start.5) | copy-done | bytes 2359320
  19.9 1.0 %copy-done.7 = bf16[6,256,256]{2,1,0:T(8,128)(2,1)} copy-done((bf16[6,256,256]{2,1,0:T(8,128)(2,1)}, bf16[6,256,256]{2,1,0:T(8,128)(2,1)S(1)}, u32[]{:S(2)}) %copy-start.7) | copy-done | bytes 786456
  20.9 1.0 %copy-done.9 = bf16[6,256,256]{2,1,0:T(8,128)(2,1)} copy-done((bf16[6,256,256]{2,1,0:T(8,128)(2,1)}, bf16[6,256,256]{2,1,0:T(8,128)(2,1)S(1)}, u32[]{:S(2)}) %copy-start.9) | copy-done | bytes 786456
  21.9 0.8 %copy.16 = f32[6,1,31]{2,0,1:T(8,128)S(1)} copy(f32[6,1,31]{2,1,0:T(1,128)} %get-tuple-element.46) | data formatting | bytes 1488
  23.0 4.1 %collective-permute-start.2 = (f32[2,32,16,128]{3,2,1,0:T(8,128)S(1)}, f32[2,32,16,128]{3,2,1,0:T(8,128)S(1)}, u32[]{:S(2)}, u32[]{:S(2)}) collective-permute-start(f32[2,32,16,128]{3,2,1,0:T(8,128)S(1)} %pad_maximum_fusion), channel_id=1, source_target_pairs={{0,1},{1,0},{2,3},{3,2},{4,5},{5,4},{6,7},{7,6},{8,9},{9,8},{10,11... | collective-permute-start | bytes 1572872 | tf_op jit(solution)/shard_map/ppermute | solution.py:395
  27.3 0.1 multiply_reduce_fusion.1.wzs
  27.4 1.2 %collective-permute-done.2.refs_0_.near = f32[2,32,16,128]{3,2,1,0:T(8,128)S(1)} collective-permute-done((f32[2,32,16,128]{3,2,1,0:T(8,128)S(1)}, f32[2,32,16,128]{3,2,1,0:T(8,128)S(1)}, u32[]{:S(2)}, u32[]{:S(2)}) %collective-permute-start.2) | collective-permute-done | bytes 524320 | tf_op jit(solution)/shard_map/ppermute | solution.py:395
  28.6 0.2 pack.2
  28.8 2.3 %collective-permute-start.3 = (f32[960,128]{1,0:T(8,128)S(1)}, f32[960,128]{1,0:T(8,128)S(1)}, u32[]{:S(2)}, u32[]{:S(2)}) collective-permute-start(f32[960,128]{1,0:T(8,128)S(1)} %get-tuple-element.25), channel_id=1, source_target_pairs={{0,1},{1,2},{2,3},{3,4},{4,5},{5,6},{6,7},{7,8},{8,9},{9,10},{10,1... | collective-permute-start | bytes 1474568 | tf_op jit(solution)/shard_map/ppermute | solution.py:431
  31.1 1.3 %collective-permute-start.4 = (f32[960,128]{1,0:T(8,128)S(1)}, f32[960,128]{1,0:T(8,128)S(1)}, u32[]{:S(2)}, u32[]{:S(2)}) collective-permute-start(f32[960,128]{1,0:T(8,128)S(1)} %get-tuple-element.26), channel_id=1, source_target_pairs={{1,0},{2,1},{3,2},{4,3},{5,4},{6,5},{7,6},{8,7},{9,8},{10,9},{11,1... | collective-permute-start | bytes 1474568 | tf_op jit(solution)/shard_map/ppermute | solution.py:432
  32.4 1.1 %copy-done.10 = bf16[6,256,256]{2,1,0:T(8,128)(2,1)S(1)} copy-done((bf16[6,256,256]{2,1,0:T(8,128)(2,1)S(1)}, bf16[6,256,256]{2,1,0:T(8,128)(2,1)}, u32[]{:S(2)}) %copy-start.10) | copy-done | bytes 786456
  33.5 6.9 %forward.1 = (f32[6,32,48,128]{3,2,1,0:T(8,128)S(1)}, f32[24,128]{1,0:T(8,128)S(1)}) custom-call(s32[1]{0:T(128)} %bitcast.parity, f32[6,32]{1,0:T(8,128)S(1)} %multiply_reduce_fusion.1.wzs, f32[32,16,128]{2,1,0:T(8,128)S(1)} %collective-permute-done.1.far_before, f32[2,32,16,128]{3,2,1,0:T(8,128)S(1)} %collective-permute-done.2.refs_0_.near, ...), custom_call_target="tpu_custom_call" | custom-call | flops 10000000000 | bytes 10000000 | tf_op jit(solution)/shard_map/forward/pallas_call | solution.py:95
  40.5 4.1 %early_adjoint.1 = (f32[256,256]{1,0:T(8,128)S(1)}, f32[4,32,32,128]{3,2,1,0:T(8,128)S(1)}) custom-call(f32[1920,128]{1,0:T(8,128)S(1)} %collective-permute-done.5.before, f32[1920,128]{1,0:T(8,128)} %collective-permute-done.6.after, f32[6,32,16,128]{3,2,1,0:T(8,128)S(1)} %copy-done, f32[6,32,48,128]{3,2,1,0:T(8,128)S(1)} %get-tuple-element.30.blurred, ...), custom_call_target="tpu_custom_call" | custom-call | flops 10000000000 | bytes 10000000 | tf_op jit(solution)/shard_map/early_adjoint/pallas_call | solution.py:95
  44.6 2.2 %late_adjoint.1 = (f32[32,16,128]{2,1,0:T(8,128)S(1)}, f32[24,128]{1,0:T(8,128)S(1)}, f32[2,32,32,128]{3,2,1,0:T(8,128)S(1)}) custom-call(f32[6,32]{1,0:T(8,128)S(1)} %multiply_reduce_fusion.1.wzs, f32[960,128]{1,0:T(8,128)S(1)} %collective-permute-done.3.before, f32[960,128]{1,0:T(8,128)S(1)} %collective-permute-done.4.after, ...), custom_call_target="tpu_custom_call" | custom-call | flops 10000000000 | bytes 10000000 | tf_op jit(solution)/shard_map/late_adjoint/pallas_call | solution.py:95
  46.8 8.7 %collective-permute-start.7 = (f32[32,16,128]{2,1,0:T(8,128)S(1)}, f32[32,16,128]{2,1,0:T(8,128)S(1)}, u32[]{:S(2)}, u32[]{:S(2)}) collective-permute-start(f32[32,16,128]{2,1,0:T(8,128)S(1)} %get-tuple-element.38.own), channel_id=1, source_target_pairs={{0,2},{1,3},{2,4},{3,5},{4,6},{5,7},{6,8},{7,9},{8,10},{9,11},{10,... | collective-permute-start | bytes 786440 | tf_op jit(solution)/shard_map/ppermute | solution.py:389
  55.5 1.5 %collective-permute-start.8 = (f32[32,16,128]{2,1,0:T(8,128)S(1)}, f32[32,16,128]{2,1,0:T(8,128)S(1)}, u32[]{:S(2)}, u32[]{:S(2)}) collective-permute-start(f32[32,16,128]{2,1,0:T(8,128)S(1)} %get-tuple-element.38.own), channel_id=1, source_target_pairs={{2,0},{3,1},{4,2},{5,3},{6,4},{7,5},{8,6},{9,7},{10,8},{11,9},{12,... | collective-permute-start | bytes 786440 | tf_op jit(solution)/shard_map/ppermute | solution.py:389
  57.0 1.2 %collective-permute-done.9 = f32[24,128]{1,0:T(8,128)S(1)} collective-permute-done((f32[24,128]{1,0:T(8,128)S(1)}, f32[24,128]{1,0:T(8,128)S(1)}, u32[]{:S(2)}, u32[]{:S(2)}) %collective-permute-start.9) | collective-permute-done | bytes 12320 | tf_op jit(solution)/shard_map/ppermute | solution.py:443
  58.2 4.6 %collective-permute-start.10 = (f32[24,128]{1,0:T(8,128)S(1)}, f32[24,128]{1,0:T(8,128)S(1)}, u32[]{:S(2)}, u32[]{:S(2)}) collective-permute-start(f32[24,128]{1,0:T(8,128)S(1)} %add.66), channel_id=1, source_target_pairs={{0,12},{1,13},{2,14},{3,15},{4,8},{5,9},{6,10},{7,11},{8,4},{9,5},... | collective-permute-start | bytes 36872 | tf_op jit(solution)/shard_map/ppermute | solution.py:443
  62.8 0.6 collective-permute-start.12
  63.3 4.4 %collective-permute-done.10 = f32[24,128]{1,0:T(8,128)S(1)} collective-permute-done((f32[24,128]{1,0:T(8,128)S(1)}, f32[24,128]{1,0:T(8,128)S(1)}, u32[]{:S(2)}, u32[]{:S(2)}) %collective-permute-start.10) | collective-permute-done | bytes 12320 | tf_op jit(solution)/shard_map/ppermute | solution.py:443
  68.0 1.8 %collective-permute-done.13.near = f32[2,32,16,128]{3,2,1,0:T(8,128)S(1)} collective-permute-done((f32[2,32,16,128]{3,2,1,0:T(8,128)S(1)}, f32[2,32,16,128]{3,2,1,0:T(8,128)S(1)}, u32[]{:S(2)}, u32[]{:S(2)}) %collective-permute-start.13) | collective-permute-done | bytes 524320 | tf_op jit(solution)/shard_map/ppermute | solution.py:395
  69.8 9.2 %iteration.1.values = f32[32,16,128]{2,1,0:T(8,128)S(1)} custom-call(s32[1]{0:T(128)} %bitcast.parity, f32[32,16,128]{2,1,0:T(8,128)S(1)} %collective-permute-done.7.far_before, f32[2,32,16,128]{3,2,1,0:T(8,128)S(1)} %collective-permute-done.13.near, f32[32,16,128]{2,1,0:T(8,128)S(1)} %get-tuple-element.38.own, ...), custom_call_target="tpu_custom_call" | custom-call | flops 20000000000 | bytes 10000000 | tf_op jit(solution)/shard_map/iteration/pallas_call | solution.py:95
  79.1 0.8 %scaled.1 = f32[32,16,128]{2,1,0:T(8,128)} custom-call(f32[32,16,128]{2,1,0:T(8,128)S(1)} %iteration.1.values, f32[24,128]{1,0:T(8,128)S(1)} %add_add_fusion.part, f32[24,128]{1,0:T(8,128)S(1)} %collective-permute-done.14.rest), custom_call_target="tpu_custom_call" | custom-call | flops 100000 | bytes 10000000 | tf_op jit(solution)/shard_map/scaled/pallas_call | solution.py:95
  (49 shorter events, 0.8 us)
Async XLA Ops:
  0.0 12.7 %copy-start.2 = (f32[6,3,31]{2,1,0:T(4,128)S(1)}, f32[6,3,31]{2,1,0:T(4,128)}, u32[]{:S(2)}) copy-start(f32[6,3,31]{2,1,0:T(4,128)} %taps_ref.1) | copy-start | bytes 6700
  0.0 22.8 %collective-permute-start = (f32[32,16,128]{2,1,0:T(8,128)}, f32[32,16,128]{2,1,0:T(8,128)S(1)}, u32[]{:S(2)}, u32[]{:S(2)}) collective-permute-start(f32[32,16,128]{2,1,0:T(8,128)} %current.1), channel_id=1, source_target_pairs={{2,0},{3,1},{4,2},{5,3},{6,4},{7,5},{8,6},{9,7},{10,8},{11,9},{12,... | collective-permute-start | bytes 786440 | tf_op jit(solution)/shard_map/ppermute | solution.py:389
  1.4 21.4 %collective-permute-start.1 = (f32[32,16,128]{2,1,0:T(8,128)}, f32[32,16,128]{2,1,0:T(8,128)S(1)}, u32[]{:S(2)}, u32[]{:S(2)}) collective-permute-start(f32[32,16,128]{2,1,0:T(8,128)} %current.1), channel_id=1, source_target_pairs={{0,2},{1,3},{2,4},{3,5},{4,6},{5,7},{6,8},{7,9},{8,10},{9,11},{10,... | collective-permute-start | bytes 786440 | tf_op jit(solution)/shard_map/ppermute | solution.py:389
  9.9 30.6 %collective-permute-start.5 = (f32[1920,128]{1,0:T(8,128)}, f32[1920,128]{1,0:T(8,128)S(1)}, u32[]{:S(2)}, u32[]{:S(2)}) collective-permute-start(f32[1920,128]{1,0:T(8,128)} %get-tuple-element.34), channel_id=1, source_target_pairs={{0,1},{1,2},{2,3},{3,4},{4,5},{5,6},{6,7},{7,8},{8,9},{9,10},{10,1... | collective-permute-start | bytes 2949128 | tf_op jit(solution)/shard_map/ppermute | solution.py:421
  11.4 29.1 %collective-permute-start.6 = (f32[1920,128]{1,0:T(8,128)}, f32[1920,128]{1,0:T(8,128)}, u32[]{:S(2)}, u32[]{:S(2)}) collective-permute-start(f32[1920,128]{1,0:T(8,128)} %get-tuple-element.35), channel_id=1, source_target_pairs={{1,0},{2,1},{3,2},{4,3},{5,4},{6,5},{7,6},{8,7},{9,8},{10,9},{11,1... | collective-permute-start | bytes 2949128 | tf_op jit(solution)/shard_map/ppermute | solution.py:422
  13.3 9.6 %copy-start.1 = (f32[32,16,128]{2,1,0:T(8,128)S(1)}, f32[32,16,128]{2,1,0:T(8,128)}, u32[]{:S(2)}) copy-start(f32[32,16,128]{2,1,0:T(8,128)} %current.1) | copy-start | bytes 786436
  17.0 1.4 %copy-start.3 = (bf16[6,256,768]{2,1,0:T(8,128)(2,1)}, bf16[6,256,768]{2,1,0:T(8,128)(2,1)S(1)}, u32[]{:S(2)}) copy-start(bf16[6,256,768]{2,1,0:T(8,128)(2,1)S(1)} %get-tuple-element.33.wz.wza) | copy-start | bytes 7077892
  18.5 1.4 %copy-start.5 = (bf16[6,256,768]{2,1,0:T(8,128)(2,1)}, bf16[6,256,768]{2,1,0:T(8,128)(2,1)S(1)}, u32[]{:S(2)}) copy-start(bf16[6,256,768]{2,1,0:T(8,128)(2,1)S(1)} %get-tuple-element.29.wz) | copy-start | bytes 7077892
  19.9 1.0 %copy-start.7 = (bf16[6,256,256]{2,1,0:T(8,128)(2,1)}, bf16[6,256,256]{2,1,0:T(8,128)(2,1)S(1)}, u32[]{:S(2)}) copy-start(bf16[6,256,256]{2,1,0:T(8,128)(2,1)S(1)} %get-tuple-element.32.wx.wxa) | copy-start | bytes 2359300
  20.9 1.0 %copy-start.9 = (bf16[6,256,256]{2,1,0:T(8,128)(2,1)}, bf16[6,256,256]{2,1,0:T(8,128)(2,1)S(1)}, u32[]{:S(2)}) copy-start(bf16[6,256,256]{2,1,0:T(8,128)(2,1)S(1)} %get-tuple-element.28.wx) | copy-start | bytes 2359300
  21.8 5.5 %copy-start = (f32[6,32,16,128]{3,2,1,0:T(8,128)S(1)}, f32[6,32,16,128]{3,2,1,0:T(8,128)}, u32[]{:S(2)}) copy-start(f32[6,32,16,128]{3,2,1,0:T(8,128)} %raw.7) | copy-start | bytes 4718596
  21.9 10.5 %copy-start.6 = (bf16[6,256,768]{2,1,0:T(8,128)(2,1)S(1)}, bf16[6,256,768]{2,1,0:T(8,128)(2,1)}, u32[]{:S(2)}) copy-start(bf16[6,256,768]{2,1,0:T(8,128)(2,1)} %copy-done.5) | copy-start | bytes 7077892
  23.0 5.6 %collective-permute-start.2 = (f32[2,32,16,128]{3,2,1,0:T(8,128)S(1)}, f32[2,32,16,128]{3,2,1,0:T(8,128)S(1)}, u32[]{:S(2)}, u32[]{:S(2)}) collective-permute-start(f32[2,32,16,128]{3,2,1,0:T(8,128)S(1)} %pad_maximum_fusion), channel_id=1, source_target_pairs={{0,1},{1,0},{2,3},{3,2},{4,5},{5,4},{6,7},{7,6},{8,9},{9,8},{10,11... | collective-permute-start | bytes 1572872 | tf_op jit(solution)/shard_map/ppermute | solution.py:395
  28.8 15.8 %collective-permute-start.3 = (f32[960,128]{1,0:T(8,128)S(1)}, f32[960,128]{1,0:T(8,128)S(1)}, u32[]{:S(2)}, u32[]{:S(2)}) collective-permute-start(f32[960,128]{1,0:T(8,128)S(1)} %get-tuple-element.25), channel_id=1, source_target_pairs={{0,1},{1,2},{2,3},{3,4},{4,5},{5,6},{6,7},{7,8},{8,9},{9,10},{10,1... | collective-permute-start | bytes 1474568 | tf_op jit(solution)/shard_map/ppermute | solution.py:431
  31.1 13.5 %collective-permute-start.4 = (f32[960,128]{1,0:T(8,128)S(1)}, f32[960,128]{1,0:T(8,128)S(1)}, u32[]{:S(2)}, u32[]{:S(2)}) collective-permute-start(f32[960,128]{1,0:T(8,128)S(1)} %get-tuple-element.26), channel_id=1, source_target_pairs={{1,0},{2,1},{3,2},{4,3},{5,4},{6,5},{7,6},{8,7},{9,8},{10,9},{11,1... | collective-permute-start | bytes 1474568 | tf_op jit(solution)/shard_map/ppermute | solution.py:432
  32.4 1.1 %copy-start.10 = (bf16[6,256,256]{2,1,0:T(8,128)(2,1)S(1)}, bf16[6,256,256]{2,1,0:T(8,128)(2,1)}, u32[]{:S(2)}) copy-start(bf16[6,256,256]{2,1,0:T(8,128)(2,1)} %copy-done.9) | copy-start | bytes 2359300
  33.5 6.9 %copy-start.4 = (bf16[6,256,768]{2,1,0:T(8,128)(2,1)S(1)}, bf16[6,256,768]{2,1,0:T(8,128)(2,1)}, u32[]{:S(2)}) copy-start(bf16[6,256,768]{2,1,0:T(8,128)(2,1)} %copy-done.3) | copy-start | bytes 7077892
  33.5 6.9 %copy-start.8 = (bf16[6,256,256]{2,1,0:T(8,128)(2,1)S(1)}, bf16[6,256,256]{2,1,0:T(8,128)(2,1)}, u32[]{:S(2)}) copy-start(bf16[6,256,256]{2,1,0:T(8,128)(2,1)} %copy-done.7) | copy-start | bytes 2359300
  44.6 25.3 %copy-start.11 = (bf16[6,256,256]{2,1,0:T(8,128)(2,1)S(1)}, bf16[6,256,256]{2,1,0:T(8,128)(2,1)}, u32[]{:S(2)}) copy-start(bf16[6,256,256]{2,1,0:T(8,128)(2,1)} %copy-done.9) | copy-start | bytes 2359300
  46.8 21.0 %collective-permute-start.7 = (f32[32,16,128]{2,1,0:T(8,128)S(1)}, f32[32,16,128]{2,1,0:T(8,128)S(1)}, u32[]{:S(2)}, u32[]{:S(2)}) collective-permute-start(f32[32,16,128]{2,1,0:T(8,128)S(1)} %get-tuple-element.38.own), channel_id=1, source_target_pairs={{0,2},{1,3},{2,4},{3,5},{4,6},{5,7},{6,8},{7,9},{8,10},{9,11},{10,... | collective-permute-start | bytes 786440 | tf_op jit(solution)/shard_map/ppermute | solution.py:389
  55.5 12.3 %collective-permute-start.8 = (f32[32,16,128]{2,1,0:T(8,128)S(1)}, f32[32,16,128]{2,1,0:T(8,128)S(1)}, u32[]{:S(2)}, u32[]{:S(2)}) collective-permute-start(f32[32,16,128]{2,1,0:T(8,128)S(1)} %get-tuple-element.38.own), channel_id=1, source_target_pairs={{2,0},{3,1},{4,2},{5,3},{6,4},{7,5},{8,6},{9,7},{10,8},{11,9},{12,... | collective-permute-start | bytes 786440 | tf_op jit(solution)/shard_map/ppermute | solution.py:389
  56.9 1.2 %collective-permute-start.9 = (f32[24,128]{1,0:T(8,128)S(1)}, f32[24,128]{1,0:T(8,128)S(1)}, u32[]{:S(2)}, u32[]{:S(2)}) collective-permute-start(f32[24,128]{1,0:T(8,128)S(1)} %get-tuple-element.39), channel_id=1, source_target_pairs={{0,1},{1,0},{2,3},{3,2},{4,5},{5,4},{6,7},{7,6},{8,9},{9,8},{10,11... | collective-permute-start | bytes 36872 | tf_op jit(solution)/shard_map/ppermute | solution.py:443
  58.2 9.6 %collective-permute-start.10 = (f32[24,128]{1,0:T(8,128)S(1)}, f32[24,128]{1,0:T(8,128)S(1)}, u32[]{:S(2)}, u32[]{:S(2)}) collective-permute-start(f32[24,128]{1,0:T(8,128)S(1)} %add.66), channel_id=1, source_target_pairs={{0,12},{1,13},{2,14},{3,15},{4,8},{5,9},{6,10},{7,11},{8,4},{9,5},... | collective-permute-start | bytes 36872 | tf_op jit(solution)/shard_map/ppermute | solution.py:443
  62.7 5.0 %collective-permute-start.11 = (f32[24,128]{1,0:T(8,128)S(1)}, f32[24,128]{1,0:T(8,128)S(1)}, u32[]{:S(2)}, u32[]{:S(2)}) collective-permute-start(f32[24,128]{1,0:T(8,128)S(1)} %add.66), channel_id=1, source_target_pairs={{0,8},{1,9},{2,10},{3,11},{4,12},{5,13},{6,14},{7,15},{8,0},{9,1},... | collective-permute-start | bytes 36872 | tf_op jit(solution)/shard_map/ppermute | solution.py:443
  62.8 5.0 %collective-permute-start.12 = (f32[24,128]{1,0:T(8,128)S(1)}, f32[24,128]{1,0:T(8,128)S(1)}, u32[]{:S(2)}, u32[]{:S(2)}) collective-permute-start(f32[24,128]{1,0:T(8,128)S(1)} %add.66), channel_id=1, source_target_pairs={{0,4},{1,5},{2,6},{3,7},{4,0},{5,1},{6,2},{7,3},{8,12},{9,13},{10,... | collective-permute-start | bytes 36872 | tf_op jit(solution)/shard_map/ppermute | solution.py:443
  67.9 2.0 %collective-permute-start.13 = (f32[2,32,16,128]{3,2,1,0:T(8,128)S(1)}, f32[2,32,16,128]{3,2,1,0:T(8,128)S(1)}, u32[]{:S(2)}, u32[]{:S(2)}) collective-permute-start(f32[2,32,16,128]{3,2,1,0:T(8,128)S(1)} %pad_maximum_fusion.1), channel_id=1, source_target_pairs={{0,1},{1,0},{2,3},{3,2},{4,5},{5,4},{6,7},{7,6},{8,9},{9,8},{10,11... | collective-permute-start | bytes 1572872 | tf_op jit(solution)/shard_map/ppermute | solution.py:395
  67.9 11.1 %collective-permute-start.14 = (f32[24,128]{1,0:T(8,128)S(1)}, f32[24,128]{1,0:T(8,128)S(1)}, u32[]{:S(2)}, u32[]{:S(2)}) collective-permute-start(f32[24,128]{1,0:T(8,128)S(1)} %add_add_fusion.part), channel_id=1, source_target_pairs={{0,2},{1,3},{2,0},{3,1},{4,6},{5,7},{6,4},{7,5},{8,10},{9,11},{10,... | collective-permute-start | bytes 36872 | tf_op jit(solution)/shard_map/ppermute | solution.py:443

commit v15 on v14

--- a/solution.py
+++ b/solution.py
@@ -270,11 +270,13 @@
 
 def weighted_sums(values, wzs, wyx, sums, at):
     planes, rows, cols = values.shape
-    for v in range(wyx.shape[0]):
-        total = jnp.zeros((rows, cols), F32)
-        for z in range(planes):
-            total = total + wzs[v, z] * values[z]
-        sums[at + v : at + v + 1, :] = jnp.sum(total * wyx[v], axis=0, keepdims=True)
+    views = wyx.shape[0]
+    totals = [jnp.zeros((rows, cols), F32)] * views
+    for z in range(planes):
+        plane = values[z]
+        totals = [totals[v] + wzs[v, z] * plane for v in range(views)]
+    for v in range(views):
+        sums[at + v : at + v + 1, :] = jnp.sum(totals[v] * wyx[v], axis=0, keepdims=True)
 
 
 def early_adjoint_kernel(chosen, before, after, raw, blurred, wy, wx, wz, acc, halos, ya, yb, xs):

time: 80.3 us -> 80.3 us (level)
  no operation moved by 1% of the time
where the time goes in v15:
time: 80.3 us; the launch traced here: 79.9 us
  starting transfers between devices  32.9 us (41%)
  Pallas kernels  28.7 us (36%)
  local copies, waits for them, and re-layouts  8.73 us (11%)
  waiting for transfers between devices  8.62 us (11%)
    pallas_call x8, Pallas kernels, call(): pl.pallas_call(kernel, out_shape=outs, in_specs=[pl.BlockSpec(memory_spac...  28.7 us
    ppermute x4, starting transfers between devices, two_slabs_away(): return (lax.ppermute(value, 'slab', up), lax.ppermute(value, 'slab', down))  17.1 us
    unnamed x25, local copies, waits for them, and re-layouts  6.8 us
    ppermute x5, waiting for transfers between devices, per_device(): lax.ppermute(sums, 'slab', [(i, i ^ d) for i in range(count)])  5.6 us
    ppermute x5, starting transfers between devices, per_device(): lax.ppermute(sums, 'slab', [(i, i ^ d) for i in range(count)])  5.27 us
    ppermute x2, starting transfers between devices, with_near(): near = lax.ppermute(passed, 'slab', swap)  4.17 us
    ppermute x2, waiting for transfers between devices, with_near(): near = lax.ppermute(passed, 'slab', swap)  3 us
    ppermute x1, starting transfers between devices, per_device(): befores.append(lax.ppermute(edges[0], 'slab', up))  2.31 us
  transfers between devices with their start and end apart: 15, of which 4 were waited for; matrix products, arithmetic and copies ran while one was open for 4% of the time, Pallas kernels for 32%

profile of v15, /device:TPU:0, one launch (start us, length us, event | category | flops | bytes accessed | tf_op | source)
XLA Modules:
  0.0 79.9 jit_solution(11147598854110027131)
XLA Ops:
  0.0 1.4 %collective-permute-start = (f32[32,16,128]{2,1,0:T(8,128)}, f32[32,16,128]{2,1,0:T(8,128)S(1)}, u32[]{:S(2)}, u32[]{:S(2)}) collective-permute-start(f32[32,16,128]{2,1,0:T(8,128)} %current.1), channel_id=1, source_target_pairs={{2,0},{3,1},{4,2},{5,3},{6,4},{7,5},{8,6},{9,7},{10,8},{11,9},{12,... | collective-permute-start | bytes 786440 | tf_op jit(solution)/shard_map/ppermute | solution.py:391
  1.4 5.5 %collective-permute-start.1 = (f32[32,16,128]{2,1,0:T(8,128)}, f32[32,16,128]{2,1,0:T(8,128)S(1)}, u32[]{:S(2)}, u32[]{:S(2)}) collective-permute-start(f32[32,16,128]{2,1,0:T(8,128)} %current.1), channel_id=1, source_target_pairs={{0,2},{1,3},{2,4},{3,5},{4,6},{5,7},{6,8},{7,9},{8,10},{9,11},{10,... | collective-permute-start | bytes 786440 | tf_op jit(solution)/shard_map/ppermute | solution.py:391
  6.9 1.3 %slice.19 = f32[4,32,16,128]{3,2,1,0:T(8,128)S(1)} slice(f32[6,32,16,128]{3,2,1,0:T(8,128)} %raw.7), slice={[0:4], [0:32], [0:16], [0:128]} | slice | bytes 2097152 | tf_op jit(solution)/shard_map/slice | solution.py:325
  8.3 1.6 %pack.3 = (f32[1920,128]{1,0:T(8,128)}, f32[1920,128]{1,0:T(8,128)}) custom-call(f32[128,16,128]{2,1,0:T(8,128)S(1)} %bitcast.16), custom_call_target="tpu_custom_call" | custom-call | flops 1000000 | bytes 10000000 | tf_op jit(solution)/shard_map/pack/pallas_call | solution.py:95
  9.9 1.5 %collective-permute-start.5 = (f32[1920,128]{1,0:T(8,128)}, f32[1920,128]{1,0:T(8,128)S(1)}, u32[]{:S(2)}, u32[]{:S(2)}) collective-permute-start(f32[1920,128]{1,0:T(8,128)} %get-tuple-element.34), channel_id=1, source_target_pairs={{0,1},{1,2},{2,3},{3,4},{4,5},{5,6},{6,7},{7,8},{8,9},{9,10},{10,1... | collective-permute-start | bytes 2949128 | tf_op jit(solution)/shard_map/ppermute | solution.py:423
  11.4 1.3 %collective-permute-start.6 = (f32[1920,128]{1,0:T(8,128)}, f32[1920,128]{1,0:T(8,128)}, u32[]{:S(2)}, u32[]{:S(2)}) collective-permute-start(f32[1920,128]{1,0:T(8,128)} %get-tuple-element.35), channel_id=1, source_target_pairs={{1,0},{2,1},{3,2},{4,3},{5,4},{6,5},{7,6},{8,7},{9,8},{10,9},{11,1... | collective-permute-start | bytes 2949128 | tf_op jit(solution)/shard_map/ppermute | solution.py:424
  12.7 0.6 fusion.12
  13.3 3.7 %weights.1 = (bf16[288,240]{1,0:T(8,128)(2,1)S(1)}, bf16[6,256,256]{2,1,0:T(8,128)(2,1)S(1)}, bf16[6,256,768]{2,1,0:T(8,128)(2,1)S(1)}, bf16[6,32,96]{2,1,0:T(8,...) custom-call(f32[6,3,31]{2,1,0:T(4,128)S(1)} %copy-done.2), custom_call_target="tpu_custom_call" | custom-call | flops 10000000000 | bytes 10000000 | tf_op jit(solution)/shard_map/weights/pallas_call | solution.py:95
  17.0 1.4 %copy-done.3 = bf16[6,256,768]{2,1,0:T(8,128)(2,1)} copy-done((bf16[6,256,768]{2,1,0:T(8,128)(2,1)}, bf16[6,256,768]{2,1,0:T(8,128)(2,1)S(1)}, u32[]{:S(2)}) %copy-start.3) | copy-done | bytes 2359320
  18.5 1.4 %copy-done.5 = bf16[6,256,768]{2,1,0:T(8,128)(2,1)} copy-done((bf16[6,256,768]{2,1,0:T(8,128)(2,1)}, bf16[6,256,768]{2,1,0:T(8,128)(2,1)S(1)}, u32[]{:S(2)}) %copy-start.5) | copy-done | bytes 2359320
  19.9 1.0 %copy-done.7 = bf16[6,256,256]{2,1,0:T(8,128)(2,1)} copy-done((bf16[6,256,256]{2,1,0:T(8,128)(2,1)}, bf16[6,256,256]{2,1,0:T(8,128)(2,1)S(1)}, u32[]{:S(2)}) %copy-start.7) | copy-done | bytes 786456
  20.9 1.0 %copy-done.9 = bf16[6,256,256]{2,1,0:T(8,128)(2,1)} copy-done((bf16[6,256,256]{2,1,0:T(8,128)(2,1)}, bf16[6,256,256]{2,1,0:T(8,128)(2,1)S(1)}, u32[]{:S(2)}) %copy-start.9) | copy-done | bytes 786456
  21.9 0.8 %copy.16 = f32[6,1,31]{2,0,1:T(8,128)S(1)} copy(f32[6,1,31]{2,1,0:T(1,128)} %get-tuple-element.46) | data formatting | bytes 1488
  23.0 4.1 %collective-permute-start.2 = (f32[2,32,16,128]{3,2,1,0:T(8,128)S(1)}, f32[2,32,16,128]{3,2,1,0:T(8,128)S(1)}, u32[]{:S(2)}, u32[]{:S(2)}) collective-permute-start(f32[2,32,16,128]{3,2,1,0:T(8,128)S(1)} %pad_maximum_fusion), channel_id=1, source_target_pairs={{0,1},{1,0},{2,3},{3,2},{4,5},{5,4},{6,7},{7,6},{8,9},{9,8},{10,11... | collective-permute-start | bytes 1572872 | tf_op jit(solution)/shard_map/ppermute | solution.py:397
  27.3 0.1 multiply_reduce_fusion.1.wzs
  27.4 1.2 %collective-permute-done.2.refs_0_.near = f32[2,32,16,128]{3,2,1,0:T(8,128)S(1)} collective-permute-done((f32[2,32,16,128]{3,2,1,0:T(8,128)S(1)}, f32[2,32,16,128]{3,2,1,0:T(8,128)S(1)}, u32[]{:S(2)}, u32[]{:S(2)}) %collective-permute-start.2) | collective-permute-done | bytes 524320 | tf_op jit(solution)/shard_map/ppermute | solution.py:397
  28.6 0.2 pack.2
  28.8 2.3 %collective-permute-start.3 = (f32[960,128]{1,0:T(8,128)S(1)}, f32[960,128]{1,0:T(8,128)S(1)}, u32[]{:S(2)}, u32[]{:S(2)}) collective-permute-start(f32[960,128]{1,0:T(8,128)S(1)} %get-tuple-element.25), channel_id=1, source_target_pairs={{0,1},{1,2},{2,3},{3,4},{4,5},{5,6},{6,7},{7,8},{8,9},{9,10},{10,1... | collective-permute-start | bytes 1474568 | tf_op jit(solution)/shard_map/ppermute | solution.py:433
  31.1 1.3 %collective-permute-start.4 = (f32[960,128]{1,0:T(8,128)S(1)}, f32[960,128]{1,0:T(8,128)S(1)}, u32[]{:S(2)}, u32[]{:S(2)}) collective-permute-start(f32[960,128]{1,0:T(8,128)S(1)} %get-tuple-element.26), channel_id=1, source_target_pairs={{1,0},{2,1},{3,2},{4,3},{5,4},{6,5},{7,6},{8,7},{9,8},{10,9},{11,1... | collective-permute-start | bytes 1474568 | tf_op jit(solution)/shard_map/ppermute | solution.py:434
  32.4 1.1 %copy-done.10 = bf16[6,256,256]{2,1,0:T(8,128)(2,1)S(1)} copy-done((bf16[6,256,256]{2,1,0:T(8,128)(2,1)S(1)}, bf16[6,256,256]{2,1,0:T(8,128)(2,1)}, u32[]{:S(2)}) %copy-start.10) | copy-done | bytes 786456
  33.5 6.9 %forward.1 = (f32[6,32,48,128]{3,2,1,0:T(8,128)S(1)}, f32[24,128]{1,0:T(8,128)S(1)}) custom-call(s32[1]{0:T(128)} %bitcast.parity, f32[6,32]{1,0:T(8,128)S(1)} %multiply_reduce_fusion.1.wzs, f32[32,16,128]{2,1,0:T(8,128)S(1)} %collective-permute-done.1.far_before, f32[2,32,16,128]{3,2,1,0:T(8,128)S(1)} %collective-permute-done.2.refs_0_.near, ...), custom_call_target="tpu_custom_call" | custom-call | flops 10000000000 | bytes 10000000 | tf_op jit(solution)/shard_map/forward/pallas_call | solution.py:95
  40.5 4.1 %early_adjoint.1 = (f32[256,256]{1,0:T(8,128)S(1)}, f32[4,32,32,128]{3,2,1,0:T(8,128)S(1)}) custom-call(f32[1920,128]{1,0:T(8,128)S(1)} %collective-permute-done.5.before, f32[1920,128]{1,0:T(8,128)} %collective-permute-done.6.after, f32[6,32,16,128]{3,2,1,0:T(8,128)S(1)} %copy-done, f32[6,32,48,128]{3,2,1,0:T(8,128)S(1)} %get-tuple-element.30.blurred, ...), custom_call_target="tpu_custom_call" | custom-call | flops 10000000000 | bytes 10000000 | tf_op jit(solution)/shard_map/early_adjoint/pallas_call | solution.py:95
  44.6 2.2 %late_adjoint.1 = (f32[32,16,128]{2,1,0:T(8,128)S(1)}, f32[24,128]{1,0:T(8,128)S(1)}, f32[2,32,32,128]{3,2,1,0:T(8,128)S(1)}) custom-call(f32[6,32]{1,0:T(8,128)S(1)} %multiply_reduce_fusion.1.wzs, f32[960,128]{1,0:T(8,128)S(1)} %collective-permute-done.3.before, f32[960,128]{1,0:T(8,128)S(1)} %collective-permute-done.4.after, ...), custom_call_target="tpu_custom_call" | custom-call | flops 10000000000 | bytes 10000000 | tf_op jit(solution)/shard_map/late_adjoint/pallas_call | solution.py:95
  46.8 8.7 %collective-permute-start.7 = (f32[32,16,128]{2,1,0:T(8,128)S(1)}, f32[32,16,128]{2,1,0:T(8,128)S(1)}, u32[]{:S(2)}, u32[]{:S(2)}) collective-permute-start(f32[32,16,128]{2,1,0:T(8,128)S(1)} %get-tuple-element.38.own), channel_id=1, source_target_pairs={{0,2},{1,3},{2,4},{3,5},{4,6},{5,7},{6,8},{7,9},{8,10},{9,11},{10,... | collective-permute-start | bytes 786440 | tf_op jit(solution)/shard_map/ppermute | solution.py:391
  55.5 1.5 %collective-permute-start.8 = (f32[32,16,128]{2,1,0:T(8,128)S(1)}, f32[32,16,128]{2,1,0:T(8,128)S(1)}, u32[]{:S(2)}, u32[]{:S(2)}) collective-permute-start(f32[32,16,128]{2,1,0:T(8,128)S(1)} %get-tuple-element.38.own), channel_id=1, source_target_pairs={{2,0},{3,1},{4,2},{5,3},{6,4},{7,5},{8,6},{9,7},{10,8},{11,9},{12,... | collective-permute-start | bytes 786440 | tf_op jit(solution)/shard_map/ppermute | solution.py:391
  57.0 1.2 %collective-permute-done.9 = f32[24,128]{1,0:T(8,128)S(1)} collective-permute-done((f32[24,128]{1,0:T(8,128)S(1)}, f32[24,128]{1,0:T(8,128)S(1)}, u32[]{:S(2)}, u32[]{:S(2)}) %collective-permute-start.9) | collective-permute-done | bytes 12320 | tf_op jit(solution)/shard_map/ppermute | solution.py:445
  58.2 4.6 %collective-permute-start.10 = (f32[24,128]{1,0:T(8,128)S(1)}, f32[24,128]{1,0:T(8,128)S(1)}, u32[]{:S(2)}, u32[]{:S(2)}) collective-permute-start(f32[24,128]{1,0:T(8,128)S(1)} %add.66), channel_id=1, source_target_pairs={{0,12},{1,13},{2,14},{3,15},{4,8},{5,9},{6,10},{7,11},{8,4},{9,5},... | collective-permute-start | bytes 36872 | tf_op jit(solution)/shard_map/ppermute | solution.py:445
  62.7 0.6 collective-permute-start.12
  63.3 4.4 %collective-permute-done.10 = f32[24,128]{1,0:T(8,128)S(1)} collective-permute-done((f32[24,128]{1,0:T(8,128)S(1)}, f32[24,128]{1,0:T(8,128)S(1)}, u32[]{:S(2)}, u32[]{:S(2)}) %collective-permute-start.10) | collective-permute-done | bytes 12320 | tf_op jit(solution)/shard_map/ppermute | solution.py:445
  68.0 1.8 %collective-permute-done.13.near = f32[2,32,16,128]{3,2,1,0:T(8,128)S(1)} collective-permute-done((f32[2,32,16,128]{3,2,1,0:T(8,128)S(1)}, f32[2,32,16,128]{3,2,1,0:T(8,128)S(1)}, u32[]{:S(2)}, u32[]{:S(2)}) %collective-permute-start.13) | collective-permute-done | bytes 524320 | tf_op jit(solution)/shard_map/ppermute | solution.py:397
  69.8 9.2 %iteration.1.values = f32[32,16,128]{2,1,0:T(8,128)S(1)} custom-call(s32[1]{0:T(128)} %bitcast.parity, f32[32,16,128]{2,1,0:T(8,128)S(1)} %collective-permute-done.7.far_before, f32[2,32,16,128]{3,2,1,0:T(8,128)S(1)} %collective-permute-done.13.near, f32[32,16,128]{2,1,0:T(8,128)S(1)} %get-tuple-element.38.own, ...), custom_call_target="tpu_custom_call" | custom-call | flops 20000000000 | bytes 10000000 | tf_op jit(solution)/shard_map/iteration/pallas_call | solution.py:95
  79.1 0.8 %scaled.1 = f32[32,16,128]{2,1,0:T(8,128)} custom-call(f32[32,16,128]{2,1,0:T(8,128)S(1)} %iteration.1.values, f32[24,128]{1,0:T(8,128)S(1)} %add_add_fusion.part, f32[24,128]{1,0:T(8,128)S(1)} %collective-permute-done.14.rest), custom_call_target="tpu_custom_call" | custom-call | flops 100000 | bytes 10000000 | tf_op jit(solution)/shard_map/scaled/pallas_call | solution.py:95
  (49 shorter events, 0.8 us)
Async XLA Ops:
  0.0 12.7 %copy-start.2 = (f32[6,3,31]{2,1,0:T(4,128)S(1)}, f32[6,3,31]{2,1,0:T(4,128)}, u32[]{:S(2)}) copy-start(f32[6,3,31]{2,1,0:T(4,128)} %taps_ref.1) | copy-start | bytes 6700
  0.0 22.8 %collective-permute-start = (f32[32,16,128]{2,1,0:T(8,128)}, f32[32,16,128]{2,1,0:T(8,128)S(1)}, u32[]{:S(2)}, u32[]{:S(2)}) collective-permute-start(f32[32,16,128]{2,1,0:T(8,128)} %current.1), channel_id=1, source_target_pairs={{2,0},{3,1},{4,2},{5,3},{6,4},{7,5},{8,6},{9,7},{10,8},{11,9},{12,... | collective-permute-start | bytes 786440 | tf_op jit(solution)/shard_map/ppermute | solution.py:391
  1.4 21.4 %collective-permute-start.1 = (f32[32,16,128]{2,1,0:T(8,128)}, f32[32,16,128]{2,1,0:T(8,128)S(1)}, u32[]{:S(2)}, u32[]{:S(2)}) collective-permute-start(f32[32,16,128]{2,1,0:T(8,128)} %current.1), channel_id=1, source_target_pairs={{0,2},{1,3},{2,4},{3,5},{4,6},{5,7},{6,8},{7,9},{8,10},{9,11},{10,... | collective-permute-start | bytes 786440 | tf_op jit(solution)/shard_map/ppermute | solution.py:391
  9.9 30.6 %collective-permute-start.5 = (f32[1920,128]{1,0:T(8,128)}, f32[1920,128]{1,0:T(8,128)S(1)}, u32[]{:S(2)}, u32[]{:S(2)}) collective-permute-start(f32[1920,128]{1,0:T(8,128)} %get-tuple-element.34), channel_id=1, source_target_pairs={{0,1},{1,2},{2,3},{3,4},{4,5},{5,6},{6,7},{7,8},{8,9},{9,10},{10,1... | collective-permute-start | bytes 2949128 | tf_op jit(solution)/shard_map/ppermute | solution.py:423
  11.4 29.1 %collective-permute-start.6 = (f32[1920,128]{1,0:T(8,128)}, f32[1920,128]{1,0:T(8,128)}, u32[]{:S(2)}, u32[]{:S(2)}) collective-permute-start(f32[1920,128]{1,0:T(8,128)} %get-tuple-element.35), channel_id=1, source_target_pairs={{1,0},{2,1},{3,2},{4,3},{5,4},{6,5},{7,6},{8,7},{9,8},{10,9},{11,1... | collective-permute-start | bytes 2949128 | tf_op jit(solution)/shard_map/ppermute | solution.py:424
  13.3 9.6 %copy-start.1 = (f32[32,16,128]{2,1,0:T(8,128)S(1)}, f32[32,16,128]{2,1,0:T(8,128)}, u32[]{:S(2)}) copy-start(f32[32,16,128]{2,1,0:T(8,128)} %current.1) | copy-start | bytes 786436
  17.0 1.4 %copy-start.3 = (bf16[6,256,768]{2,1,0:T(8,128)(2,1)}, bf16[6,256,768]{2,1,0:T(8,128)(2,1)S(1)}, u32[]{:S(2)}) copy-start(bf16[6,256,768]{2,1,0:T(8,128)(2,1)S(1)} %get-tuple-element.33.wz.wza) | copy-start | bytes 7077892
  18.5 1.4 %copy-start.5 = (bf16[6,256,768]{2,1,0:T(8,128)(2,1)}, bf16[6,256,768]{2,1,0:T(8,128)(2,1)S(1)}, u32[]{:S(2)}) copy-start(bf16[6,256,768]{2,1,0:T(8,128)(2,1)S(1)} %get-tuple-element.29.wz) | copy-start | bytes 7077892
  19.9 1.0 %copy-start.7 = (bf16[6,256,256]{2,1,0:T(8,128)(2,1)}, bf16[6,256,256]{2,1,0:T(8,128)(2,1)S(1)}, u32[]{:S(2)}) copy-start(bf16[6,256,256]{2,1,0:T(8,128)(2,1)S(1)} %get-tuple-element.32.wx.wxa) | copy-start | bytes 2359300
  20.9 1.0 %copy-start.9 = (bf16[6,256,256]{2,1,0:T(8,128)(2,1)}, bf16[6,256,256]{2,1,0:T(8,128)(2,1)S(1)}, u32[]{:S(2)}) copy-start(bf16[6,256,256]{2,1,0:T(8,128)(2,1)S(1)} %get-tuple-element.28.wx) | copy-start | bytes 2359300
  21.8 5.5 %copy-start = (f32[6,32,16,128]{3,2,1,0:T(8,128)S(1)}, f32[6,32,16,128]{3,2,1,0:T(8,128)}, u32[]{:S(2)}) copy-start(f32[6,32,16,128]{3,2,1,0:T(8,128)} %raw.7) | copy-start | bytes 4718596
  21.9 10.5 %copy-start.6 = (bf16[6,256,768]{2,1,0:T(8,128)(2,1)S(1)}, bf16[6,256,768]{2,1,0:T(8,128)(2,1)}, u32[]{:S(2)}) copy-start(bf16[6,256,768]{2,1,0:T(8,128)(2,1)} %copy-done.5) | copy-start | bytes 7077892
  23.0 5.6 %collective-permute-start.2 = (f32[2,32,16,128]{3,2,1,0:T(8,128)S(1)}, f32[2,32,16,128]{3,2,1,0:T(8,128)S(1)}, u32[]{:S(2)}, u32[]{:S(2)}) collective-permute-start(f32[2,32,16,128]{3,2,1,0:T(8,128)S(1)} %pad_maximum_fusion), channel_id=1, source_target_pairs={{0,1},{1,0},{2,3},{3,2},{4,5},{5,4},{6,7},{7,6},{8,9},{9,8},{10,11... | collective-permute-start | bytes 1572872 | tf_op jit(solution)/shard_map/ppermute | solution.py:397
  28.8 15.8 %collective-permute-start.3 = (f32[960,128]{1,0:T(8,128)S(1)}, f32[960,128]{1,0:T(8,128)S(1)}, u32[]{:S(2)}, u32[]{:S(2)}) collective-permute-start(f32[960,128]{1,0:T(8,128)S(1)} %get-tuple-element.25), channel_id=1, source_target_pairs={{0,1},{1,2},{2,3},{3,4},{4,5},{5,6},{6,7},{7,8},{8,9},{9,10},{10,1... | collective-permute-start | bytes 1474568 | tf_op jit(solution)/shard_map/ppermute | solution.py:433
  31.1 13.5 %collective-permute-start.4 = (f32[960,128]{1,0:T(8,128)S(1)}, f32[960,128]{1,0:T(8,128)S(1)}, u32[]{:S(2)}, u32[]{:S(2)}) collective-permute-start(f32[960,128]{1,0:T(8,128)S(1)} %get-tuple-element.26), channel_id=1, source_target_pairs={{1,0},{2,1},{3,2},{4,3},{5,4},{6,5},{7,6},{8,7},{9,8},{10,9},{11,1... | collective-permute-start | bytes 1474568 | tf_op jit(solution)/shard_map/ppermute | solution.py:434
  32.4 1.1 %copy-start.10 = (bf16[6,256,256]{2,1,0:T(8,128)(2,1)S(1)}, bf16[6,256,256]{2,1,0:T(8,128)(2,1)}, u32[]{:S(2)}) copy-start(bf16[6,256,256]{2,1,0:T(8,128)(2,1)} %copy-done.9) | copy-start | bytes 2359300
  33.5 6.9 %copy-start.4 = (bf16[6,256,768]{2,1,0:T(8,128)(2,1)S(1)}, bf16[6,256,768]{2,1,0:T(8,128)(2,1)}, u32[]{:S(2)}) copy-start(bf16[6,256,768]{2,1,0:T(8,128)(2,1)} %copy-done.3) | copy-start | bytes 7077892
  33.5 6.9 %copy-start.8 = (bf16[6,256,256]{2,1,0:T(8,128)(2,1)S(1)}, bf16[6,256,256]{2,1,0:T(8,128)(2,1)}, u32[]{:S(2)}) copy-start(bf16[6,256,256]{2,1,0:T(8,128)(2,1)} %copy-done.7) | copy-start | bytes 2359300
  44.6 25.3 %copy-start.11 = (bf16[6,256,256]{2,1,0:T(8,128)(2,1)S(1)}, bf16[6,256,256]{2,1,0:T(8,128)(2,1)}, u32[]{:S(2)}) copy-start(bf16[6,256,256]{2,1,0:T(8,128)(2,1)} %copy-done.9) | copy-start | bytes 2359300
  46.8 21.0 %collective-permute-start.7 = (f32[32,16,128]{2,1,0:T(8,128)S(1)}, f32[32,16,128]{2,1,0:T(8,128)S(1)}, u32[]{:S(2)}, u32[]{:S(2)}) collective-permute-start(f32[32,16,128]{2,1,0:T(8,128)S(1)} %get-tuple-element.38.own), channel_id=1, source_target_pairs={{0,2},{1,3},{2,4},{3,5},{4,6},{5,7},{6,8},{7,9},{8,10},{9,11},{10,... | collective-permute-start | bytes 786440 | tf_op jit(solution)/shard_map/ppermute | solution.py:391
  55.5 12.3 %collective-permute-start.8 = (f32[32,16,128]{2,1,0:T(8,128)S(1)}, f32[32,16,128]{2,1,0:T(8,128)S(1)}, u32[]{:S(2)}, u32[]{:S(2)}) collective-permute-start(f32[32,16,128]{2,1,0:T(8,128)S(1)} %get-tuple-element.38.own), channel_id=1, source_target_pairs={{2,0},{3,1},{4,2},{5,3},{6,4},{7,5},{8,6},{9,7},{10,8},{11,9},{12,... | collective-permute-start | bytes 786440 | tf_op jit(solution)/shard_map/ppermute | solution.py:391
  56.9 1.2 %collective-permute-start.9 = (f32[24,128]{1,0:T(8,128)S(1)}, f32[24,128]{1,0:T(8,128)S(1)}, u32[]{:S(2)}, u32[]{:S(2)}) collective-permute-start(f32[24,128]{1,0:T(8,128)S(1)} %get-tuple-element.39), channel_id=1, source_target_pairs={{0,1},{1,0},{2,3},{3,2},{4,5},{5,4},{6,7},{7,6},{8,9},{9,8},{10,11... | collective-permute-start | bytes 36872 | tf_op jit(solution)/shard_map/ppermute | solution.py:445
  58.2 9.6 %collective-permute-start.10 = (f32[24,128]{1,0:T(8,128)S(1)}, f32[24,128]{1,0:T(8,128)S(1)}, u32[]{:S(2)}, u32[]{:S(2)}) collective-permute-start(f32[24,128]{1,0:T(8,128)S(1)} %add.66), channel_id=1, source_target_pairs={{0,12},{1,13},{2,14},{3,15},{4,8},{5,9},{6,10},{7,11},{8,4},{9,5},... | collective-permute-start | bytes 36872 | tf_op jit(solution)/shard_map/ppermute | solution.py:445
  62.7 5.0 %collective-permute-start.11 = (f32[24,128]{1,0:T(8,128)S(1)}, f32[24,128]{1,0:T(8,128)S(1)}, u32[]{:S(2)}, u32[]{:S(2)}) collective-permute-start(f32[24,128]{1,0:T(8,128)S(1)} %add.66), channel_id=1, source_target_pairs={{0,8},{1,9},{2,10},{3,11},{4,12},{5,13},{6,14},{7,15},{8,0},{9,1},... | collective-permute-start | bytes 36872 | tf_op jit(solution)/shard_map/ppermute | solution.py:445
  62.7 5.0 %collective-permute-start.12 = (f32[24,128]{1,0:T(8,128)S(1)}, f32[24,128]{1,0:T(8,128)S(1)}, u32[]{:S(2)}, u32[]{:S(2)}) collective-permute-start(f32[24,128]{1,0:T(8,128)S(1)} %add.66), channel_id=1, source_target_pairs={{0,4},{1,5},{2,6},{3,7},{4,0},{5,1},{6,2},{7,3},{8,12},{9,13},{10,... | collective-permute-start | bytes 36872 | tf_op jit(solution)/shard_map/ppermute | solution.py:445
  67.9 2.0 %collective-permute-start.13 = (f32[2,32,16,128]{3,2,1,0:T(8,128)S(1)}, f32[2,32,16,128]{3,2,1,0:T(8,128)S(1)}, u32[]{:S(2)}, u32[]{:S(2)}) collective-permute-start(f32[2,32,16,128]{3,2,1,0:T(8,128)S(1)} %pad_maximum_fusion.1), channel_id=1, source_target_pairs={{0,1},{1,0},{2,3},{3,2},{4,5},{5,4},{6,7},{7,6},{8,9},{9,8},{10,11... | collective-permute-start | bytes 1572872 | tf_op jit(solution)/shard_map/ppermute | solution.py:397
  67.9 11.1 %collective-permute-start.14 = (f32[24,128]{1,0:T(8,128)S(1)}, f32[24,128]{1,0:T(8,128)S(1)}, u32[]{:S(2)}, u32[]{:S(2)}) collective-permute-start(f32[24,128]{1,0:T(8,128)S(1)} %add_add_fusion.part), channel_id=1, source_target_pairs={{0,2},{1,3},{2,0},{3,1},{4,6},{5,7},{6,4},{7,5},{8,10},{9,11},{10,... | collective-permute-start | bytes 36872 | tf_op jit(solution)/shard_map/ppermute | solution.py:445
